TPU v7x, 32 devices: a whole 2x2x4 slice. The times are simulated.
32 devices in a mesh: cols: 32 (over z, y, x, core).
Axes of the slice: x: 2, y: 2, z: 4, core: 2. Of those that a mesh axis runs over, the one named last changes fastest.
Arguments:
- suction_initial: float32 [128, 16384], P(None, 'cols'), may hold values from -6 to 6
- warmth_initial: float32 [128, 16384], P(None, 'cols'), may hold values from -5 to 5
- soil_class: int32 [128, 16384], P(None, 'cols'), may hold values from 0 to 7
- top_boundary_warmth: float32 [16384], P('cols'), may hold values from -6 to 6
- neighbour_couplings: int32 [2, 128], replicated, may hold values from 0 to 1
- k_sat: float32 [8], replicated, may hold values from 0.1 to 1
- heat_cond: float32 [8], replicated, may hold values from 0.5 to 2
Outputs:
- suction_iterated: float32 [128, 16384], P(None, 'cols')
- warmth_iterated: float32 [128, 16384], P(None, 'cols')
All inputs are finite; a program needn't handle non-finite values.
Results may differ from a plain program's by a relative error of at most 0.000066.
Values sent between devices are 32-bit elements; how exact they have to be, the bound alone decides.
No kernel may reach another device: no remote copies, remote signals or barrier semaphores. Data moves between devices by JAX's collectives and lax.ppermute only.
A program may use at most 128 MiB of HBM per device.

v0:
```python
import functools

import jax
import jax.numpy as jnp
from jax import lax
from jax.experimental import pallas as pl
from jax.experimental.pallas import tpu as pltpu
from jax.sharding import PartitionSpec as P

SPAN = 256
ITERS = 2
PAIR_DEV = 4
LANES = 128
PARTS = 8
VMEM_LIMIT = 48 * 1024 * 1024


def shift_down(value, steps):
    return pltpu.roll(value, steps, axis=0)


def shift_up(value, steps):
    return pltpu.roll(value, PARTS - steps, axis=0)


def pack_kernel(suction, warmth, classes, top, out):
    n, _, w, cells = out.shape
    fields = (suction[...], warmth[...], classes[...].astype(jnp.float32))
    for f, field in enumerate(fields):
        turned = field.T
        for b in range(2):
            out[:, 2 * f + b] = turned[b * SPAN : (b + 1) * SPAN].reshape(n, w, cells)
    surface = jnp.concatenate(
        [top[0:1, :SPAN], top[0:1, SPAN:], jnp.zeros((cells - 2, SPAN), jnp.float32)], axis=0
    )
    out[:, 6] = surface.T.reshape(n, w, cells)


def unpack_kernel(got, suction, warmth):
    n, _, w, cells = got.shape
    for f, out in enumerate((suction, warmth)):
        for b in range(2):
            out[:, b * SPAN : (b + 1) * SPAN] = got[:, 2 * f + b].reshape(n * w, cells).T


def solve(rows, steps, matrix, ratio, lead, value, update):
    c_prev = a_prev = d_prev = None
    for j in range(steps):
        above, main, below, source = matrix(j)
        if j == 0:
            r = 1.0 / main
            a_prev = above * r
            d_prev = source * r
        else:
            r = 1.0 / (main - above * c_prev)
            over = above * r
            a_prev = a_prev * over
            d_prev = source * r + d_prev * over
        c_prev = below * r
        ratio[j] = c_prev
        lead[j] = a_prev
        value[j] = d_prev
    last_c, last_a, last_d = c_prev, a_prev, d_prev
    p_first, a_first, d_first = ratio[steps - 2], lead[steps - 2], value[steps - 2]
    for j in range(steps - 3, -1, -1):
        c = ratio[j]
        p_first = c * p_first
        a_first = lead[j] + c * a_first
        d_first = value[j] + c * d_first
    g = 1.0 / (1.0 - last_c * shift_up(a_first, 1))
    up = last_c * shift_up(p_first, 1) * g
    down = last_a * g
    own = (last_d + last_c * shift_up(d_first, 1)) * g
    step = 1
    while step < PARTS:
        g = 1.0 / (1.0 - up * shift_up(down, step) - down * shift_down(up, step))
        own = (own + up * shift_up(own, step) + down * shift_down(own, step)) * g
        up = up * shift_up(up, step) * g
        down = down * shift_down(down, step) * g
        step *= 2
    over = shift_down(own, 1)
    x = own
    update(steps - 1, x)
    for j in range(steps - 2, -1, -1):
        x = ratio[j] * x + (lead[j] * over + value[j])
        update(j, x)


def step_kernel(
    n, w, got, couplings, k_sat, heat_cond, out,
    head, warm, perm, conduct, stored, energy, wet, melt, cond, water, heat, ratio, lead, value, load,
):
    kn, _, kw, cells = got.shape
    half = n * w
    width = 2 * half
    steps = cells // PARTS

    def take(field, target, change):
        for b in range(2):
            turned = got[:, 2 * field + b].reshape(half, cells).T
            for q in range(half // LANES):
                load[2 * b + q] = turned[:, q * LANES : (q + 1) * LANES]
        for j in range(steps):
            for q in range(width // LANES):
                change(j, slice(q * LANES, (q + 1) * LANES), load[q, pl.ds(j, PARTS, stride=steps), :])

    def take_head(j, lanes, v):
        head[j, :, lanes] = v

    def take_warm(j, lanes, v):
        warm[j, :, lanes] = v

    def take_class(j, lanes, v):
        k = jnp.full_like(v, k_sat[0])
        lam = jnp.full_like(v, heat_cond[0])
        for c in range(1, k_sat.shape[0]):
            here = v >= c
            k = jnp.where(here, k_sat[c], k)
            lam = jnp.where(here, heat_cond[c], lam)
        perm[j, :, lanes] = k
        conduct[j, :, lanes] = lam

    take(0, head, take_head)
    take(1, warm, take_warm)
    take(2, perm, take_class)
    surface = got[:, 6].reshape(half, cells).T[0:2]
    top = jnp.concatenate([surface[0:1], surface[1:2]], axis=1)

    pair_rows = couplings[...].astype(jnp.float32)
    lane_dev = lax.broadcasted_iota(jnp.int32, (couplings.shape[1], half), 1) // w
    pair_id = lax.broadcasted_iota(jnp.int32, (couplings.shape[1], half), 0)
    dev = lax.broadcasted_iota(jnp.int32, (PARTS, half), 1) // w
    chosen = []
    for s in range(1, PAIR_DEV + 1):
        upper_at = (pair_id == lane_dev * PAIR_DEV + s - 1).astype(jnp.float32)
        lower_at = (pair_id == (lane_dev - s) * PAIR_DEV + s - 1).astype(jnp.float32)
        upper = jnp.dot(pair_rows, upper_at, preferred_element_type=jnp.float32)[0:1]
        lower = jnp.dot(pair_rows, lower_at, preferred_element_type=jnp.float32)[1:2]
        upper = jnp.broadcast_to(upper, (PARTS, half)) > 0.5
        lower = jnp.broadcast_to(lower, (PARTS, half)) > 0.5
        scale = jnp.where(dev + s < n, 0.25, 0.0)
        chosen.append((upper, lower, scale))

    first_part = lax.broadcasted_iota(jnp.int32, (PARTS, width), 0) == 0
    last_part = lax.broadcasted_iota(jnp.int32, (PARTS, width), 0) == PARTS - 1

    for j in range(steps):
        h, t = head[j], warm[j]
        s0 = jax.nn.sigmoid(h)
        f0 = jax.nn.sigmoid(2.0 * t)
        m0 = 0.05 + 0.4 * s0
        wet[j] = s0
        stored[j] = s0
        energy[j] = (1.0 + 2.0 * m0) * t + 2.0 * m0 * f0

    def lateral(j, _):
        h, t, c = head[j], warm[j], cond[j]
        h0, h1 = h[:, :half], h[:, half:]
        t0, t1 = t[:, :half], t[:, half:]
        c0, c1 = c[:, :half], c[:, half:]
        zero = jnp.zeros((PARTS, half), jnp.float32)
        w0, w1, q0, q1 = zero, zero, zero, zero
        for s in range(1, PAIR_DEV + 1):
            upper, lower, scale = chosen[s - 1]
            back = half - s * w
            h_low = pltpu.roll(jnp.where(lower, h1, h0), back, axis=1)
            t_low = pltpu.roll(jnp.where(lower, t1, t0), back, axis=1)
            c_low = pltpu.roll(jnp.where(lower, c1, c0), back, axis=1)
            flow = (
                scale
                * (jnp.where(upper, c1, c0) + c_low)
                * (jnp.where(upper, h1, h0) - h_low + 0.5)
            )
            carried = flow * jnp.where(flow > 0.0, jnp.where(upper, t1, t0), t_low)
            flow_in = pltpu.roll(flow, s * w, axis=1)
            carried_in = pltpu.roll(carried, s * w, axis=1)
            w0 = w0 - jnp.where(upper, 0.0, flow) + jnp.where(lower, 0.0, flow_in)
            w1 = w1 - jnp.where(upper, flow, 0.0) + jnp.where(lower, flow_in, 0.0)
            q0 = q0 - jnp.where(upper, 0.0, carried) + jnp.where(lower, 0.0, carried_in)
            q1 = q1 - jnp.where(upper, carried, 0.0) + jnp.where(lower, carried_in, 0.0)
        water[j, :, :half] = w0
        water[j, :, half:] = w1
        heat[j, :, :half] = 2.0 * q0
        heat[j, :, half:] = 2.0 * q1
        return 0

    def iteration(_, carry):
        for j in range(steps):
            s, f = wet[j], jax.nn.sigmoid(2.0 * warm[j])
            melt[j] = f
            cond[j] = perm[j] * (f * s * s + 0.02)
        lax.fori_loop(0, steps, lateral, 0)

        def faces(field, potential):
            face_of, flux_of = [], []
            for j in range(steps):
                if j + 1 < steps:
                    c_next, h_next = field(j + 1), potential(j + 1)
                    face = 0.5 * (field(j) + c_next)
                else:
                    c_next, h_next = shift_up(field(0), 1), shift_up(potential(0), 1)
                    face = jnp.where(last_part, 0.0, 0.5 * (field(j) + c_next))
                face_of.append(face)
                flux_of.append(h_next - potential(j))
            return face_of, flux_of

        k_face, rise = faces(lambda j: cond[j], lambda j: head[j])
        k_top = jnp.where(first_part, 0.0, shift_down(k_face[-1], 1))
        q_face = [k * (1.0 - d) for k, d in zip(k_face, rise)]
        q_top = jnp.where(first_part, 0.0, shift_down(q_face[-1], 1))

        def water_matrix(j):
            above = k_top if j == 0 else k_face[j - 1]
            into = q_top if j == 0 else q_face[j - 1]
            s = wet[j]
            main = 0.8 * s * (1.0 - s) + 0.02 + above + k_face[j]
            source = water[j] + into - q_face[j] - 2.0 * (0.4 * (s - stored[j]))
            return above, main, k_face[j], source

        def water_done(j, x):
            h = head[j] + x
            head[j] = h
            wet[j] = jax.nn.sigmoid(h)

        solve(cells, steps, water_matrix, ratio, lead, value, water_done)

        l_face, drop = faces(lambda j: conduct[j] * (1.5 - 0.5 * melt[j]), lambda j: warm[j])
        l_top = jnp.where(first_part, 0.0, shift_down(l_face[-1], 1))
        g_face = [-l * d for l, d in zip(l_face, drop)]
        g_top = jnp.where(first_part, 0.0, shift_down(g_face[-1], 1))
        surface_lam = jnp.where(first_part, 2.0 * conduct[0] * (1.5 - 0.5 * melt[0]), 0.0)

        def heat_matrix(j):
            above = l_top if j == 0 else l_face[j - 1]
            into = g_top if j == 0 else g_face[j - 1]
            t, f = warm[j], melt[j]
            m = 0.05 + 0.4 * wet[j]
            now = (1.0 + 2.0 * m) * t + 2.0 * m * f
            main = 2.0 * (1.0 + 2.0 * m + 4.0 * m * f * (1.0 - f)) + above + l_face[j]
            source = heat[j] + into - g_face[j] - 2.0 * (now - energy[j])
            if j == 0:
                main = main + surface_lam
                source = source + surface_lam * (top - t)
            return above, main, l_face[j], source

        def heat_done(j, x):
            warm[j] = warm[j] + x

        solve(cells, steps, heat_matrix, ratio, lead, value, heat_done)
        return carry

    lax.fori_loop(0, ITERS, iteration, 0)

    for f, field in enumerate((head, warm)):
        for j in range(steps):
            for q in range(width // LANES):
                load[q, pl.ds(j, PARTS, stride=steps), :] = field[j, :, q * LANES : (q + 1) * LANES]
        for b in range(2):
            turned = jnp.concatenate([load[2 * b + q] for q in range(half // LANES)], axis=1).T
            out[:, 2 * f + b] = turned.reshape(kn, kw, cells)


def whole(memory=pltpu.VMEM):
    return pl.BlockSpec(memory_space=memory)


def exchange(chunks):
    return lax.all_to_all(chunks, "cols", split_axis=0, concat_axis=0, tiled=True)


def on_device(suction, warmth, classes, top, couplings, k_sat, heat_cond):
    n = lax.axis_size("cols")
    cells, width = suction.shape
    w = SPAN // n
    steps = cells // PARTS
    params = pltpu.CompilerParams(vmem_limit_bytes=VMEM_LIMIT)
    f32 = jnp.float32

    fit = w % 8 == 0
    kn, kw = (n, w) if fit else (SPAN // 8, 8)

    def to_chunks(a):
        if fit:
            return a
        fields = a.shape[1]
        return jnp.moveaxis(jnp.moveaxis(a, 1, 0).reshape(fields, n, w, cells), 0, 1)

    def from_chunks(a):
        if fit:
            return a
        fields = a.shape[1]
        return jnp.moveaxis(jnp.moveaxis(a, 1, 0).reshape(fields, kn, kw, cells), 0, 1)

    packed = pl.pallas_call(
        pack_kernel,
        out_shape=jax.ShapeDtypeStruct((kn, 7, kw, cells), f32),
        in_specs=[whole()] * 4,
        out_specs=whole(),
        compiler_params=params,
        name="pack",
    )(suction, warmth, classes, top.reshape(1, width))
    got = from_chunks(exchange(to_chunks(packed)))

    padded = jnp.zeros((8, couplings.shape[1]), couplings.dtype).at[:2].set(couplings)
    column = pltpu.VMEM((steps, PARTS, width), f32)
    solved = pl.pallas_call(
        functools.partial(step_kernel, n, w),
        out_shape=jax.ShapeDtypeStruct((kn, 4, kw, cells), f32),
        in_specs=[whole(), whole(), whole(pltpu.SMEM), whole(pltpu.SMEM)],
        out_specs=whole(),
        scratch_shapes=[column] * 14 + [pltpu.VMEM((width // LANES, cells, LANES), f32)],
        compiler_params=params,
        name="steps",
    )(got, padded, k_sat, heat_cond)
    back = from_chunks(exchange(to_chunks(solved)))
    return pl.pallas_call(
        unpack_kernel,
        out_shape=(jax.ShapeDtypeStruct((cells, width), f32),) * 2,
        in_specs=[whole()],
        out_specs=(whole(), whole()),
        compiler_params=params,
        name="unpack",
    )(back)


def solution(mesh):
    placed = (P(None, "cols"), P(None, "cols"), P(None, "cols"), P("cols"), P(), P(), P())
    return jax.shard_map(
        on_device,
        mesh=mesh,
        in_specs=placed,
        out_specs=(P(None, "cols"), P(None, "cols")),
        check_vma=False,
    )
```

profile of v0, /device:TPU:0, one launch (start us, length us, event | category | flops | bytes accessed | tf_op | source)
XLA Modules:
  0.0 64.9 jit_solution(6531299299515569946)
XLA Ops:
  0.6 0.0 copy-start
  0.6 0.9 %copy-done = f32[128,512]{1,0:T(8,128)S(1)} copy-done((f32[128,512]{1,0:T(8,128)S(1)}, f32[128,512]{1,0:T(8,128)}, u32[]{:S(2)}) %copy-start) | copy-done | bytes 262168
  1.6 0.0 copy-start.1
  1.6 0.9 %copy-done.1 = f32[128,512]{1,0:T(8,128)S(1)} copy-done((f32[128,512]{1,0:T(8,128)S(1)}, f32[128,512]{1,0:T(8,128)}, u32[]{:S(2)}) %copy-start.1) | copy-done | bytes 262168
  2.5 0.0 copy-start.2
  2.5 0.9 %copy-done.2 = s32[128,512]{1,0:T(8,128)S(1)} copy-done((s32[128,512]{1,0:T(8,128)S(1)}, s32[128,512]{1,0:T(8,128)}, u32[]{:S(2)}) %copy-start.2) | copy-done | bytes 262168
  3.5 0.0 copy-start.3
  3.5 0.7 %copy-done.3 = f32[512]{0:T(512)S(1)} copy-done((f32[512]{0:T(512)S(1)}, f32[512]{0:T(512)}, u32[]{:S(2)}) %copy-start.3) | copy-done | bytes 2072
  4.2 1.2 %pack.1 = f32[32,7,8,128]{3,2,1,0:T(8,128)} custom-call(f32[128,512]{1,0:T(8,128)S(1)} %copy-done, f32[128,512]{1,0:T(8,128)S(1)} %copy-done.1, s32[128,512]{1,0:T(8,128)S(1)} %copy-done.2, f32[1,512]{1,0:T(1,128)S(1)} %bitcast.1), custom_call_target="tpu_custom_call" | custom-call | tf_op jit(solution)/shard_map/pack/pallas_call | solution.py:294
  5.4 0.0 copy-start.6
  5.4 7.3 %all-to-all-start = ((f32[32,7,8,128]{3,2,1,0:T(8,128)}), f32[32,7,8,128]{3,2,1,0:T(8,128)S(1)}, u32[]{:S(2)}, u32[]{:S(2)}) async-start(f32[32,7,8,128]{3,2,1,0:T(8,128)} %pack.1), calls=%async_computation | async-start | bytes 1835008 | tf_op jit(solution)/shard_map/all_to_all | solution.py:268
  12.7 0.0 copy-done.6
  12.7 0.0 copy-start.4
  12.7 0.0 copy-start.5
  12.8 23.4 %all-to-all-done.got = f32[32,7,8,128]{3,2,1,0:T(8,128)S(1)} async-done(((f32[32,7,8,128]{3,2,1,0:T(8,128)}), f32[32,7,8,128]{3,2,1,0:T(8,128)S(1)}, u32[]{:S(2)}, u32[]{:S(2)}) %all-to-all-start) | async-done | bytes 917536 | tf_op jit(solution)/shard_map/all_to_all | solution.py:268
  36.1 0.0 copy-done.4
  36.1 0.0 copy-done.5
  36.1 8.9 %steps.1 = f32[32,4,8,128]{3,2,1,0:T(8,128)S(1)} custom-call(f32[32,7,8,128]{3,2,1,0:T(8,128)S(1)} %all-to-all-done.got, s32[8,128]{1,0:T(8,128)S(1)} %scatter.4.couplings, f32[8]{0:T(128)S(1)} %copy-done.4, f32[8]{0:T(128)S(1)} %copy-done.5), custom_call_target="tpu_custom_call" | custom-call | tf_op jit(solution)/shard_map/steps/pallas_call | solution.py:306
  45.0 19.0 %all_to_all.10.got = f32[32,4,8,128]{3,2,1,0:T(8,128)S(1)} all-to-all(f32[32,4,8,128]{3,2,1,0:T(8,128)S(1)} %steps.1), channel_id=1, replica_groups=mesh['cols'=32] {'cols'}, dimensions={0} | all-to-all | bytes 1048576 | tf_op jit(solution)/shard_map/all_to_all | solution.py:268
  64.0 0.9 %unpack.1 = (f32[128,512]{1,0:T(8,128)}, f32[128,512]{1,0:T(8,128)}) custom-call(f32[32,4,8,128]{3,2,1,0:T(8,128)S(1)} %all_to_all.10.got), custom_call_target="tpu_custom_call" | custom-call | tf_op jit(solution)/shard_map/unpack/pallas_call | solution.py:316
  (1 shorter events, 0.0 us)
Async XLA Ops:
  0.6 1.0 %copy-start = (f32[128,512]{1,0:T(8,128)S(1)}, f32[128,512]{1,0:T(8,128)}, u32[]{:S(2)}) copy-start(f32[128,512]{1,0:T(8,128)} %suction.1) | copy-start | bytes 786436
  1.6 0.9 %copy-start.1 = (f32[128,512]{1,0:T(8,128)S(1)}, f32[128,512]{1,0:T(8,128)}, u32[]{:S(2)}) copy-start(f32[128,512]{1,0:T(8,128)} %warmth.1) | copy-start | bytes 786436
  2.5 0.9 %copy-start.2 = (s32[128,512]{1,0:T(8,128)S(1)}, s32[128,512]{1,0:T(8,128)}, u32[]{:S(2)}) copy-start(s32[128,512]{1,0:T(8,128)} %classes.1) | copy-start | bytes 786436
  3.5 0.7 %copy-start.3 = (f32[512]{0:T(512)S(1)}, f32[512]{0:T(512)}, u32[]{:S(2)}) copy-start(f32[512]{0:T(512)} %param.12) | copy-start | bytes 6148
  5.4 7.3 %copy-start.6 = (s32[2,128]{1,0:T(2,128)S(1)}, s32[2,128]{1,0:T(2,128)}, u32[]{:S(2)}) copy-start(s32[2,128]{1,0:T(2,128)} %param.13) | copy-start | bytes 3076
  5.4 30.7 %all-to-all-start = ((f32[32,7,8,128]{3,2,1,0:T(8,128)}), f32[32,7,8,128]{3,2,1,0:T(8,128)S(1)}, u32[]{:S(2)}, u32[]{:S(2)}) async-start(f32[32,7,8,128]{3,2,1,0:T(8,128)} %pack.1), calls=%async_computation | async-start | bytes 1835008 | tf_op jit(solution)/shard_map/all_to_all | solution.py:268
  12.7 23.4 %copy-start.4 = (f32[8]{0:T(128)S(1)}, f32[8]{0:T(128)}, u32[]{:S(2)}) copy-start(f32[8]{0:T(128)} %k_sat.1) | copy-start | bytes 100
  12.7 23.4 %copy-start.5 = (f32[8]{0:T(128)S(1)}, f32[8]{0:T(128)}, u32[]{:S(2)}) copy-start(f32[8]{0:T(128)} %heat_cond.1) | copy-start | bytes 100
where the time goes:
time: 65.3 us; the launch traced here: 64.9 us
  waiting for transfers between devices  23.4 us (36%)
  blocking collectives  19 us (29%)
  Pallas kernels  11.1 us (17%)
  starting transfers between devices  7.3 us (11%)
  local copies, waits for them, and re-layouts  3.54 us (5%)
  between operations  0.69 us (1%)
    all_to_all x1, waiting for transfers between devices, exchange(): lax.all_to_all(chunks, 'cols', split_axis=0, concat_axis=0, tiled=True)  23.4 us
    all_to_all x1, blocking collectives, exchange(): lax.all_to_all(chunks, 'cols', split_axis=0, concat_axis=0, tiled=True)  19 us
    pallas_call x1, Pallas kernels, on_device(): pl.pallas_call(functools.partial(step_kernel, n, w), out_shape=jax.ShapeD...  8.89 us
    all_to_all x1, starting transfers between devices, exchange(): lax.all_to_all(chunks, 'cols', split_axis=0, concat_axis=0, tiled=True)  7.3 us
    unnamed x14, local copies, waits for them, and re-layouts  3.54 us
  transfers between devices with their start and end apart: 1, of which 1 were waited for; matrix products, arithmetic and copies ran while one was open for 0% of the time, Pallas kernels for 0%

commit v1 on v0

v1 whole, which is shorter than its diff:
```python
import functools

import jax
import jax.numpy as jnp
from jax import lax
from jax.experimental import pallas as pl
from jax.experimental.pallas import tpu as pltpu
from jax.sharding import PartitionSpec as P

SPAN = 256
ITERS = 2
PAIR_DEV = 4
LANES = 128
CHUNKS = SPAN // LANES
SUB = 8
ROWS = SUB // 2
TILES = LANES // ROWS
GROUPS = 2
WIDTH = 2 * LANES
VMEM_LIMIT = 48 * 1024 * 1024


def regroup(first, second):
    upper = lax.broadcasted_iota(jnp.int32, first.shape, 1) < ROWS
    return (
        jnp.where(upper, first, pltpu.roll(second, ROWS, axis=1)),
        jnp.where(upper, pltpu.roll(first, ROWS, axis=1), second),
    )


def pack_kernel(chunk, suction, warmth, classes, out, room, class_room, sems):
    cells = suction.shape[0]
    copies = []
    for f, field in enumerate((suction, warmth, classes)):
        for b in range(2):
            here = pl.ds(b * SPAN + chunk * LANES, LANES)
            target = class_room.at[b] if f == 2 else room.at[f, b]
            copy = pltpu.make_async_copy(field.at[:, here], target, sems.at[f, b])
            copy.start()
            copies.append(copy)
    for f in range(3):
        turned = []
        for b in range(2):
            copies[2 * f + b].wait()
            value = class_room[b].astype(jnp.float32) if f == 2 else room[f, b]
            turned.append(value.T.reshape(TILES // 2, SUB, cells))
        even, odd = regroup(*turned)
        for m in range(TILES // 2):
            out[2 * m, f] = even[m]
            out[2 * m + 1, f] = odd[m]


def columns_of(tiles, field, cells):
    even = jnp.stack([tiles[2 * m, field] for m in range(TILES // 2)])
    odd = jnp.stack([tiles[2 * m + 1, field] for m in range(TILES // 2)])
    return [v.reshape(LANES, cells).T for v in regroup(even, odd)]


def unpack_kernel(*refs):
    chunks, (suction, warmth) = refs[:CHUNKS], refs[CHUNKS:]
    cells = suction.shape[0]
    for f, out in enumerate((suction, warmth)):
        for c, chunk in enumerate(chunks):
            for b, value in enumerate(columns_of(chunk, f, cells)):
                out[:, b * SPAN + c * LANES : b * SPAN + (c + 1) * LANES] = value


def reciprocal(x):
    r = pl.reciprocal(x, approx=True)
    return r * (2.0 - x * r)


def sigmoid(x):
    return 0.5 + 0.5 * jnp.tanh(0.5 * x)


def following(value):
    first, second = value[:, :WIDTH], value[:, WIDTH:]
    return jnp.concatenate([second, pltpu.roll(first, SUB - 1, axis=0)], axis=1)


def preceding(value):
    first, second = value[:, :WIDTH], value[:, WIDTH:]
    return jnp.concatenate([pltpu.roll(second, 1, axis=0), first], axis=1)


def solve(steps, matrix, ratio, lead, value, update):
    c_prev = a_prev = d_prev = None
    for j in range(steps):
        above, main, below, source = matrix(j)
        if j == 0:
            r = reciprocal(main)
            a_prev = above * r
            d_prev = source * r
        else:
            r = reciprocal(main - above * c_prev)
            over = above * r
            a_prev = a_prev * over
            d_prev = source * r + d_prev * over
        c_prev = below * r
        ratio[j] = c_prev
        lead[j] = a_prev
        value[j] = d_prev
    last_c, last_a, last_d = c_prev, a_prev, d_prev
    p_first, a_first, d_first = ratio[steps - 2], lead[steps - 2], value[steps - 2]
    for j in range(steps - 3, -1, -1):
        c = ratio[j]
        p_first = c * p_first
        a_first = lead[j] + c * a_first
        d_first = value[j] + c * d_first
    g = reciprocal(1.0 - last_c * following(a_first))
    up = last_c * following(p_first) * g
    down = last_a * g
    own = (last_d + last_c * following(d_first)) * g
    step = 0
    while step < SUB:
        if step == 0:
            after, before = following, preceding
        else:
            after = functools.partial(pltpu.roll, shift=SUB - step, axis=0)
            before = functools.partial(pltpu.roll, shift=step, axis=0)
        g = reciprocal(1.0 - up * after(down) - down * before(up))
        own = (own + up * after(own) + down * before(own)) * g
        up = up * after(up) * g
        down = down * before(down) * g
        step = max(1, 2 * step)
    over = preceding(own)
    x = own
    update(steps - 1, x)
    for j in range(steps - 2, -1, -1):
        x = ratio[j] * x + (lead[j] * over + value[j])
        update(j, x)


def step_kernel(
    n, w, chunk, got, surface, couplings, k_sat, heat_cond, out,
    head, warm, perm, conduct, stored, energy, wet, melt, cond, water, heat, ratio, lead, value, load,
):
    cells = got.shape[-1]
    steps = cells // (SUB * GROUPS)
    stride = steps * GROUPS

    def lanes_of(g, b):
        return slice((g * 2 + b) * LANES, (g * 2 + b + 1) * LANES)

    def take(field, change):
        for b, turned in enumerate(columns_of(got, field, cells)):
            load[b] = turned
            for j in range(steps):
                for g in range(GROUPS):
                    change(j, lanes_of(g, b), load[b, pl.ds(g * steps + j, SUB, stride=stride), :])

    def take_head(j, lanes, v):
        head[j, :, lanes] = v

    def take_warm(j, lanes, v):
        warm[j, :, lanes] = v

    def take_class(j, lanes, v):
        k = jnp.full_like(v, k_sat[0])
        lam = jnp.full_like(v, heat_cond[0])
        for c in range(1, k_sat.shape[0]):
            here = v >= c
            k = jnp.where(here, k_sat[c], k)
            lam = jnp.where(here, heat_cond[c], lam)
        perm[j, :, lanes] = k
        conduct[j, :, lanes] = lam

    take(0, take_head)
    take(1, take_warm)
    take(2, take_class)

    me = lax.axis_index("cols")
    lane_dev = lax.broadcasted_iota(jnp.int32, (n, LANES), 1) // w
    row_dev = lax.broadcasted_iota(jnp.int32, (n, LANES), 0)
    tops = []
    for b in range(2):
        rows = surface[:, b * SPAN + chunk * LANES : b * SPAN + (chunk + 1) * LANES]
        rows = jnp.where(lane_dev == me, rows, 0.0)
        reach = w
        while reach < LANES:
            rows = rows + pltpu.roll(rows, reach, axis=1)
            reach *= 2
        tops.append(jnp.sum(jnp.where(row_dev == lane_dev, rows, 0.0), axis=0, keepdims=True))
    top = jnp.concatenate(tops * GROUPS, axis=1)

    pair_rows = couplings[...].astype(jnp.float32)
    pairs = couplings.shape[1]
    pair_dev = lax.broadcasted_iota(jnp.int32, (pairs, LANES), 1) // w
    pair_id = lax.broadcasted_iota(jnp.int32, (pairs, LANES), 0)
    dev = lax.broadcasted_iota(jnp.int32, (SUB, LANES), 1) // w
    chosen = []
    for s in range(1, PAIR_DEV + 1):
        upper_at = (pair_id == pair_dev * PAIR_DEV + s - 1).astype(jnp.float32)
        lower_at = (pair_id == (pair_dev - s) * PAIR_DEV + s - 1).astype(jnp.float32)
        upper = jnp.dot(pair_rows, upper_at, preferred_element_type=jnp.float32)[0:1]
        lower = jnp.dot(pair_rows, lower_at, preferred_element_type=jnp.float32)[1:2]
        upper = jnp.broadcast_to(upper, (SUB, LANES)) > 0.5
        lower = jnp.broadcast_to(lower, (SUB, LANES)) > 0.5
        scale = jnp.where(dev + s < n, 0.25, 0.0)
        chosen.append((upper, lower, scale))

    part = lax.broadcasted_iota(jnp.int32, (SUB, GROUPS * WIDTH), 0)
    group = lax.broadcasted_iota(jnp.int32, (SUB, GROUPS * WIDTH), 1) // WIDTH
    first_part = jnp.logical_and(part == 0, group == 0)
    last_part = jnp.logical_and(part == SUB - 1, group == GROUPS - 1)

    for j in range(steps):
        h, t = head[j], warm[j]
        s0 = sigmoid(h)
        f0 = sigmoid(2.0 * t)
        m0 = 0.05 + 0.4 * s0
        wet[j] = s0
        stored[j] = s0
        energy[j] = (1.0 + 2.0 * m0) * t + 2.0 * m0 * f0

    def lateral(j, _):
        for g in range(GROUPS):
            l0, l1 = lanes_of(g, 0), lanes_of(g, 1)
            h0, h1 = head[j, :, l0], head[j, :, l1]
            t0, t1 = warm[j, :, l0], warm[j, :, l1]
            c0, c1 = cond[j, :, l0], cond[j, :, l1]
            zero = jnp.zeros((SUB, LANES), jnp.float32)
            w0, w1, q0, q1 = zero, zero, zero, zero
            for s in range(1, PAIR_DEV + 1):
                upper, lower, scale = chosen[s - 1]
                back = LANES - s * w
                h_low = pltpu.roll(jnp.where(lower, h1, h0), back, axis=1)
                t_low = pltpu.roll(jnp.where(lower, t1, t0), back, axis=1)
                c_low = pltpu.roll(jnp.where(lower, c1, c0), back, axis=1)
                flow = (
                    scale
                    * (jnp.where(upper, c1, c0) + c_low)
                    * (jnp.where(upper, h1, h0) - h_low + 0.5)
                )
                carried = flow * jnp.where(flow > 0.0, jnp.where(upper, t1, t0), t_low)
                flow_in = pltpu.roll(flow, s * w, axis=1)
                carried_in = pltpu.roll(carried, s * w, axis=1)
                w0 = w0 - jnp.where(upper, 0.0, flow) + jnp.where(lower, 0.0, flow_in)
                w1 = w1 - jnp.where(upper, flow, 0.0) + jnp.where(lower, flow_in, 0.0)
                q0 = q0 - jnp.where(upper, 0.0, carried) + jnp.where(lower, 0.0, carried_in)
                q1 = q1 - jnp.where(upper, carried, 0.0) + jnp.where(lower, carried_in, 0.0)
            water[j, :, l0] = w0
            water[j, :, l1] = w1
            heat[j, :, l0] = 2.0 * q0
            heat[j, :, l1] = 2.0 * q1
        return 0

    def faces(field, potential):
        face_of, rise_of = [], []
        for j in range(steps):
            if j + 1 < steps:
                c_next, v_next = field(j + 1), potential(j + 1)
                face = 0.5 * (field(j) + c_next)
            else:
                c_next, v_next = following(field(0)), following(potential(0))
                face = jnp.where(last_part, 0.0, 0.5 * (field(j) + c_next))
            face_of.append(face)
            rise_of.append(v_next - potential(j))
        return face_of, rise_of

    def iteration(_, carry):
        for j in range(steps):
            s, f = wet[j], sigmoid(2.0 * warm[j])
            melt[j] = f
            cond[j] = perm[j] * (f * s * s + 0.02)
        lax.fori_loop(0, steps, lateral, 0)

        k_face, rise = faces(lambda j: cond[j], lambda j: head[j])
        k_top = jnp.where(first_part, 0.0, preceding(k_face[-1]))
        q_face = [k * (1.0 - d) for k, d in zip(k_face, rise)]
        q_top = jnp.where(first_part, 0.0, preceding(q_face[-1]))

        def water_matrix(j):
            above = k_top if j == 0 else k_face[j - 1]
            into = q_top if j == 0 else q_face[j - 1]
            s = wet[j]
            main = 0.8 * s * (1.0 - s) + 0.02 + above + k_face[j]
            source = water[j] + into - q_face[j] - 0.8 * (s - stored[j])
            return above, main, k_face[j], source

        def water_done(j, x):
            h = head[j] + x
            head[j] = h
            wet[j] = sigmoid(h)

        solve(steps, water_matrix, ratio, lead, value, water_done)

        l_face, rise = faces(lambda j: conduct[j] * (1.5 - 0.5 * melt[j]), lambda j: warm[j])
        l_top = jnp.where(first_part, 0.0, preceding(l_face[-1]))
        g_face = [-l * d for l, d in zip(l_face, rise)]
        g_top = jnp.where(first_part, 0.0, preceding(g_face[-1]))
        surface_lam = jnp.where(first_part, 2.0 * conduct[0] * (1.5 - 0.5 * melt[0]), 0.0)

        def heat_matrix(j):
            above = l_top if j == 0 else l_face[j - 1]
            into = g_top if j == 0 else g_face[j - 1]
            t, f = warm[j], melt[j]
            m = 0.05 + 0.4 * wet[j]
            now = (1.0 + 2.0 * m) * t + 2.0 * m * f
            main = 2.0 * (1.0 + 2.0 * m + 4.0 * m * f * (1.0 - f)) + above + l_face[j]
            source = heat[j] + into - g_face[j] - 2.0 * (now - energy[j])
            if j == 0:
                main = main + surface_lam
                source = source + surface_lam * (top - t)
            return above, main, l_face[j], source

        def heat_done(j, x):
            warm[j] = warm[j] + x

        solve(steps, heat_matrix, ratio, lead, value, heat_done)
        return carry

    lax.fori_loop(0, ITERS, iteration, 0)

    for f, field in enumerate((head, warm)):
        turned = []
        for b in range(2):
            for j in range(steps):
                for g in range(GROUPS):
                    load[b, pl.ds(g * steps + j, SUB, stride=stride), :] = field[j, :, lanes_of(g, b)]
            turned.append(load[b].T.reshape(TILES // 2, SUB, cells))
        even, odd = regroup(*turned)
        for m in range(TILES // 2):
            out[2 * m, f] = even[m]
            out[2 * m + 1, f] = odd[m]


def whole(memory=pltpu.VMEM):
    return pl.BlockSpec(memory_space=memory)


def exchange(tiles, n):
    w = LANES // n
    _, fields, _, cells = tiles.shape
    if w != ROWS:
        tiles = tiles.reshape(TILES, fields, 2, ROWS, cells).transpose(1, 2, 0, 3, 4)
        tiles = tiles.reshape(fields, 2, n, w, cells).transpose(2, 0, 1, 3, 4)
    tiles = lax.all_to_all(tiles, "cols", split_axis=0, concat_axis=0, tiled=True)
    if w != ROWS:
        tiles = tiles.transpose(1, 2, 0, 3, 4).reshape(fields, 2, TILES, ROWS, cells)
        tiles = tiles.transpose(2, 0, 1, 3, 4).reshape(TILES, fields, SUB, cells)
    return tiles


def on_device(suction, warmth, classes, top, couplings, k_sat, heat_cond):
    n = lax.axis_size("cols")
    cells, width = suction.shape
    w = LANES // n
    steps = cells // (SUB * GROUPS)
    params = pltpu.CompilerParams(vmem_limit_bytes=VMEM_LIMIT)
    f32 = jnp.float32

    surface = lax.all_gather(top, "cols")
    got = []
    for c in range(CHUNKS):
        packed = pl.pallas_call(
            functools.partial(pack_kernel, c),
            out_shape=jax.ShapeDtypeStruct((TILES, 3, SUB, cells), f32),
            in_specs=[whole(pltpu.HBM)] * 3,
            out_specs=whole(),
            scratch_shapes=[
                pltpu.VMEM((2, 2, cells, LANES), f32),
                pltpu.VMEM((2, cells, LANES), classes.dtype),
                pltpu.SemaphoreType.DMA((3, 2)),
            ],
            compiler_params=params,
            name="pack",
        )(suction, warmth, classes)
        got.append(exchange(packed, n))

    column = pltpu.VMEM((steps, SUB, GROUPS * WIDTH), f32)
    back = []
    for c in range(CHUNKS):
        solved = pl.pallas_call(
            functools.partial(step_kernel, n, w, c),
            out_shape=jax.ShapeDtypeStruct((TILES, 2, SUB, cells), f32),
            in_specs=[whole(), whole(), whole(), whole(pltpu.SMEM), whole(pltpu.SMEM)],
            out_specs=whole(),
            scratch_shapes=[column] * 14 + [pltpu.VMEM((2, cells, LANES), f32)],
            compiler_params=params,
            cost_estimate=pl.CostEstimate(flops=100_000_000, bytes_accessed=2_000_000, transcendentals=0),
            name="steps",
        )(got[c], surface, couplings, k_sat, heat_cond)
        back.append(exchange(solved, n))
    return pl.pallas_call(
        unpack_kernel,
        out_shape=(jax.ShapeDtypeStruct((cells, width), f32),) * 2,
        in_specs=[whole()] * CHUNKS,
        out_specs=(whole(), whole()),
        compiler_params=params,
        name="unpack",
    )(*back)


def solution(mesh):
    placed = (P(None, "cols"), P(None, "cols"), P(None, "cols"), P("cols"), P(), P(), P())
    return jax.shard_map(
        on_device,
        mesh=mesh,
        in_specs=placed,
        out_specs=(P(None, "cols"), P(None, "cols")),
        check_vma=False,
    )
```

time: 65.3 us -> 104 us (1.59)
  blocking collectives: 19 us -> 54.6 us
  waiting for transfers between devices: 23.4 us -> 17.1 us
  starting transfers between devices: 7.3 us -> 12.6 us
  Pallas kernels: 11.1 us -> 14.9 us
    all_gather x0 -> x1, blocking collectives: none -> 41.9 us  [on_device(): surface = lax.all_gather(top, 'cols')]
    all_to_all x1, blocking collectives: 19 us -> 12.7 us  [exchange(): lax.all_to_all(tiles, 'cols', split_axis=0, concat_axis=0, tiled=True)]
    all_to_all x1 -> x3, waiting for transfers between devices: 23.4 us -> 17.1 us  [exchange(): lax.all_to_all(tiles, 'cols', split_axis=0, concat_axis=0, tiled=True)]
    all_to_all x1 -> x3, starting transfers between devices: 7.3 us -> 12.6 us  [exchange(): lax.all_to_all(tiles, 'cols', split_axis=0, concat_axis=0, tiled=True)]
    pallas_call x2 -> x4, Pallas kernels: 10.1 us -> 14 us  [the longest x2 11 us: on_device(): pl.pallas_call(functools.partial(step_kernel, n, w, c), out_shape=jax.Sha...]
    unnamed x14 -> x21, local copies, waits for them, and re-layouts: 3.54 us -> 3.55 us
  transfers between devices with their start and end apart: 1 -> 3, of which waited for: 1 -> 2; matrix products, arithmetic and copies ran while one was open for 0% -> 0% of each run, Pallas kernels for 0% -> 12%
where the time goes in v1:
time: 104 us
  blocking collectives  54.6 us (52%)
  waiting for transfers between devices  17.1 us (16%)
  Pallas kernels  14.9 us (14%)
  starting transfers between devices  12.6 us (12%)
  local copies, waits for them, and re-layouts  3.55 us (3%)
    all_gather x1, blocking collectives, on_device(): surface = lax.all_gather(top, 'cols')  41.9 us
    all_to_all x3, waiting for transfers between devices, exchange(): lax.all_to_all(tiles, 'cols', split_axis=0, concat_axis=0, tiled=True)  17.1 us
    all_to_all x1, blocking collectives, exchange(): lax.all_to_all(tiles, 'cols', split_axis=0, concat_axis=0, tiled=True)  12.7 us
    all_to_all x3, starting transfers between devices, exchange(): lax.all_to_all(tiles, 'cols', split_axis=0, concat_axis=0, tiled=True)  12.6 us
    pallas_call x2, Pallas kernels, on_device(): pl.pallas_call(functools.partial(step_kernel, n, w, c), out_shape=jax.Sha...  11 us
    unnamed x21, local copies, waits for them, and re-layouts  3.55 us
    pallas_call x2, Pallas kernels, on_device(): pl.pallas_call(functools.partial(pack_kernel, c), out_shape=jax.ShapeDtyp...  2.95 us
  transfers between devices with their start and end apart: 3, of which 2 were waited for; matrix products, arithmetic and copies ran while one was open for 0% of the time, Pallas kernels for 12%

profile of v1, /device:TPU:0, one launch (start us, length us, event | category | flops | bytes accessed | tf_op | source)
XLA Modules:
  0.0 103.6 jit_solution(8764443010154020326)
XLA Ops:
  0.6 0.0 copy-start
  0.6 0.9 copy-done
  1.6 0.0 copy-start.2
  1.6 0.9 copy-done.2
  2.5 0.0 copy-start.4
  2.5 0.9 copy-done.4
  3.5 1.5 %pack.3 = f32[32,3,8,128]{3,2,1,0:T(8,128)} custom-call(f32[128,512]{1,0:T(8,128)S(1)} %copy-done, f32[128,512]{1,0:T(8,128)S(1)} %copy-done.2, s32[128,512]{1,0:T(8,128)S(1)} %copy-done.4), custom_call_target="tpu_custom_call" | custom-call | tf_op jit(solution)/shard_map/pack/pallas_call | solution.py:357
  5.0 0.0 copy-start.1
  5.0 0.0 copy-start.3
  5.0 0.0 copy-start.5
  5.0 7.3 %all-to-all-start.2 = ((f32[32,3,8,128]{3,2,1,0:T(8,128)}), f32[32,3,8,128]{3,2,1,0:T(8,128)S(1)}, u32[]{:S(2)}, u32[]{:S(2)}) async-start(f32[32,3,8,128]{3,2,1,0:T(8,128)} %pack.3), calls=%async_computation.2 | async-start | bytes 786432 | tf_op jit(solution)/shard_map/all_to_all | solution.py:339
  12.3 0.0 copy-done.1
  12.3 0.0 copy-done.3
  12.3 0.0 copy-done.5
  12.3 1.5 %pack.2 = f32[32,3,8,128]{3,2,1,0:T(8,128)} custom-call(f32[128,512]{1,0:T(8,128)S(1)} %copy-done.1, f32[128,512]{1,0:T(8,128)S(1)} %copy-done.3, s32[128,512]{1,0:T(8,128)S(1)} %copy-done.5), custom_call_target="tpu_custom_call" | custom-call | tf_op jit(solution)/shard_map/pack/pallas_call | solution.py:357
  13.8 11.7 %all-to-all-done.2.got = f32[32,3,8,128]{3,2,1,0:T(8,128)S(1)} async-done(((f32[32,3,8,128]{3,2,1,0:T(8,128)}), f32[32,3,8,128]{3,2,1,0:T(8,128)S(1)}, u32[]{:S(2)}, u32[]{:S(2)}) %all-to-all-start.2) | async-done | bytes 393248 | tf_op jit(solution)/shard_map/all_to_all | solution.py:339
  25.5 0.0 copy-start.9
  25.5 2.7 %all-to-all-start = ((f32[32,3,8,128]{3,2,1,0:T(8,128)}), f32[32,3,8,128]{3,2,1,0:T(8,128)S(1)}, u32[]{:S(2)}, u32[]{:S(2)}) async-start(f32[32,3,8,128]{3,2,1,0:T(8,128)} %pack.2), calls=%async_computation | async-start | bytes 786432 | tf_op jit(solution)/shard_map/all_to_all | solution.py:339
  28.2 0.0 copy-done.9
  28.2 41.9 %all-gather.1 = f32[32,1,512]{2,1,0:T(1,128)S(1)} all-gather(f32[1,1,512]{2,1,0:T(1,128)S(1)} %bitcast.6), channel_id=2, replica_groups=mesh['cols'=32] {'cols'}, dimensions={0}, use_global_device_ids=true | all-gather | bytes 67584 | tf_op jit(solution)/shard_map/all_gather | solution.py:354
  70.2 0.0 copy-start.8
  70.2 0.0 copy-start.7
  70.2 0.6 copy-done.8
  70.8 0.0 copy-done.6
  70.9 0.0 copy-done.7
  70.9 5.9 %steps.3 = f32[32,2,8,128]{3,2,1,0:T(8,128)} custom-call(f32[32,3,8,128]{3,2,1,0:T(8,128)S(1)} %all-to-all-done.2.got, f32[32,512]{1,0:T(8,128)S(1)} %bitcast.4, s32[2,128]{1,0:T(2,128)S(1)} %copy-done.6, f32[8]{0:T(128)S(1)} %copy-done.7, f32[8]{0:T(128)S(1)} %copy-done.8), custom_call_target="tpu_custom_call" | custom-call | flops 100000000 | bytes 2000000 | tf_op jit(solution)/shard_map/steps/pallas_call | solution.py:375
  76.7 0.0 all-to-all-done.got
  76.7 2.6 %all-to-all-start.3 = ((f32[32,2,8,128]{3,2,1,0:T(8,128)}), f32[32,2,8,128]{3,2,1,0:T(8,128)S(1)}, u32[]{:S(2)}, u32[]{:S(2)}) async-start(f32[32,2,8,128]{3,2,1,0:T(8,128)} %steps.3), calls=%async_computation.3 | async-start | bytes 524288 | tf_op jit(solution)/shard_map/all_to_all | solution.py:339
  79.3 5.1 %steps.2 = f32[32,2,8,128]{3,2,1,0:T(8,128)S(1)} custom-call(f32[32,3,8,128]{3,2,1,0:T(8,128)S(1)} %all-to-all-done.got, f32[32,512]{1,0:T(8,128)S(1)} %bitcast.5, s32[2,128]{1,0:T(2,128)S(1)} %copy-done.6, f32[8]{0:T(128)S(1)} %copy-done.7, f32[8]{0:T(128)S(1)} %copy-done.8), custom_call_target="tpu_custom_call" | custom-call | flops 100000000 | bytes 2000000 | tf_op jit(solution)/shard_map/steps/pallas_call | solution.py:375
  84.5 5.4 %all-to-all-done.3.refs_1_ = f32[32,2,8,128]{3,2,1,0:T(8,128)S(1)} async-done(((f32[32,2,8,128]{3,2,1,0:T(8,128)}), f32[32,2,8,128]{3,2,1,0:T(8,128)S(1)}, u32[]{:S(2)}, u32[]{:S(2)}) %all-to-all-start.3) | async-done | bytes 262176 | tf_op jit(solution)/shard_map/all_to_all | solution.py:339
  89.9 12.7 %all_to_all.20.refs_0_ = f32[32,2,8,128]{3,2,1,0:T(8,128)S(1)} all-to-all(f32[32,2,8,128]{3,2,1,0:T(8,128)S(1)} %steps.2), channel_id=1, replica_groups=mesh['cols'=32] {'cols'}, dimensions={0} | all-to-all | bytes 524288 | tf_op jit(solution)/shard_map/all_to_all | solution.py:339
  102.6 0.9 unpack.1
  (2 shorter events, 0.0 us)
Async XLA Ops:
  0.6 1.0 copy-start
  1.6 0.9 copy-start.2
  2.5 0.9 copy-start.4
  5.0 7.3 %copy-start.1 = (f32[128,512]{1,0:T(8,128)S(1)}, f32[128,512]{1,0:T(8,128)}, u32[]{:S(2)}) copy-start(f32[128,512]{1,0:T(8,128)} %suction.3) | copy-start | bytes 786436
  5.0 7.3 %copy-start.3 = (f32[128,512]{1,0:T(8,128)S(1)}, f32[128,512]{1,0:T(8,128)}, u32[]{:S(2)}) copy-start(f32[128,512]{1,0:T(8,128)} %warmth.3) | copy-start | bytes 786436
  5.0 7.3 %copy-start.5 = (s32[128,512]{1,0:T(8,128)S(1)}, s32[128,512]{1,0:T(8,128)}, u32[]{:S(2)}) copy-start(s32[128,512]{1,0:T(8,128)} %classes.3) | copy-start | bytes 786436
  5.0 20.5 %all-to-all-start.2 = ((f32[32,3,8,128]{3,2,1,0:T(8,128)}), f32[32,3,8,128]{3,2,1,0:T(8,128)S(1)}, u32[]{:S(2)}, u32[]{:S(2)}) async-start(f32[32,3,8,128]{3,2,1,0:T(8,128)} %pack.3), calls=%async_computation.2 | async-start | bytes 786432 | tf_op jit(solution)/shard_map/all_to_all | solution.py:339
  25.5 2.7 %copy-start.9 = (f32[512]{0:T(512)S(1)}, f32[512]{0:T(512)}, u32[]{:S(2)}) copy-start(f32[512]{0:T(512)} %param.10) | copy-start | bytes 6148
  25.5 51.2 %all-to-all-start = ((f32[32,3,8,128]{3,2,1,0:T(8,128)}), f32[32,3,8,128]{3,2,1,0:T(8,128)S(1)}, u32[]{:S(2)}, u32[]{:S(2)}) async-start(f32[32,3,8,128]{3,2,1,0:T(8,128)} %pack.2), calls=%async_computation | async-start | bytes 786432 | tf_op jit(solution)/shard_map/all_to_all | solution.py:339
  70.2 0.7 copy-start.8
  70.2 0.7 copy-start.6
  70.2 0.7 copy-start.7
  76.7 13.2 %all-to-all-start.3 = ((f32[32,2,8,128]{3,2,1,0:T(8,128)}), f32[32,2,8,128]{3,2,1,0:T(8,128)S(1)}, u32[]{:S(2)}, u32[]{:S(2)}) async-start(f32[32,2,8,128]{3,2,1,0:T(8,128)} %steps.3), calls=%async_computation.3 | async-start | bytes 524288 | tf_op jit(solution)/shard_map/all_to_all | solution.py:339

commit v2 on v0

--- a/solution.py
+++ b/solution.py
@@ -12,7 +12,17 @@
 PAIR_DEV = 4
 LANES = 128
 PARTS = 8
-VMEM_LIMIT = 48 * 1024 * 1024
+VMEM_LIMIT = 32 * 1024 * 1024
+PACK_LIMIT = 60 * 1024 * 1024
+
+
+def reciprocal(x):
+    r = pl.reciprocal(x, approx=True)
+    return r * (2.0 - x * r)
+
+
+def sigmoid(x):
+    return 0.5 + 0.5 * jnp.tanh(0.5 * x)
 
 
 def shift_down(value, steps):
@@ -23,13 +33,21 @@
     return pltpu.roll(value, PARTS - steps, axis=0)
 
 
-def pack_kernel(suction, warmth, classes, top, out):
+def pack_kernel(suction, warmth, classes, top, out, room, class_room, sems):
     n, _, w, cells = out.shape
-    fields = (suction[...], warmth[...], classes[...].astype(jnp.float32))
-    for f, field in enumerate(fields):
-        turned = field.T
-        for b in range(2):
-            out[:, 2 * f + b] = turned[b * SPAN : (b + 1) * SPAN].reshape(n, w, cells)
+    copies = []
+    for f, field in enumerate((suction, warmth, classes)):
+        for b in range(2):
+            target = class_room.at[b] if f == 2 else room.at[f, b]
+            copies.append(
+                pltpu.make_async_copy(field.at[:, pl.ds(b * SPAN, SPAN)], target, sems.at[f, b])
+            )
+            copies[-1].start()
+    for f in range(3):
+        for b in range(2):
+            copies[2 * f + b].wait()
+            value = class_room[b].astype(jnp.float32) if f == 2 else room[f, b]
+            out[:, 2 * f + b] = value.T.reshape(n, w, cells)
     surface = jnp.concatenate(
         [top[0:1, :SPAN], top[0:1, SPAN:], jnp.zeros((cells - 2, SPAN), jnp.float32)], axis=0
     )
@@ -48,11 +66,11 @@
     for j in range(steps):
         above, main, below, source = matrix(j)
         if j == 0:
-            r = 1.0 / main
+            r = reciprocal(main)
             a_prev = above * r
             d_prev = source * r
         else:
-            r = 1.0 / (main - above * c_prev)
+            r = reciprocal(main - above * c_prev)
             over = above * r
             a_prev = a_prev * over
             d_prev = source * r + d_prev * over
@@ -67,13 +85,13 @@
         p_first = c * p_first
         a_first = lead[j] + c * a_first
         d_first = value[j] + c * d_first
-    g = 1.0 / (1.0 - last_c * shift_up(a_first, 1))
+    g = reciprocal(1.0 - last_c * shift_up(a_first, 1))
     up = last_c * shift_up(p_first, 1) * g
     down = last_a * g
     own = (last_d + last_c * shift_up(d_first, 1)) * g
     step = 1
     while step < PARTS:
-        g = 1.0 / (1.0 - up * shift_up(down, step) - down * shift_down(up, step))
+        g = reciprocal(1.0 - up * shift_up(down, step) - down * shift_down(up, step))
         own = (own + up * shift_up(own, step) + down * shift_down(own, step)) * g
         up = up * shift_up(up, step) * g
         down = down * shift_down(down, step) * g
@@ -146,8 +164,8 @@
 
     for j in range(steps):
         h, t = head[j], warm[j]
-        s0 = jax.nn.sigmoid(h)
-        f0 = jax.nn.sigmoid(2.0 * t)
+        s0 = sigmoid(h)
+        f0 = sigmoid(2.0 * t)
         m0 = 0.05 + 0.4 * s0
         wet[j] = s0
         stored[j] = s0
@@ -186,7 +204,7 @@
 
     def iteration(_, carry):
         for j in range(steps):
-            s, f = wet[j], jax.nn.sigmoid(2.0 * warm[j])
+            s, f = wet[j], sigmoid(2.0 * warm[j])
             melt[j] = f
             cond[j] = perm[j] * (f * s * s + 0.02)
         lax.fori_loop(0, steps, lateral, 0)
@@ -220,7 +238,7 @@
         def water_done(j, x):
             h = head[j] + x
             head[j] = h
-            wet[j] = jax.nn.sigmoid(h)
+            wet[j] = sigmoid(h)
 
         solve(cells, steps, water_matrix, ratio, lead, value, water_done)
 
@@ -294,9 +312,14 @@
     packed = pl.pallas_call(
         pack_kernel,
         out_shape=jax.ShapeDtypeStruct((kn, 7, kw, cells), f32),
-        in_specs=[whole()] * 4,
+        in_specs=[whole(pltpu.HBM)] * 3 + [whole()],
         out_specs=whole(),
-        compiler_params=params,
+        scratch_shapes=[
+            pltpu.VMEM((2, 2, cells, SPAN), f32),
+            pltpu.VMEM((2, cells, SPAN), classes.dtype),
+            pltpu.SemaphoreType.DMA((3, 2)),
+        ],
+        compiler_params=pltpu.CompilerParams(vmem_limit_bytes=PACK_LIMIT),
         name="pack",
     )(suction, warmth, classes, top.reshape(1, width))
     got = from_chunks(exchange(to_chunks(packed)))

time: 65.3 us -> 63.9 us (0.979)
  local copies, waits for them, and re-layouts: 3.54 us -> 0.02 us
  Pallas kernels: 11.1 us -> 13.3 us
    unnamed x14 -> x6, local copies, waits for them, and re-layouts: 3.54 us -> 0.02 us
    pallas_call x1, Pallas kernels: 1.24 us -> 3.21 us  [on_device(): pl.pallas_call(pack_kernel, out_shape=jax.ShapeDtypeStruct((kn, 7, kw, ce...]
where the time goes in v2:
time: 63.9 us; the launch traced here: 63.7 us
  waiting for transfers between devices  23.4 us (37%)
  blocking collectives  19 us (30%)
  Pallas kernels  13.3 us (21%)
  starting transfers between devices  7.3 us (11%)
  between operations  0.69 us (1%)
    all_to_all x1, waiting for transfers between devices, exchange(): lax.all_to_all(chunks, 'cols', split_axis=0, concat_axis=0, tiled=True)  23.4 us
    all_to_all x1, blocking collectives, exchange(): lax.all_to_all(chunks, 'cols', split_axis=0, concat_axis=0, tiled=True)  19 us
    pallas_call x1, Pallas kernels, on_device(): pl.pallas_call(functools.partial(step_kernel, n, w), out_shape=jax.ShapeD...  9.15 us
    all_to_all x1, starting transfers between devices, exchange(): lax.all_to_all(chunks, 'cols', split_axis=0, concat_axis=0, tiled=True)  7.3 us
    pallas_call x1, Pallas kernels, on_device(): pl.pallas_call(pack_kernel, out_shape=jax.ShapeDtypeStruct((kn, 7, kw, ce...  3.21 us
  transfers between devices with their start and end apart: 1, of which 1 were waited for; matrix products, arithmetic and copies ran while one was open for 0% of the time, Pallas kernels for 0%

profile of v2, /device:TPU:0, one launch (start us, length us, event | category | flops | bytes accessed | tf_op | source)
XLA Modules:
  0.0 63.7 jit_solution(15415330928973605172)
XLA Ops:
  0.6 3.2 %pack.1 = f32[32,7,8,128]{3,2,1,0:T(8,128)} custom-call(f32[128,512]{1,0:T(8,128)} %suction.1, f32[128,512]{1,0:T(8,128)} %warmth.1, s32[128,512]{1,0:T(8,128)} %classes.1, f32[1,512]{1,0:T(1,128)} %bitcast.1), custom_call_target="tpu_custom_call" | custom-call | tf_op jit(solution)/shard_map/pack/pallas_call | solution.py:312
  3.8 0.0 copy-start.2
  3.9 7.3 %all-to-all-start = ((f32[32,7,8,128]{3,2,1,0:T(8,128)}), f32[32,7,8,128]{3,2,1,0:T(8,128)S(1)}, u32[]{:S(2)}, u32[]{:S(2)}) async-start(f32[32,7,8,128]{3,2,1,0:T(8,128)} %pack.1), calls=%async_computation | async-start | bytes 1835008 | tf_op jit(solution)/shard_map/all_to_all | solution.py:286
  11.2 0.0 copy-done.2
  11.2 0.0 copy-start
  11.2 0.0 copy-start.1
  11.2 23.4 %all-to-all-done.got = f32[32,7,8,128]{3,2,1,0:T(8,128)S(1)} async-done(((f32[32,7,8,128]{3,2,1,0:T(8,128)}), f32[32,7,8,128]{3,2,1,0:T(8,128)S(1)}, u32[]{:S(2)}, u32[]{:S(2)}) %all-to-all-start) | async-done | bytes 917536 | tf_op jit(solution)/shard_map/all_to_all | solution.py:286
  34.6 0.0 copy-done
  34.6 0.0 copy-done.1
  34.6 9.1 %steps.1 = f32[32,4,8,128]{3,2,1,0:T(8,128)S(1)} custom-call(f32[32,7,8,128]{3,2,1,0:T(8,128)S(1)} %all-to-all-done.got, s32[8,128]{1,0:T(8,128)S(1)} %scatter.4.couplings, f32[8]{0:T(128)S(1)} %copy-done, f32[8]{0:T(128)S(1)} %copy-done.1), custom_call_target="tpu_custom_call" | custom-call | tf_op jit(solution)/shard_map/steps/pallas_call | solution.py:329
  43.8 19.0 %all_to_all.10.got = f32[32,4,8,128]{3,2,1,0:T(8,128)S(1)} all-to-all(f32[32,4,8,128]{3,2,1,0:T(8,128)S(1)} %steps.1), channel_id=1, replica_groups=mesh['cols'=32] {'cols'}, dimensions={0} | all-to-all | bytes 1048576 | tf_op jit(solution)/shard_map/all_to_all | solution.py:286
  62.7 0.9 %unpack.1 = (f32[128,512]{1,0:T(8,128)}, f32[128,512]{1,0:T(8,128)}) custom-call(f32[32,4,8,128]{3,2,1,0:T(8,128)S(1)} %all_to_all.10.got), custom_call_target="tpu_custom_call" | custom-call | tf_op jit(solution)/shard_map/unpack/pallas_call | solution.py:339
  (1 shorter events, 0.0 us)
Async XLA Ops:
  3.8 7.3 %copy-start.2 = (s32[2,128]{1,0:T(2,128)S(1)}, s32[2,128]{1,0:T(2,128)}, u32[]{:S(2)}) copy-start(s32[2,128]{1,0:T(2,128)} %param.13) | copy-start | bytes 3076
  3.9 30.7 %all-to-all-start = ((f32[32,7,8,128]{3,2,1,0:T(8,128)}), f32[32,7,8,128]{3,2,1,0:T(8,128)S(1)}, u32[]{:S(2)}, u32[]{:S(2)}) async-start(f32[32,7,8,128]{3,2,1,0:T(8,128)} %pack.1), calls=%async_computation | async-start | bytes 1835008 | tf_op jit(solution)/shard_map/all_to_all | solution.py:286
  11.2 23.4 %copy-start = (f32[8]{0:T(128)S(1)}, f32[8]{0:T(128)}, u32[]{:S(2)}) copy-start(f32[8]{0:T(128)} %k_sat.1) | copy-start | bytes 100
  11.2 23.4 %copy-start.1 = (f32[8]{0:T(128)S(1)}, f32[8]{0:T(128)}, u32[]{:S(2)}) copy-start(f32[8]{0:T(128)} %heat_cond.1) | copy-start | bytes 100

commit v3 on v1

v3 whole, which is shorter than its diff:
```python
import functools

import jax
import jax.numpy as jnp
from jax import lax
from jax.experimental import pallas as pl
from jax.experimental.pallas import tpu as pltpu
from jax.sharding import PartitionSpec as P

SPAN = 256
ITERS = 2
PAIR_DEV = 4
LANES = 128
SUB = 8
GROUPS = 2
WIDTH = 2 * SPAN
VMEM_LIMIT = 32 * 1024 * 1024
PACK_LIMIT = 60 * 1024 * 1024


def pack_kernel(suction, warmth, classes, top, out, room, class_room, turned, in_sems, out_sems):
    n, _, w, cells = turned.shape
    tiles = SPAN // LANES
    part = LANES // w
    into, sent = [], []
    for f, field in enumerate((suction, warmth, classes)):
        for q in range(2 * tiles):
            target = class_room.at[q] if f == 2 else room.at[f, q]
            into.append(
                pltpu.make_async_copy(field.at[:, pl.ds(q * LANES, LANES)], target, in_sems.at[f, q])
            )
            into[-1].start()

    def send(slot):
        sent.append(pltpu.make_async_copy(turned.at[:, slot], out.at[:, slot], out_sems.at[slot]))
        sent[-1].start()

    surface = jnp.concatenate(
        [top[0:1, :SPAN], top[0:1, SPAN:], jnp.zeros((cells - 2, SPAN), jnp.float32)], axis=0
    )
    turned[:, 6] = surface.T.reshape(n, w, cells)
    send(6)
    for f in range(3):
        for b in range(2):
            for i in range(tiles):
                q = b * tiles + i
                into[2 * tiles * f + q].wait()
                value = class_room[q].astype(jnp.float32) if f == 2 else room[f, q]
                turned[i * part : (i + 1) * part, 2 * f + b] = value.T.reshape(part, w, cells)
            send(2 * f + b)
    for copy in sent:
        copy.wait()


def unpack_kernel(got, suction, warmth, room, sems):
    n, _, w, cells = got.shape
    sent = []
    for f, out in enumerate((suction, warmth)):
        for b in range(2):
            here = pl.ds(b * SPAN, SPAN)
            room[f, b] = got[:, 2 * f + b].reshape(n * w, cells).T
            sent.append(pltpu.make_async_copy(room.at[f, b], out.at[:, here], sems.at[f, b]))
            sent[-1].start()
    for copy in sent:
        copy.wait()


def reciprocal(x):
    r = pl.reciprocal(x, approx=True)
    return r * (2.0 - x * r)


def sigmoid(x):
    return 0.5 + 0.5 * jnp.tanh(0.5 * x)


def following(value):
    first, second = value[:, :WIDTH], value[:, WIDTH:]
    return jnp.concatenate([second, pltpu.roll(first, SUB - 1, axis=0)], axis=1)


def preceding(value):
    first, second = value[:, :WIDTH], value[:, WIDTH:]
    return jnp.concatenate([pltpu.roll(second, 1, axis=0), first], axis=1)


def solve(steps, matrix, ratio, lead, value, update):
    c_prev = a_prev = d_prev = None
    for j in range(steps):
        above, main, below, source = matrix(j)
        if j == 0:
            r = reciprocal(main)
            a_prev = above * r
            d_prev = source * r
        else:
            r = reciprocal(main - above * c_prev)
            over = above * r
            a_prev = a_prev * over
            d_prev = source * r + d_prev * over
        c_prev = below * r
        ratio[j] = c_prev
        lead[j] = a_prev
        value[j] = d_prev
    last_c, last_a, last_d = c_prev, a_prev, d_prev
    p_first, a_first, d_first = ratio[steps - 2], lead[steps - 2], value[steps - 2]
    for j in range(steps - 3, -1, -1):
        c = ratio[j]
        p_first = c * p_first
        a_first = lead[j] + c * a_first
        d_first = value[j] + c * d_first
    g = reciprocal(1.0 - last_c * following(a_first))
    up = last_c * following(p_first) * g
    down = last_a * g
    own = (last_d + last_c * following(d_first)) * g
    step = 0
    while step < SUB:
        if step == 0:
            after, before = following, preceding
        else:
            after = functools.partial(pltpu.roll, shift=SUB - step, axis=0)
            before = functools.partial(pltpu.roll, shift=step, axis=0)
        g = reciprocal(1.0 - up * after(down) - down * before(up))
        own = (own + up * after(own) + down * before(own)) * g
        up = up * after(up) * g
        down = down * before(down) * g
        step = max(1, 2 * step)
    over = preceding(own)
    x = own
    update(steps - 1, x)
    for j in range(steps - 2, -1, -1):
        x = ratio[j] * x + (lead[j] * over + value[j])
        update(j, x)


def step_kernel(
    n, w, got, couplings, k_sat, heat_cond, out,
    head, warm, perm, conduct, stored, energy, wet, melt, cond, water, heat, ratio, lead, value, load,
):
    kn, _, kw, cells = got.shape
    steps = cells // (SUB * GROUPS)
    stride = steps * GROUPS

    def lanes_of(g, b):
        return slice((g * 2 + b) * SPAN, (g * 2 + b + 1) * SPAN)

    def take(field, change):
        for b in range(2):
            turned = got[:, 2 * field + b].reshape(SPAN, cells).T
            for q in range(SPAN // LANES):
                load[q] = turned[:, q * LANES : (q + 1) * LANES]
            for j in range(steps):
                for g in range(GROUPS):
                    for q in range(SPAN // LANES):
                        here = (g * 2 + b) * SPAN + q * LANES
                        value = load[q, pl.ds(g * steps + j, SUB, stride=stride), :]
                        change(j, slice(here, here + LANES), value)

    def take_head(j, lanes, v):
        head[j, :, lanes] = v

    def take_warm(j, lanes, v):
        warm[j, :, lanes] = v

    def take_class(j, lanes, v):
        k = jnp.full_like(v, k_sat[0])
        lam = jnp.full_like(v, heat_cond[0])
        for c in range(1, k_sat.shape[0]):
            here = v >= c
            k = jnp.where(here, k_sat[c], k)
            lam = jnp.where(here, heat_cond[c], lam)
        perm[j, :, lanes] = k
        conduct[j, :, lanes] = lam

    take(0, take_head)
    take(1, take_warm)
    take(2, take_class)

    surface = got[:, 6].reshape(SPAN, cells).T[0:2]
    top = jnp.concatenate([surface[0:1], surface[1:2]] * GROUPS, axis=1)

    pair_rows = couplings[...].astype(jnp.float32)
    pairs = couplings.shape[1]
    pair_dev = lax.broadcasted_iota(jnp.int32, (pairs, SPAN), 1) // w
    pair_id = lax.broadcasted_iota(jnp.int32, (pairs, SPAN), 0)
    dev = lax.broadcasted_iota(jnp.int32, (SUB, SPAN), 1) // w
    chosen = []
    for s in range(1, PAIR_DEV + 1):
        upper_at = (pair_id == pair_dev * PAIR_DEV + s - 1).astype(jnp.float32)
        lower_at = (pair_id == (pair_dev - s) * PAIR_DEV + s - 1).astype(jnp.float32)
        upper = jnp.dot(pair_rows, upper_at, preferred_element_type=jnp.float32)[0:1]
        lower = jnp.dot(pair_rows, lower_at, preferred_element_type=jnp.float32)[1:2]
        upper = jnp.broadcast_to(upper, (SUB, SPAN)) > 0.5
        lower = jnp.broadcast_to(lower, (SUB, SPAN)) > 0.5
        scale = jnp.where(dev + s < n, 0.25, 0.0)
        chosen.append((upper, lower, scale))

    part = lax.broadcasted_iota(jnp.int32, (SUB, GROUPS * WIDTH), 0)
    group = lax.broadcasted_iota(jnp.int32, (SUB, GROUPS * WIDTH), 1) // WIDTH
    first_part = jnp.logical_and(part == 0, group == 0)
    last_part = jnp.logical_and(part == SUB - 1, group == GROUPS - 1)

    for j in range(steps):
        h, t = head[j], warm[j]
        s0 = sigmoid(h)
        f0 = sigmoid(2.0 * t)
        m0 = 0.05 + 0.4 * s0
        wet[j] = s0
        stored[j] = s0
        energy[j] = (1.0 + 2.0 * m0) * t + 2.0 * m0 * f0

    def lateral(j):
        for g in range(GROUPS):
            l0, l1 = lanes_of(g, 0), lanes_of(g, 1)
            h0, h1 = head[j, :, l0], head[j, :, l1]
            t0, t1 = warm[j, :, l0], warm[j, :, l1]
            c0, c1 = cond[j, :, l0], cond[j, :, l1]
            water_all = water_1 = heat_all = heat_1 = None
            for s in range(1, PAIR_DEV + 1):
                upper, lower, scale = chosen[s - 1]
                back = SPAN - s * w
                h_low = pltpu.roll(jnp.where(lower, h1, h0), back, axis=1)
                t_low = pltpu.roll(jnp.where(lower, t1, t0), back, axis=1)
                c_low = pltpu.roll(jnp.where(lower, c1, c0), back, axis=1)
                flow = (
                    scale
                    * (jnp.where(upper, c1, c0) + c_low)
                    * (jnp.where(upper, h1, h0) - h_low + 0.5)
                )
                carried = flow * jnp.where(flow > 0.0, jnp.where(upper, t1, t0), t_low)
                flow_in = pltpu.roll(flow, s * w, axis=1)
                carried_in = pltpu.roll(carried, s * w, axis=1)
                net = flow_in - flow
                net_1 = jnp.where(lower, flow_in, 0.0) - jnp.where(upper, flow, 0.0)
                brought = carried_in - carried
                brought_1 = jnp.where(lower, carried_in, 0.0) - jnp.where(upper, carried, 0.0)
                if s == 1:
                    water_all, water_1, heat_all, heat_1 = net, net_1, brought, brought_1
                else:
                    water_all, water_1 = water_all + net, water_1 + net_1
                    heat_all, heat_1 = heat_all + brought, heat_1 + brought_1
            water[j, :, l0] = water_all - water_1
            water[j, :, l1] = water_1
            heat[j, :, l0] = 2.0 * (heat_all - heat_1)
            heat[j, :, l1] = 2.0 * heat_1

    def faces(field, potential):
        face_of, rise_of = [], []
        for j in range(steps):
            if j + 1 < steps:
                c_next, v_next = field(j + 1), potential(j + 1)
                face = 0.5 * (field(j) + c_next)
            else:
                c_next, v_next = following(field(0)), following(potential(0))
                face = jnp.where(last_part, 0.0, 0.5 * (field(j) + c_next))
            face_of.append(face)
            rise_of.append(v_next - potential(j))
        return face_of, rise_of

    def iteration(_, carry):
        for j in range(steps):
            s, f = wet[j], sigmoid(2.0 * warm[j])
            melt[j] = f
            cond[j] = perm[j] * (f * s * s + 0.02)
        for j in range(steps):
            lateral(j)

        k_face, rise = faces(lambda j: cond[j], lambda j: head[j])
        k_top = jnp.where(first_part, 0.0, preceding(k_face[-1]))
        q_face = [k * (1.0 - d) for k, d in zip(k_face, rise)]
        q_top = jnp.where(first_part, 0.0, preceding(q_face[-1]))

        def water_matrix(j):
            above = k_top if j == 0 else k_face[j - 1]
            into = q_top if j == 0 else q_face[j - 1]
            s = wet[j]
            main = 0.8 * s * (1.0 - s) + 0.02 + above + k_face[j]
            source = water[j] + into - q_face[j] - 0.8 * (s - stored[j])
            return above, main, k_face[j], source

        def water_done(j, x):
            h = head[j] + x
            head[j] = h
            wet[j] = sigmoid(h)

        solve(steps, water_matrix, ratio, lead, value, water_done)

        l_face, rise = faces(lambda j: conduct[j] * (1.5 - 0.5 * melt[j]), lambda j: warm[j])
        l_top = jnp.where(first_part, 0.0, preceding(l_face[-1]))
        g_face = [-l * d for l, d in zip(l_face, rise)]
        g_top = jnp.where(first_part, 0.0, preceding(g_face[-1]))
        surface_lam = jnp.where(first_part, 2.0 * conduct[0] * (1.5 - 0.5 * melt[0]), 0.0)

        def heat_matrix(j):
            above = l_top if j == 0 else l_face[j - 1]
            into = g_top if j == 0 else g_face[j - 1]
            t, f = warm[j], melt[j]
            m = 0.05 + 0.4 * wet[j]
            now = (1.0 + 2.0 * m) * t + 2.0 * m * f
            main = 2.0 * (1.0 + 2.0 * m + 4.0 * m * f * (1.0 - f)) + above + l_face[j]
            source = heat[j] + into - g_face[j] - 2.0 * (now - energy[j])
            if j == 0:
                main = main + surface_lam
                source = source + surface_lam * (top - t)
            return above, main, l_face[j], source

        def heat_done(j, x):
            warm[j] = warm[j] + x

        solve(steps, heat_matrix, ratio, lead, value, heat_done)
        return carry

    lax.fori_loop(0, ITERS, iteration, 0)

    for f, field in enumerate((head, warm)):
        for b in range(2):
            for j in range(steps):
                for g in range(GROUPS):
                    for q in range(SPAN // LANES):
                        here = (g * 2 + b) * SPAN + q * LANES
                        load[q, pl.ds(g * steps + j, SUB, stride=stride), :] = field[j, :, here : here + LANES]
            turned = jnp.concatenate([load[q] for q in range(SPAN // LANES)], axis=1).T
            out[:, 2 * f + b] = turned.reshape(kn, kw, cells)


def whole(memory=pltpu.VMEM):
    return pl.BlockSpec(memory_space=memory)


def exchange(chunks):
    return lax.all_to_all(chunks, "cols", split_axis=0, concat_axis=0, tiled=True)


def on_device(suction, warmth, classes, top, couplings, k_sat, heat_cond):
    n = lax.axis_size("cols")
    cells, width = suction.shape
    w = SPAN // n
    steps = cells // (SUB * GROUPS)
    params = pltpu.CompilerParams(vmem_limit_bytes=VMEM_LIMIT)
    f32 = jnp.float32

    fit = w % 8 == 0
    kn, kw = (n, w) if fit else (SPAN // 8, 8)

    def to_chunks(a):
        if fit:
            return a
        fields = a.shape[1]
        return jnp.moveaxis(jnp.moveaxis(a, 1, 0).reshape(fields, n, w, cells), 0, 1)

    def from_chunks(a):
        if fit:
            return a
        fields = a.shape[1]
        return jnp.moveaxis(jnp.moveaxis(a, 1, 0).reshape(fields, kn, kw, cells), 0, 1)

    packed = pl.pallas_call(
        pack_kernel,
        out_shape=jax.ShapeDtypeStruct((kn, 7, kw, cells), f32),
        in_specs=[whole(pltpu.HBM)] * 3 + [whole()],
        out_specs=whole(pltpu.HBM),
        scratch_shapes=[
            pltpu.VMEM((2, width // LANES, cells, LANES), f32),
            pltpu.VMEM((width // LANES, cells, LANES), classes.dtype),
            pltpu.VMEM((kn, 7, kw, cells), f32),
            pltpu.SemaphoreType.DMA((3, width // LANES)),
            pltpu.SemaphoreType.DMA((7,)),
        ],
        compiler_params=pltpu.CompilerParams(vmem_limit_bytes=PACK_LIMIT),
        name="pack",
    )(suction, warmth, classes, top.reshape(1, width))
    got = from_chunks(exchange(to_chunks(packed)))

    column = pltpu.VMEM((steps, SUB, GROUPS * width), f32)
    solved = pl.pallas_call(
        functools.partial(step_kernel, n, w),
        out_shape=jax.ShapeDtypeStruct((kn, 4, kw, cells), f32),
        in_specs=[whole(), whole(), whole(pltpu.SMEM), whole(pltpu.SMEM)],
        out_specs=whole(),
        scratch_shapes=[column] * 14 + [pltpu.VMEM((SPAN // LANES, cells, LANES), f32)],
        compiler_params=params,
        name="steps",
    )(got, couplings, k_sat, heat_cond)
    back = from_chunks(exchange(to_chunks(solved)))
    return pl.pallas_call(
        unpack_kernel,
        out_shape=(jax.ShapeDtypeStruct((cells, width), f32),) * 2,
        in_specs=[whole()],
        out_specs=(whole(pltpu.HBM), whole(pltpu.HBM)),
        scratch_shapes=[pltpu.VMEM((2, 2, cells, SPAN), f32), pltpu.SemaphoreType.DMA((2, 2))],
        compiler_params=params,
        name="unpack",
    )(back)


def solution(mesh):
    placed = (P(None, "cols"), P(None, "cols"), P(None, "cols"), P("cols"), P(), P(), P())
    return jax.shard_map(
        on_device,
        mesh=mesh,
        in_specs=placed,
        out_specs=(P(None, "cols"), P(None, "cols")),
        check_vma=False,
    )
```

time: 104 us -> 63.1 us (0.61)
  waiting for transfers between devices: 17.1 us -> 0 us
  starting transfers between devices: 12.6 us -> 0 us
  blocking collectives: 54.6 us -> 49.7 us
  local copies, waits for them, and re-layouts: 3.55 us -> 0.02 us
  Pallas kernels: 14.9 us -> 12.4 us
    all_gather x1 -> x0, blocking collectives: 41.9 us -> none  [on_device(): surface = lax.all_gather(top, 'cols')]
    all_to_all x1 -> x2, blocking collectives: 12.7 us -> 49.7 us  [exchange(): lax.all_to_all(chunks, 'cols', split_axis=0, concat_axis=0, tiled=True)]
    all_to_all x3 -> x0, waiting for transfers between devices: 17.1 us -> none  [exchange(): lax.all_to_all(tiles, 'cols', split_axis=0, concat_axis=0, tiled=True)]
    all_to_all x3 -> x0, starting transfers between devices: 12.6 us -> none  [exchange(): lax.all_to_all(tiles, 'cols', split_axis=0, concat_axis=0, tiled=True)]
    unnamed x21 -> x6, local copies, waits for them, and re-layouts: 3.55 us -> 0.02 us
    pallas_call x4 -> x2, Pallas kernels: 14 us -> 11.5 us  [the longest x1 7.91 us: on_device(): pl.pallas_call(functools.partial(step_kernel, n, w), out_shape=jax.ShapeD...]
  transfers between devices with their start and end apart: 3 -> 0, of which waited for: 2 -> 0; matrix products, arithmetic and copies ran while one was open for 0% -> 0% of each run, Pallas kernels for 12% -> 0%
where the time goes in v3:
time: 63.1 us; the launch traced here: 62.8 us
  blocking collectives  49.7 us (79%)
  Pallas kernels  12.4 us (20%)
  between operations  0.67 us (1%)
    all_to_all x2, blocking collectives, exchange(): lax.all_to_all(chunks, 'cols', split_axis=0, concat_axis=0, tiled=True)  49.7 us
    pallas_call x1, Pallas kernels, on_device(): pl.pallas_call(functools.partial(step_kernel, n, w), out_shape=jax.ShapeD...  7.91 us
    pallas_call x1, Pallas kernels, on_device(): pl.pallas_call(pack_kernel, out_shape=jax.ShapeDtypeStruct((kn, 7, kw, ce...  3.56 us

profile of v3, /device:TPU:0, one launch (start us, length us, event | category | flops | bytes accessed | tf_op | source)
XLA Modules:
  0.0 62.8 jit_solution(6706784985290356369)
XLA Ops:
  0.6 3.6 %pack.1 = f32[32,7,8,128]{3,2,1,0:T(8,128)} custom-call(f32[128,512]{1,0:T(8,128)} %suction.1, f32[128,512]{1,0:T(8,128)} %warmth.1, s32[128,512]{1,0:T(8,128)} %classes.1, f32[1,512]{1,0:T(1,128)} %bitcast.1), custom_call_target="tpu_custom_call" | custom-call | tf_op jit(solution)/shard_map/pack/pallas_call | solution.py:356
  4.2 0.0 copy-start
  4.2 0.0 copy-start.1
  4.2 0.0 copy-start.2
  4.2 30.7 %all_to_all.10.got = f32[32,7,8,128]{3,2,1,0:T(8,128)S(1)} all-to-all(f32[32,7,8,128]{3,2,1,0:T(8,128)} %pack.1), channel_id=1, replica_groups=mesh['cols'=32] {'cols'}, dimensions={0} | all-to-all | bytes 1835008 | tf_op jit(solution)/shard_map/all_to_all | solution.py:330
  35.0 0.0 copy-done
  35.0 0.0 copy-done.1
  35.0 0.0 copy-done.2
  35.0 7.9 %steps.1 = f32[32,4,8,128]{3,2,1,0:T(8,128)S(1)} custom-call(f32[32,7,8,128]{3,2,1,0:T(8,128)S(1)} %all_to_all.10.got, s32[2,128]{1,0:T(2,128)S(1)} %copy-done, f32[8]{0:T(128)S(1)} %copy-done.1, f32[8]{0:T(128)S(1)} %copy-done.2), custom_call_target="tpu_custom_call" | custom-call | tf_op jit(solution)/shard_map/steps/pallas_call | solution.py:374
  42.9 19.0 %all_to_all.11.got = f32[32,4,8,128]{3,2,1,0:T(8,128)S(1)} all-to-all(f32[32,4,8,128]{3,2,1,0:T(8,128)S(1)} %steps.1), channel_id=1, replica_groups=mesh['cols'=32] {'cols'}, dimensions={0} | all-to-all | bytes 1048576 | tf_op jit(solution)/shard_map/all_to_all | solution.py:330
  61.9 0.9 %unpack.1 = (f32[128,512]{1,0:T(8,128)}, f32[128,512]{1,0:T(8,128)}) custom-call(f32[32,4,8,128]{3,2,1,0:T(8,128)S(1)} %all_to_all.11.got), custom_call_target="tpu_custom_call" | custom-call | tf_op jit(solution)/shard_map/unpack/pallas_call | solution.py:384
Async XLA Ops:
  4.2 30.8 %copy-start = (s32[2,128]{1,0:T(2,128)S(1)}, s32[2,128]{1,0:T(2,128)}, u32[]{:S(2)}) copy-start(s32[2,128]{1,0:T(2,128)} %couplings.1) | copy-start | bytes 3076
  4.2 30.8 %copy-start.1 = (f32[8]{0:T(128)S(1)}, f32[8]{0:T(128)}, u32[]{:S(2)}) copy-start(f32[8]{0:T(128)} %k_sat.1) | copy-start | bytes 100
  4.2 30.8 %copy-start.2 = (f32[8]{0:T(128)S(1)}, f32[8]{0:T(128)}, u32[]{:S(2)}) copy-start(f32[8]{0:T(128)} %heat_cond.1) | copy-start | bytes 100

commit v4 on v1

v4 whole, which is shorter than its diff:
```python
import functools

import jax
import jax.numpy as jnp
from jax import lax
from jax.experimental import pallas as pl
from jax.experimental.pallas import tpu as pltpu
from jax.sharding import PartitionSpec as P

SPAN = 256
PAIR_DEV = 4
LANES = 128
CHUNKS = SPAN // LANES
TEAM = 16
OWN = LANES // TEAM
SUB = 8
GROUPS = 2
WIDTH = 2 * LANES
ALL = GROUPS * WIDTH
EDGE = PAIR_DEV * OWN
VMEM_LIMIT = 32 * 1024 * 1024
PACK_LIMIT = 60 * 1024 * 1024
DISTANCES = range(1, PAIR_DEV + 1)
F32 = jnp.float32


def cut_count(n):
    return min(n // TEAM - 1, 2)


def place(cut):
    team = lax.axis_index("cols") // TEAM
    return team, lax.rem(team, 2) == cut


def sign_of(cut):
    return jnp.where(place(cut)[1], 1.0, -1.0).astype(F32)


def reciprocal(x):
    r = pl.reciprocal(x, approx=True)
    return r * (2.0 - x * r)


def sigmoid(x):
    return 0.5 + 0.5 * jnp.tanh(0.5 * x)


def passage(h, t, k):
    s = sigmoid(h)
    return k * (sigmoid(2.0 * t) * s * s + 0.02)


def lanes_of(g, b):
    return slice((g * 2 + b) * LANES, (g * 2 + b + 1) * LANES)


def following(value):
    first, second = value[:, :WIDTH], value[:, WIDTH:]
    return jnp.concatenate([second, pltpu.roll(first, SUB - 1, axis=0)], axis=1)


def preceding(value):
    first, second = value[:, :WIDTH], value[:, WIDTH:]
    return jnp.concatenate([pltpu.roll(second, 1, axis=0), first], axis=1)


def solve(steps, matrix, ratio, lead, value, update):
    c_prev = a_prev = d_prev = None
    for j in range(steps):
        above, main, below, source = matrix(j)
        if j == 0:
            r = reciprocal(main)
            a_prev = above * r
            d_prev = source * r
        else:
            r = reciprocal(main - above * c_prev)
            over = above * r
            a_prev = a_prev * over
            d_prev = source * r + d_prev * over
        c_prev = below * r
        ratio[j] = c_prev
        lead[j] = a_prev
        value[j] = d_prev
    last_c, last_a, last_d = c_prev, a_prev, d_prev
    p_first, a_first, d_first = ratio[steps - 2], lead[steps - 2], value[steps - 2]
    for j in range(steps - 3, -1, -1):
        c = ratio[j]
        p_first = c * p_first
        a_first = lead[j] + c * a_first
        d_first = value[j] + c * d_first
    g = reciprocal(1.0 - last_c * following(a_first))
    up = last_c * following(p_first) * g
    down = last_a * g
    own = (last_d + last_c * following(d_first)) * g
    step = 0
    while step < SUB:
        if step == 0:
            after, before = following, preceding
        else:
            after = functools.partial(pltpu.roll, shift=SUB - step, axis=0)
            before = functools.partial(pltpu.roll, shift=step, axis=0)
        g = reciprocal(1.0 - up * after(down) - down * before(up))
        own = (own + up * after(own) + down * before(own)) * g
        up = up * after(up) * g
        down = down * before(down) * g
        step = max(1, 2 * step)
    over = preceding(own)
    x = own
    update(steps - 1, x)
    for j in range(steps - 2, -1, -1):
        x = ratio[j] * x + (lead[j] * over + value[j])
        update(j, x)


def pack_kernel(suction, warmth, classes, top, out, room, class_room, turned, in_sems, out_sems):
    cells = turned.shape[-1]
    quarters = 2 * CHUNKS
    into, sent = [], []
    for f, field in enumerate((suction, warmth, classes)):
        for q in range(quarters):
            target = class_room.at[q] if f == 2 else room.at[f, q]
            into.append(
                pltpu.make_async_copy(field.at[:, pl.ds(q * LANES, LANES)], target, in_sems.at[f, q])
            )
            into[-1].start()

    def send(slot, value):
        turned[:, slot] = value.T.reshape(TEAM, OWN, cells)
        sent.append(pltpu.make_async_copy(turned.at[:, slot], out.at[:, slot], out_sems.at[slot]))
        sent[-1].start()

    rows = [top[0:1, q * LANES : (q + 1) * LANES] for q in range(quarters)]
    send(3 * quarters, jnp.concatenate(rows + [jnp.zeros((cells - quarters, LANES), F32)], axis=0))
    for f in range(3):
        for q in range(quarters):
            into[f * quarters + q].wait()
            send(f * quarters + q, class_room[q].astype(F32) if f == 2 else room[f, q])
    for copy in sent:
        copy.wait()


def unpack_kernel(got, suction, warmth, room, sems):
    cells = got.shape[-1]
    sent = []
    for f, out in enumerate((suction, warmth)):
        for q in range(2 * CHUNKS):
            room[f, q] = got[:, f * 2 * CHUNKS + q].reshape(LANES, cells).T
            here = out.at[:, pl.ds(q * LANES, LANES)]
            sent.append(pltpu.make_async_copy(room.at[f, q], here, sems.at[f, q]))
            sent[-1].start()
    for copy in sent:
        copy.wait()


def mask_rows(cuts):
    return 3 * PAIR_DEV + cuts * (2 * PAIR_DEV + 1)


def cut_row(cut):
    return 3 * PAIR_DEV + cut * (2 * PAIR_DEV + 1)


def mask_kernel(n, couplings, out):
    pair_rows = couplings[...].astype(F32)
    pairs = couplings.shape[1]
    pair_id = lax.broadcasted_iota(jnp.int32, (pairs, LANES), 0)
    lane = lax.broadcasted_iota(jnp.int32, (pairs, LANES), 1)
    lane_1 = lax.broadcasted_iota(jnp.int32, (SUB, LANES), 1)

    def chosen(dev, s):
        at = (pair_id == dev * PAIR_DEV + s - 1).astype(F32)
        found = jnp.dot(pair_rows, at, preferred_element_type=F32)
        return found[0:1], found[1:2]

    def put(row, value):
        out[row] = jnp.broadcast_to(value, (SUB, LANES))

    team = lax.axis_index("cols") // TEAM
    dev = team * TEAM + lane // OWN
    for s in DISTANCES:
        put(s - 1, chosen(dev, s)[0])
        put(PAIR_DEV + s - 1, chosen(dev - s, s)[1])
        put(2 * PAIR_DEV + s - 1, jnp.where(lane_1 // OWN + s < TEAM, 0.25, 0.0))
    block = lax.rem(lane_1 // EDGE, 2)
    edge = lax.rem(lane, EDGE) // OWN
    edge_1 = lax.rem(lane_1, EDGE) // OWN
    for cut in range(cut_count(n)):
        _, above = place(cut)
        row = cut_row(cut)
        partner = jnp.where(above, team + 1, team - 1)
        there = jnp.logical_and(partner >= 0, partner < n // TEAM)
        factor = jnp.where(there, 0.25, 0.0) * sign_of(cut)
        for s in DISTANCES:
            start = team * TEAM + jnp.where(above, TEAM - PAIR_DEV, -s)
            up, down = chosen(start + edge, s)
            mine = jnp.where(above, up, down)
            inward = jnp.where(above, edge_1, PAIR_DEV - 1 - edge_1)
            active = jnp.logical_and(inward >= PAIR_DEV - s, jnp.abs(mine - block.astype(F32)) < 0.5)
            put(row + s - 1, jnp.where(active, factor, 0.0))
            apart = jnp.where(above, PAIR_DEV - s, s - PAIR_DEV)
            up, down = chosen(start + edge + apart, s)
            theirs = jnp.where(above, down, up)
            put(row + PAIR_DEV + s - 1, jnp.where(jnp.abs(theirs - block.astype(F32)) < 0.5, 1.0, 0.0))
        outward = jnp.where(above, LANES - 1 - lane_1, lane_1)
        put(row + 2 * PAIR_DEV, jnp.where(outward < EDGE, 1.0, 0.0))


def edge_shift(cut, m):
    return lax.rem(EDGE * m + jnp.where(place(cut)[1], EDGE, 0), LANES)


def halo_of(cut, value):
    part = lax.broadcasted_iota(jnp.int32, (SUB, LANES), 1) // EDGE
    packed = None
    for m in range(2 * GROUPS):
        moved = pltpu.roll(value[:, m * LANES : (m + 1) * LANES], edge_shift(cut, m), axis=1)
        packed = moved if m == 0 else jnp.where(part == m, moved, packed)
    return packed


def first_kernel(chunk, cuts, *refs):
    got, k_sat, heat_cond = refs[:3]
    head, warm, perm, conduct, wet, melt, cond, energy, top = refs[3:12]
    halos, load = refs[12 : 12 + cuts], refs[-1]
    cells = got.shape[-1]
    steps = head.shape[0]
    stride = steps * GROUPS

    def take(field, change):
        for b in range(2):
            load[b] = got[:, (field * 2 + b) * CHUNKS + chunk].reshape(LANES, cells).T
            for j in range(steps):
                for g in range(GROUPS):
                    change(j, lanes_of(g, b), load[b, pl.ds(g * steps + j, SUB, stride=stride), :])

    def take_head(j, lanes, v):
        head[j, :, lanes] = v

    def take_warm(j, lanes, v):
        warm[j, :, lanes] = v

    def take_class(j, lanes, v):
        k = jnp.full_like(v, k_sat[0])
        lam = jnp.full_like(v, heat_cond[0])
        for c in range(1, k_sat.shape[0]):
            here = v >= c
            k = jnp.where(here, k_sat[c], k)
            lam = jnp.where(here, heat_cond[c], lam)
        perm[j, :, lanes] = k
        conduct[j, :, lanes] = lam

    take(0, take_head)
    take(1, take_warm)
    take(2, take_class)
    surface = got[:, 6 * CHUNKS].reshape(LANES, cells).T[0:SUB]
    rows = [surface[b * CHUNKS + chunk : b * CHUNKS + chunk + 1] for b in range(2)]
    top[...] = jnp.concatenate(rows * GROUPS, axis=1)
    for j in range(steps):
        h, t, k = head[j], warm[j], perm[j]
        s, f = sigmoid(h), sigmoid(2.0 * t)
        m = 0.05 + 0.4 * s
        wet[j] = s
        melt[j] = f
        cond[j] = k * (f * s * s + 0.02)
        energy[j] = (1.0 + 2.0 * m) * t + 2.0 * m * f
        for cut in range(cuts):
            for i, v in enumerate((h, t, k)):
                halos[cut][i, j] = halo_of(cut, v)


def team_kernel(masks, head, warm, cond, water, heat):
    steps = head.shape[0]
    upper = [masks[s - 1] > 0.5 for s in DISTANCES]
    lower = [masks[PAIR_DEV + s - 1] > 0.5 for s in DISTANCES]
    for j in range(steps):
        for g in range(GROUPS):
            l0, l1 = lanes_of(g, 0), lanes_of(g, 1)
            h0, h1 = head[j, :, l0], head[j, :, l1]
            t0, t1 = warm[j, :, l0], warm[j, :, l1]
            c0, c1 = cond[j, :, l0], cond[j, :, l1]
            total = None
            for s in DISTANCES:
                up, low = upper[s - 1], lower[s - 1]
                back = LANES - s * OWN
                h_low = pltpu.roll(jnp.where(low, h1, h0), back, axis=1)
                t_low = pltpu.roll(jnp.where(low, t1, t0), back, axis=1)
                c_low = pltpu.roll(jnp.where(low, c1, c0), back, axis=1)
                flow = (
                    masks[2 * PAIR_DEV + s - 1]
                    * (jnp.where(up, c1, c0) + c_low)
                    * (jnp.where(up, h1, h0) - h_low + 0.5)
                )
                carried = flow * jnp.where(flow > 0.0, jnp.where(up, t1, t0), t_low)
                flow_in = pltpu.roll(flow, s * OWN, axis=1)
                carried_in = pltpu.roll(carried, s * OWN, axis=1)
                part = (
                    flow_in - flow,
                    jnp.where(low, flow_in, 0.0) - jnp.where(up, flow, 0.0),
                    carried_in - carried,
                    jnp.where(low, carried_in, 0.0) - jnp.where(up, carried, 0.0),
                )
                total = part if total is None else [a + b for a, b in zip(total, part)]
            water[j, :, l0] = total[0] - total[1]
            water[j, :, l1] = total[1]
            heat[j, :, l0] = 2.0 * (total[2] - total[3])
            heat[j, :, l1] = 2.0 * total[3]


def cross_flows(cut, masks, mine, theirs):
    row = cut_row(cut)
    sign = sign_of(cut)
    above = place(cut)[1]
    lane = lax.broadcasted_iota(jnp.int32, (SUB, LANES), 1)
    first_block = lax.rem(lane, 2 * EDGE) < EDGE
    h, t, k = mine
    c = passage(h, t, k)
    far = [theirs[0], theirs[1], passage(*theirs)]
    other = [
        jnp.where(first_block, pltpu.roll(v, LANES - EDGE, axis=1), pltpu.roll(v, EDGE, axis=1)) for v in far
    ]
    water = heat = jnp.zeros((SUB, LANES), F32)
    for s in DISTANCES:
        same = masks[row + PAIR_DEV + s - 1] > 0.5
        picked = [jnp.where(same, a, b) for a, b in zip(far, other)]
        apart = (PAIR_DEV - s) * OWN
        if apart:
            shift = jnp.where(above, apart, LANES - apart)
            picked = [pltpu.roll(v, shift, axis=1) for v in picked]
        h_far, t_far, c_far = picked
        flow = masks[row + s - 1] * (c + c_far) * (sign * (h - h_far) + 0.5)
        water = water - flow
        heat = heat - flow * jnp.where(flow > 0.0, t, t_far)
    return water, heat


def advance(steps, cuts, masks, head, warm, conduct, stored, energy, wet, melt, cond, water, heat, top,
            mine, theirs, new_head, new_warm, new_wet, inflow, warm_inflow, ratio, lead, value, finish):
    for j in range(steps):
        w_parts = [water[j, :, m * LANES : (m + 1) * LANES] for m in range(2 * GROUPS)]
        q_parts = [heat[j, :, m * LANES : (m + 1) * LANES] for m in range(2 * GROUPS)]
        for cut in range(cuts):
            beside = masks[cut_row(cut) + 2 * PAIR_DEV]
            w_far, q_far = cross_flows(cut, masks, mine(cut, j), theirs(cut, j))
            for m in range(2 * GROUPS):
                shift = lax.rem(LANES - edge_shift(cut, m), LANES)
                w_parts[m] = w_parts[m] + beside * pltpu.roll(w_far, shift, axis=1)
                q_parts[m] = q_parts[m] + 2.0 * beside * pltpu.roll(q_far, shift, axis=1)
        for m in range(2 * GROUPS):
            inflow[j, :, m * LANES : (m + 1) * LANES] = w_parts[m]
            warm_inflow[j, :, m * LANES : (m + 1) * LANES] = q_parts[m]

    part = lax.broadcasted_iota(jnp.int32, (SUB, ALL), 0)
    group = lax.broadcasted_iota(jnp.int32, (SUB, ALL), 1) // WIDTH
    first_part = jnp.logical_and(part == 0, group == 0)
    last_part = jnp.logical_and(part == SUB - 1, group == GROUPS - 1)

    def faces(fields, potential):
        face_of, rise_of = [], []
        for j in range(steps):
            if j + 1 < steps:
                c_next, v_next = fields[j + 1], potential[j + 1]
                face = 0.5 * (fields[j] + c_next)
            else:
                c_next, v_next = following(fields[0]), following(potential[0])
                face = jnp.where(last_part, 0.0, 0.5 * (fields[j] + c_next))
            face_of.append(face)
            rise_of.append(v_next - potential[j])
        return face_of, rise_of

    k_face, rise = faces([cond[j] for j in range(steps)], head)
    k_top = jnp.where(first_part, 0.0, preceding(k_face[-1]))
    q_face = [k * (1.0 - d) for k, d in zip(k_face, rise)]
    q_top = jnp.where(first_part, 0.0, preceding(q_face[-1]))

    def water_matrix(j):
        above = k_top if j == 0 else k_face[j - 1]
        into = q_top if j == 0 else q_face[j - 1]
        s = wet[j]
        main = 0.8 * s * (1.0 - s) + 0.02 + above + k_face[j]
        source = inflow[j] + into - q_face[j] - 0.8 * (s - stored[j])
        return above, main, k_face[j], source

    def water_done(j, x):
        h = head[j] + x
        new_head[j] = h
        new_wet[j] = sigmoid(h)

    solve(steps, water_matrix, ratio, lead, value, water_done)

    l_cell = [conduct[j] * (1.5 - 0.5 * melt[j]) for j in range(steps)]
    l_face, rise = faces(l_cell, warm)
    l_top = jnp.where(first_part, 0.0, preceding(l_face[-1]))
    g_face = [l * d for l, d in zip(l_face, rise)]
    g_top = jnp.where(first_part, 0.0, preceding(g_face[-1]))
    surface_lam = jnp.where(first_part, 2.0 * l_cell[0], 0.0)

    def heat_matrix(j):
        above = l_top if j == 0 else l_face[j - 1]
        out_of = g_top if j == 0 else g_face[j - 1]
        t, f = warm[j], melt[j]
        m2 = 0.1 + 0.8 * new_wet[j]
        now = (1.0 + m2) * t + m2 * f
        main = 2.0 + 2.0 * m2 * (1.0 + 2.0 * f * (1.0 - f)) + above + l_face[j]
        source = warm_inflow[j] - out_of + g_face[j] - 2.0 * (now - energy[j])
        if j == 0:
            main = main + surface_lam
            source = source + surface_lam * (top[...] - t)
        return above, main, l_face[j], source

    def heat_done(j, x):
        t = warm[j] + x
        new_warm[j] = t
        finish(j, t)

    solve(steps, heat_matrix, ratio, lead, value, heat_done)


def middle_kernel(cuts, *refs):
    masks, head, warm, perm, conduct, wet, melt, cond, energy, top, water, heat = refs[:12]
    own, far = refs[12 : 12 + cuts], refs[12 + cuts : 12 + 2 * cuts]
    new_head, new_warm, new_wet, new_melt, new_cond = refs[12 + 2 * cuts : 17 + 2 * cuts]
    halos = refs[17 + 2 * cuts : 17 + 3 * cuts]
    inflow, warm_inflow, ratio, lead, value = refs[17 + 3 * cuts :]

    def finish(j, t):
        s, f = new_wet[j], sigmoid(2.0 * t)
        new_melt[j] = f
        new_cond[j] = perm[j] * (f * s * s + 0.02)
        for cut in range(cuts):
            halos[cut][0, j] = halo_of(cut, new_head[j])
            halos[cut][1, j] = halo_of(cut, t)

    advance(
        head.shape[0], cuts, masks, head, warm, conduct, wet, energy, wet, melt, cond, water, heat, top,
        lambda cut, j: [own[cut][i, j] for i in range(3)],
        lambda cut, j: [far[cut][i, j] for i in range(3)],
        new_head, new_warm, new_wet, inflow, warm_inflow, ratio, lead, value, finish,
    )


def last_kernel(chunk, cuts, *refs):
    masks, head, warm, conduct, stored, wet, melt, cond, energy, top, water, heat = refs[:12]
    own, far = refs[12 : 12 + cuts], refs[12 + cuts : 12 + 2 * cuts]
    own_k, far_k = refs[12 + 2 * cuts : 12 + 3 * cuts], refs[12 + 3 * cuts : 12 + 4 * cuts]
    others = refs[12 + 4 * cuts : -10]
    out, new_head, new_warm, new_wet, inflow, warm_inflow, ratio, lead, value, load = refs[-10:]
    steps = head.shape[0]
    cells = steps * GROUPS * SUB
    stride = steps * GROUPS
    advance(
        steps, cuts, masks, head, warm, conduct, stored, energy, wet, melt, cond, water, heat, top,
        lambda cut, j: [own[cut][0, j], own[cut][1, j], own_k[cut][2, j]],
        lambda cut, j: [far[cut][0, j], far[cut][1, j], far_k[cut][2, j]],
        new_head, new_warm, new_wet, inflow, warm_inflow, ratio, lead, value, lambda j, t: None,
    )
    final = chunk == CHUNKS - 1
    for f, field in enumerate((new_head, new_warm)):
        for b in range(2):
            slot = f * 2 + b
            for j in range(steps):
                for g in range(GROUPS):
                    load[slot, pl.ds(g * steps + j, SUB, stride=stride), :] = field[j, :, lanes_of(g, b)]
            turned = load[slot].T.reshape(TEAM, OWN, cells)
            if final:
                out[:, slot * CHUNKS + chunk] = turned
                for c, other in enumerate(others):
                    out[:, slot * CHUNKS + c] = other[:, slot]
            else:
                out[:, slot] = turned


def whole(memory=pltpu.VMEM):
    return pl.BlockSpec(memory_space=memory)


def call(kernel, name, args, outs, scratch=(), specs=None, out_specs=None, limit=VMEM_LIMIT, work=2_000_000):
    return pl.pallas_call(
        kernel,
        out_shape=[jax.ShapeDtypeStruct(shape, F32) for shape in outs],
        in_specs=specs or [whole()] * len(args),
        out_specs=out_specs or [whole()] * len(outs),
        scratch_shapes=scratch,
        compiler_params=pltpu.CompilerParams(vmem_limit_bytes=limit),
        cost_estimate=pl.CostEstimate(flops=work, bytes_accessed=work, transcendentals=0),
        name=name,
    )(*args)


def exchange(tiles, n):
    teams = [list(range(start, start + TEAM)) for start in range(0, n, TEAM)]
    return lax.all_to_all(
        tiles, "cols", split_axis=0, concat_axis=0, tiled=True, axis_index_groups=teams
    )


def swap(cut, n, value):
    pairs = []
    for team in range(cut, n // TEAM - 1, 2):
        for i in range(team * TEAM, (team + 1) * TEAM):
            pairs += [(i, i + TEAM), (i + TEAM, i)]
    return lax.ppermute(value, "cols", pairs)


def on_device(suction, warmth, classes, top, couplings, k_sat, heat_cond):
    n = lax.axis_size("cols")
    cells, width = suction.shape
    steps = cells // (SUB * GROUPS)
    quarters = width // LANES
    cuts = cut_count(n)
    column = (steps, SUB, ALL)
    halo = (steps, SUB, LANES)
    room = pltpu.VMEM(column, F32)
    smem = whole(pltpu.SMEM)
    hbm = whole(pltpu.HBM)

    masks = call(
        functools.partial(mask_kernel, n), "masks", (couplings,), [(mask_rows(cuts), SUB, LANES)]
    )[0]
    packed = call(
        pack_kernel,
        "pack",
        (suction, warmth, classes, top.reshape(1, width)),
        [(TEAM, 3 * quarters + 1, OWN, cells)],
        scratch=[
            pltpu.VMEM((2, quarters, cells, LANES), F32),
            pltpu.VMEM((quarters, cells, LANES), classes.dtype),
            pltpu.VMEM((TEAM, 3 * quarters + 1, OWN, cells), F32),
            pltpu.SemaphoreType.DMA((3, quarters)),
            pltpu.SemaphoreType.DMA((3 * quarters + 1,)),
        ],
        specs=[hbm, hbm, hbm, whole()],
        out_specs=[hbm],
        limit=PACK_LIMIT,
    )[0]
    got = exchange(packed, n)

    first, sides = [], []
    for c in range(CHUNKS):
        values = call(
            functools.partial(first_kernel, c, cuts),
            "first",
            (got, k_sat, heat_cond),
            [column] * 8 + [(1, ALL)] + [(3,) + halo] * cuts,
            scratch=[pltpu.VMEM((2, cells, LANES), F32)],
            specs=[whole(), smem, smem],
        )
        first.append(values[:9])
        mine = values[9:]
        sides.append((mine, [swap(cut, n, v) for cut, v in enumerate(mine)]))

    second, later = [], []
    for c in range(CHUNKS):
        head, warm, perm, conduct, wet, melt, cond, energy, surface = first[c]
        water, heat = call(team_kernel, "team", (masks, head, warm, cond), [column] * 2)
        mine, theirs = sides[c]
        values = call(
            functools.partial(middle_kernel, cuts),
            "middle",
            (masks, head, warm, perm, conduct, wet, melt, cond, energy, surface, water, heat, *mine, *theirs),
            [column] * 5 + [(2,) + halo] * cuts,
            scratch=[room] * 5,
        )
        second.append(values[:5])
        mine = values[5:]
        later.append((mine, [swap(cut, n, v) for cut, v in enumerate(mine)]))

    done = []
    for c in range(CHUNKS):
        conduct, stored, energy, surface = first[c][3], first[c][4], first[c][7], first[c][8]
        head, warm, wet, melt, cond = second[c]
        water, heat = call(team_kernel, "team", (masks, head, warm, cond), [column] * 2)
        mine, theirs = later[c]
        mine_k, theirs_k = sides[c]
        final = c == CHUNKS - 1
        done += call(
            functools.partial(last_kernel, c, cuts),
            "last",
            (
                masks, head, warm, conduct, stored, wet, melt, cond, energy, surface, water, heat,
                *mine, *theirs, *mine_k, *theirs_k, *(done if final else ()),
            ),
            [(TEAM, 2 * quarters if final else 4, OWN, cells)],
            scratch=[room] * 8 + [pltpu.VMEM((4, cells, LANES), F32)],
        )
    back = exchange(done[-1], n)
    return tuple(
        call(
            unpack_kernel,
            "unpack",
            (back,),
            [(cells, width)] * 2,
            scratch=[
                pltpu.VMEM((2, quarters, cells, LANES), F32),
                pltpu.SemaphoreType.DMA((2, quarters)),
            ],
            out_specs=[hbm, hbm],
        )
    )


def solution(mesh):
    placed = (P(None, "cols"), P(None, "cols"), P(None, "cols"), P("cols"), P(), P(), P())
    return jax.shard_map(
        on_device,
        mesh=mesh,
        in_specs=placed,
        out_specs=(P(None, "cols"), P(None, "cols")),
        check_vma=False,
    )
```

time: 104 us -> 63.2 us (0.61)
  blocking collectives: 54.6 us -> 33.5 us
  waiting for transfers between devices: 17.1 us -> 0.01 us
  Pallas kernels: 14.9 us -> 22.2 us
  starting transfers between devices: 12.6 us -> 6.11 us
  local copies, waits for them, and re-layouts: 3.55 us -> 0.29 us
    all_gather x1 -> x0, blocking collectives: 41.9 us -> none  [on_device(): surface = lax.all_gather(top, 'cols')]
    all_to_all x1 -> x2, blocking collectives: 12.7 us -> 33.5 us  [exchange(): lax.all_to_all(tiles, 'cols', split_axis=0, concat_axis=0, tiled=True, ax...]
    all_to_all x3 -> x0, waiting for transfers between devices: 17.1 us -> none  [exchange(): lax.all_to_all(tiles, 'cols', split_axis=0, concat_axis=0, tiled=True)]
    all_to_all x3 -> x0, starting transfers between devices: 12.6 us -> none  [exchange(): lax.all_to_all(tiles, 'cols', split_axis=0, concat_axis=0, tiled=True)]
    pallas_call x5 -> x13, Pallas kernels: 14.9 us -> 22.2 us  [call(): pl.pallas_call(kernel, out_shape=[jax.ShapeDtypeStruct(shape, F32) for sh...]
    ppermute x0 -> x4, starting transfers between devices: none -> 6.11 us  [swap(): return lax.ppermute(value, 'cols', pairs)]
    unnamed x21 -> x6, local copies, waits for them, and re-layouts: 3.55 us -> 0.29 us
  transfers between devices with their start and end apart: 3 -> 4, of which waited for: 2 -> 0; matrix products, arithmetic and copies ran while one was open for 0% -> 0% of each run, Pallas kernels for 12% -> 25%
where the time goes in v4:
time: 63.2 us; the launch traced here: 62.8 us
  blocking collectives  33.5 us (53%)
  Pallas kernels  22.2 us (35%)
  starting transfers between devices  6.11 us (10%)
  between operations  0.74 us (1%)
    all_to_all x2, blocking collectives, exchange(): lax.all_to_all(tiles, 'cols', split_axis=0, concat_axis=0, tiled=True, ax...  33.5 us
    pallas_call x13, Pallas kernels, call(): pl.pallas_call(kernel, out_shape=[jax.ShapeDtypeStruct(shape, F32) for sh...  22.2 us
    ppermute x4, starting transfers between devices, swap(): return lax.ppermute(value, 'cols', pairs)  6.11 us
  transfers between devices with their start and end apart: 4, of which 0 were waited for; matrix products, arithmetic and copies ran while one was open for 0% of the time, Pallas kernels for 25%

profile of v4, /device:TPU:0, one launch (start us, length us, event | category | flops | bytes accessed | tf_op | source)
XLA Modules:
  0.0 62.8 jit_solution(3463370005200767715)
XLA Ops:
  0.6 3.6 %pack.1 = f32[16,13,8,128]{3,2,1,0:T(8,128)} custom-call(f32[128,512]{1,0:T(8,128)} %suction.1, f32[128,512]{1,0:T(8,128)} %warmth.1, s32[128,512]{1,0:T(8,128)} %classes.1, f32[1,512]{1,0:T(1,128)} %bitcast.1), custom_call_target="tpu_custom_call" | custom-call | flops 2000000 | bytes 2000000 | tf_op jit(solution)/shard_map/pack/pallas_call | solution.py:478
  4.3 0.0 copy-start
  4.3 0.0 copy-start.1
  4.3 20.4 %all_to_all.10.refs_0_ = f32[16,13,8,128]{3,2,1,0:T(8,128)S(1)} all-to-all(f32[16,13,8,128]{3,2,1,0:T(8,128)} %pack.1), channel_id=1, replica_groups={{0,1,2,3,4,5,6,7,8,9,10,11,12,13,14,15},{16,17,18,19,20,21,22,23,24,25,..., dimensions={0} | all-to-all | bytes 1703936 | tf_op jit(solution)/shard_map/all_to_all | solution.py:492
  24.6 0.0 copy-done
  24.6 0.0 copy-done.1
  24.6 1.0 %first.3 = (f32[8,8,512]{2,1,0:T(8,128)S(1)}, f32[8,8,512]{2,1,0:T(8,128)S(1)}, f32[8,8,512]{2,1,0:T(8,128)S(1)}, f32[8,8,512]{2,1,0:T(8,128)S(1)}, f32[8,8,512]...) custom-call(f32[16,13,8,128]{3,2,1,0:T(8,128)S(1)} %all_to_all.10.re, ...), custom_call_target="tpu_custom_call" | custom-call | flops 2000000 | bytes 2000000 | tf_op jit(solution)/shard_map/first/pallas_call | solution.py:478
  25.7 2.7 %collective-permute-start.2 = (f32[3,8,8,128]{3,2,1,0:T(8,128)S(1)}, f32[3,8,8,128]{3,2,1,0:T(8,128)S(1)}, u32[]{:S(2)}, u32[]{:S(2)}) collective-permute-start(f32[3,8,8,128]{3,2,1,0:T(8,128)S(1)} %get-tuple-element.73.refs_12_.refs_14_), channel_id=1, source_target_pairs={{0,16},{16,0},{1,17},{17,1},{2,18},{18,2},{3,19},{19,3},{4,20},{20... | collective-permute-start | bytes 294920 | tf_op jit(solution)/shard_map/ppermute | solution.py:502
  28.3 1.0 %first.2 = (f32[8,8,512]{2,1,0:T(8,128)S(1)}, f32[8,8,512]{2,1,0:T(8,128)S(1)}, f32[8,8,512]{2,1,0:T(8,128)S(1)}, f32[8,8,512]{2,1,0:T(8,128)S(1)}, f32[8,8,512]...) custom-call(f32[16,13,8,128]{3,2,1,0:T(8,128)S(1)} %all_to_all.10.re, ...), custom_call_target="tpu_custom_call" | custom-call | flops 2000000 | bytes 2000000 | tf_op jit(solution)/shard_map/first/pallas_call | solution.py:478
  29.4 0.0 copy-start.2
  29.4 0.4 collective-permute-start
  29.8 0.3 copy-done.2
  30.0 0.3 masks.1.refs_0_
  30.3 2.9 %team.6 = (f32[8,8,512]{2,1,0:T(8,128)S(1)}, f32[8,8,512]{2,1,0:T(8,128)S(1)}) custom-call(f32[21,8,128]{2,1,0:T(8,128)S(1)} %masks.1.refs_0_, f32[8,8,512]{2,1,0:T(8,128)S(1)} %get-tuple-element.62.head.refs_1_, f32[8,8,512]{2,1,0:T(8,128)S(1)} %get-tuple-element.63.warm.refs_2_, f32[8,8,512]{2,1,0:T(8,128)S(1)} %get-tuple-element.68.cond.refs_7_), custom_call_target="tpu_custom_call" | custom-call | flops 2000000 | bytes 2000000 | tf_op jit(solution)/shard_map/team/pallas_call | solution.py:478
  33.3 2.9 %team.4 = (f32[8,8,512]{2,1,0:T(8,128)S(1)}, f32[8,8,512]{2,1,0:T(8,128)S(1)}) custom-call(f32[21,8,128]{2,1,0:T(8,128)S(1)} %masks.1.refs_0_, f32[8,8,512]{2,1,0:T(8,128)S(1)} %get-tuple-element.42.head.refs_1_, f32[8,8,512]{2,1,0:T(8,128)S(1)} %get-tuple-element.43.warm.refs_2_, f32[8,8,512]{2,1,0:T(8,128)S(1)} %get-tuple-element.48.cond.refs_7_), custom_call_target="tpu_custom_call" | custom-call | flops 2000000 | bytes 2000000 | tf_op jit(solution)/shard_map/team/pallas_call | solution.py:478
  36.2 0.0 collective-permute-done.2.refs_13_.refs_15_
  36.2 0.8 %middle.3 = (f32[8,8,512]{2,1,0:T(8,128)S(1)}, f32[8,8,512]{2,1,0:T(8,128)S(1)}, f32[8,8,512]{2,1,0:T(8,128)S(1)}, f32[8,8,512]{2,1,0:T(8,128)S(1)}, f32[8,8,512...) custom-call(f32[21,8,128]{2,1,0:T(8,128)S(1)} %masks.1.refs_0_, f32[8,8,512]{2,1,0:T(8,128)S(1)} %get-tuple-element.62.head.refs_1_, ...), custom_call_target="tpu_custom_call" | custom-call | flops 2000000 | bytes 2000000 | tf_op jit(solution)/shard_map/middle/pallas_call | solution.py:478
  37.1 2.4 %collective-permute-start.3 = (f32[2,8,8,128]{3,2,1,0:T(8,128)S(1)}, f32[2,8,8,128]{3,2,1,0:T(8,128)S(1)}, u32[]{:S(2)}, u32[]{:S(2)}) collective-permute-start(f32[2,8,8,128]{3,2,1,0:T(8,128)S(1)} %get-tuple-element.81.refs_12_), channel_id=1, source_target_pairs={{0,16},{16,0},{1,17},{17,1},{2,18},{18,2},{3,19},{19,3},{4,20},{20... | collective-permute-start | bytes 196616 | tf_op jit(solution)/shard_map/ppermute | solution.py:502
  39.5 0.0 collective-permute-done.refs_13_.refs_15_
  39.5 0.8 %middle.2 = (f32[8,8,512]{2,1,0:T(8,128)S(1)}, f32[8,8,512]{2,1,0:T(8,128)S(1)}, f32[8,8,512]{2,1,0:T(8,128)S(1)}, f32[8,8,512]{2,1,0:T(8,128)S(1)}, f32[8,8,512...) custom-call(f32[21,8,128]{2,1,0:T(8,128)S(1)} %masks.1.refs_0_, f32[8,8,512]{2,1,0:T(8,128)S(1)} %get-tuple-element.42.head.refs_1_, ...), custom_call_target="tpu_custom_call" | custom-call | flops 2000000 | bytes 2000000 | tf_op jit(solution)/shard_map/middle/pallas_call | solution.py:478
  40.3 0.7 %collective-permute-start.1 = (f32[2,8,8,128]{3,2,1,0:T(8,128)S(1)}, f32[2,8,8,128]{3,2,1,0:T(8,128)S(1)}, u32[]{:S(2)}, u32[]{:S(2)}) collective-permute-start(f32[2,8,8,128]{3,2,1,0:T(8,128)S(1)} %get-tuple-element.61.refs_12_), channel_id=1, source_target_pairs={{0,16},{16,0},{1,17},{17,1},{2,18},{18,2},{3,19},{19,3},{4,20},{20... | collective-permute-start | bytes 196616 | tf_op jit(solution)/shard_map/ppermute | solution.py:502
  41.0 2.9 %team.7 = (f32[8,8,512]{2,1,0:T(8,128)S(1)}, f32[8,8,512]{2,1,0:T(8,128)S(1)}) custom-call(f32[21,8,128]{2,1,0:T(8,128)S(1)} %masks.1.refs_0_, f32[8,8,512]{2,1,0:T(8,128)S(1)} %get-tuple-element.74.head.refs_1_, f32[8,8,512]{2,1,0:T(8,128)S(1)} %get-tuple-element.75.warm.refs_2_, f32[8,8,512]{2,1,0:T(8,128)S(1)} %get-tuple-element.78.cond.refs_7_), custom_call_target="tpu_custom_call" | custom-call | flops 2000000 | bytes 2000000 | tf_op jit(solution)/shard_map/team/pallas_call | solution.py:478
  43.9 2.9 %team.5 = (f32[8,8,512]{2,1,0:T(8,128)S(1)}, f32[8,8,512]{2,1,0:T(8,128)S(1)}) custom-call(f32[21,8,128]{2,1,0:T(8,128)S(1)} %masks.1.refs_0_, f32[8,8,512]{2,1,0:T(8,128)S(1)} %get-tuple-element.54.head.refs_1_, f32[8,8,512]{2,1,0:T(8,128)S(1)} %get-tuple-element.55.warm.refs_2_, f32[8,8,512]{2,1,0:T(8,128)S(1)} %get-tuple-element.58.cond.refs_7_), custom_call_target="tpu_custom_call" | custom-call | flops 2000000 | bytes 2000000 | tf_op jit(solution)/shard_map/team/pallas_call | solution.py:478
  46.9 0.0 collective-permute-done.3.refs_13_
  46.9 0.9 %last.2.refs_16_ = f32[16,4,8,128]{3,2,1,0:T(8,128)S(1)} custom-call(f32[21,8,128]{2,1,0:T(8,128)S(1)} %masks.1.refs_0_, f32[8,8,512]{2,1,0:T(8,128)S(1)} %get-tuple-element.74.head.refs_1_, f32[8,8,512]{2,1,0:T(8,128)S(1)} %get-tuple-element.75.warm.refs_2_, f32[8,8,512]{2,1,0:T(8,128)S(1)} %get-tuple-element.65.refs_4_.refs_3_, ...), custom_call_target="tpu_custom_call" | custom-call | flops 2000000 | bytes 2000000 | tf_op jit(solution)/shard_map/last/pallas_call | solution.py:478
  47.8 0.0 collective-permute-done.1.refs_13_
  47.8 0.9 %last.3 = f32[16,8,8,128]{3,2,1,0:T(8,128)S(1)} custom-call(f32[21,8,128]{2,1,0:T(8,128)S(1)} %masks.1.refs_0_, f32[8,8,512]{2,1,0:T(8,128)S(1)} %get-tuple-element.54.head.refs_1_, f32[8,8,512]{2,1,0:T(8,128)S(1)} %get-tuple-element.55.warm.refs_2_, f32[8,8,512]{2,1,0:T(8,128)S(1)} %get-tuple-element.45.refs_4_.refs_3_, ...), custom_call_target="tpu_custom_call" | custom-call | flops 2000000 | bytes 2000000 | tf_op jit(solution)/shard_map/last/pallas_call | solution.py:478
  48.7 13.2 %all_to_all.11.got = f32[16,8,8,128]{3,2,1,0:T(8,128)S(1)} all-to-all(f32[16,8,8,128]{3,2,1,0:T(8,128)S(1)} %last.3), channel_id=1, replica_groups={{0,1,2,3,4,5,6,7,8,9,10,11,12,13,14,15},{16,17,18,19,20,21,22,23,24,25,..., dimensions={0} | all-to-all | bytes 1048576 | tf_op jit(solution)/shard_map/all_to_all | solution.py:492
  61.9 0.9 %unpack.1 = (f32[128,512]{1,0:T(8,128)}, f32[128,512]{1,0:T(8,128)}) custom-call(f32[16,8,8,128]{3,2,1,0:T(8,128)S(1)} %all_to_all.11.got), custom_call_target="tpu_custom_call" | custom-call | flops 2000000 | bytes 2000000 | tf_op jit(solution)/shard_map/unpack/pallas_call | solution.py:478
Async XLA Ops:
  4.3 20.4 %copy-start = (f32[8]{0:T(128)S(1)}, f32[8]{0:T(128)}, u32[]{:S(2)}) copy-start(f32[8]{0:T(128)} %refs_1_.3) | copy-start | bytes 100
  4.3 20.4 %copy-start.1 = (f32[8]{0:T(128)S(1)}, f32[8]{0:T(128)}, u32[]{:S(2)}) copy-start(f32[8]{0:T(128)} %refs_2_.3) | copy-start | bytes 100
  25.7 10.5 %collective-permute-start.2 = (f32[3,8,8,128]{3,2,1,0:T(8,128)S(1)}, f32[3,8,8,128]{3,2,1,0:T(8,128)S(1)}, u32[]{:S(2)}, u32[]{:S(2)}) collective-permute-start(f32[3,8,8,128]{3,2,1,0:T(8,128)S(1)} %get-tuple-element.73.refs_12_.refs_14_), channel_id=1, source_target_pairs={{0,16},{16,0},{1,17},{17,1},{2,18},{18,2},{3,19},{19,3},{4,20},{20... | collective-permute-start | bytes 294920 | tf_op jit(solution)/shard_map/ppermute | solution.py:502
  29.4 0.7 %copy-start.2 = (s32[2,128]{1,0:T(2,128)S(1)}, s32[2,128]{1,0:T(2,128)}, u32[]{:S(2)}) copy-start(s32[2,128]{1,0:T(2,128)} %couplings.1) | copy-start | bytes 3076
  29.4 10.1 %collective-permute-start = (f32[3,8,8,128]{3,2,1,0:T(8,128)S(1)}, f32[3,8,8,128]{3,2,1,0:T(8,128)S(1)}, u32[]{:S(2)}, u32[]{:S(2)}) collective-permute-start(f32[3,8,8,128]{3,2,1,0:T(8,128)S(1)} %get-tuple-element.53.refs_12_.refs_14_), channel_id=1, source_target_pairs={{0,16},{16,0},{1,17},{17,1},{2,18},{18,2},{3,19},{19,3},{4,20},{20... | collective-permute-start | bytes 294920 | tf_op jit(solution)/shard_map/ppermute | solution.py:502
  37.1 9.8 %collective-permute-start.3 = (f32[2,8,8,128]{3,2,1,0:T(8,128)S(1)}, f32[2,8,8,128]{3,2,1,0:T(8,128)S(1)}, u32[]{:S(2)}, u32[]{:S(2)}) collective-permute-start(f32[2,8,8,128]{3,2,1,0:T(8,128)S(1)} %get-tuple-element.81.refs_12_), channel_id=1, source_target_pairs={{0,16},{16,0},{1,17},{17,1},{2,18},{18,2},{3,19},{19,3},{4,20},{20... | collective-permute-start | bytes 196616 | tf_op jit(solution)/shard_map/ppermute | solution.py:502
  40.3 7.5 %collective-permute-start.1 = (f32[2,8,8,128]{3,2,1,0:T(8,128)S(1)}, f32[2,8,8,128]{3,2,1,0:T(8,128)S(1)}, u32[]{:S(2)}, u32[]{:S(2)}) collective-permute-start(f32[2,8,8,128]{3,2,1,0:T(8,128)S(1)} %get-tuple-element.61.refs_12_), channel_id=1, source_target_pairs={{0,16},{16,0},{1,17},{17,1},{2,18},{18,2},{3,19},{19,3},{4,20},{20... | collective-permute-start | bytes 196616 | tf_op jit(solution)/shard_map/ppermute | solution.py:502

commit v5 on v4

--- a/solution.py
+++ b/solution.py
@@ -227,39 +227,32 @@
     steps = head.shape[0]
     stride = steps * GROUPS
 
-    def take(field, change):
+    for field in range(3):
         for b in range(2):
-            load[b] = got[:, (field * 2 + b) * CHUNKS + chunk].reshape(LANES, cells).T
-            for j in range(steps):
-                for g in range(GROUPS):
-                    change(j, lanes_of(g, b), load[b, pl.ds(g * steps + j, SUB, stride=stride), :])
-
-    def take_head(j, lanes, v):
-        head[j, :, lanes] = v
-
-    def take_warm(j, lanes, v):
-        warm[j, :, lanes] = v
-
-    def take_class(j, lanes, v):
+            load[field * 2 + b] = got[:, (field * 2 + b) * CHUNKS + chunk].reshape(LANES, cells).T
+    surface = got[:, 6 * CHUNKS].reshape(LANES, cells).T[0:SUB]
+    rows = [surface[b * CHUNKS + chunk : b * CHUNKS + chunk + 1] for b in range(2)]
+    top[...] = jnp.concatenate(rows * GROUPS, axis=1)
+
+    def fetch(field, j):
+        parts = [
+            load[field * 2 + b, pl.ds(g * steps + j, SUB, stride=stride), :]
+            for g in range(GROUPS)
+            for b in range(2)
+        ]
+        return jnp.concatenate(parts, axis=1)
+
+    for j in range(steps):
+        h, t, v = [fetch(field, j) for field in range(3)]
         k = jnp.full_like(v, k_sat[0])
         lam = jnp.full_like(v, heat_cond[0])
         for c in range(1, k_sat.shape[0]):
             here = v >= c
             k = jnp.where(here, k_sat[c], k)
             lam = jnp.where(here, heat_cond[c], lam)
-        perm[j, :, lanes] = k
-        conduct[j, :, lanes] = lam
-
-    take(0, take_head)
-    take(1, take_warm)
-    take(2, take_class)
-    surface = got[:, 6 * CHUNKS].reshape(LANES, cells).T[0:SUB]
-    rows = [surface[b * CHUNKS + chunk : b * CHUNKS + chunk + 1] for b in range(2)]
-    top[...] = jnp.concatenate(rows * GROUPS, axis=1)
-    for j in range(steps):
-        h, t, k = head[j], warm[j], perm[j]
         s, f = sigmoid(h), sigmoid(2.0 * t)
         m = 0.05 + 0.4 * s
+        head[j], warm[j], perm[j], conduct[j] = h, t, k, lam
         wet[j] = s
         melt[j] = f
         cond[j] = k * (f * s * s + 0.02)
@@ -269,7 +262,7 @@
                 halos[cut][i, j] = halo_of(cut, v)
 
 
-def team_kernel(masks, head, warm, cond, water, heat):
+def team_kernel(masks, head, warm, cond, water_out, heat_out, water, heat):
     steps = head.shape[0]
     upper = [masks[s - 1] > 0.5 for s in DISTANCES]
     lower = [masks[PAIR_DEV + s - 1] > 0.5 for s in DISTANCES]
@@ -305,6 +298,8 @@
             water[j, :, l1] = total[1]
             heat[j, :, l0] = 2.0 * (total[2] - total[3])
             heat[j, :, l1] = 2.0 * total[3]
+    water_out[...] = water[...]
+    heat_out[...] = heat[...]
 
 
 def cross_flows(cut, masks, mine, theirs):
@@ -542,7 +537,7 @@
             "first",
             (got, k_sat, heat_cond),
             [column] * 8 + [(1, ALL)] + [(3,) + halo] * cuts,
-            scratch=[pltpu.VMEM((2, cells, LANES), F32)],
+            scratch=[pltpu.VMEM((6, cells, LANES), F32)],
             specs=[whole(), smem, smem],
         )
         first.append(values[:9])
@@ -552,7 +547,7 @@
     second, later = [], []
     for c in range(CHUNKS):
         head, warm, perm, conduct, wet, melt, cond, energy, surface = first[c]
-        water, heat = call(team_kernel, "team", (masks, head, warm, cond), [column] * 2)
+        water, heat = call(team_kernel, "team", (masks, head, warm, cond), [column] * 2, scratch=[room] * 2)
         mine, theirs = sides[c]
         values = call(
             functools.partial(middle_kernel, cuts),
@@ -569,7 +564,7 @@
     for c in range(CHUNKS):
         conduct, stored, energy, surface = first[c][3], first[c][4], first[c][7], first[c][8]
         head, warm, wet, melt, cond = second[c]
-        water, heat = call(team_kernel, "team", (masks, head, warm, cond), [column] * 2)
+        water, heat = call(team_kernel, "team", (masks, head, warm, cond), [column] * 2, scratch=[room] * 2)
         mine, theirs = later[c]
         mine_k, theirs_k = sides[c]
         final = c == CHUNKS - 1

time: 63.2 us -> 63.1 us (level)
  no operation moved by 1% of the time
where the time goes in v5:
time: 63.1 us; the launch traced here: 62.8 us
  blocking collectives  33.5 us (53%)
  Pallas kernels  22.1 us (35%)
  starting transfers between devices  6.11 us (10%)
  between operations  0.75 us (1%)
    all_to_all x2, blocking collectives, exchange(): lax.all_to_all(tiles, 'cols', split_axis=0, concat_axis=0, tiled=True, ax...  33.5 us
    pallas_call x13, Pallas kernels, call(): pl.pallas_call(kernel, out_shape=[jax.ShapeDtypeStruct(shape, F32) for sh...  22.1 us
    ppermute x4, starting transfers between devices, swap(): return lax.ppermute(value, 'cols', pairs)  6.11 us
  transfers between devices with their start and end apart: 4, of which 0 were waited for; matrix products, arithmetic and copies ran while one was open for 0% of the time, Pallas kernels for 25%

profile of v5, /device:TPU:0, one launch (start us, length us, event | category | flops | bytes accessed | tf_op | source)
XLA Modules:
  0.0 62.8 jit_solution(11633258885336686903)
XLA Ops:
  0.6 3.6 %pack.1 = f32[16,13,8,128]{3,2,1,0:T(8,128)} custom-call(f32[128,512]{1,0:T(8,128)} %suction.1, f32[128,512]{1,0:T(8,128)} %warmth.1, s32[128,512]{1,0:T(8,128)} %classes.1, f32[1,512]{1,0:T(1,128)} %bitcast.1), custom_call_target="tpu_custom_call" | custom-call | flops 2000000 | bytes 2000000 | tf_op jit(solution)/shard_map/pack/pallas_call | solution.py:473
  4.3 0.0 copy-start
  4.3 0.0 copy-start.1
  4.3 20.4 %all_to_all.10.refs_0_ = f32[16,13,8,128]{3,2,1,0:T(8,128)S(1)} all-to-all(f32[16,13,8,128]{3,2,1,0:T(8,128)} %pack.1), channel_id=1, replica_groups={{0,1,2,3,4,5,6,7,8,9,10,11,12,13,14,15},{16,17,18,19,20,21,22,23,24,25,..., dimensions={0} | all-to-all | bytes 1703936 | tf_op jit(solution)/shard_map/all_to_all | solution.py:487
  24.6 0.0 copy-done
  24.6 0.0 copy-done.1
  24.6 1.0 %first.3 = (f32[8,8,512]{2,1,0:T(8,128)S(1)}, f32[8,8,512]{2,1,0:T(8,128)S(1)}, f32[8,8,512]{2,1,0:T(8,128)S(1)}, f32[8,8,512]{2,1,0:T(8,128)S(1)}, f32[8,8,512]...) custom-call(f32[16,13,8,128]{3,2,1,0:T(8,128)S(1)} %all_to_all.10.re, ...), custom_call_target="tpu_custom_call" | custom-call | flops 2000000 | bytes 2000000 | tf_op jit(solution)/shard_map/first/pallas_call | solution.py:473
  25.6 2.7 %collective-permute-start.2 = (f32[3,8,8,128]{3,2,1,0:T(8,128)S(1)}, f32[3,8,8,128]{3,2,1,0:T(8,128)S(1)}, u32[]{:S(2)}, u32[]{:S(2)}) collective-permute-start(f32[3,8,8,128]{3,2,1,0:T(8,128)S(1)} %get-tuple-element.73.refs_12_.refs_14_), channel_id=1, source_target_pairs={{0,16},{16,0},{1,17},{17,1},{2,18},{18,2},{3,19},{19,3},{4,20},{20... | collective-permute-start | bytes 294920 | tf_op jit(solution)/shard_map/ppermute | solution.py:497
  28.3 1.0 %first.2 = (f32[8,8,512]{2,1,0:T(8,128)S(1)}, f32[8,8,512]{2,1,0:T(8,128)S(1)}, f32[8,8,512]{2,1,0:T(8,128)S(1)}, f32[8,8,512]{2,1,0:T(8,128)S(1)}, f32[8,8,512]...) custom-call(f32[16,13,8,128]{3,2,1,0:T(8,128)S(1)} %all_to_all.10.re, ...), custom_call_target="tpu_custom_call" | custom-call | flops 2000000 | bytes 2000000 | tf_op jit(solution)/shard_map/first/pallas_call | solution.py:473
  29.3 0.0 copy-start.2
  29.3 0.4 collective-permute-start
  29.7 0.3 copy-done.2
  30.0 0.3 masks.1.refs_0_
  30.2 2.9 %team.6 = (f32[8,8,512]{2,1,0:T(8,128)S(1)}, f32[8,8,512]{2,1,0:T(8,128)S(1)}) custom-call(f32[21,8,128]{2,1,0:T(8,128)S(1)} %masks.1.refs_0_, f32[8,8,512]{2,1,0:T(8,128)S(1)} %get-tuple-element.62.head.refs_1_, f32[8,8,512]{2,1,0:T(8,128)S(1)} %get-tuple-element.63.warm.refs_2_, f32[8,8,512]{2,1,0:T(8,128)S(1)} %get-tuple-element.68.cond.refs_7_), custom_call_target="tpu_custom_call" | custom-call | flops 2000000 | bytes 2000000 | tf_op jit(solution)/shard_map/team/pallas_call | solution.py:473
  33.2 2.9 %team.4 = (f32[8,8,512]{2,1,0:T(8,128)S(1)}, f32[8,8,512]{2,1,0:T(8,128)S(1)}) custom-call(f32[21,8,128]{2,1,0:T(8,128)S(1)} %masks.1.refs_0_, f32[8,8,512]{2,1,0:T(8,128)S(1)} %get-tuple-element.42.head.refs_1_, f32[8,8,512]{2,1,0:T(8,128)S(1)} %get-tuple-element.43.warm.refs_2_, f32[8,8,512]{2,1,0:T(8,128)S(1)} %get-tuple-element.48.cond.refs_7_), custom_call_target="tpu_custom_call" | custom-call | flops 2000000 | bytes 2000000 | tf_op jit(solution)/shard_map/team/pallas_call | solution.py:473
  36.2 0.0 collective-permute-done.2.refs_13_.refs_15_
  36.2 0.8 %middle.3 = (f32[8,8,512]{2,1,0:T(8,128)S(1)}, f32[8,8,512]{2,1,0:T(8,128)S(1)}, f32[8,8,512]{2,1,0:T(8,128)S(1)}, f32[8,8,512]{2,1,0:T(8,128)S(1)}, f32[8,8,512...) custom-call(f32[21,8,128]{2,1,0:T(8,128)S(1)} %masks.1.refs_0_, f32[8,8,512]{2,1,0:T(8,128)S(1)} %get-tuple-element.62.head.refs_1_, ...), custom_call_target="tpu_custom_call" | custom-call | flops 2000000 | bytes 2000000 | tf_op jit(solution)/shard_map/middle/pallas_call | solution.py:473
  37.0 2.4 %collective-permute-start.3 = (f32[2,8,8,128]{3,2,1,0:T(8,128)S(1)}, f32[2,8,8,128]{3,2,1,0:T(8,128)S(1)}, u32[]{:S(2)}, u32[]{:S(2)}) collective-permute-start(f32[2,8,8,128]{3,2,1,0:T(8,128)S(1)} %get-tuple-element.81.refs_12_), channel_id=1, source_target_pairs={{0,16},{16,0},{1,17},{17,1},{2,18},{18,2},{3,19},{19,3},{4,20},{20... | collective-permute-start | bytes 196616 | tf_op jit(solution)/shard_map/ppermute | solution.py:497
  39.4 0.0 collective-permute-done.refs_13_.refs_15_
  39.4 0.8 %middle.2 = (f32[8,8,512]{2,1,0:T(8,128)S(1)}, f32[8,8,512]{2,1,0:T(8,128)S(1)}, f32[8,8,512]{2,1,0:T(8,128)S(1)}, f32[8,8,512]{2,1,0:T(8,128)S(1)}, f32[8,8,512...) custom-call(f32[21,8,128]{2,1,0:T(8,128)S(1)} %masks.1.refs_0_, f32[8,8,512]{2,1,0:T(8,128)S(1)} %get-tuple-element.42.head.refs_1_, ...), custom_call_target="tpu_custom_call" | custom-call | flops 2000000 | bytes 2000000 | tf_op jit(solution)/shard_map/middle/pallas_call | solution.py:473
  40.3 0.7 %collective-permute-start.1 = (f32[2,8,8,128]{3,2,1,0:T(8,128)S(1)}, f32[2,8,8,128]{3,2,1,0:T(8,128)S(1)}, u32[]{:S(2)}, u32[]{:S(2)}) collective-permute-start(f32[2,8,8,128]{3,2,1,0:T(8,128)S(1)} %get-tuple-element.61.refs_12_), channel_id=1, source_target_pairs={{0,16},{16,0},{1,17},{17,1},{2,18},{18,2},{3,19},{19,3},{4,20},{20... | collective-permute-start | bytes 196616 | tf_op jit(solution)/shard_map/ppermute | solution.py:497
  40.9 2.9 %team.7 = (f32[8,8,512]{2,1,0:T(8,128)S(1)}, f32[8,8,512]{2,1,0:T(8,128)S(1)}) custom-call(f32[21,8,128]{2,1,0:T(8,128)S(1)} %masks.1.refs_0_, f32[8,8,512]{2,1,0:T(8,128)S(1)} %get-tuple-element.74.head.refs_1_, f32[8,8,512]{2,1,0:T(8,128)S(1)} %get-tuple-element.75.warm.refs_2_, f32[8,8,512]{2,1,0:T(8,128)S(1)} %get-tuple-element.78.cond.refs_7_), custom_call_target="tpu_custom_call" | custom-call | flops 2000000 | bytes 2000000 | tf_op jit(solution)/shard_map/team/pallas_call | solution.py:473
  43.9 2.9 %team.5 = (f32[8,8,512]{2,1,0:T(8,128)S(1)}, f32[8,8,512]{2,1,0:T(8,128)S(1)}) custom-call(f32[21,8,128]{2,1,0:T(8,128)S(1)} %masks.1.refs_0_, f32[8,8,512]{2,1,0:T(8,128)S(1)} %get-tuple-element.54.head.refs_1_, f32[8,8,512]{2,1,0:T(8,128)S(1)} %get-tuple-element.55.warm.refs_2_, f32[8,8,512]{2,1,0:T(8,128)S(1)} %get-tuple-element.58.cond.refs_7_), custom_call_target="tpu_custom_call" | custom-call | flops 2000000 | bytes 2000000 | tf_op jit(solution)/shard_map/team/pallas_call | solution.py:473
  46.8 0.0 collective-permute-done.3.refs_13_
  46.8 0.9 %last.2.refs_16_ = f32[16,4,8,128]{3,2,1,0:T(8,128)S(1)} custom-call(f32[21,8,128]{2,1,0:T(8,128)S(1)} %masks.1.refs_0_, f32[8,8,512]{2,1,0:T(8,128)S(1)} %get-tuple-element.74.head.refs_1_, f32[8,8,512]{2,1,0:T(8,128)S(1)} %get-tuple-element.75.warm.refs_2_, f32[8,8,512]{2,1,0:T(8,128)S(1)} %get-tuple-element.65.refs_4_.refs_3_, ...), custom_call_target="tpu_custom_call" | custom-call | flops 2000000 | bytes 2000000 | tf_op jit(solution)/shard_map/last/pallas_call | solution.py:473
  47.8 0.0 collective-permute-done.1.refs_13_
  47.8 0.9 %last.3 = f32[16,8,8,128]{3,2,1,0:T(8,128)S(1)} custom-call(f32[21,8,128]{2,1,0:T(8,128)S(1)} %masks.1.refs_0_, f32[8,8,512]{2,1,0:T(8,128)S(1)} %get-tuple-element.54.head.refs_1_, f32[8,8,512]{2,1,0:T(8,128)S(1)} %get-tuple-element.55.warm.refs_2_, f32[8,8,512]{2,1,0:T(8,128)S(1)} %get-tuple-element.45.refs_4_.refs_3_, ...), custom_call_target="tpu_custom_call" | custom-call | flops 2000000 | bytes 2000000 | tf_op jit(solution)/shard_map/last/pallas_call | solution.py:473
  48.7 13.2 %all_to_all.11.got = f32[16,8,8,128]{3,2,1,0:T(8,128)S(1)} all-to-all(f32[16,8,8,128]{3,2,1,0:T(8,128)S(1)} %last.3), channel_id=1, replica_groups={{0,1,2,3,4,5,6,7,8,9,10,11,12,13,14,15},{16,17,18,19,20,21,22,23,24,25,..., dimensions={0} | all-to-all | bytes 1048576 | tf_op jit(solution)/shard_map/all_to_all | solution.py:487
  61.8 0.9 %unpack.1 = (f32[128,512]{1,0:T(8,128)}, f32[128,512]{1,0:T(8,128)}) custom-call(f32[16,8,8,128]{3,2,1,0:T(8,128)S(1)} %all_to_all.11.got), custom_call_target="tpu_custom_call" | custom-call | flops 2000000 | bytes 2000000 | tf_op jit(solution)/shard_map/unpack/pallas_call | solution.py:473
Async XLA Ops:
  4.3 20.4 %copy-start = (f32[8]{0:T(128)S(1)}, f32[8]{0:T(128)}, u32[]{:S(2)}) copy-start(f32[8]{0:T(128)} %refs_1_.3) | copy-start | bytes 100
  4.3 20.4 %copy-start.1 = (f32[8]{0:T(128)S(1)}, f32[8]{0:T(128)}, u32[]{:S(2)}) copy-start(f32[8]{0:T(128)} %refs_2_.3) | copy-start | bytes 100
  25.6 10.5 %collective-permute-start.2 = (f32[3,8,8,128]{3,2,1,0:T(8,128)S(1)}, f32[3,8,8,128]{3,2,1,0:T(8,128)S(1)}, u32[]{:S(2)}, u32[]{:S(2)}) collective-permute-start(f32[3,8,8,128]{3,2,1,0:T(8,128)S(1)} %get-tuple-element.73.refs_12_.refs_14_), channel_id=1, source_target_pairs={{0,16},{16,0},{1,17},{17,1},{2,18},{18,2},{3,19},{19,3},{4,20},{20... | collective-permute-start | bytes 294920 | tf_op jit(solution)/shard_map/ppermute | solution.py:497
  29.3 0.7 %copy-start.2 = (s32[2,128]{1,0:T(2,128)S(1)}, s32[2,128]{1,0:T(2,128)}, u32[]{:S(2)}) copy-start(s32[2,128]{1,0:T(2,128)} %couplings.1) | copy-start | bytes 3076
  29.3 10.1 %collective-permute-start = (f32[3,8,8,128]{3,2,1,0:T(8,128)S(1)}, f32[3,8,8,128]{3,2,1,0:T(8,128)S(1)}, u32[]{:S(2)}, u32[]{:S(2)}) collective-permute-start(f32[3,8,8,128]{3,2,1,0:T(8,128)S(1)} %get-tuple-element.53.refs_12_.refs_14_), channel_id=1, source_target_pairs={{0,16},{16,0},{1,17},{17,1},{2,18},{18,2},{3,19},{19,3},{4,20},{20... | collective-permute-start | bytes 294920 | tf_op jit(solution)/shard_map/ppermute | solution.py:497
  37.0 9.8 %collective-permute-start.3 = (f32[2,8,8,128]{3,2,1,0:T(8,128)S(1)}, f32[2,8,8,128]{3,2,1,0:T(8,128)S(1)}, u32[]{:S(2)}, u32[]{:S(2)}) collective-permute-start(f32[2,8,8,128]{3,2,1,0:T(8,128)S(1)} %get-tuple-element.81.refs_12_), channel_id=1, source_target_pairs={{0,16},{16,0},{1,17},{17,1},{2,18},{18,2},{3,19},{19,3},{4,20},{20... | collective-permute-start | bytes 196616 | tf_op jit(solution)/shard_map/ppermute | solution.py:497
  40.3 7.5 %collective-permute-start.1 = (f32[2,8,8,128]{3,2,1,0:T(8,128)S(1)}, f32[2,8,8,128]{3,2,1,0:T(8,128)S(1)}, u32[]{:S(2)}, u32[]{:S(2)}) collective-permute-start(f32[2,8,8,128]{3,2,1,0:T(8,128)S(1)} %get-tuple-element.61.refs_12_), channel_id=1, source_target_pairs={{0,16},{16,0},{1,17},{17,1},{2,18},{18,2},{3,19},{19,3},{4,20},{20... | collective-permute-start | bytes 196616 | tf_op jit(solution)/shard_map/ppermute | solution.py:497

commit v6 on v5

--- a/solution.py
+++ b/solution.py
@@ -113,46 +113,6 @@
         update(j, x)
 
 
-def pack_kernel(suction, warmth, classes, top, out, room, class_room, turned, in_sems, out_sems):
-    cells = turned.shape[-1]
-    quarters = 2 * CHUNKS
-    into, sent = [], []
-    for f, field in enumerate((suction, warmth, classes)):
-        for q in range(quarters):
-            target = class_room.at[q] if f == 2 else room.at[f, q]
-            into.append(
-                pltpu.make_async_copy(field.at[:, pl.ds(q * LANES, LANES)], target, in_sems.at[f, q])
-            )
-            into[-1].start()
-
-    def send(slot, value):
-        turned[:, slot] = value.T.reshape(TEAM, OWN, cells)
-        sent.append(pltpu.make_async_copy(turned.at[:, slot], out.at[:, slot], out_sems.at[slot]))
-        sent[-1].start()
-
-    rows = [top[0:1, q * LANES : (q + 1) * LANES] for q in range(quarters)]
-    send(3 * quarters, jnp.concatenate(rows + [jnp.zeros((cells - quarters, LANES), F32)], axis=0))
-    for f in range(3):
-        for q in range(quarters):
-            into[f * quarters + q].wait()
-            send(f * quarters + q, class_room[q].astype(F32) if f == 2 else room[f, q])
-    for copy in sent:
-        copy.wait()
-
-
-def unpack_kernel(got, suction, warmth, room, sems):
-    cells = got.shape[-1]
-    sent = []
-    for f, out in enumerate((suction, warmth)):
-        for q in range(2 * CHUNKS):
-            room[f, q] = got[:, f * 2 * CHUNKS + q].reshape(LANES, cells).T
-            here = out.at[:, pl.ds(q * LANES, LANES)]
-            sent.append(pltpu.make_async_copy(room.at[f, q], here, sems.at[f, q]))
-            sent[-1].start()
-    for copy in sent:
-        copy.wait()
-
-
 def mask_rows(cuts):
     return 3 * PAIR_DEV + cuts * (2 * PAIR_DEV + 1)
 
@@ -161,7 +121,7 @@
     return 3 * PAIR_DEV + cut * (2 * PAIR_DEV + 1)
 
 
-def mask_kernel(n, couplings, out):
+def fill_masks(n, couplings, out):
     pair_rows = couplings[...].astype(F32)
     pairs = couplings.shape[1]
     pair_id = lax.broadcasted_iota(jnp.int32, (pairs, LANES), 0)
@@ -206,6 +166,52 @@
         put(row + 2 * PAIR_DEV, jnp.where(outward < EDGE, 1.0, 0.0))
 
 
+def pack_kernel(
+    n, suction, warmth, classes, top, couplings, out, masks, room, class_room, turned, pairs, in_sems, out_sems, pair_sem
+):
+    cells = turned.shape[-1]
+    pair_copy = pltpu.make_async_copy(couplings, pairs, pair_sem)
+    pair_copy.start()
+    quarters = 2 * CHUNKS
+    into, sent = [], []
+    for f, field in enumerate((suction, warmth, classes)):
+        for q in range(quarters):
+            target = class_room.at[q] if f == 2 else room.at[f, q]
+            into.append(
+                pltpu.make_async_copy(field.at[:, pl.ds(q * LANES, LANES)], target, in_sems.at[f, q])
+            )
+            into[-1].start()
+
+    def send(slot, value):
+        turned[:, slot] = value.T.reshape(TEAM, OWN, cells)
+        sent.append(pltpu.make_async_copy(turned.at[:, slot], out.at[:, slot], out_sems.at[slot]))
+        sent[-1].start()
+
+    rows = [top[0:1, q * LANES : (q + 1) * LANES] for q in range(quarters)]
+    send(3 * quarters, jnp.concatenate(rows + [jnp.zeros((cells - quarters, LANES), F32)], axis=0))
+    pair_copy.wait()
+    fill_masks(n, pairs, masks)
+    for f in range(3):
+        for q in range(quarters):
+            into[f * quarters + q].wait()
+            send(f * quarters + q, class_room[q].astype(F32) if f == 2 else room[f, q])
+    for copy in sent:
+        copy.wait()
+
+
+def unpack_kernel(got, suction, warmth, room, sems):
+    cells = got.shape[-1]
+    sent = []
+    for f, out in enumerate((suction, warmth)):
+        for q in range(2 * CHUNKS):
+            room[f, q] = got[:, f * 2 * CHUNKS + q].reshape(LANES, cells).T
+            here = out.at[:, pl.ds(q * LANES, LANES)]
+            sent.append(pltpu.make_async_copy(room.at[f, q], here, sems.at[f, q]))
+            sent[-1].start()
+    for copy in sent:
+        copy.wait()
+
+
 def edge_shift(cut, m):
     return lax.rem(EDGE * m + jnp.where(place(cut)[1], EDGE, 0), LANES)
 
@@ -262,11 +268,12 @@
                 halos[cut][i, j] = halo_of(cut, v)
 
 
-def team_kernel(masks, head, warm, cond, water_out, heat_out, water, heat):
+def team_kernel(masks, head, warm, cond, water, heat):
     steps = head.shape[0]
     upper = [masks[s - 1] > 0.5 for s in DISTANCES]
     lower = [masks[PAIR_DEV + s - 1] > 0.5 for s in DISTANCES]
-    for j in range(steps):
+
+    def step(j, _):
         for g in range(GROUPS):
             l0, l1 = lanes_of(g, 0), lanes_of(g, 1)
             h0, h1 = head[j, :, l0], head[j, :, l1]
@@ -298,8 +305,8 @@
             water[j, :, l1] = total[1]
             heat[j, :, l0] = 2.0 * (total[2] - total[3])
             heat[j, :, l1] = 2.0 * total[3]
-    water_out[...] = water[...]
-    heat_out[...] = heat[...]
+
+    lax.fori_loop(0, steps, step, None)
 
 
 def cross_flows(cut, masks, mine, theirs):
@@ -509,25 +516,24 @@
     smem = whole(pltpu.SMEM)
     hbm = whole(pltpu.HBM)
 
-    masks = call(
-        functools.partial(mask_kernel, n), "masks", (couplings,), [(mask_rows(cuts), SUB, LANES)]
-    )[0]
-    packed = call(
-        pack_kernel,
+    packed, masks = call(
+        functools.partial(pack_kernel, n),
         "pack",
-        (suction, warmth, classes, top.reshape(1, width)),
-        [(TEAM, 3 * quarters + 1, OWN, cells)],
+        (suction, warmth, classes, top.reshape(1, width), couplings),
+        [(TEAM, 3 * quarters + 1, OWN, cells), (mask_rows(cuts), SUB, LANES)],
         scratch=[
             pltpu.VMEM((2, quarters, cells, LANES), F32),
             pltpu.VMEM((quarters, cells, LANES), classes.dtype),
             pltpu.VMEM((TEAM, 3 * quarters + 1, OWN, cells), F32),
+            pltpu.VMEM(couplings.shape, couplings.dtype),
             pltpu.SemaphoreType.DMA((3, quarters)),
             pltpu.SemaphoreType.DMA((3 * quarters + 1,)),
+            pltpu.SemaphoreType.DMA,
         ],
-        specs=[hbm, hbm, hbm, whole()],
-        out_specs=[hbm],
+        specs=[hbm, hbm, hbm, whole(), hbm],
+        out_specs=[hbm, whole()],
         limit=PACK_LIMIT,
-    )[0]
+    )
     got = exchange(packed, n)
 
     first, sides = [], []
@@ -547,7 +553,7 @@
     second, later = [], []
     for c in range(CHUNKS):
         head, warm, perm, conduct, wet, melt, cond, energy, surface = first[c]
-        water, heat = call(team_kernel, "team", (masks, head, warm, cond), [column] * 2, scratch=[room] * 2)
+        water, heat = call(team_kernel, "team", (masks, head, warm, cond), [column] * 2)
         mine, theirs = sides[c]
         values = call(
             functools.partial(middle_kernel, cuts),
@@ -564,7 +570,7 @@
     for c in range(CHUNKS):
         conduct, stored, energy, surface = first[c][3], first[c][4], first[c][7], first[c][8]
         head, warm, wet, melt, cond = second[c]
-        water, heat = call(team_kernel, "team", (masks, head, warm, cond), [column] * 2, scratch=[room] * 2)
+        water, heat = call(team_kernel, "team", (masks, head, warm, cond), [column] * 2)
         mine, theirs = later[c]
         mine_k, theirs_k = sides[c]
         final = c == CHUNKS - 1

time: 63.1 us -> 61.4 us (0.973)
  Pallas kernels: 22.1 us -> 16.5 us
  waiting for transfers between devices: 0.01 us -> 4.64 us
  starting transfers between devices: 6.11 us -> 5.25 us
    pallas_call x13 -> x12, Pallas kernels: 22.1 us -> 16.5 us  [call(): pl.pallas_call(kernel, out_shape=[jax.ShapeDtypeStruct(shape, F32) for sh...]
    ppermute x4, waiting for transfers between devices: 0.01 us -> 4.64 us  [swap(): return lax.ppermute(value, 'cols', pairs)]
    ppermute x4, starting transfers between devices: 6.11 us -> 5.25 us  [swap(): return lax.ppermute(value, 'cols', pairs)]
  transfers between devices with their start and end apart: 4 -> 4, of which waited for: 0 -> 3; matrix products, arithmetic and copies ran while one was open for 0% -> 0% of each run, Pallas kernels for 25% -> 15%
where the time goes in v6:
time: 61.4 us; the launch traced here: 61 us
  blocking collectives  33.9 us (55%)
  Pallas kernels  16.5 us (27%)
  starting transfers between devices  5.25 us (9%)
  waiting for transfers between devices  4.64 us (8%)
  between operations  0.74 us (1%)
    all_to_all x2, blocking collectives, exchange(): lax.all_to_all(tiles, 'cols', split_axis=0, concat_axis=0, tiled=True, ax...  33.9 us
    pallas_call x12, Pallas kernels, call(): pl.pallas_call(kernel, out_shape=[jax.ShapeDtypeStruct(shape, F32) for sh...  16.5 us
    ppermute x4, starting transfers between devices, swap(): return lax.ppermute(value, 'cols', pairs)  5.25 us
    ppermute x4, waiting for transfers between devices, swap(): return lax.ppermute(value, 'cols', pairs)  4.64 us
  transfers between devices with their start and end apart: 4, of which 3 were waited for; matrix products, arithmetic and copies ran while one was open for 0% of the time, Pallas kernels for 15%

profile of v6, /device:TPU:0, one launch (start us, length us, event | category | flops | bytes accessed | tf_op | source)
XLA Modules:
  0.0 61.0 jit_solution(1644271887003591632)
XLA Ops:
  0.6 4.7 %pack.1 = (f32[16,13,8,128]{3,2,1,0:T(8,128)}, f32[21,8,128]{2,1,0:T(8,128)}) custom-call(f32[128,512]{1,0:T(8,128)} %suction.1, f32[128,512]{1,0:T(8,128)} %warmth.1, s32[128,512]{1,0:T(8,128)} %classes.1, f32[1,512]{1,0:T(1,128)} %bitcast.1, s32[2,128]{1,0:T(2,128)} %couplings.1), custom_call_target="tpu_custom_call" | custom-call | flops 2000000 | bytes 2000000 | tf_op jit(solution)/shard_map/pack/pallas_call | solution.py:480
  5.3 0.0 copy-start.1
  5.3 0.0 copy-start.2
  5.3 20.4 %all_to_all.10.refs_0_ = f32[16,13,8,128]{3,2,1,0:T(8,128)S(1)} all-to-all(f32[16,13,8,128]{3,2,1,0:T(8,128)} %get-tuple-element.45), channel_id=1, replica_groups={{0,1,2,3,4,5,6,7,8,9,10,11,12,13,14,15},{16,17,18,19,20,21,22,23,24,25,..., dimensions={0} | all-to-all | bytes 1703936 | tf_op jit(solution)/shard_map/all_to_all | solution.py:494
  25.7 0.0 copy-done.1
  25.7 0.0 copy-done.2
  25.7 1.0 %first.3 = (f32[8,8,512]{2,1,0:T(8,128)S(1)}, f32[8,8,512]{2,1,0:T(8,128)S(1)}, f32[8,8,512]{2,1,0:T(8,128)S(1)}, f32[8,8,512]{2,1,0:T(8,128)S(1)}, f32[8,8,512]...) custom-call(f32[16,13,8,128]{3,2,1,0:T(8,128)S(1)} %all_to_all.10.re, ...), custom_call_target="tpu_custom_call" | custom-call | flops 2000000 | bytes 2000000 | tf_op jit(solution)/shard_map/first/pallas_call | solution.py:480
  26.7 0.0 copy-start
  26.7 2.7 %collective-permute-start.2 = (f32[3,8,8,128]{3,2,1,0:T(8,128)S(1)}, f32[3,8,8,128]{3,2,1,0:T(8,128)S(1)}, u32[]{:S(2)}, u32[]{:S(2)}) collective-permute-start(f32[3,8,8,128]{3,2,1,0:T(8,128)S(1)} %get-tuple-element.77.refs_12_.refs_14_), channel_id=1, source_target_pairs={{0,16},{16,0},{1,17},{17,1},{2,18},{18,2},{3,19},{19,3},{4,20},{20... | collective-permute-start | bytes 294920 | tf_op jit(solution)/shard_map/ppermute | solution.py:504
  29.4 1.0 %first.2 = (f32[8,8,512]{2,1,0:T(8,128)S(1)}, f32[8,8,512]{2,1,0:T(8,128)S(1)}, f32[8,8,512]{2,1,0:T(8,128)S(1)}, f32[8,8,512]{2,1,0:T(8,128)S(1)}, f32[8,8,512]...) custom-call(f32[16,13,8,128]{3,2,1,0:T(8,128)S(1)} %all_to_all.10.re, ...), custom_call_target="tpu_custom_call" | custom-call | flops 2000000 | bytes 2000000 | tf_op jit(solution)/shard_map/first/pallas_call | solution.py:480
  30.4 0.4 collective-permute-start
  30.8 0.0 copy-done
  30.8 1.4 %team.6 = (f32[8,8,512]{2,1,0:T(8,128)S(1)}, f32[8,8,512]{2,1,0:T(8,128)S(1)}) custom-call(f32[21,8,128]{2,1,0:T(8,128)S(1)} %copy-done, f32[8,8,512]{2,1,0:T(8,128)S(1)} %get-tuple-element.66.head.refs_1_, f32[8,8,512]{2,1,0:T(8,128)S(1)} %get-tuple-element.67.warm.refs_2_, f32[8,8,512]{2,1,0:T(8,128)S(1)} %get-tuple-element.72.cond.refs_7_), custom_call_target="tpu_custom_call" | custom-call | flops 2000000 | bytes 2000000 | tf_op jit(solution)/shard_map/team/pallas_call | solution.py:480
  32.1 1.4 %team.4 = (f32[8,8,512]{2,1,0:T(8,128)S(1)}, f32[8,8,512]{2,1,0:T(8,128)S(1)}) custom-call(f32[21,8,128]{2,1,0:T(8,128)S(1)} %copy-done, f32[8,8,512]{2,1,0:T(8,128)S(1)} %get-tuple-element.46.head.refs_1_, f32[8,8,512]{2,1,0:T(8,128)S(1)} %get-tuple-element.47.warm.refs_2_, f32[8,8,512]{2,1,0:T(8,128)S(1)} %get-tuple-element.52.cond.refs_7_), custom_call_target="tpu_custom_call" | custom-call | flops 2000000 | bytes 2000000 | tf_op jit(solution)/shard_map/team/pallas_call | solution.py:480
  33.5 3.1 %collective-permute-done.2.refs_13_.refs_15_ = f32[3,8,8,128]{3,2,1,0:T(8,128)S(1)} collective-permute-done((f32[3,8,8,128]{3,2,1,0:T(8,128)S(1)}, f32[3,8,8,128]{3,2,1,0:T(8,128)S(1)}, u32[]{:S(2)}, u32[]{:S(2)}) %collective-permute-start.2) | collective-permute-done | bytes 98336 | tf_op jit(solution)/shard_map/ppermute | solution.py:504
  36.6 0.8 %middle.3 = (f32[8,8,512]{2,1,0:T(8,128)S(1)}, f32[8,8,512]{2,1,0:T(8,128)S(1)}, f32[8,8,512]{2,1,0:T(8,128)S(1)}, f32[8,8,512]{2,1,0:T(8,128)S(1)}, f32[8,8,512...) custom-call(f32[21,8,128]{2,1,0:T(8,128)S(1)} %copy-done, f32[8,8,512]{2,1,0:T(8,128)S(1)} %get-tuple-element.66.head.refs_1_, ...), custom_call_target="tpu_custom_call" | custom-call | flops 2000000 | bytes 2000000 | tf_op jit(solution)/shard_map/middle/pallas_call | solution.py:480
  37.4 0.1 collective-permute-start.3
  37.5 0.9 %collective-permute-done.refs_13_.refs_15_ = f32[3,8,8,128]{3,2,1,0:T(8,128)S(1)} collective-permute-done((f32[3,8,8,128]{3,2,1,0:T(8,128)S(1)}, f32[3,8,8,128]{3,2,1,0:T(8,128)S(1)}, u32[]{:S(2)}, u32[]{:S(2)}) %collective-permute-start) | collective-permute-done | bytes 98336 | tf_op jit(solution)/shard_map/ppermute | solution.py:504
  38.3 0.8 %middle.2 = (f32[8,8,512]{2,1,0:T(8,128)S(1)}, f32[8,8,512]{2,1,0:T(8,128)S(1)}, f32[8,8,512]{2,1,0:T(8,128)S(1)}, f32[8,8,512]{2,1,0:T(8,128)S(1)}, f32[8,8,512...) custom-call(f32[21,8,128]{2,1,0:T(8,128)S(1)} %copy-done, f32[8,8,512]{2,1,0:T(8,128)S(1)} %get-tuple-element.46.head.refs_1_, ...), custom_call_target="tpu_custom_call" | custom-call | flops 2000000 | bytes 2000000 | tf_op jit(solution)/shard_map/middle/pallas_call | solution.py:480
  39.2 2.1 %collective-permute-start.1 = (f32[2,8,8,128]{3,2,1,0:T(8,128)S(1)}, f32[2,8,8,128]{3,2,1,0:T(8,128)S(1)}, u32[]{:S(2)}, u32[]{:S(2)}) collective-permute-start(f32[2,8,8,128]{3,2,1,0:T(8,128)S(1)} %get-tuple-element.65.refs_12_), channel_id=1, source_target_pairs={{0,16},{16,0},{1,17},{17,1},{2,18},{18,2},{3,19},{19,3},{4,20},{20... | collective-permute-start | bytes 196616 | tf_op jit(solution)/shard_map/ppermute | solution.py:504
  41.3 1.4 %team.7 = (f32[8,8,512]{2,1,0:T(8,128)S(1)}, f32[8,8,512]{2,1,0:T(8,128)S(1)}) custom-call(f32[21,8,128]{2,1,0:T(8,128)S(1)} %copy-done, f32[8,8,512]{2,1,0:T(8,128)S(1)} %get-tuple-element.78.head.refs_1_, f32[8,8,512]{2,1,0:T(8,128)S(1)} %get-tuple-element.79.warm.refs_2_, f32[8,8,512]{2,1,0:T(8,128)S(1)} %get-tuple-element.82.cond.refs_7_), custom_call_target="tpu_custom_call" | custom-call | flops 2000000 | bytes 2000000 | tf_op jit(solution)/shard_map/team/pallas_call | solution.py:480
  42.7 1.4 %team.5 = (f32[8,8,512]{2,1,0:T(8,128)S(1)}, f32[8,8,512]{2,1,0:T(8,128)S(1)}) custom-call(f32[21,8,128]{2,1,0:T(8,128)S(1)} %copy-done, f32[8,8,512]{2,1,0:T(8,128)S(1)} %get-tuple-element.58.head.refs_1_, f32[8,8,512]{2,1,0:T(8,128)S(1)} %get-tuple-element.59.warm.refs_2_, f32[8,8,512]{2,1,0:T(8,128)S(1)} %get-tuple-element.62.cond.refs_7_), custom_call_target="tpu_custom_call" | custom-call | flops 2000000 | bytes 2000000 | tf_op jit(solution)/shard_map/team/pallas_call | solution.py:480
  44.0 0.7 %collective-permute-done.3.refs_13_ = f32[2,8,8,128]{3,2,1,0:T(8,128)S(1)} collective-permute-done((f32[2,8,8,128]{3,2,1,0:T(8,128)S(1)}, f32[2,8,8,128]{3,2,1,0:T(8,128)S(1)}, u32[]{:S(2)}, u32[]{:S(2)}) %collective-permute-start.3) | collective-permute-done | bytes 65568 | tf_op jit(solution)/shard_map/ppermute | solution.py:504
  44.7 0.9 %last.2.refs_16_ = f32[16,4,8,128]{3,2,1,0:T(8,128)S(1)} custom-call(f32[21,8,128]{2,1,0:T(8,128)S(1)} %copy-done, f32[8,8,512]{2,1,0:T(8,128)S(1)} %get-tuple-element.78.head.refs_1_, f32[8,8,512]{2,1,0:T(8,128)S(1)} %get-tuple-element.79.warm.refs_2_, f32[8,8,512]{2,1,0:T(8,128)S(1)} %get-tuple-element.69.refs_4_.refs_3_, ...), custom_call_target="tpu_custom_call" | custom-call | flops 2000000 | bytes 2000000 | tf_op jit(solution)/shard_map/last/pallas_call | solution.py:480
  45.6 0.0 collective-permute-done.1.refs_13_
  45.6 0.9 %last.3 = f32[16,8,8,128]{3,2,1,0:T(8,128)S(1)} custom-call(f32[21,8,128]{2,1,0:T(8,128)S(1)} %copy-done, f32[8,8,512]{2,1,0:T(8,128)S(1)} %get-tuple-element.58.head.refs_1_, f32[8,8,512]{2,1,0:T(8,128)S(1)} %get-tuple-element.59.warm.refs_2_, f32[8,8,512]{2,1,0:T(8,128)S(1)} %get-tuple-element.49.refs_4_.refs_3_, ...), custom_call_target="tpu_custom_call" | custom-call | flops 2000000 | bytes 2000000 | tf_op jit(solution)/shard_map/last/pallas_call | solution.py:480
  46.5 13.6 %all_to_all.11.got = f32[16,8,8,128]{3,2,1,0:T(8,128)S(1)} all-to-all(f32[16,8,8,128]{3,2,1,0:T(8,128)S(1)} %last.3), channel_id=1, replica_groups={{0,1,2,3,4,5,6,7,8,9,10,11,12,13,14,15},{16,17,18,19,20,21,22,23,24,25,..., dimensions={0} | all-to-all | bytes 1048576 | tf_op jit(solution)/shard_map/all_to_all | solution.py:494
  60.1 0.9 %unpack.1 = (f32[128,512]{1,0:T(8,128)}, f32[128,512]{1,0:T(8,128)}) custom-call(f32[16,8,8,128]{3,2,1,0:T(8,128)S(1)} %all_to_all.11.got), custom_call_target="tpu_custom_call" | custom-call | flops 2000000 | bytes 2000000 | tf_op jit(solution)/shard_map/unpack/pallas_call | solution.py:480
Async XLA Ops:
  5.3 20.4 %copy-start.1 = (f32[8]{0:T(128)S(1)}, f32[8]{0:T(128)}, u32[]{:S(2)}) copy-start(f32[8]{0:T(128)} %refs_1_.3) | copy-start | bytes 100
  5.3 20.4 %copy-start.2 = (f32[8]{0:T(128)S(1)}, f32[8]{0:T(128)}, u32[]{:S(2)}) copy-start(f32[8]{0:T(128)} %refs_2_.3) | copy-start | bytes 100
  26.7 4.1 %copy-start = (f32[21,8,128]{2,1,0:T(8,128)S(1)}, f32[21,8,128]{2,1,0:T(8,128)}, u32[]{:S(2)}) copy-start(f32[21,8,128]{2,1,0:T(8,128)} %get-tuple-element.44.masks.refs_0_) | copy-start | bytes 258052
  26.7 9.9 %collective-permute-start.2 = (f32[3,8,8,128]{3,2,1,0:T(8,128)S(1)}, f32[3,8,8,128]{3,2,1,0:T(8,128)S(1)}, u32[]{:S(2)}, u32[]{:S(2)}) collective-permute-start(f32[3,8,8,128]{3,2,1,0:T(8,128)S(1)} %get-tuple-element.77.refs_12_.refs_14_), channel_id=1, source_target_pairs={{0,16},{16,0},{1,17},{17,1},{2,18},{18,2},{3,19},{19,3},{4,20},{20... | collective-permute-start | bytes 294920 | tf_op jit(solution)/shard_map/ppermute | solution.py:504
  30.4 8.0 %collective-permute-start = (f32[3,8,8,128]{3,2,1,0:T(8,128)S(1)}, f32[3,8,8,128]{3,2,1,0:T(8,128)S(1)}, u32[]{:S(2)}, u32[]{:S(2)}) collective-permute-start(f32[3,8,8,128]{3,2,1,0:T(8,128)S(1)} %get-tuple-element.57.refs_12_.refs_14_), channel_id=1, source_target_pairs={{0,16},{16,0},{1,17},{17,1},{2,18},{18,2},{3,19},{19,3},{4,20},{20... | collective-permute-start | bytes 294920 | tf_op jit(solution)/shard_map/ppermute | solution.py:504
  37.4 7.3 %collective-permute-start.3 = (f32[2,8,8,128]{3,2,1,0:T(8,128)S(1)}, f32[2,8,8,128]{3,2,1,0:T(8,128)S(1)}, u32[]{:S(2)}, u32[]{:S(2)}) collective-permute-start(f32[2,8,8,128]{3,2,1,0:T(8,128)S(1)} %get-tuple-element.85.refs_12_), channel_id=1, source_target_pairs={{0,16},{16,0},{1,17},{17,1},{2,18},{18,2},{3,19},{19,3},{4,20},{20... | collective-permute-start | bytes 196616 | tf_op jit(solution)/shard_map/ppermute | solution.py:504
  39.2 6.5 %collective-permute-start.1 = (f32[2,8,8,128]{3,2,1,0:T(8,128)S(1)}, f32[2,8,8,128]{3,2,1,0:T(8,128)S(1)}, u32[]{:S(2)}, u32[]{:S(2)}) collective-permute-start(f32[2,8,8,128]{3,2,1,0:T(8,128)S(1)} %get-tuple-element.65.refs_12_), channel_id=1, source_target_pairs={{0,16},{16,0},{1,17},{17,1},{2,18},{18,2},{3,19},{19,3},{4,20},{20... | collective-permute-start | bytes 196616 | tf_op jit(solution)/shard_map/ppermute | solution.py:504

commit v7 on v6

--- a/solution.py
+++ b/solution.py
@@ -21,6 +21,7 @@
 VMEM_LIMIT = 32 * 1024 * 1024
 PACK_LIMIT = 60 * 1024 * 1024
 DISTANCES = range(1, PAIR_DEV + 1)
+SENDS = 4
 F32 = jnp.float32
 
 
@@ -121,7 +122,7 @@
     return 3 * PAIR_DEV + cut * (2 * PAIR_DEV + 1)
 
 
-def fill_masks(n, couplings, out):
+def mask_kernel(n, couplings, out):
     pair_rows = couplings[...].astype(F32)
     pairs = couplings.shape[1]
     pair_id = lax.broadcasted_iota(jnp.int32, (pairs, LANES), 0)
@@ -166,48 +167,42 @@
         put(row + 2 * PAIR_DEV, jnp.where(outward < EDGE, 1.0, 0.0))
 
 
-def pack_kernel(
-    n, suction, warmth, classes, top, couplings, out, masks, room, class_room, turned, pairs, in_sems, out_sems, pair_sem
-):
+def pack_kernel(suction, warmth, classes, top, out, room, class_room, turned, in_sems, out_sems):
     cells = turned.shape[-1]
-    pair_copy = pltpu.make_async_copy(couplings, pairs, pair_sem)
-    pair_copy.start()
     quarters = 2 * CHUNKS
-    into, sent = [], []
+    into = []
     for f, field in enumerate((suction, warmth, classes)):
+        into.append(pltpu.make_async_copy(field, class_room if f == 2 else room.at[f], in_sems.at[f]))
+        into[-1].start()
+
+    def put(slot, value):
+        turned[:, slot] = value.T.reshape(TEAM, OWN, cells)
+
+    rows = [top[0:1, q * LANES : (q + 1) * LANES] for q in range(quarters)]
+    put(3 * quarters, jnp.concatenate(rows + [jnp.zeros((cells - quarters, LANES), F32)], axis=0))
+    for f in range(3):
+        into[f].wait()
         for q in range(quarters):
-            target = class_room.at[q] if f == 2 else room.at[f, q]
-            into.append(
-                pltpu.make_async_copy(field.at[:, pl.ds(q * LANES, LANES)], target, in_sems.at[f, q])
-            )
-            into[-1].start()
-
-    def send(slot, value):
-        turned[:, slot] = value.T.reshape(TEAM, OWN, cells)
-        sent.append(pltpu.make_async_copy(turned.at[:, slot], out.at[:, slot], out_sems.at[slot]))
+            lanes = slice(q * LANES, (q + 1) * LANES)
+            put(f * quarters + q, class_room[:, lanes].astype(F32) if f == 2 else room[f, :, lanes])
+    sent = []
+    for i in range(SENDS):
+        rows = pl.ds(i * (TEAM // SENDS), TEAM // SENDS)
+        sent.append(pltpu.make_async_copy(turned.at[rows], out.at[rows], out_sems.at[i]))
         sent[-1].start()
-
-    rows = [top[0:1, q * LANES : (q + 1) * LANES] for q in range(quarters)]
-    send(3 * quarters, jnp.concatenate(rows + [jnp.zeros((cells - quarters, LANES), F32)], axis=0))
-    pair_copy.wait()
-    fill_masks(n, pairs, masks)
-    for f in range(3):
-        for q in range(quarters):
-            into[f * quarters + q].wait()
-            send(f * quarters + q, class_room[q].astype(F32) if f == 2 else room[f, q])
     for copy in sent:
         copy.wait()
 
 
 def unpack_kernel(got, suction, warmth, room, sems):
     cells = got.shape[-1]
+    quarters = 2 * CHUNKS
     sent = []
     for f, out in enumerate((suction, warmth)):
-        for q in range(2 * CHUNKS):
-            room[f, q] = got[:, f * 2 * CHUNKS + q].reshape(LANES, cells).T
-            here = out.at[:, pl.ds(q * LANES, LANES)]
-            sent.append(pltpu.make_async_copy(room.at[f, q], here, sems.at[f, q]))
-            sent[-1].start()
+        for q in range(quarters):
+            room[f, :, q * LANES : (q + 1) * LANES] = got[:, f * quarters + q].reshape(LANES, cells).T
+        sent.append(pltpu.make_async_copy(room.at[f], out, sems.at[f]))
+        sent[-1].start()
     for copy in sent:
         copy.wait()
 
@@ -516,24 +511,25 @@
     smem = whole(pltpu.SMEM)
     hbm = whole(pltpu.HBM)
 
-    packed, masks = call(
-        functools.partial(pack_kernel, n),
+    masks = call(
+        functools.partial(mask_kernel, n), "masks", (couplings,), [(mask_rows(cuts), SUB, LANES)]
+    )[0]
+    packed = call(
+        pack_kernel,
         "pack",
-        (suction, warmth, classes, top.reshape(1, width), couplings),
-        [(TEAM, 3 * quarters + 1, OWN, cells), (mask_rows(cuts), SUB, LANES)],
+        (suction, warmth, classes, top.reshape(1, width)),
+        [(TEAM, 3 * quarters + 1, OWN, cells)],
         scratch=[
-            pltpu.VMEM((2, quarters, cells, LANES), F32),
-            pltpu.VMEM((quarters, cells, LANES), classes.dtype),
+            pltpu.VMEM((2, cells, width), F32),
+            pltpu.VMEM((cells, width), classes.dtype),
             pltpu.VMEM((TEAM, 3 * quarters + 1, OWN, cells), F32),
-            pltpu.VMEM(couplings.shape, couplings.dtype),
-            pltpu.SemaphoreType.DMA((3, quarters)),
-            pltpu.SemaphoreType.DMA((3 * quarters + 1,)),
-            pltpu.SemaphoreType.DMA,
+            pltpu.SemaphoreType.DMA((3,)),
+            pltpu.SemaphoreType.DMA((SENDS,)),
         ],
-        specs=[hbm, hbm, hbm, whole(), hbm],
-        out_specs=[hbm, whole()],
+        specs=[hbm, hbm, hbm, whole()],
+        out_specs=[hbm],
         limit=PACK_LIMIT,
-    )
+    )[0]
     got = exchange(packed, n)
 
     first, sides = [], []
@@ -592,8 +588,8 @@
             (back,),
             [(cells, width)] * 2,
             scratch=[
-                pltpu.VMEM((2, quarters, cells, LANES), F32),
-                pltpu.SemaphoreType.DMA((2, quarters)),
+                pltpu.VMEM((2, cells, width), F32),
+                pltpu.SemaphoreType.DMA((2,)),
             ],
             out_specs=[hbm, hbm],
         )

time: 61.4 us -> 59.7 us (0.972)
  Pallas kernels: 16.5 us -> 15.1 us
    pallas_call x12 -> x13, Pallas kernels: 16.5 us -> 15.1 us  [call(): pl.pallas_call(kernel, out_shape=[jax.ShapeDtypeStruct(shape, F32) for sh...]
  transfers between devices with their start and end apart: 4 -> 4, of which waited for: 3 -> 3; matrix products, arithmetic and copies ran while one was open for 0% -> 0% of each run, Pallas kernels for 15% -> 16%
where the time goes in v7:
time: 59.7 us; the launch traced here: 59.4 us
  blocking collectives  33.9 us (57%)
  Pallas kernels  15.1 us (25%)
  starting transfers between devices  5.28 us (9%)
  waiting for transfers between devices  4.06 us (7%)
  between operations  0.74 us (1%)
    all_to_all x2, blocking collectives, exchange(): lax.all_to_all(tiles, 'cols', split_axis=0, concat_axis=0, tiled=True, ax...  33.9 us
    pallas_call x13, Pallas kernels, call(): pl.pallas_call(kernel, out_shape=[jax.ShapeDtypeStruct(shape, F32) for sh...  15.1 us
    ppermute x4, starting transfers between devices, swap(): return lax.ppermute(value, 'cols', pairs)  5.28 us
    ppermute x4, waiting for transfers between devices, swap(): return lax.ppermute(value, 'cols', pairs)  4.06 us
  transfers between devices with their start and end apart: 4, of which 3 were waited for; matrix products, arithmetic and copies ran while one was open for 0% of the time, Pallas kernels for 16%

profile of v7, /device:TPU:0, one launch (start us, length us, event | category | flops | bytes accessed | tf_op | source)
XLA Modules:
  0.0 59.4 jit_solution(4875418854981216151)
XLA Ops:
  0.6 3.0 %pack.1 = f32[16,13,8,128]{3,2,1,0:T(8,128)} custom-call(f32[128,512]{1,0:T(8,128)} %suction.1, f32[128,512]{1,0:T(8,128)} %warmth.1, s32[128,512]{1,0:T(8,128)} %classes.1, f32[1,512]{1,0:T(1,128)} %bitcast.1), custom_call_target="tpu_custom_call" | custom-call | flops 2000000 | bytes 2000000 | tf_op jit(solution)/shard_map/pack/pallas_call | solution.py:475
  3.6 0.0 copy-start
  3.7 0.0 copy-start.1
  3.7 20.4 %all_to_all.10.refs_0_ = f32[16,13,8,128]{3,2,1,0:T(8,128)S(1)} all-to-all(f32[16,13,8,128]{3,2,1,0:T(8,128)} %pack.1), channel_id=1, replica_groups={{0,1,2,3,4,5,6,7,8,9,10,11,12,13,14,15},{16,17,18,19,20,21,22,23,24,25,..., dimensions={0} | all-to-all | bytes 1703936 | tf_op jit(solution)/shard_map/all_to_all | solution.py:489
  24.0 0.0 copy-done
  24.0 0.0 copy-done.1
  24.0 1.0 %first.3 = (f32[8,8,512]{2,1,0:T(8,128)S(1)}, f32[8,8,512]{2,1,0:T(8,128)S(1)}, f32[8,8,512]{2,1,0:T(8,128)S(1)}, f32[8,8,512]{2,1,0:T(8,128)S(1)}, f32[8,8,512]...) custom-call(f32[16,13,8,128]{3,2,1,0:T(8,128)S(1)} %all_to_all.10.re, ...), custom_call_target="tpu_custom_call" | custom-call | flops 2000000 | bytes 2000000 | tf_op jit(solution)/shard_map/first/pallas_call | solution.py:475
  25.0 2.7 %collective-permute-start.2 = (f32[3,8,8,128]{3,2,1,0:T(8,128)S(1)}, f32[3,8,8,128]{3,2,1,0:T(8,128)S(1)}, u32[]{:S(2)}, u32[]{:S(2)}) collective-permute-start(f32[3,8,8,128]{3,2,1,0:T(8,128)S(1)} %get-tuple-element.73.refs_12_.refs_14_), channel_id=1, source_target_pairs={{0,16},{16,0},{1,17},{17,1},{2,18},{18,2},{3,19},{19,3},{4,20},{20... | collective-permute-start | bytes 294920 | tf_op jit(solution)/shard_map/ppermute | solution.py:499
  27.7 1.0 %first.2 = (f32[8,8,512]{2,1,0:T(8,128)S(1)}, f32[8,8,512]{2,1,0:T(8,128)S(1)}, f32[8,8,512]{2,1,0:T(8,128)S(1)}, f32[8,8,512]{2,1,0:T(8,128)S(1)}, f32[8,8,512]...) custom-call(f32[16,13,8,128]{3,2,1,0:T(8,128)S(1)} %all_to_all.10.re, ...), custom_call_target="tpu_custom_call" | custom-call | flops 2000000 | bytes 2000000 | tf_op jit(solution)/shard_map/first/pallas_call | solution.py:475
  28.7 0.0 copy-start.2
  28.7 0.4 collective-permute-start
  29.1 0.3 copy-done.2
  29.4 0.3 masks.1.refs_0_
  29.6 1.4 %team.6 = (f32[8,8,512]{2,1,0:T(8,128)S(1)}, f32[8,8,512]{2,1,0:T(8,128)S(1)}) custom-call(f32[21,8,128]{2,1,0:T(8,128)S(1)} %masks.1.refs_0_, f32[8,8,512]{2,1,0:T(8,128)S(1)} %get-tuple-element.62.head.refs_1_, f32[8,8,512]{2,1,0:T(8,128)S(1)} %get-tuple-element.63.warm.refs_2_, f32[8,8,512]{2,1,0:T(8,128)S(1)} %get-tuple-element.68.cond.refs_7_), custom_call_target="tpu_custom_call" | custom-call | flops 2000000 | bytes 2000000 | tf_op jit(solution)/shard_map/team/pallas_call | solution.py:475
  31.0 1.4 %team.4 = (f32[8,8,512]{2,1,0:T(8,128)S(1)}, f32[8,8,512]{2,1,0:T(8,128)S(1)}) custom-call(f32[21,8,128]{2,1,0:T(8,128)S(1)} %masks.1.refs_0_, f32[8,8,512]{2,1,0:T(8,128)S(1)} %get-tuple-element.42.head.refs_1_, f32[8,8,512]{2,1,0:T(8,128)S(1)} %get-tuple-element.43.warm.refs_2_, f32[8,8,512]{2,1,0:T(8,128)S(1)} %get-tuple-element.48.cond.refs_7_), custom_call_target="tpu_custom_call" | custom-call | flops 2000000 | bytes 2000000 | tf_op jit(solution)/shard_map/team/pallas_call | solution.py:475
  32.4 2.5 %collective-permute-done.2.refs_13_.refs_15_ = f32[3,8,8,128]{3,2,1,0:T(8,128)S(1)} collective-permute-done((f32[3,8,8,128]{3,2,1,0:T(8,128)S(1)}, f32[3,8,8,128]{3,2,1,0:T(8,128)S(1)}, u32[]{:S(2)}, u32[]{:S(2)}) %collective-permute-start.2) | collective-permute-done | bytes 98336 | tf_op jit(solution)/shard_map/ppermute | solution.py:499
  34.9 0.8 %middle.3 = (f32[8,8,512]{2,1,0:T(8,128)S(1)}, f32[8,8,512]{2,1,0:T(8,128)S(1)}, f32[8,8,512]{2,1,0:T(8,128)S(1)}, f32[8,8,512]{2,1,0:T(8,128)S(1)}, f32[8,8,512...) custom-call(f32[21,8,128]{2,1,0:T(8,128)S(1)} %masks.1.refs_0_, f32[8,8,512]{2,1,0:T(8,128)S(1)} %get-tuple-element.62.head.refs_1_, ...), custom_call_target="tpu_custom_call" | custom-call | flops 2000000 | bytes 2000000 | tf_op jit(solution)/shard_map/middle/pallas_call | solution.py:475
  35.7 0.1 collective-permute-start.3
  35.8 0.8 %collective-permute-done.refs_13_.refs_15_ = f32[3,8,8,128]{3,2,1,0:T(8,128)S(1)} collective-permute-done((f32[3,8,8,128]{3,2,1,0:T(8,128)S(1)}, f32[3,8,8,128]{3,2,1,0:T(8,128)S(1)}, u32[]{:S(2)}, u32[]{:S(2)}) %collective-permute-start) | collective-permute-done | bytes 98336 | tf_op jit(solution)/shard_map/ppermute | solution.py:499
  36.6 0.8 %middle.2 = (f32[8,8,512]{2,1,0:T(8,128)S(1)}, f32[8,8,512]{2,1,0:T(8,128)S(1)}, f32[8,8,512]{2,1,0:T(8,128)S(1)}, f32[8,8,512]{2,1,0:T(8,128)S(1)}, f32[8,8,512...) custom-call(f32[21,8,128]{2,1,0:T(8,128)S(1)} %masks.1.refs_0_, f32[8,8,512]{2,1,0:T(8,128)S(1)} %get-tuple-element.42.head.refs_1_, ...), custom_call_target="tpu_custom_call" | custom-call | flops 2000000 | bytes 2000000 | tf_op jit(solution)/shard_map/middle/pallas_call | solution.py:475
  37.5 2.2 %collective-permute-start.1 = (f32[2,8,8,128]{3,2,1,0:T(8,128)S(1)}, f32[2,8,8,128]{3,2,1,0:T(8,128)S(1)}, u32[]{:S(2)}, u32[]{:S(2)}) collective-permute-start(f32[2,8,8,128]{3,2,1,0:T(8,128)S(1)} %get-tuple-element.61.refs_12_), channel_id=1, source_target_pairs={{0,16},{16,0},{1,17},{17,1},{2,18},{18,2},{3,19},{19,3},{4,20},{20... | collective-permute-start | bytes 196616 | tf_op jit(solution)/shard_map/ppermute | solution.py:499
  39.6 1.4 %team.7 = (f32[8,8,512]{2,1,0:T(8,128)S(1)}, f32[8,8,512]{2,1,0:T(8,128)S(1)}) custom-call(f32[21,8,128]{2,1,0:T(8,128)S(1)} %masks.1.refs_0_, f32[8,8,512]{2,1,0:T(8,128)S(1)} %get-tuple-element.74.head.refs_1_, f32[8,8,512]{2,1,0:T(8,128)S(1)} %get-tuple-element.75.warm.refs_2_, f32[8,8,512]{2,1,0:T(8,128)S(1)} %get-tuple-element.78.cond.refs_7_), custom_call_target="tpu_custom_call" | custom-call | flops 2000000 | bytes 2000000 | tf_op jit(solution)/shard_map/team/pallas_call | solution.py:475
  41.0 1.4 %team.5 = (f32[8,8,512]{2,1,0:T(8,128)S(1)}, f32[8,8,512]{2,1,0:T(8,128)S(1)}) custom-call(f32[21,8,128]{2,1,0:T(8,128)S(1)} %masks.1.refs_0_, f32[8,8,512]{2,1,0:T(8,128)S(1)} %get-tuple-element.54.head.refs_1_, f32[8,8,512]{2,1,0:T(8,128)S(1)} %get-tuple-element.55.warm.refs_2_, f32[8,8,512]{2,1,0:T(8,128)S(1)} %get-tuple-element.58.cond.refs_7_), custom_call_target="tpu_custom_call" | custom-call | flops 2000000 | bytes 2000000 | tf_op jit(solution)/shard_map/team/pallas_call | solution.py:475
  42.4 0.7 %collective-permute-done.3.refs_13_ = f32[2,8,8,128]{3,2,1,0:T(8,128)S(1)} collective-permute-done((f32[2,8,8,128]{3,2,1,0:T(8,128)S(1)}, f32[2,8,8,128]{3,2,1,0:T(8,128)S(1)}, u32[]{:S(2)}, u32[]{:S(2)}) %collective-permute-start.3) | collective-permute-done | bytes 65568 | tf_op jit(solution)/shard_map/ppermute | solution.py:499
  43.0 0.9 %last.2.refs_16_ = f32[16,4,8,128]{3,2,1,0:T(8,128)S(1)} custom-call(f32[21,8,128]{2,1,0:T(8,128)S(1)} %masks.1.refs_0_, f32[8,8,512]{2,1,0:T(8,128)S(1)} %get-tuple-element.74.head.refs_1_, f32[8,8,512]{2,1,0:T(8,128)S(1)} %get-tuple-element.75.warm.refs_2_, f32[8,8,512]{2,1,0:T(8,128)S(1)} %get-tuple-element.65.refs_4_.refs_3_, ...), custom_call_target="tpu_custom_call" | custom-call | flops 2000000 | bytes 2000000 | tf_op jit(solution)/shard_map/last/pallas_call | solution.py:475
  44.0 0.0 collective-permute-done.1.refs_13_
  44.0 0.9 %last.3 = f32[16,8,8,128]{3,2,1,0:T(8,128)S(1)} custom-call(f32[21,8,128]{2,1,0:T(8,128)S(1)} %masks.1.refs_0_, f32[8,8,512]{2,1,0:T(8,128)S(1)} %get-tuple-element.54.head.refs_1_, f32[8,8,512]{2,1,0:T(8,128)S(1)} %get-tuple-element.55.warm.refs_2_, f32[8,8,512]{2,1,0:T(8,128)S(1)} %get-tuple-element.45.refs_4_.refs_3_, ...), custom_call_target="tpu_custom_call" | custom-call | flops 2000000 | bytes 2000000 | tf_op jit(solution)/shard_map/last/pallas_call | solution.py:475
  44.9 13.6 %all_to_all.11.got = f32[16,8,8,128]{3,2,1,0:T(8,128)S(1)} all-to-all(f32[16,8,8,128]{3,2,1,0:T(8,128)S(1)} %last.3), channel_id=1, replica_groups={{0,1,2,3,4,5,6,7,8,9,10,11,12,13,14,15},{16,17,18,19,20,21,22,23,24,25,..., dimensions={0} | all-to-all | bytes 1048576 | tf_op jit(solution)/shard_map/all_to_all | solution.py:489
  58.5 0.9 %unpack.1 = (f32[128,512]{1,0:T(8,128)}, f32[128,512]{1,0:T(8,128)}) custom-call(f32[16,8,8,128]{3,2,1,0:T(8,128)S(1)} %all_to_all.11.got), custom_call_target="tpu_custom_call" | custom-call | flops 2000000 | bytes 2000000 | tf_op jit(solution)/shard_map/unpack/pallas_call | solution.py:475
Async XLA Ops:
  3.6 20.4 %copy-start = (f32[8]{0:T(128)S(1)}, f32[8]{0:T(128)}, u32[]{:S(2)}) copy-start(f32[8]{0:T(128)} %refs_1_.3) | copy-start | bytes 100
  3.7 20.4 %copy-start.1 = (f32[8]{0:T(128)S(1)}, f32[8]{0:T(128)}, u32[]{:S(2)}) copy-start(f32[8]{0:T(128)} %refs_2_.3) | copy-start | bytes 100
  25.0 9.9 %collective-permute-start.2 = (f32[3,8,8,128]{3,2,1,0:T(8,128)S(1)}, f32[3,8,8,128]{3,2,1,0:T(8,128)S(1)}, u32[]{:S(2)}, u32[]{:S(2)}) collective-permute-start(f32[3,8,8,128]{3,2,1,0:T(8,128)S(1)} %get-tuple-element.73.refs_12_.refs_14_), channel_id=1, source_target_pairs={{0,16},{16,0},{1,17},{17,1},{2,18},{18,2},{3,19},{19,3},{4,20},{20... | collective-permute-start | bytes 294920 | tf_op jit(solution)/shard_map/ppermute | solution.py:499
  28.7 0.7 %copy-start.2 = (s32[2,128]{1,0:T(2,128)S(1)}, s32[2,128]{1,0:T(2,128)}, u32[]{:S(2)}) copy-start(s32[2,128]{1,0:T(2,128)} %couplings.1) | copy-start | bytes 3076
  28.7 7.9 %collective-permute-start = (f32[3,8,8,128]{3,2,1,0:T(8,128)S(1)}, f32[3,8,8,128]{3,2,1,0:T(8,128)S(1)}, u32[]{:S(2)}, u32[]{:S(2)}) collective-permute-start(f32[3,8,8,128]{3,2,1,0:T(8,128)S(1)} %get-tuple-element.53.refs_12_.refs_14_), channel_id=1, source_target_pairs={{0,16},{16,0},{1,17},{17,1},{2,18},{18,2},{3,19},{19,3},{4,20},{20... | collective-permute-start | bytes 294920 | tf_op jit(solution)/shard_map/ppermute | solution.py:499
  35.7 7.3 %collective-permute-start.3 = (f32[2,8,8,128]{3,2,1,0:T(8,128)S(1)}, f32[2,8,8,128]{3,2,1,0:T(8,128)S(1)}, u32[]{:S(2)}, u32[]{:S(2)}) collective-permute-start(f32[2,8,8,128]{3,2,1,0:T(8,128)S(1)} %get-tuple-element.81.refs_12_), channel_id=1, source_target_pairs={{0,16},{16,0},{1,17},{17,1},{2,18},{18,2},{3,19},{19,3},{4,20},{20... | collective-permute-start | bytes 196616 | tf_op jit(solution)/shard_map/ppermute | solution.py:499
  37.5 6.5 %collective-permute-start.1 = (f32[2,8,8,128]{3,2,1,0:T(8,128)S(1)}, f32[2,8,8,128]{3,2,1,0:T(8,128)S(1)}, u32[]{:S(2)}, u32[]{:S(2)}) collective-permute-start(f32[2,8,8,128]{3,2,1,0:T(8,128)S(1)} %get-tuple-element.61.refs_12_), channel_id=1, source_target_pairs={{0,16},{16,0},{1,17},{17,1},{2,18},{18,2},{3,19},{19,3},{4,20},{20... | collective-permute-start | bytes 196616 | tf_op jit(solution)/shard_map/ppermute | solution.py:499

commit v8 on v7

--- a/solution.py
+++ b/solution.py
@@ -220,10 +220,43 @@
     return packed
 
 
-def first_kernel(chunk, cuts, *refs):
-    got, k_sat, heat_cond = refs[:3]
-    head, warm, perm, conduct, wet, melt, cond, energy, top = refs[3:12]
-    halos, load = refs[12 : 12 + cuts], refs[-1]
+def edge_kernel(cuts, got, k_sat, *refs):
+    halos, load = refs[:-1], refs[-1]
+    cells = got.shape[-1]
+    steps = halos[0].shape[1]
+    stride = steps * GROUPS
+    second = lax.broadcasted_iota(jnp.int32, (SUB, LANES), 1) >= 2 * EDGE
+    for chunk in range(CHUNKS):
+        for cut in range(cuts):
+            start = jnp.where(place(cut)[1], TEAM - PAIR_DEV, 0)
+            for f in range(3):
+                rows = [
+                    got[pl.ds(start, PAIR_DEV), (f * 2 + b) * CHUNKS + chunk].reshape(EDGE, cells)
+                    for b in range(2)
+                ]
+                slot = (chunk * cuts + cut) * 3 + f
+                load[slot] = jnp.concatenate(rows * GROUPS, axis=0).T
+    for chunk in range(CHUNKS):
+        for cut in range(cuts):
+            for f in range(3):
+                slot = (chunk * cuts + cut) * 3 + f
+                for j in range(steps):
+                    v = jnp.where(
+                        second,
+                        load[slot, pl.ds(steps + j, SUB, stride=stride), :],
+                        load[slot, pl.ds(j, SUB, stride=stride), :],
+                    )
+                    if f == 2:
+                        k = jnp.full_like(v, k_sat[0])
+                        for c in range(1, k_sat.shape[0]):
+                            k = jnp.where(v >= c, k_sat[c], k)
+                        v = k
+                    halos[chunk * cuts + cut][f, j] = v
+
+
+def first_kernel(
+    chunk, got, k_sat, heat_cond, head, warm, perm, conduct, wet, melt, cond, energy, top, load
+):
     cells = got.shape[-1]
     steps = head.shape[0]
     stride = steps * GROUPS
@@ -258,9 +291,6 @@
         melt[j] = f
         cond[j] = k * (f * s * s + 0.02)
         energy[j] = (1.0 + 2.0 * m) * t + 2.0 * m * f
-        for cut in range(cuts):
-            for i, v in enumerate((h, t, k)):
-                halos[cut][i, j] = halo_of(cut, v)
 
 
 def team_kernel(masks, head, warm, cond, water, heat):
@@ -532,24 +562,37 @@
     )[0]
     got = exchange(packed, n)
 
-    first, sides = [], []
-    for c in range(CHUNKS):
-        values = call(
-            functools.partial(first_kernel, c, cuts),
+    edges = call(
+        functools.partial(edge_kernel, cuts),
+        "edges",
+        (got, k_sat),
+        [(3,) + halo] * (CHUNKS * cuts),
+        scratch=[pltpu.VMEM((3 * CHUNKS * cuts, cells, LANES), F32)],
+        specs=[whole(), smem],
+    )
+    first = [
+        call(
+            functools.partial(first_kernel, c),
             "first",
             (got, k_sat, heat_cond),
-            [column] * 8 + [(1, ALL)] + [(3,) + halo] * cuts,
+            [column] * 8 + [(1, ALL)],
             scratch=[pltpu.VMEM((6, cells, LANES), F32)],
             specs=[whole(), smem, smem],
         )
-        first.append(values[:9])
-        mine = values[9:]
+        for c in range(CHUNKS)
+    ]
+    flows, sides = [], []
+    for c in range(CHUNKS):
+        mine = tuple(edges[c * cuts : (c + 1) * cuts])
+        if c:
+            mine, flows[-1] = lax.optimization_barrier((mine, flows[-1]))
         sides.append((mine, [swap(cut, n, v) for cut, v in enumerate(mine)]))
+        flows.append(tuple(call(team_kernel, "team", (masks, first[c][0], first[c][1], first[c][6]), [column] * 2)))
 
     second, later = [], []
     for c in range(CHUNKS):
         head, warm, perm, conduct, wet, melt, cond, energy, surface = first[c]
-        water, heat = call(team_kernel, "team", (masks, head, warm, cond), [column] * 2)
+        water, heat = flows[c]
         mine, theirs = sides[c]
         values = call(
             functools.partial(middle_kernel, cuts),

time: 59.7 us -> 60.3 us (1.010)
  blocking collectives: 33.9 us -> 14.1 us
  waiting for transfers between devices: 4.06 us -> 17.2 us
  starting transfers between devices: 5.28 us -> 12.1 us
  Pallas kernels: 15.1 us -> 15.8 us
    all_to_all x2 -> x1, blocking collectives: 33.9 us -> 14.1 us  [exchange(): lax.all_to_all(tiles, 'cols', split_axis=0, concat_axis=0, tiled=True, ax...]
    all_to_all x0 -> x1, waiting for transfers between devices: none -> 13.8 us  [exchange(): lax.all_to_all(tiles, 'cols', split_axis=0, concat_axis=0, tiled=True, ax...]
    all_to_all x0 -> x1, starting transfers between devices: none -> 6.3 us  [exchange(): lax.all_to_all(tiles, 'cols', split_axis=0, concat_axis=0, tiled=True, ax...]
    pallas_call x13 -> x14, Pallas kernels: 15.1 us -> 15.8 us  [call(): pl.pallas_call(kernel, out_shape=[jax.ShapeDtypeStruct(shape, F32) for sh...]
  transfers between devices with their start and end apart: 4 -> 5, of which waited for: 3 -> 3; matrix products, arithmetic and copies ran while one was open for 0% -> 0% of each run, Pallas kernels for 16% -> 17%
where the time goes in v8:
time: 60.3 us; the launch traced here: 60 us
  waiting for transfers between devices  17.2 us (29%)
  Pallas kernels  15.8 us (26%)
  blocking collectives  14.1 us (23%)
  starting transfers between devices  12.1 us (20%)
  between operations  0.77 us (1%)
    pallas_call x14, Pallas kernels, call(): pl.pallas_call(kernel, out_shape=[jax.ShapeDtypeStruct(shape, F32) for sh...  15.8 us
    all_to_all x1, blocking collectives, exchange(): lax.all_to_all(tiles, 'cols', split_axis=0, concat_axis=0, tiled=True, ax...  14.1 us
    all_to_all x1, waiting for transfers between devices, exchange(): lax.all_to_all(tiles, 'cols', split_axis=0, concat_axis=0, tiled=True, ax...  13.8 us
    all_to_all x1, starting transfers between devices, exchange(): lax.all_to_all(tiles, 'cols', split_axis=0, concat_axis=0, tiled=True, ax...  6.3 us
    ppermute x4, starting transfers between devices, swap(): return lax.ppermute(value, 'cols', pairs)  5.78 us
    ppermute x4, waiting for transfers between devices, swap(): return lax.ppermute(value, 'cols', pairs)  3.45 us
  transfers between devices with their start and end apart: 5, of which 3 were waited for; matrix products, arithmetic and copies ran while one was open for 0% of the time, Pallas kernels for 17%

profile of v8, /device:TPU:0, one launch (start us, length us, event | category | flops | bytes accessed | tf_op | source)
XLA Modules:
  0.0 60.0 jit_solution(4407391548617404510)
XLA Ops:
  0.6 3.0 %pack.1 = f32[16,13,8,128]{3,2,1,0:T(8,128)} custom-call(f32[128,512]{1,0:T(8,128)} %suction.1, f32[128,512]{1,0:T(8,128)} %warmth.1, s32[128,512]{1,0:T(8,128)} %classes.1, f32[1,512]{1,0:T(1,128)} %bitcast.1), custom_call_target="tpu_custom_call" | custom-call | flops 2000000 | bytes 2000000 | tf_op jit(solution)/shard_map/pack/pallas_call | solution.py:505
  3.6 0.0 copy-start.2
  3.6 6.3 %all-to-all-start = ((f32[16,13,8,128]{3,2,1,0:T(8,128)}), f32[16,13,8,128]{3,2,1,0:T(8,128)S(1)}, u32[]{:S(2)}, u32[]{:S(2)}) async-start(f32[16,13,8,128]{3,2,1,0:T(8,128)} %pack.1), calls=%async_computation | async-start | bytes 1703936 | tf_op jit(solution)/shard_map/all_to_all | solution.py:519
  10.0 0.0 copy-done.2
  10.0 0.0 copy-start
  10.0 0.3 masks.1.refs_0_
  10.2 13.8 %all-to-all-done.got = f32[16,13,8,128]{3,2,1,0:T(8,128)S(1)} async-done(((f32[16,13,8,128]{3,2,1,0:T(8,128)}), f32[16,13,8,128]{3,2,1,0:T(8,128)S(1)}, u32[]{:S(2)}, u32[]{:S(2)}) %all-to-all-start) | async-done | bytes 852000 | tf_op jit(solution)/shard_map/all_to_all | solution.py:519
  24.0 0.0 copy-done
  24.0 0.8 %edges.1 = (f32[3,8,8,128]{3,2,1,0:T(8,128)S(1)}, f32[3,8,8,128]{3,2,1,0:T(8,128)S(1)}) custom-call(f32[16,13,8,128]{3,2,1,0:T(8,128)S(1)} %all-to-all-done.got, f32[8]{0:T(128)S(1)} %copy-done), custom_call_target="tpu_custom_call" | custom-call | flops 2000000 | bytes 2000000 | tf_op jit(solution)/shard_map/edges/pallas_call | solution.py:505
  24.8 0.0 copy-start.1
  24.8 2.7 %collective-permute-start.2 = (f32[3,8,8,128]{3,2,1,0:T(8,128)S(1)}, f32[3,8,8,128]{3,2,1,0:T(8,128)S(1)}, u32[]{:S(2)}, u32[]{:S(2)}) collective-permute-start(f32[3,8,8,128]{3,2,1,0:T(8,128)S(1)} %get-tuple-element.79.refs_12_.refs_14_), channel_id=1, source_target_pairs={{0,16},{16,0},{1,17},{17,1},{2,18},{18,2},{3,19},{19,3},{4,20},{20... | collective-permute-start | bytes 294920 | tf_op jit(solution)/shard_map/ppermute | solution.py:529
  27.5 0.0 copy-done.1
  27.5 0.9 %first.3 = (f32[8,8,512]{2,1,0:T(8,128)S(1)}, f32[8,8,512]{2,1,0:T(8,128)S(1)}, f32[8,8,512]{2,1,0:T(8,128)S(1)}, f32[8,8,512]{2,1,0:T(8,128)S(1)}, f32[8,8,512]...) custom-call(f32[16,13,8,128]{3,2,1,0:T(8,128)S(1)} %all-to-all-done., ...), custom_call_target="tpu_custom_call" | custom-call | flops 2000000 | bytes 2000000 | tf_op jit(solution)/shard_map/first/pallas_call | solution.py:505
  28.4 1.4 %team.5 = (f32[8,8,512]{2,1,0:T(8,128)S(1)}, f32[8,8,512]{2,1,0:T(8,128)S(1)}) custom-call(f32[21,8,128]{2,1,0:T(8,128)S(1)} %masks.1.refs_0_, f32[8,8,512]{2,1,0:T(8,128)S(1)} %get-tuple-element.57.head.refs_1_, f32[8,8,512]{2,1,0:T(8,128)S(1)} %get-tuple-element.58.warm.refs_2_, f32[8,8,512]{2,1,0:T(8,128)S(1)} %get-tuple-element.59.cond.refs_7_), custom_call_target="tpu_custom_call" | custom-call | flops 2000000 | bytes 2000000 | tf_op jit(solution)/shard_map/team/pallas_call | solution.py:505
  29.8 0.6 %collective-permute-start = (f32[3,8,8,128]{3,2,1,0:T(8,128)S(1)}, f32[3,8,8,128]{3,2,1,0:T(8,128)S(1)}, u32[]{:S(2)}, u32[]{:S(2)}) collective-permute-start(f32[3,8,8,128]{3,2,1,0:T(8,128)S(1)} %get-tuple-element.62.refs_12_.refs_14_), channel_id=1, source_target_pairs={{0,16},{16,0},{1,17},{17,1},{2,18},{18,2},{3,19},{19,3},{4,20},{20... | collective-permute-start | bytes 294920 | tf_op jit(solution)/shard_map/ppermute | solution.py:529
  30.4 0.9 %first.2 = (f32[8,8,512]{2,1,0:T(8,128)S(1)}, f32[8,8,512]{2,1,0:T(8,128)S(1)}, f32[8,8,512]{2,1,0:T(8,128)S(1)}, f32[8,8,512]{2,1,0:T(8,128)S(1)}, f32[8,8,512]...) custom-call(f32[16,13,8,128]{3,2,1,0:T(8,128)S(1)} %all-to-all-done., ...), custom_call_target="tpu_custom_call" | custom-call | flops 2000000 | bytes 2000000 | tf_op jit(solution)/shard_map/first/pallas_call | solution.py:505
  31.4 1.4 %team.4 = (f32[8,8,512]{2,1,0:T(8,128)S(1)}, f32[8,8,512]{2,1,0:T(8,128)S(1)}) custom-call(f32[21,8,128]{2,1,0:T(8,128)S(1)} %masks.1.refs_0_, f32[8,8,512]{2,1,0:T(8,128)S(1)} %get-tuple-element.45.head.refs_1_, f32[8,8,512]{2,1,0:T(8,128)S(1)} %get-tuple-element.46.warm.refs_2_, f32[8,8,512]{2,1,0:T(8,128)S(1)} %get-tuple-element.51.cond.refs_7_), custom_call_target="tpu_custom_call" | custom-call | flops 2000000 | bytes 2000000 | tf_op jit(solution)/shard_map/team/pallas_call | solution.py:505
  32.7 0.0 collective-permute-done.2.refs_13_.refs_15_
  32.7 0.8 %middle.3 = (f32[8,8,512]{2,1,0:T(8,128)S(1)}, f32[8,8,512]{2,1,0:T(8,128)S(1)}, f32[8,8,512]{2,1,0:T(8,128)S(1)}, f32[8,8,512]{2,1,0:T(8,128)S(1)}, f32[8,8,512...) custom-call(f32[21,8,128]{2,1,0:T(8,128)S(1)} %masks.1.refs_0_, f32[8,8,512]{2,1,0:T(8,128)S(1)} %get-tuple-element.57.head.refs_1_, ...), custom_call_target="tpu_custom_call" | custom-call | flops 2000000 | bytes 2000000 | tf_op jit(solution)/shard_map/middle/pallas_call | solution.py:505
  33.6 2.4 %collective-permute-start.3 = (f32[2,8,8,128]{3,2,1,0:T(8,128)S(1)}, f32[2,8,8,128]{3,2,1,0:T(8,128)S(1)}, u32[]{:S(2)}, u32[]{:S(2)}) collective-permute-start(f32[2,8,8,128]{3,2,1,0:T(8,128)S(1)} %get-tuple-element.87.refs_12_), channel_id=1, source_target_pairs={{0,16},{16,0},{1,17},{17,1},{2,18},{18,2},{3,19},{19,3},{4,20},{20... | collective-permute-start | bytes 196616 | tf_op jit(solution)/shard_map/ppermute | solution.py:529
  36.0 1.9 %collective-permute-done.refs_13_.refs_15_ = f32[3,8,8,128]{3,2,1,0:T(8,128)S(1)} collective-permute-done((f32[3,8,8,128]{3,2,1,0:T(8,128)S(1)}, f32[3,8,8,128]{3,2,1,0:T(8,128)S(1)}, u32[]{:S(2)}, u32[]{:S(2)}) %collective-permute-start) | collective-permute-done | bytes 98336 | tf_op jit(solution)/shard_map/ppermute | solution.py:529
  38.0 0.8 %middle.2 = (f32[8,8,512]{2,1,0:T(8,128)S(1)}, f32[8,8,512]{2,1,0:T(8,128)S(1)}, f32[8,8,512]{2,1,0:T(8,128)S(1)}, f32[8,8,512]{2,1,0:T(8,128)S(1)}, f32[8,8,512...) custom-call(f32[21,8,128]{2,1,0:T(8,128)S(1)} %masks.1.refs_0_, f32[8,8,512]{2,1,0:T(8,128)S(1)} %get-tuple-element.45.head.refs_1_, ...), custom_call_target="tpu_custom_call" | custom-call | flops 2000000 | bytes 2000000 | tf_op jit(solution)/shard_map/middle/pallas_call | solution.py:505
  38.8 0.1 collective-permute-start.1
  38.9 1.4 %team.7 = (f32[8,8,512]{2,1,0:T(8,128)S(1)}, f32[8,8,512]{2,1,0:T(8,128)S(1)}) custom-call(f32[21,8,128]{2,1,0:T(8,128)S(1)} %masks.1.refs_0_, f32[8,8,512]{2,1,0:T(8,128)S(1)} %get-tuple-element.80.head.refs_1_, f32[8,8,512]{2,1,0:T(8,128)S(1)} %get-tuple-element.81.warm.refs_2_, f32[8,8,512]{2,1,0:T(8,128)S(1)} %get-tuple-element.84.cond.refs_7_), custom_call_target="tpu_custom_call" | custom-call | flops 2000000 | bytes 2000000 | tf_op jit(solution)/shard_map/team/pallas_call | solution.py:505
  40.2 1.4 %team.6 = (f32[8,8,512]{2,1,0:T(8,128)S(1)}, f32[8,8,512]{2,1,0:T(8,128)S(1)}) custom-call(f32[21,8,128]{2,1,0:T(8,128)S(1)} %masks.1.refs_0_, f32[8,8,512]{2,1,0:T(8,128)S(1)} %get-tuple-element.63.head.refs_1_, f32[8,8,512]{2,1,0:T(8,128)S(1)} %get-tuple-element.64.warm.refs_2_, f32[8,8,512]{2,1,0:T(8,128)S(1)} %get-tuple-element.67.cond.refs_7_), custom_call_target="tpu_custom_call" | custom-call | flops 2000000 | bytes 2000000 | tf_op jit(solution)/shard_map/team/pallas_call | solution.py:505
  41.6 0.0 collective-permute-done.3.refs_13_
  41.6 0.9 %last.2.refs_16_ = f32[16,4,8,128]{3,2,1,0:T(8,128)S(1)} custom-call(f32[21,8,128]{2,1,0:T(8,128)S(1)} %masks.1.refs_0_, f32[8,8,512]{2,1,0:T(8,128)S(1)} %get-tuple-element.80.head.refs_1_, f32[8,8,512]{2,1,0:T(8,128)S(1)} %get-tuple-element.81.warm.refs_2_, f32[8,8,512]{2,1,0:T(8,128)S(1)} %get-tuple-element.72.refs_4_.refs_3_, ...), custom_call_target="tpu_custom_call" | custom-call | flops 2000000 | bytes 2000000 | tf_op jit(solution)/shard_map/last/pallas_call | solution.py:505
  42.5 1.5 %collective-permute-done.1.refs_13_ = f32[2,8,8,128]{3,2,1,0:T(8,128)S(1)} collective-permute-done((f32[2,8,8,128]{3,2,1,0:T(8,128)S(1)}, f32[2,8,8,128]{3,2,1,0:T(8,128)S(1)}, u32[]{:S(2)}, u32[]{:S(2)}) %collective-permute-start.1) | collective-permute-done | bytes 65568 | tf_op jit(solution)/shard_map/ppermute | solution.py:529
  44.0 0.9 %last.3 = f32[16,8,8,128]{3,2,1,0:T(8,128)S(1)} custom-call(f32[21,8,128]{2,1,0:T(8,128)S(1)} %masks.1.refs_0_, f32[8,8,512]{2,1,0:T(8,128)S(1)} %get-tuple-element.63.head.refs_1_, f32[8,8,512]{2,1,0:T(8,128)S(1)} %get-tuple-element.64.warm.refs_2_, f32[8,8,512]{2,1,0:T(8,128)S(1)} %get-tuple-element.48.refs_4_.refs_3_, ...), custom_call_target="tpu_custom_call" | custom-call | flops 2000000 | bytes 2000000 | tf_op jit(solution)/shard_map/last/pallas_call | solution.py:505
  44.9 14.1 %all_to_all.10.got = f32[16,8,8,128]{3,2,1,0:T(8,128)S(1)} all-to-all(f32[16,8,8,128]{3,2,1,0:T(8,128)S(1)} %last.3), channel_id=1, replica_groups={{0,1,2,3,4,5,6,7,8,9,10,11,12,13,14,15},{16,17,18,19,20,21,22,23,24,25,..., dimensions={0} | all-to-all | bytes 1048576 | tf_op jit(solution)/shard_map/all_to_all | solution.py:519
  59.0 0.9 %unpack.1 = (f32[128,512]{1,0:T(8,128)}, f32[128,512]{1,0:T(8,128)}) custom-call(f32[16,8,8,128]{3,2,1,0:T(8,128)S(1)} %all_to_all.10.got), custom_call_target="tpu_custom_call" | custom-call | flops 2000000 | bytes 2000000 | tf_op jit(solution)/shard_map/unpack/pallas_call | solution.py:505
Async XLA Ops:
  3.6 6.3 %copy-start.2 = (s32[2,128]{1,0:T(2,128)S(1)}, s32[2,128]{1,0:T(2,128)}, u32[]{:S(2)}) copy-start(s32[2,128]{1,0:T(2,128)} %couplings.1) | copy-start | bytes 3076
  3.6 20.4 %all-to-all-start = ((f32[16,13,8,128]{3,2,1,0:T(8,128)}), f32[16,13,8,128]{3,2,1,0:T(8,128)S(1)}, u32[]{:S(2)}, u32[]{:S(2)}) async-start(f32[16,13,8,128]{3,2,1,0:T(8,128)} %pack.1), calls=%async_computation | async-start | bytes 1703936 | tf_op jit(solution)/shard_map/all_to_all | solution.py:519
  10.0 14.1 %copy-start = (f32[8]{0:T(128)S(1)}, f32[8]{0:T(128)}, u32[]{:S(2)}) copy-start(f32[8]{0:T(128)} %k_sat.5) | copy-start | bytes 100
  24.8 2.7 %copy-start.1 = (f32[8]{0:T(128)S(1)}, f32[8]{0:T(128)}, u32[]{:S(2)}) copy-start(f32[8]{0:T(128)} %heat_cond.3) | copy-start | bytes 100
  24.8 7.9 %collective-permute-start.2 = (f32[3,8,8,128]{3,2,1,0:T(8,128)S(1)}, f32[3,8,8,128]{3,2,1,0:T(8,128)S(1)}, u32[]{:S(2)}, u32[]{:S(2)}) collective-permute-start(f32[3,8,8,128]{3,2,1,0:T(8,128)S(1)} %get-tuple-element.79.refs_12_.refs_14_), channel_id=1, source_target_pairs={{0,16},{16,0},{1,17},{17,1},{2,18},{18,2},{3,19},{19,3},{4,20},{20... | collective-permute-start | bytes 294920 | tf_op jit(solution)/shard_map/ppermute | solution.py:529
  29.8 8.2 %collective-permute-start = (f32[3,8,8,128]{3,2,1,0:T(8,128)S(1)}, f32[3,8,8,128]{3,2,1,0:T(8,128)S(1)}, u32[]{:S(2)}, u32[]{:S(2)}) collective-permute-start(f32[3,8,8,128]{3,2,1,0:T(8,128)S(1)} %get-tuple-element.62.refs_12_.refs_14_), channel_id=1, source_target_pairs={{0,16},{16,0},{1,17},{17,1},{2,18},{18,2},{3,19},{19,3},{4,20},{20... | collective-permute-start | bytes 294920 | tf_op jit(solution)/shard_map/ppermute | solution.py:529
  33.6 8.0 %collective-permute-start.3 = (f32[2,8,8,128]{3,2,1,0:T(8,128)S(1)}, f32[2,8,8,128]{3,2,1,0:T(8,128)S(1)}, u32[]{:S(2)}, u32[]{:S(2)}) collective-permute-start(f32[2,8,8,128]{3,2,1,0:T(8,128)S(1)} %get-tuple-element.87.refs_12_), channel_id=1, source_target_pairs={{0,16},{16,0},{1,17},{17,1},{2,18},{18,2},{3,19},{19,3},{4,20},{20... | collective-permute-start | bytes 196616 | tf_op jit(solution)/shard_map/ppermute | solution.py:529
  38.8 5.2 %collective-permute-start.1 = (f32[2,8,8,128]{3,2,1,0:T(8,128)S(1)}, f32[2,8,8,128]{3,2,1,0:T(8,128)S(1)}, u32[]{:S(2)}, u32[]{:S(2)}) collective-permute-start(f32[2,8,8,128]{3,2,1,0:T(8,128)S(1)} %get-tuple-element.70.refs_12_), channel_id=1, source_target_pairs={{0,16},{16,0},{1,17},{17,1},{2,18},{18,2},{3,19},{19,3},{4,20},{20... | collective-permute-start | bytes 196616 | tf_op jit(solution)/shard_map/ppermute | solution.py:529

commit v9 on v8

--- a/solution.py
+++ b/solution.py
@@ -223,7 +223,7 @@
 def edge_kernel(cuts, got, k_sat, *refs):
     halos, load = refs[:-1], refs[-1]
     cells = got.shape[-1]
-    steps = halos[0].shape[1]
+    steps = halos[0].shape[0]
     stride = steps * GROUPS
     second = lax.broadcasted_iota(jnp.int32, (SUB, LANES), 1) >= 2 * EDGE
     for chunk in range(CHUNKS):
@@ -251,7 +251,7 @@
                         for c in range(1, k_sat.shape[0]):
                             k = jnp.where(v >= c, k_sat[c], k)
                         v = k
-                    halos[chunk * cuts + cut][f, j] = v
+                    halos[slot][j] = v
 
 
 def first_kernel(
@@ -445,40 +445,38 @@
 
 def middle_kernel(cuts, *refs):
     masks, head, warm, perm, conduct, wet, melt, cond, energy, top, water, heat = refs[:12]
-    own, far = refs[12 : 12 + cuts], refs[12 + cuts : 12 + 2 * cuts]
-    new_head, new_warm, new_wet, new_melt, new_cond = refs[12 + 2 * cuts : 17 + 2 * cuts]
-    halos = refs[17 + 2 * cuts : 17 + 3 * cuts]
-    inflow, warm_inflow, ratio, lead, value = refs[17 + 3 * cuts :]
+    own, far = refs[12 : 12 + 3 * cuts], refs[12 + 3 * cuts : 12 + 6 * cuts]
+    new_head, new_warm, new_wet, new_melt, new_cond = refs[12 + 6 * cuts : 17 + 6 * cuts]
+    halos = refs[17 + 6 * cuts : 17 + 8 * cuts]
+    inflow, warm_inflow, ratio, lead, value = refs[17 + 8 * cuts :]
 
     def finish(j, t):
         s, f = new_wet[j], sigmoid(2.0 * t)
         new_melt[j] = f
         new_cond[j] = perm[j] * (f * s * s + 0.02)
         for cut in range(cuts):
-            halos[cut][0, j] = halo_of(cut, new_head[j])
-            halos[cut][1, j] = halo_of(cut, t)
+            halos[2 * cut][j] = halo_of(cut, new_head[j])
+            halos[2 * cut + 1][j] = halo_of(cut, t)
 
     advance(
         head.shape[0], cuts, masks, head, warm, conduct, wet, energy, wet, melt, cond, water, heat, top,
-        lambda cut, j: [own[cut][i, j] for i in range(3)],
-        lambda cut, j: [far[cut][i, j] for i in range(3)],
+        lambda cut, j: [own[3 * cut + i][j] for i in range(3)],
+        lambda cut, j: [far[3 * cut + i][j] for i in range(3)],
         new_head, new_warm, new_wet, inflow, warm_inflow, ratio, lead, value, finish,
     )
 
 
 def last_kernel(chunk, cuts, *refs):
     masks, head, warm, conduct, stored, wet, melt, cond, energy, top, water, heat = refs[:12]
-    own, far = refs[12 : 12 + cuts], refs[12 + cuts : 12 + 2 * cuts]
-    own_k, far_k = refs[12 + 2 * cuts : 12 + 3 * cuts], refs[12 + 3 * cuts : 12 + 4 * cuts]
-    others = refs[12 + 4 * cuts : -10]
+    own, far, others = refs[12 : 12 + 3 * cuts], refs[12 + 3 * cuts : 12 + 6 * cuts], refs[12 + 6 * cuts : -10]
     out, new_head, new_warm, new_wet, inflow, warm_inflow, ratio, lead, value, load = refs[-10:]
     steps = head.shape[0]
     cells = steps * GROUPS * SUB
     stride = steps * GROUPS
     advance(
         steps, cuts, masks, head, warm, conduct, stored, energy, wet, melt, cond, water, heat, top,
-        lambda cut, j: [own[cut][0, j], own[cut][1, j], own_k[cut][2, j]],
-        lambda cut, j: [far[cut][0, j], far[cut][1, j], far_k[cut][2, j]],
+        lambda cut, j: [own[3 * cut + i][j] for i in range(3)],
+        lambda cut, j: [far[3 * cut + i][j] for i in range(3)],
         new_head, new_warm, new_wet, inflow, warm_inflow, ratio, lead, value, lambda j, t: None,
     )
     final = chunk == CHUNKS - 1
@@ -566,7 +564,7 @@
         functools.partial(edge_kernel, cuts),
         "edges",
         (got, k_sat),
-        [(3,) + halo] * (CHUNKS * cuts),
+        [halo] * (3 * CHUNKS * cuts),
         scratch=[pltpu.VMEM((3 * CHUNKS * cuts, cells, LANES), F32)],
         specs=[whole(), smem],
     )
@@ -583,10 +581,10 @@
     ]
     flows, sides = [], []
     for c in range(CHUNKS):
-        mine = tuple(edges[c * cuts : (c + 1) * cuts])
+        mine = tuple(edges[3 * c * cuts : 3 * (c + 1) * cuts])
         if c:
             mine, flows[-1] = lax.optimization_barrier((mine, flows[-1]))
-        sides.append((mine, [swap(cut, n, v) for cut, v in enumerate(mine)]))
+        sides.append((mine, [swap(i // 3, n, v) for i, v in enumerate(mine)]))
         flows.append(tuple(call(team_kernel, "team", (masks, first[c][0], first[c][1], first[c][6]), [column] * 2)))
 
     second, later = [], []
@@ -598,12 +596,18 @@
             functools.partial(middle_kernel, cuts),
             "middle",
             (masks, head, warm, perm, conduct, wet, melt, cond, energy, surface, water, heat, *mine, *theirs),
-            [column] * 5 + [(2,) + halo] * cuts,
+            [column] * 5 + [halo] * (2 * cuts),
             scratch=[room] * 5,
         )
         second.append(values[:5])
-        mine = values[5:]
-        later.append((mine, [swap(cut, n, v) for cut, v in enumerate(mine)]))
+        sent = values[5:]
+        came = [swap(i // 2, n, v) for i, v in enumerate(sent)]
+        later.append(
+            [
+                [v for cut in range(cuts) for v in (*new[2 * cut : 2 * cut + 2], old[3 * cut + 2])]
+                for new, old in ((sent, mine), (came, theirs))
+            ]
+        )
 
     done = []
     for c in range(CHUNKS):
@@ -611,14 +615,13 @@
         head, warm, wet, melt, cond = second[c]
         water, heat = call(team_kernel, "team", (masks, head, warm, cond), [column] * 2)
         mine, theirs = later[c]
-        mine_k, theirs_k = sides[c]
         final = c == CHUNKS - 1
         done += call(
             functools.partial(last_kernel, c, cuts),
             "last",
             (
                 masks, head, warm, conduct, stored, wet, melt, cond, energy, surface, water, heat,
-                *mine, *theirs, *mine_k, *theirs_k, *(done if final else ()),
+                *mine, *theirs, *(done if final else ()),
             ),
             [(TEAM, 2 * quarters if final else 4, OWN, cells)],
             scratch=[room] * 8 + [pltpu.VMEM((4, cells, LANES), F32)],

time: 60.3 us -> 66.5 us (1.10)
  blocking collectives: 14.1 us -> 33.5 us
  waiting for transfers between devices: 17.2 us -> 0.91 us
  starting transfers between devices: 12.1 us -> 15.2 us
    all_to_all x1 -> x2, blocking collectives: 14.1 us -> 33.5 us  [exchange(): lax.all_to_all(tiles, 'cols', split_axis=0, concat_axis=0, tiled=True, ax...]
    all_to_all x1 -> x0, waiting for transfers between devices: 13.8 us -> none  [exchange(): lax.all_to_all(tiles, 'cols', split_axis=0, concat_axis=0, tiled=True, ax...]
    ppermute x4 -> x10, starting transfers between devices: 5.78 us -> 15.2 us  [swap(): return lax.ppermute(value, 'cols', pairs)]
    all_to_all x1 -> x0, starting transfers between devices: 6.3 us -> none  [exchange(): lax.all_to_all(tiles, 'cols', split_axis=0, concat_axis=0, tiled=True, ax...]
    ppermute x4 -> x10, waiting for transfers between devices: 3.45 us -> 0.91 us  [swap(): return lax.ppermute(value, 'cols', pairs)]
  transfers between devices with their start and end apart: 5 -> 10, of which waited for: 3 -> 1; matrix products, arithmetic and copies ran while one was open for 0% -> 0% of each run, Pallas kernels for 17% -> 15%
where the time goes in v9:
time: 66.5 us; the launch traced here: 66.3 us
  blocking collectives  33.5 us (50%)
  Pallas kernels  15.8 us (24%)
  starting transfers between devices  15.2 us (23%)
  waiting for transfers between devices  0.91 us (1%)
  between operations  0.79 us (1%)
    all_to_all x2, blocking collectives, exchange(): lax.all_to_all(tiles, 'cols', split_axis=0, concat_axis=0, tiled=True, ax...  33.5 us
    pallas_call x14, Pallas kernels, call(): pl.pallas_call(kernel, out_shape=[jax.ShapeDtypeStruct(shape, F32) for sh...  15.8 us
    ppermute x10, starting transfers between devices, swap(): return lax.ppermute(value, 'cols', pairs)  15.2 us
  transfers between devices with their start and end apart: 10, of which 1 were waited for; matrix products, arithmetic and copies ran while one was open for 0% of the time, Pallas kernels for 15%

profile of v9, /device:TPU:0, one launch (start us, length us, event | category | flops | bytes accessed | tf_op | source)
XLA Modules:
  0.0 66.3 jit_solution(10935534427203956713)
XLA Ops:
  0.6 3.0 %pack.1 = f32[16,13,8,128]{3,2,1,0:T(8,128)} custom-call(f32[128,512]{1,0:T(8,128)} %suction.1, f32[128,512]{1,0:T(8,128)} %warmth.1, s32[128,512]{1,0:T(8,128)} %classes.1, f32[1,512]{1,0:T(1,128)} %bitcast.1), custom_call_target="tpu_custom_call" | custom-call | flops 2000000 | bytes 2000000 | tf_op jit(solution)/shard_map/pack/pallas_call | solution.py:503
  3.6 0.0 copy-start
  3.6 20.4 %all_to_all.10.got = f32[16,13,8,128]{3,2,1,0:T(8,128)S(1)} all-to-all(f32[16,13,8,128]{3,2,1,0:T(8,128)} %pack.1), channel_id=1, replica_groups={{0,1,2,3,4,5,6,7,8,9,10,11,12,13,14,15},{16,17,18,19,20,21,22,23,24,25,..., dimensions={0} | all-to-all | bytes 1703936 | tf_op jit(solution)/shard_map/all_to_all | solution.py:517
  24.0 0.8 %edges.1 = (f32[8,8,128]{2,1,0:T(8,128)S(1)}, f32[8,8,128]{2,1,0:T(8,128)S(1)}, f32[8,8,128]{2,1,0:T(8,128)S(1)}, f32[8,8,128]{2,1,0:T(8,128)S(1)}, f32[8,8,128]{2,1,0:T(8,128)S(1)}, /*index=5*/f32[8,8,128]{2,1,0:T(8,128)S(1)}) custom-call(f32[16,13,8,128]{3,2,1,0:T(8,128)S(1)} %all_to_all.10.got, f32[8]{0:T(128)S(1)} %copy-done), custom_call_target="tpu_custom_call" | custom-call | flops 2000000 | bytes 2000000 | tf_op jit(solution)/shard_map/edges/pallas_call | solution.py:503
  24.8 0.0 copy-start.2
  24.8 2.7 %collective-permute-start.7 = (f32[8,8,128]{2,1,0:T(8,128)S(1)}, f32[8,8,128]{2,1,0:T(8,128)S(1)}, u32[]{:S(2)}, u32[]{:S(2)}) collective-permute-start(f32[8,8,128]{2,1,0:T(8,128)S(1)} %get-tuple-element.94.refs_14_), channel_id=1, source_target_pairs={{0,16},{16,0},{1,17},{17,1},{2,18},{18,2},{3,19},{19,3},{4,20},{20... | collective-permute-start | bytes 98312 | tf_op jit(solution)/shard_map/ppermute | solution.py:527
  27.5 0.3 masks.1.refs_0_
  27.8 0.7 %collective-permute-start.5 = (f32[8,8,128]{2,1,0:T(8,128)S(1)}, f32[8,8,128]{2,1,0:T(8,128)S(1)}, u32[]{:S(2)}, u32[]{:S(2)}) collective-permute-start(f32[8,8,128]{2,1,0:T(8,128)S(1)} %get-tuple-element.92.refs_12_), channel_id=1, source_target_pairs={{0,16},{16,0},{1,17},{17,1},{2,18},{18,2},{3,19},{19,3},{4,20},{20... | collective-permute-start | bytes 98312 | tf_op jit(solution)/shard_map/ppermute | solution.py:527
  28.4 2.3 %collective-permute-start.6 = (f32[8,8,128]{2,1,0:T(8,128)S(1)}, f32[8,8,128]{2,1,0:T(8,128)S(1)}, u32[]{:S(2)}, u32[]{:S(2)}) collective-permute-start(f32[8,8,128]{2,1,0:T(8,128)S(1)} %get-tuple-element.93.refs_13_), channel_id=1, source_target_pairs={{0,16},{16,0},{1,17},{17,1},{2,18},{18,2},{3,19},{19,3},{4,20},{20... | collective-permute-start | bytes 98312 | tf_op jit(solution)/shard_map/ppermute | solution.py:527
  30.8 0.9 %first.3 = (f32[8,8,512]{2,1,0:T(8,128)S(1)}, f32[8,8,512]{2,1,0:T(8,128)S(1)}, f32[8,8,512]{2,1,0:T(8,128)S(1)}, f32[8,8,512]{2,1,0:T(8,128)S(1)}, f32[8,8,512]...) custom-call(f32[16,13,8,128]{3,2,1,0:T(8,128)S(1)} %all_to_all.10.go, ...), custom_call_target="tpu_custom_call" | custom-call | flops 2000000 | bytes 2000000 | tf_op jit(solution)/shard_map/first/pallas_call | solution.py:503
  31.7 1.4 %team.5 = (f32[8,8,512]{2,1,0:T(8,128)S(1)}, f32[8,8,512]{2,1,0:T(8,128)S(1)}) custom-call(f32[21,8,128]{2,1,0:T(8,128)S(1)} %masks.1.refs_0_, f32[8,8,512]{2,1,0:T(8,128)S(1)} %get-tuple-element.67.head.refs_1_, f32[8,8,512]{2,1,0:T(8,128)S(1)} %get-tuple-element.68.warm.refs_2_, f32[8,8,512]{2,1,0:T(8,128)S(1)} %get-tuple-element.69.cond.refs_7_), custom_call_target="tpu_custom_call" | custom-call | flops 2000000 | bytes 2000000 | tf_op jit(solution)/shard_map/team/pallas_call | solution.py:503
  33.0 0.7 %collective-permute-start = (f32[8,8,128]{2,1,0:T(8,128)S(1)}, f32[8,8,128]{2,1,0:T(8,128)S(1)}, u32[]{:S(2)}, u32[]{:S(2)}) collective-permute-start(f32[8,8,128]{2,1,0:T(8,128)S(1)} %get-tuple-element.72.refs_12_), channel_id=1, source_target_pairs={{0,16},{16,0},{1,17},{17,1},{2,18},{18,2},{3,19},{19,3},{4,20},{20... | collective-permute-start | bytes 98312 | tf_op jit(solution)/shard_map/ppermute | solution.py:527
  33.7 2.3 %collective-permute-start.1 = (f32[8,8,128]{2,1,0:T(8,128)S(1)}, f32[8,8,128]{2,1,0:T(8,128)S(1)}, u32[]{:S(2)}, u32[]{:S(2)}) collective-permute-start(f32[8,8,128]{2,1,0:T(8,128)S(1)} %get-tuple-element.73.refs_13_), channel_id=1, source_target_pairs={{0,16},{16,0},{1,17},{17,1},{2,18},{18,2},{3,19},{19,3},{4,20},{20... | collective-permute-start | bytes 98312 | tf_op jit(solution)/shard_map/ppermute | solution.py:527
  36.0 0.6 collective-permute-start.2
  36.6 0.9 %first.2 = (f32[8,8,512]{2,1,0:T(8,128)S(1)}, f32[8,8,512]{2,1,0:T(8,128)S(1)}, f32[8,8,512]{2,1,0:T(8,128)S(1)}, f32[8,8,512]{2,1,0:T(8,128)S(1)}, f32[8,8,512]...) custom-call(f32[16,13,8,128]{3,2,1,0:T(8,128)S(1)} %all_to_all.10.go, ...), custom_call_target="tpu_custom_call" | custom-call | flops 2000000 | bytes 2000000 | tf_op jit(solution)/shard_map/first/pallas_call | solution.py:503
  37.6 1.4 %team.4 = (f32[8,8,512]{2,1,0:T(8,128)S(1)}, f32[8,8,512]{2,1,0:T(8,128)S(1)}) custom-call(f32[21,8,128]{2,1,0:T(8,128)S(1)} %masks.1.refs_0_, f32[8,8,512]{2,1,0:T(8,128)S(1)} %get-tuple-element.53.head.refs_1_, f32[8,8,512]{2,1,0:T(8,128)S(1)} %get-tuple-element.54.warm.refs_2_, f32[8,8,512]{2,1,0:T(8,128)S(1)} %get-tuple-element.59.cond.refs_7_), custom_call_target="tpu_custom_call" | custom-call | flops 2000000 | bytes 2000000 | tf_op jit(solution)/shard_map/team/pallas_call | solution.py:503
  39.0 0.0 collective-permute-done.6.refs_16_
  39.0 0.8 %middle.3 = (f32[8,8,512]{2,1,0:T(8,128)S(1)}, f32[8,8,512]{2,1,0:T(8,128)S(1)}, f32[8,8,512]{2,1,0:T(8,128)S(1)}, f32[8,8,512]{2,1,0:T(8,128)S(1)}, f32[8,8,512...) custom-call(f32[21,8,128]{2,1,0:T(8,128)S(1)} %masks.1.refs_0_, ...), custom_call_target="tpu_custom_call" | custom-call | flops 2000000 | bytes 2000000 | tf_op jit(solution)/shard_map/middle/pallas_call | solution.py:503
  39.8 2.4 %collective-permute-start.8 = (f32[8,8,128]{2,1,0:T(8,128)S(1)}, f32[8,8,128]{2,1,0:T(8,128)S(1)}, u32[]{:S(2)}, u32[]{:S(2)}) collective-permute-start(f32[8,8,128]{2,1,0:T(8,128)S(1)} %get-tuple-element.102.refs_12_), channel_id=1, source_target_pairs={{0,16},{16,0},{1,17},{17,1},{2,18},{18,2},{3,19},{19,3},{4,20},{20... | collective-permute-start | bytes 98312 | tf_op jit(solution)/shard_map/ppermute | solution.py:527
  42.2 0.6 collective-permute-start.9
  42.8 0.0 collective-permute-done.refs_15_
  42.8 0.8 %middle.2 = (f32[8,8,512]{2,1,0:T(8,128)S(1)}, f32[8,8,512]{2,1,0:T(8,128)S(1)}, f32[8,8,512]{2,1,0:T(8,128)S(1)}, f32[8,8,512]{2,1,0:T(8,128)S(1)}, f32[8,8,512...) custom-call(f32[21,8,128]{2,1,0:T(8,128)S(1)} %masks.1.refs_0_, ...), custom_call_target="tpu_custom_call" | custom-call | flops 2000000 | bytes 2000000 | tf_op jit(solution)/shard_map/middle/pallas_call | solution.py:503
  43.7 2.4 %collective-permute-start.3 = (f32[8,8,128]{2,1,0:T(8,128)S(1)}, f32[8,8,128]{2,1,0:T(8,128)S(1)}, u32[]{:S(2)}, u32[]{:S(2)}) collective-permute-start(f32[8,8,128]{2,1,0:T(8,128)S(1)} %get-tuple-element.82.refs_12_), channel_id=1, source_target_pairs={{0,16},{16,0},{1,17},{17,1},{2,18},{18,2},{3,19},{19,3},{4,20},{20... | collective-permute-start | bytes 98312 | tf_op jit(solution)/shard_map/ppermute | solution.py:527
  46.1 0.6 collective-permute-start.4
  46.7 1.4 %team.7 = (f32[8,8,512]{2,1,0:T(8,128)S(1)}, f32[8,8,512]{2,1,0:T(8,128)S(1)}) custom-call(f32[21,8,128]{2,1,0:T(8,128)S(1)} %masks.1.refs_0_, f32[8,8,512]{2,1,0:T(8,128)S(1)} %get-tuple-element.95.head.refs_1_, f32[8,8,512]{2,1,0:T(8,128)S(1)} %get-tuple-element.96.warm.refs_2_, f32[8,8,512]{2,1,0:T(8,128)S(1)} %get-tuple-element.99.cond.refs_7_), custom_call_target="tpu_custom_call" | custom-call | flops 2000000 | bytes 2000000 | tf_op jit(solution)/shard_map/team/pallas_call | solution.py:503
  48.0 1.4 %team.6 = (f32[8,8,512]{2,1,0:T(8,128)S(1)}, f32[8,8,512]{2,1,0:T(8,128)S(1)}) custom-call(f32[21,8,128]{2,1,0:T(8,128)S(1)} %masks.1.refs_0_, f32[8,8,512]{2,1,0:T(8,128)S(1)} %get-tuple-element.75.head.refs_1_, f32[8,8,512]{2,1,0:T(8,128)S(1)} %get-tuple-element.76.warm.refs_2_, f32[8,8,512]{2,1,0:T(8,128)S(1)} %get-tuple-element.79.cond.refs_7_), custom_call_target="tpu_custom_call" | custom-call | flops 2000000 | bytes 2000000 | tf_op jit(solution)/shard_map/team/pallas_call | solution.py:503
  49.4 0.0 collective-permute-done.9.refs_16_
  49.4 0.9 %last.2.refs_18_ = f32[16,4,8,128]{3,2,1,0:T(8,128)S(1)} custom-call(f32[21,8,128]{2,1,0:T(8,128)S(1)} %masks.1.refs_0_, f32[8,8,512]{2,1,0:T(8,128)S(1)} %get-tuple-element.95.head.refs_1_, f32[8,8,512]{2,1,0:T(8,128)S(1)} %get-tuple-element.96.warm.refs_2_, f32[8,8,512]{2,1,0:T(8,128)S(1)} %get-tuple-element.85.refs_4_.refs_3_, ...), custom_call_target="tpu_custom_call" | custom-call | flops 2000000 | bytes 2000000 | tf_op jit(solution)/shard_map/last/pallas_call | solution.py:503
  50.4 0.9 %collective-permute-done.4.refs_16_ = f32[8,8,128]{2,1,0:T(8,128)S(1)} collective-permute-done((f32[8,8,128]{2,1,0:T(8,128)S(1)}, f32[8,8,128]{2,1,0:T(8,128)S(1)}, u32[]{:S(2)}, u32[]{:S(2)}) %collective-permute-start.4) | collective-permute-done | bytes 32800 | tf_op jit(solution)/shard_map/ppermute | solution.py:527
  51.2 0.9 %last.3 = f32[16,8,8,128]{3,2,1,0:T(8,128)S(1)} custom-call(f32[21,8,128]{2,1,0:T(8,128)S(1)} %masks.1.refs_0_, f32[8,8,512]{2,1,0:T(8,128)S(1)} %get-tuple-element.75.head.refs_1_, f32[8,8,512]{2,1,0:T(8,128)S(1)} %get-tuple-element.76.warm.refs_2_, f32[8,8,512]{2,1,0:T(8,128)S(1)} %get-tuple-element.56.refs_4_.refs_3_, ...), custom_call_target="tpu_custom_call" | custom-call | flops 2000000 | bytes 2000000 | tf_op jit(solution)/shard_map/last/pallas_call | solution.py:503
  52.1 13.2 %all_to_all.11.got = f32[16,8,8,128]{3,2,1,0:T(8,128)S(1)} all-to-all(f32[16,8,8,128]{3,2,1,0:T(8,128)S(1)} %last.3), channel_id=1, replica_groups={{0,1,2,3,4,5,6,7,8,9,10,11,12,13,14,15},{16,17,18,19,20,21,22,23,24,25,..., dimensions={0} | all-to-all | bytes 1048576 | tf_op jit(solution)/shard_map/all_to_all | solution.py:517
  65.3 0.9 %unpack.1 = (f32[128,512]{1,0:T(8,128)}, f32[128,512]{1,0:T(8,128)}) custom-call(f32[16,8,8,128]{3,2,1,0:T(8,128)S(1)} %all_to_all.11.got), custom_call_target="tpu_custom_call" | custom-call | flops 2000000 | bytes 2000000 | tf_op jit(solution)/shard_map/unpack/pallas_call | solution.py:503
  (10 shorter events, 0.0 us)
Async XLA Ops:
  3.6 20.4 %copy-start = (f32[8]{0:T(128)S(1)}, f32[8]{0:T(128)}, u32[]{:S(2)}) copy-start(f32[8]{0:T(128)} %k_sat.5) | copy-start | bytes 100
  24.8 2.7 %copy-start.2 = (s32[2,128]{1,0:T(2,128)S(1)}, s32[2,128]{1,0:T(2,128)}, u32[]{:S(2)}) copy-start(s32[2,128]{1,0:T(2,128)} %couplings.1) | copy-start | bytes 3076
  24.8 11.2 %collective-permute-start.7 = (f32[8,8,128]{2,1,0:T(8,128)S(1)}, f32[8,8,128]{2,1,0:T(8,128)S(1)}, u32[]{:S(2)}, u32[]{:S(2)}) collective-permute-start(f32[8,8,128]{2,1,0:T(8,128)S(1)} %get-tuple-element.94.refs_14_), channel_id=1, source_target_pairs={{0,16},{16,0},{1,17},{17,1},{2,18},{18,2},{3,19},{19,3},{4,20},{20... | collective-permute-start | bytes 98312 | tf_op jit(solution)/shard_map/ppermute | solution.py:527
  27.7 3.0 %copy-start.1 = (f32[8]{0:T(128)S(1)}, f32[8]{0:T(128)}, u32[]{:S(2)}) copy-start(f32[8]{0:T(128)} %heat_cond.3) | copy-start | bytes 100
  27.8 11.2 %collective-permute-start.5 = (f32[8,8,128]{2,1,0:T(8,128)S(1)}, f32[8,8,128]{2,1,0:T(8,128)S(1)}, u32[]{:S(2)}, u32[]{:S(2)}) collective-permute-start(f32[8,8,128]{2,1,0:T(8,128)S(1)} %get-tuple-element.92.refs_12_), channel_id=1, source_target_pairs={{0,16},{16,0},{1,17},{17,1},{2,18},{18,2},{3,19},{19,3},{4,20},{20... | collective-permute-start | bytes 98312 | tf_op jit(solution)/shard_map/ppermute | solution.py:527
  28.4 10.5 %collective-permute-start.6 = (f32[8,8,128]{2,1,0:T(8,128)S(1)}, f32[8,8,128]{2,1,0:T(8,128)S(1)}, u32[]{:S(2)}, u32[]{:S(2)}) collective-permute-start(f32[8,8,128]{2,1,0:T(8,128)S(1)} %get-tuple-element.93.refs_13_), channel_id=1, source_target_pairs={{0,16},{16,0},{1,17},{17,1},{2,18},{18,2},{3,19},{19,3},{4,20},{20... | collective-permute-start | bytes 98312 | tf_op jit(solution)/shard_map/ppermute | solution.py:527
  33.0 9.8 %collective-permute-start = (f32[8,8,128]{2,1,0:T(8,128)S(1)}, f32[8,8,128]{2,1,0:T(8,128)S(1)}, u32[]{:S(2)}, u32[]{:S(2)}) collective-permute-start(f32[8,8,128]{2,1,0:T(8,128)S(1)} %get-tuple-element.72.refs_12_), channel_id=1, source_target_pairs={{0,16},{16,0},{1,17},{17,1},{2,18},{18,2},{3,19},{19,3},{4,20},{20... | collective-permute-start | bytes 98312 | tf_op jit(solution)/shard_map/ppermute | solution.py:527
  33.7 9.1 %collective-permute-start.1 = (f32[8,8,128]{2,1,0:T(8,128)S(1)}, f32[8,8,128]{2,1,0:T(8,128)S(1)}, u32[]{:S(2)}, u32[]{:S(2)}) collective-permute-start(f32[8,8,128]{2,1,0:T(8,128)S(1)} %get-tuple-element.73.refs_13_), channel_id=1, source_target_pairs={{0,16},{16,0},{1,17},{17,1},{2,18},{18,2},{3,19},{19,3},{4,20},{20... | collective-permute-start | bytes 98312 | tf_op jit(solution)/shard_map/ppermute | solution.py:527
  36.0 6.8 %collective-permute-start.2 = (f32[8,8,128]{2,1,0:T(8,128)S(1)}, f32[8,8,128]{2,1,0:T(8,128)S(1)}, u32[]{:S(2)}, u32[]{:S(2)}) collective-permute-start(f32[8,8,128]{2,1,0:T(8,128)S(1)} %get-tuple-element.74.refs_14_), channel_id=1, source_target_pairs={{0,16},{16,0},{1,17},{17,1},{2,18},{18,2},{3,19},{19,3},{4,20},{20... | collective-permute-start | bytes 98312 | tf_op jit(solution)/shard_map/ppermute | solution.py:527
  39.8 9.6 %collective-permute-start.8 = (f32[8,8,128]{2,1,0:T(8,128)S(1)}, f32[8,8,128]{2,1,0:T(8,128)S(1)}, u32[]{:S(2)}, u32[]{:S(2)}) collective-permute-start(f32[8,8,128]{2,1,0:T(8,128)S(1)} %get-tuple-element.102.refs_12_), channel_id=1, source_target_pairs={{0,16},{16,0},{1,17},{17,1},{2,18},{18,2},{3,19},{19,3},{4,20},{20... | collective-permute-start | bytes 98312 | tf_op jit(solution)/shard_map/ppermute | solution.py:527
  42.2 7.2 %collective-permute-start.9 = (f32[8,8,128]{2,1,0:T(8,128)S(1)}, f32[8,8,128]{2,1,0:T(8,128)S(1)}, u32[]{:S(2)}, u32[]{:S(2)}) collective-permute-start(f32[8,8,128]{2,1,0:T(8,128)S(1)} %get-tuple-element.103.refs_13_), channel_id=1, source_target_pairs={{0,16},{16,0},{1,17},{17,1},{2,18},{18,2},{3,19},{19,3},{4,20},{20... | collective-permute-start | bytes 98312 | tf_op jit(solution)/shard_map/ppermute | solution.py:527
  43.7 6.6 %collective-permute-start.3 = (f32[8,8,128]{2,1,0:T(8,128)S(1)}, f32[8,8,128]{2,1,0:T(8,128)S(1)}, u32[]{:S(2)}, u32[]{:S(2)}) collective-permute-start(f32[8,8,128]{2,1,0:T(8,128)S(1)} %get-tuple-element.82.refs_12_), channel_id=1, source_target_pairs={{0,16},{16,0},{1,17},{17,1},{2,18},{18,2},{3,19},{19,3},{4,20},{20... | collective-permute-start | bytes 98312 | tf_op jit(solution)/shard_map/ppermute | solution.py:527
  46.1 5.2 %collective-permute-start.4 = (f32[8,8,128]{2,1,0:T(8,128)S(1)}, f32[8,8,128]{2,1,0:T(8,128)S(1)}, u32[]{:S(2)}, u32[]{:S(2)}) collective-permute-start(f32[8,8,128]{2,1,0:T(8,128)S(1)} %get-tuple-element.83.refs_13_), channel_id=1, source_target_pairs={{0,16},{16,0},{1,17},{17,1},{2,18},{18,2},{3,19},{19,3},{4,20},{20... | collective-permute-start | bytes 98312 | tf_op jit(solution)/shard_map/ppermute | solution.py:527

commit v10 on v8

--- a/solution.py
+++ b/solution.py
@@ -19,9 +19,7 @@
 ALL = GROUPS * WIDTH
 EDGE = PAIR_DEV * OWN
 VMEM_LIMIT = 32 * 1024 * 1024
-PACK_LIMIT = 60 * 1024 * 1024
 DISTANCES = range(1, PAIR_DEV + 1)
-SENDS = 4
 F32 = jnp.float32
 
 
@@ -167,31 +165,26 @@
         put(row + 2 * PAIR_DEV, jnp.where(outward < EDGE, 1.0, 0.0))
 
 
-def pack_kernel(suction, warmth, classes, top, out, room, class_room, turned, in_sems, out_sems):
-    cells = turned.shape[-1]
+def pack_kernel(suction, warmth, classes, surface, out, room, class_room, top, in_sems):
+    cells = out.shape[-1]
     quarters = 2 * CHUNKS
     into = []
-    for f, field in enumerate((suction, warmth, classes)):
-        into.append(pltpu.make_async_copy(field, class_room if f == 2 else room.at[f], in_sems.at[f]))
+    for f, field in enumerate((suction, warmth, classes, surface)):
+        target = (room.at[0], room.at[1], class_room, top)[f]
+        into.append(pltpu.make_async_copy(field, target, in_sems.at[f]))
         into[-1].start()
 
     def put(slot, value):
-        turned[:, slot] = value.T.reshape(TEAM, OWN, cells)
-
-    rows = [top[0:1, q * LANES : (q + 1) * LANES] for q in range(quarters)]
-    put(3 * quarters, jnp.concatenate(rows + [jnp.zeros((cells - quarters, LANES), F32)], axis=0))
+        out[:, slot] = value.T.reshape(TEAM, OWN, cells)
+
     for f in range(3):
         into[f].wait()
         for q in range(quarters):
             lanes = slice(q * LANES, (q + 1) * LANES)
             put(f * quarters + q, class_room[:, lanes].astype(F32) if f == 2 else room[f, :, lanes])
-    sent = []
-    for i in range(SENDS):
-        rows = pl.ds(i * (TEAM // SENDS), TEAM // SENDS)
-        sent.append(pltpu.make_async_copy(turned.at[rows], out.at[rows], out_sems.at[i]))
-        sent[-1].start()
-    for copy in sent:
-        copy.wait()
+    into[3].wait()
+    rows = [top[0:1, q * LANES : (q + 1) * LANES] for q in range(quarters)]
+    put(3 * quarters, jnp.concatenate(rows + [jnp.zeros((cells - quarters, LANES), F32)], axis=0))
 
 
 def unpack_kernel(got, suction, warmth, room, sems):
@@ -547,18 +540,15 @@
     packed = call(
         pack_kernel,
         "pack",
-        (suction, warmth, classes, top.reshape(1, width)),
+        [pltpu.with_memory_space_constraint(v, pltpu.HBM) for v in (suction, warmth, classes, top.reshape(1, width))],
         [(TEAM, 3 * quarters + 1, OWN, cells)],
         scratch=[
             pltpu.VMEM((2, cells, width), F32),
             pltpu.VMEM((cells, width), classes.dtype),
-            pltpu.VMEM((TEAM, 3 * quarters + 1, OWN, cells), F32),
-            pltpu.SemaphoreType.DMA((3,)),
-            pltpu.SemaphoreType.DMA((SENDS,)),
+            pltpu.VMEM((1, width), F32),
+            pltpu.SemaphoreType.DMA((4,)),
         ],
-        specs=[hbm, hbm, hbm, whole()],
-        out_specs=[hbm],
-        limit=PACK_LIMIT,
+        specs=[hbm] * 4,
     )[0]
     got = exchange(packed, n)
 
@@ -584,8 +574,6 @@
     flows, sides = [], []
     for c in range(CHUNKS):
         mine = tuple(edges[c * cuts : (c + 1) * cuts])
-        if c:
-            mine, flows[-1] = lax.optimization_barrier((mine, flows[-1]))
         sides.append((mine, [swap(cut, n, v) for cut, v in enumerate(mine)]))
         flows.append(tuple(call(team_kernel, "team", (masks, first[c][0], first[c][1], first[c][6]), [column] * 2)))
 

time: 60.3 us -> 57.7 us (0.957)
  blocking collectives: 14.1 us -> 33.7 us
  waiting for transfers between devices: 17.2 us -> 2.64 us
  starting transfers between devices: 12.1 us -> 6.05 us
  Pallas kernels: 15.8 us -> 14.2 us
    all_to_all x1 -> x2, blocking collectives: 14.1 us -> 33.7 us  [exchange(): lax.all_to_all(tiles, 'cols', split_axis=0, concat_axis=0, tiled=True, ax...]
    all_to_all x1 -> x0, waiting for transfers between devices: 13.8 us -> none  [exchange(): lax.all_to_all(tiles, 'cols', split_axis=0, concat_axis=0, tiled=True, ax...]
    all_to_all x1 -> x0, starting transfers between devices: 6.3 us -> none  [exchange(): lax.all_to_all(tiles, 'cols', split_axis=0, concat_axis=0, tiled=True, ax...]
    pallas_call x14, Pallas kernels: 15.8 us -> 14.2 us  [call(): pl.pallas_call(kernel, out_shape=[jax.ShapeDtypeStruct(shape, F32) for sh...]
    ppermute x4, waiting for transfers between devices: 3.45 us -> 2.64 us  [swap(): return lax.ppermute(value, 'cols', pairs)]
  transfers between devices with their start and end apart: 5 -> 4, of which waited for: 3 -> 2; matrix products, arithmetic and copies ran while one was open for 0% -> 0% of each run, Pallas kernels for 17% -> 18%
where the time goes in v10:
time: 57.7 us; the launch traced here: 57.4 us
  blocking collectives  33.7 us (58%)
  Pallas kernels  14.2 us (25%)
  starting transfers between devices  6.05 us (10%)
  waiting for transfers between devices  2.64 us (5%)
  between operations  0.73 us (1%)
    all_to_all x2, blocking collectives, exchange(): lax.all_to_all(tiles, 'cols', split_axis=0, concat_axis=0, tiled=True, ax...  33.7 us
    pallas_call x14, Pallas kernels, call(): pl.pallas_call(kernel, out_shape=[jax.ShapeDtypeStruct(shape, F32) for sh...  14.2 us
    ppermute x4, starting transfers between devices, swap(): return lax.ppermute(value, 'cols', pairs)  6.05 us
    ppermute x4, waiting for transfers between devices, swap(): return lax.ppermute(value, 'cols', pairs)  2.64 us
  transfers between devices with their start and end apart: 4, of which 2 were waited for; matrix products, arithmetic and copies ran while one was open for 0% of the time, Pallas kernels for 18%

profile of v10, /device:TPU:0, one launch (start us, length us, event | category | flops | bytes accessed | tf_op | source)
XLA Modules:
  0.0 57.4 jit_solution(5857450189419994416)
XLA Ops:
  0.6 1.5 %pack.1 = f32[16,13,8,128]{3,2,1,0:T(8,128)S(1)} custom-call(f32[128,512]{1,0:T(8,128)} %suction.1, f32[128,512]{1,0:T(8,128)} %warmth.1, s32[128,512]{1,0:T(8,128)} %classes.1, f32[1,512]{1,0:T(1,128)} %bitcast.1), custom_call_target="tpu_custom_call" | custom-call | flops 2000000 | bytes 2000000 | tf_op jit(solution)/shard_map/pack/pallas_call | solution.py:498
  2.1 0.0 copy-start
  2.1 20.1 %all_to_all.10.got = f32[16,13,8,128]{3,2,1,0:T(8,128)S(1)} all-to-all(f32[16,13,8,128]{3,2,1,0:T(8,128)S(1)} %pack.1), channel_id=1, replica_groups={{0,1,2,3,4,5,6,7,8,9,10,11,12,13,14,15},{16,17,18,19,20,21,22,23,24,25,..., dimensions={0} | all-to-all | bytes 1703936 | tf_op jit(solution)/shard_map/all_to_all | solution.py:512
  22.3 0.0 copy-done
  22.3 0.8 %edges.1 = (f32[3,8,8,128]{3,2,1,0:T(8,128)S(1)}, f32[3,8,8,128]{3,2,1,0:T(8,128)S(1)}) custom-call(f32[16,13,8,128]{3,2,1,0:T(8,128)S(1)} %all_to_all.10.got, f32[8]{0:T(128)S(1)} %copy-done), custom_call_target="tpu_custom_call" | custom-call | flops 2000000 | bytes 2000000 | tf_op jit(solution)/shard_map/edges/pallas_call | solution.py:498
  23.1 0.0 copy-start.2
  23.1 2.7 %collective-permute-start.2 = (f32[3,8,8,128]{3,2,1,0:T(8,128)S(1)}, f32[3,8,8,128]{3,2,1,0:T(8,128)S(1)}, u32[]{:S(2)}, u32[]{:S(2)}) collective-permute-start(f32[3,8,8,128]{3,2,1,0:T(8,128)S(1)} %get-tuple-element.73.refs_12_.refs_14_), channel_id=1, source_target_pairs={{0,16},{16,0},{1,17},{17,1},{2,18},{18,2},{3,19},{19,3},{4,20},{20... | collective-permute-start | bytes 294920 | tf_op jit(solution)/shard_map/ppermute | solution.py:522
  25.8 0.0 copy-start.1
  25.8 0.3 collective-permute-start
  26.1 0.0 copy-done.2
  26.1 0.3 masks.1.refs_0_
  26.4 0.1 copy-done.1
  26.4 0.9 %first.3 = (f32[8,8,512]{2,1,0:T(8,128)S(1)}, f32[8,8,512]{2,1,0:T(8,128)S(1)}, f32[8,8,512]{2,1,0:T(8,128)S(1)}, f32[8,8,512]{2,1,0:T(8,128)S(1)}, f32[8,8,512]...) custom-call(f32[16,13,8,128]{3,2,1,0:T(8,128)S(1)} %all_to_all.10.go, ...), custom_call_target="tpu_custom_call" | custom-call | flops 2000000 | bytes 2000000 | tf_op jit(solution)/shard_map/first/pallas_call | solution.py:498
  27.4 1.4 %team.6 = (f32[8,8,512]{2,1,0:T(8,128)S(1)}, f32[8,8,512]{2,1,0:T(8,128)S(1)}) custom-call(f32[21,8,128]{2,1,0:T(8,128)S(1)} %masks.1.refs_0_, f32[8,8,512]{2,1,0:T(8,128)S(1)} %get-tuple-element.62.head.refs_1_, f32[8,8,512]{2,1,0:T(8,128)S(1)} %get-tuple-element.63.warm.refs_2_, f32[8,8,512]{2,1,0:T(8,128)S(1)} %get-tuple-element.68.cond.refs_7_), custom_call_target="tpu_custom_call" | custom-call | flops 2000000 | bytes 2000000 | tf_op jit(solution)/shard_map/team/pallas_call | solution.py:498
  28.7 0.9 %first.2 = (f32[8,8,512]{2,1,0:T(8,128)S(1)}, f32[8,8,512]{2,1,0:T(8,128)S(1)}, f32[8,8,512]{2,1,0:T(8,128)S(1)}, f32[8,8,512]{2,1,0:T(8,128)S(1)}, f32[8,8,512]...) custom-call(f32[16,13,8,128]{3,2,1,0:T(8,128)S(1)} %all_to_all.10.go, ...), custom_call_target="tpu_custom_call" | custom-call | flops 2000000 | bytes 2000000 | tf_op jit(solution)/shard_map/first/pallas_call | solution.py:498
  29.7 1.4 %team.4 = (f32[8,8,512]{2,1,0:T(8,128)S(1)}, f32[8,8,512]{2,1,0:T(8,128)S(1)}) custom-call(f32[21,8,128]{2,1,0:T(8,128)S(1)} %masks.1.refs_0_, f32[8,8,512]{2,1,0:T(8,128)S(1)} %get-tuple-element.42.head.refs_1_, f32[8,8,512]{2,1,0:T(8,128)S(1)} %get-tuple-element.43.warm.refs_2_, f32[8,8,512]{2,1,0:T(8,128)S(1)} %get-tuple-element.48.cond.refs_7_), custom_call_target="tpu_custom_call" | custom-call | flops 2000000 | bytes 2000000 | tf_op jit(solution)/shard_map/team/pallas_call | solution.py:498
  31.0 1.9 %collective-permute-done.2.refs_13_.refs_15_ = f32[3,8,8,128]{3,2,1,0:T(8,128)S(1)} collective-permute-done((f32[3,8,8,128]{3,2,1,0:T(8,128)S(1)}, f32[3,8,8,128]{3,2,1,0:T(8,128)S(1)}, u32[]{:S(2)}, u32[]{:S(2)}) %collective-permute-start.2) | collective-permute-done | bytes 98336 | tf_op jit(solution)/shard_map/ppermute | solution.py:522
  33.0 0.8 %middle.3 = (f32[8,8,512]{2,1,0:T(8,128)S(1)}, f32[8,8,512]{2,1,0:T(8,128)S(1)}, f32[8,8,512]{2,1,0:T(8,128)S(1)}, f32[8,8,512]{2,1,0:T(8,128)S(1)}, f32[8,8,512...) custom-call(f32[21,8,128]{2,1,0:T(8,128)S(1)} %masks.1.refs_0_, f32[8,8,512]{2,1,0:T(8,128)S(1)} %get-tuple-element.62.head.refs_1_, ...), custom_call_target="tpu_custom_call" | custom-call | flops 2000000 | bytes 2000000 | tf_op jit(solution)/shard_map/middle/pallas_call | solution.py:498
  33.8 0.7 %collective-permute-start.3 = (f32[2,8,8,128]{3,2,1,0:T(8,128)S(1)}, f32[2,8,8,128]{3,2,1,0:T(8,128)S(1)}, u32[]{:S(2)}, u32[]{:S(2)}) collective-permute-start(f32[2,8,8,128]{3,2,1,0:T(8,128)S(1)} %get-tuple-element.81.refs_12_), channel_id=1, source_target_pairs={{0,16},{16,0},{1,17},{17,1},{2,18},{18,2},{3,19},{19,3},{4,20},{20... | collective-permute-start | bytes 196616 | tf_op jit(solution)/shard_map/ppermute | solution.py:522
  34.5 0.0 collective-permute-done.refs_13_.refs_15_
  34.5 0.8 %middle.2 = (f32[8,8,512]{2,1,0:T(8,128)S(1)}, f32[8,8,512]{2,1,0:T(8,128)S(1)}, f32[8,8,512]{2,1,0:T(8,128)S(1)}, f32[8,8,512]{2,1,0:T(8,128)S(1)}, f32[8,8,512...) custom-call(f32[21,8,128]{2,1,0:T(8,128)S(1)} %masks.1.refs_0_, f32[8,8,512]{2,1,0:T(8,128)S(1)} %get-tuple-element.42.head.refs_1_, ...), custom_call_target="tpu_custom_call" | custom-call | flops 2000000 | bytes 2000000 | tf_op jit(solution)/shard_map/middle/pallas_call | solution.py:498
  35.3 2.4 %collective-permute-start.1 = (f32[2,8,8,128]{3,2,1,0:T(8,128)S(1)}, f32[2,8,8,128]{3,2,1,0:T(8,128)S(1)}, u32[]{:S(2)}, u32[]{:S(2)}) collective-permute-start(f32[2,8,8,128]{3,2,1,0:T(8,128)S(1)} %get-tuple-element.61.refs_12_), channel_id=1, source_target_pairs={{0,16},{16,0},{1,17},{17,1},{2,18},{18,2},{3,19},{19,3},{4,20},{20... | collective-permute-start | bytes 196616 | tf_op jit(solution)/shard_map/ppermute | solution.py:522
  37.7 1.4 %team.7 = (f32[8,8,512]{2,1,0:T(8,128)S(1)}, f32[8,8,512]{2,1,0:T(8,128)S(1)}) custom-call(f32[21,8,128]{2,1,0:T(8,128)S(1)} %masks.1.refs_0_, f32[8,8,512]{2,1,0:T(8,128)S(1)} %get-tuple-element.74.head.refs_1_, f32[8,8,512]{2,1,0:T(8,128)S(1)} %get-tuple-element.75.warm.refs_2_, f32[8,8,512]{2,1,0:T(8,128)S(1)} %get-tuple-element.78.cond.refs_7_), custom_call_target="tpu_custom_call" | custom-call | flops 2000000 | bytes 2000000 | tf_op jit(solution)/shard_map/team/pallas_call | solution.py:498
  39.1 1.4 %team.5 = (f32[8,8,512]{2,1,0:T(8,128)S(1)}, f32[8,8,512]{2,1,0:T(8,128)S(1)}) custom-call(f32[21,8,128]{2,1,0:T(8,128)S(1)} %masks.1.refs_0_, f32[8,8,512]{2,1,0:T(8,128)S(1)} %get-tuple-element.54.head.refs_1_, f32[8,8,512]{2,1,0:T(8,128)S(1)} %get-tuple-element.55.warm.refs_2_, f32[8,8,512]{2,1,0:T(8,128)S(1)} %get-tuple-element.58.cond.refs_7_), custom_call_target="tpu_custom_call" | custom-call | flops 2000000 | bytes 2000000 | tf_op jit(solution)/shard_map/team/pallas_call | solution.py:498
  40.4 0.7 %collective-permute-done.3.refs_13_ = f32[2,8,8,128]{3,2,1,0:T(8,128)S(1)} collective-permute-done((f32[2,8,8,128]{3,2,1,0:T(8,128)S(1)}, f32[2,8,8,128]{3,2,1,0:T(8,128)S(1)}, u32[]{:S(2)}, u32[]{:S(2)}) %collective-permute-start.3) | collective-permute-done | bytes 65568 | tf_op jit(solution)/shard_map/ppermute | solution.py:522
  41.1 0.9 %last.2.refs_16_ = f32[16,4,8,128]{3,2,1,0:T(8,128)S(1)} custom-call(f32[21,8,128]{2,1,0:T(8,128)S(1)} %masks.1.refs_0_, f32[8,8,512]{2,1,0:T(8,128)S(1)} %get-tuple-element.74.head.refs_1_, f32[8,8,512]{2,1,0:T(8,128)S(1)} %get-tuple-element.75.warm.refs_2_, f32[8,8,512]{2,1,0:T(8,128)S(1)} %get-tuple-element.65.refs_4_.refs_3_, ...), custom_call_target="tpu_custom_call" | custom-call | flops 2000000 | bytes 2000000 | tf_op jit(solution)/shard_map/last/pallas_call | solution.py:498
  42.0 0.0 collective-permute-done.1.refs_13_
  42.0 0.9 %last.3 = f32[16,8,8,128]{3,2,1,0:T(8,128)S(1)} custom-call(f32[21,8,128]{2,1,0:T(8,128)S(1)} %masks.1.refs_0_, f32[8,8,512]{2,1,0:T(8,128)S(1)} %get-tuple-element.54.head.refs_1_, f32[8,8,512]{2,1,0:T(8,128)S(1)} %get-tuple-element.55.warm.refs_2_, f32[8,8,512]{2,1,0:T(8,128)S(1)} %get-tuple-element.45.refs_4_.refs_3_, ...), custom_call_target="tpu_custom_call" | custom-call | flops 2000000 | bytes 2000000 | tf_op jit(solution)/shard_map/last/pallas_call | solution.py:498
  42.9 13.6 %all_to_all.11.got = f32[16,8,8,128]{3,2,1,0:T(8,128)S(1)} all-to-all(f32[16,8,8,128]{3,2,1,0:T(8,128)S(1)} %last.3), channel_id=1, replica_groups={{0,1,2,3,4,5,6,7,8,9,10,11,12,13,14,15},{16,17,18,19,20,21,22,23,24,25,..., dimensions={0} | all-to-all | bytes 1048576 | tf_op jit(solution)/shard_map/all_to_all | solution.py:512
  56.5 0.9 %unpack.1 = (f32[128,512]{1,0:T(8,128)}, f32[128,512]{1,0:T(8,128)}) custom-call(f32[16,8,8,128]{3,2,1,0:T(8,128)S(1)} %all_to_all.11.got), custom_call_target="tpu_custom_call" | custom-call | flops 2000000 | bytes 2000000 | tf_op jit(solution)/shard_map/unpack/pallas_call | solution.py:498
Async XLA Ops:
  2.1 20.2 %copy-start = (f32[8]{0:T(128)S(1)}, f32[8]{0:T(128)}, u32[]{:S(2)}) copy-start(f32[8]{0:T(128)} %k_sat.5) | copy-start | bytes 100
  23.1 3.0 %copy-start.2 = (s32[2,128]{1,0:T(2,128)S(1)}, s32[2,128]{1,0:T(2,128)}, u32[]{:S(2)}) copy-start(s32[2,128]{1,0:T(2,128)} %couplings.1) | copy-start | bytes 3076
  23.1 9.9 %collective-permute-start.2 = (f32[3,8,8,128]{3,2,1,0:T(8,128)S(1)}, f32[3,8,8,128]{3,2,1,0:T(8,128)S(1)}, u32[]{:S(2)}, u32[]{:S(2)}) collective-permute-start(f32[3,8,8,128]{3,2,1,0:T(8,128)S(1)} %get-tuple-element.73.refs_12_.refs_14_), channel_id=1, source_target_pairs={{0,16},{16,0},{1,17},{17,1},{2,18},{18,2},{3,19},{19,3},{4,20},{20... | collective-permute-start | bytes 294920 | tf_op jit(solution)/shard_map/ppermute | solution.py:522
  25.8 0.7 %copy-start.1 = (f32[8]{0:T(128)S(1)}, f32[8]{0:T(128)}, u32[]{:S(2)}) copy-start(f32[8]{0:T(128)} %heat_cond.3) | copy-start | bytes 100
  25.8 8.7 %collective-permute-start = (f32[3,8,8,128]{3,2,1,0:T(8,128)S(1)}, f32[3,8,8,128]{3,2,1,0:T(8,128)S(1)}, u32[]{:S(2)}, u32[]{:S(2)}) collective-permute-start(f32[3,8,8,128]{3,2,1,0:T(8,128)S(1)} %get-tuple-element.53.refs_12_.refs_14_), channel_id=1, source_target_pairs={{0,16},{16,0},{1,17},{17,1},{2,18},{18,2},{3,19},{19,3},{4,20},{20... | collective-permute-start | bytes 294920 | tf_op jit(solution)/shard_map/ppermute | solution.py:522
  33.8 7.3 %collective-permute-start.3 = (f32[2,8,8,128]{3,2,1,0:T(8,128)S(1)}, f32[2,8,8,128]{3,2,1,0:T(8,128)S(1)}, u32[]{:S(2)}, u32[]{:S(2)}) collective-permute-start(f32[2,8,8,128]{3,2,1,0:T(8,128)S(1)} %get-tuple-element.81.refs_12_), channel_id=1, source_target_pairs={{0,16},{16,0},{1,17},{17,1},{2,18},{18,2},{3,19},{19,3},{4,20},{20... | collective-permute-start | bytes 196616 | tf_op jit(solution)/shard_map/ppermute | solution.py:522
  35.3 6.7 %collective-permute-start.1 = (f32[2,8,8,128]{3,2,1,0:T(8,128)S(1)}, f32[2,8,8,128]{3,2,1,0:T(8,128)S(1)}, u32[]{:S(2)}, u32[]{:S(2)}) collective-permute-start(f32[2,8,8,128]{3,2,1,0:T(8,128)S(1)} %get-tuple-element.61.refs_12_), channel_id=1, source_target_pairs={{0,16},{16,0},{1,17},{17,1},{2,18},{18,2},{3,19},{19,3},{4,20},{20... | collective-permute-start | bytes 196616 | tf_op jit(solution)/shard_map/ppermute | solution.py:522

commit v11 on v10

--- a/solution.py
+++ b/solution.py
@@ -30,6 +30,10 @@
 def place(cut):
     team = lax.axis_index("cols") // TEAM
     return team, lax.rem(team, 2) == cut
+
+
+def far_edge(above):
+    return jnp.where(above, 0, PAIR_DEV - 1)
 
 
 def sign_of(cut):
@@ -159,7 +163,7 @@
             put(row + s - 1, jnp.where(active, factor, 0.0))
             apart = jnp.where(above, PAIR_DEV - s, s - PAIR_DEV)
             up, down = chosen(start + edge + apart, s)
-            theirs = jnp.where(above, down, up)
+            theirs = jnp.where(edge_1 == far_edge(jnp.logical_not(above)), 0.0, jnp.where(above, down, up))
             put(row + PAIR_DEV + s - 1, jnp.where(jnp.abs(theirs - block.astype(F32)) < 0.5, 1.0, 0.0))
         outward = jnp.where(above, LANES - 1 - lane_1, lane_1)
         put(row + 2 * PAIR_DEV, jnp.where(outward < EDGE, 1.0, 0.0))
@@ -213,8 +217,44 @@
     return packed
 
 
-def edge_kernel(cuts, got, k_sat, *refs):
-    halos, load = refs[:-1], refs[-1]
+def needed_block(cut, couplings):
+    team, above = place(cut)
+    pair = (team * TEAM + jnp.where(above, TEAM - PAIR_DEV, -1)) * PAIR_DEV + PAIR_DEV - 1
+    return couplings[jnp.where(above, 0, 1), jnp.maximum(pair, 0)]
+
+
+def pieces(above):
+    spare = PAIR_DEV + far_edge(above)
+    parts = [j if j < PAIR_DEV else j + jnp.where(above, 1, 0) for j in range(2 * PAIR_DEV - 1)]
+    return [(part, lax.rem((spare - part) * OWN + LANES, LANES)) for part in parts]
+
+
+def halo_parts():
+    return lax.rem(lax.broadcasted_iota(jnp.int32, (SUB, LANES), 1) // OWN, 2 * PAIR_DEV)
+
+
+def squeeze(cut, block, values):
+    above = place(cut)[1]
+    part = halo_parts()
+    single = jnp.where(block == 1, far_edge(above), -1)
+    values = [jnp.where(part == single, pltpu.roll(v, LANES - EDGE, axis=1), v) for v in values]
+    spare = part == PAIR_DEV + far_edge(above)
+    return [
+        jnp.where(spare, pltpu.roll(values[-1], shift, axis=1), v)
+        for v, (_, shift) in zip(values[:-1], pieces(above))
+    ]
+
+
+def unsqueeze(cut, values):
+    part = halo_parts()
+    last = values[0]
+    for v, (piece, shift) in zip(values, pieces(jnp.logical_not(place(cut)[1]))):
+        last = jnp.where(part == piece, pltpu.roll(v, lax.rem(LANES - shift, LANES), axis=1), last)
+    return list(values) + [last]
+
+
+def edge_kernel(cuts, got, couplings, k_sat, *refs):
+    halos, sent, load = refs[: CHUNKS * cuts], refs[CHUNKS * cuts : -1], refs[-1]
     cells = got.shape[-1]
     steps = halos[0].shape[1]
     stride = steps * GROUPS
@@ -233,6 +273,7 @@
         for cut in range(cuts):
             for f in range(3):
                 slot = (chunk * cuts + cut) * 3 + f
+                values = []
                 for j in range(steps):
                     v = jnp.where(
                         second,
@@ -245,6 +286,9 @@
                             k = jnp.where(v >= c, k_sat[c], k)
                         v = k
                     halos[chunk * cuts + cut][f, j] = v
+                    values.append(v)
+                for j, v in enumerate(squeeze(cut, needed_block(cut, couplings), values)):
+                    sent[chunk * cuts + cut][f, j] = v
 
 
 def first_kernel(
@@ -437,26 +481,35 @@
 
 
 def middle_kernel(cuts, *refs):
-    masks, head, warm, perm, conduct, wet, melt, cond, energy, top, water, heat = refs[:12]
-    own, far = refs[12 : 12 + cuts], refs[12 + cuts : 12 + 2 * cuts]
-    new_head, new_warm, new_wet, new_melt, new_cond = refs[12 + 2 * cuts : 17 + 2 * cuts]
-    halos = refs[17 + 2 * cuts : 17 + 3 * cuts]
-    inflow, warm_inflow, ratio, lead, value = refs[17 + 3 * cuts :]
+    masks, head, warm, perm, conduct, wet, melt, cond, energy, top, water, heat, couplings = refs[:13]
+    own, far = refs[13 : 13 + cuts], refs[13 + cuts : 13 + 2 * cuts]
+    new_head, new_warm, new_wet, new_melt, new_cond = refs[13 + 2 * cuts : 18 + 2 * cuts]
+    halos, sent = refs[18 + 2 * cuts : 18 + 3 * cuts], refs[18 + 3 * cuts : 18 + 4 * cuts]
+    inflow, warm_inflow, ratio, lead, value = refs[18 + 4 * cuts :]
+    steps = head.shape[0]
+    packed = {}
 
     def finish(j, t):
         s, f = new_wet[j], sigmoid(2.0 * t)
         new_melt[j] = f
         new_cond[j] = perm[j] * (f * s * s + 0.02)
         for cut in range(cuts):
-            halos[cut][0, j] = halo_of(cut, new_head[j])
-            halos[cut][1, j] = halo_of(cut, t)
-
+            for i, v in enumerate((new_head[j], t)):
+                packed[cut, i, j] = halo_of(cut, v)
+                halos[cut][i, j] = packed[cut, i, j]
+
+    theirs = [[unsqueeze(cut, [far[cut][i, j] for j in range(steps - 1)]) for i in range(3)] for cut in range(cuts)]
     advance(
-        head.shape[0], cuts, masks, head, warm, conduct, wet, energy, wet, melt, cond, water, heat, top,
+        steps, cuts, masks, head, warm, conduct, wet, energy, wet, melt, cond, water, heat, top,
         lambda cut, j: [own[cut][i, j] for i in range(3)],
-        lambda cut, j: [far[cut][i, j] for i in range(3)],
+        lambda cut, j: [theirs[cut][i][j] for i in range(3)],
         new_head, new_warm, new_wet, inflow, warm_inflow, ratio, lead, value, finish,
     )
+    for cut in range(cuts):
+        for i in range(2):
+            values = squeeze(cut, needed_block(cut, couplings), [packed[cut, i, j] for j in range(steps)])
+            for j, v in enumerate(values):
+                sent[cut][i, j] = v
 
 
 def last_kernel(chunk, cuts, *refs):
@@ -468,10 +521,14 @@
     steps = head.shape[0]
     cells = steps * GROUPS * SUB
     stride = steps * GROUPS
+    theirs = [
+        [unsqueeze(cut, [source[i, j] for j in range(steps - 1)]) for source, i in ((far[cut], 0), (far[cut], 1), (far_k[cut], 2))]
+        for cut in range(cuts)
+    ]
     advance(
         steps, cuts, masks, head, warm, conduct, stored, energy, wet, melt, cond, water, heat, top,
         lambda cut, j: [own[cut][0, j], own[cut][1, j], own_k[cut][2, j]],
-        lambda cut, j: [far[cut][0, j], far[cut][1, j], far_k[cut][2, j]],
+        lambda cut, j: [theirs[cut][i][j] for i in range(3)],
         new_head, new_warm, new_wet, inflow, warm_inflow, ratio, lead, value, lambda j, t: None,
     )
     final = chunk == CHUNKS - 1
@@ -530,6 +587,7 @@
     cuts = cut_count(n)
     column = (steps, SUB, ALL)
     halo = (steps, SUB, LANES)
+    squeezed = (steps - 1, SUB, LANES)
     room = pltpu.VMEM(column, F32)
     smem = whole(pltpu.SMEM)
     hbm = whole(pltpu.HBM)
@@ -555,10 +613,10 @@
     edges = call(
         functools.partial(edge_kernel, cuts),
         "edges",
-        (got, k_sat),
-        [(3,) + halo] * (CHUNKS * cuts),
+        (got, couplings, k_sat),
+        [(3,) + halo] * (CHUNKS * cuts) + [(3,) + squeezed] * (CHUNKS * cuts),
         scratch=[pltpu.VMEM((3 * CHUNKS * cuts, cells, LANES), F32)],
-        specs=[whole(), smem],
+        specs=[whole(), smem, smem],
     )
     first = [
         call(
@@ -573,8 +631,9 @@
     ]
     flows, sides = [], []
     for c in range(CHUNKS):
-        mine = tuple(edges[c * cuts : (c + 1) * cuts])
-        sides.append((mine, [swap(cut, n, v) for cut, v in enumerate(mine)]))
+        mine = edges[c * cuts : (c + 1) * cuts]
+        sent = edges[(CHUNKS + c) * cuts : (CHUNKS + c + 1) * cuts]
+        sides.append((mine, [swap(cut, n, v) for cut, v in enumerate(sent)]))
         flows.append(tuple(call(team_kernel, "team", (masks, first[c][0], first[c][1], first[c][6]), [column] * 2)))
 
     second, later = [], []
@@ -585,13 +644,14 @@
         values = call(
             functools.partial(middle_kernel, cuts),
             "middle",
-            (masks, head, warm, perm, conduct, wet, melt, cond, energy, surface, water, heat, *mine, *theirs),
-            [column] * 5 + [(2,) + halo] * cuts,
+            (masks, head, warm, perm, conduct, wet, melt, cond, energy, surface, water, heat, couplings, *mine, *theirs),
+            [column] * 5 + [(2,) + halo] * cuts + [(2,) + squeezed] * cuts,
             scratch=[room] * 5,
+            specs=[whole()] * 12 + [smem] + [whole()] * (2 * cuts),
         )
         second.append(values[:5])
-        mine = values[5:]
-        later.append((mine, [swap(cut, n, v) for cut, v in enumerate(mine)]))
+        mine, sent = values[5 : 5 + cuts], values[5 + cuts :]
+        later.append((mine, [swap(cut, n, v) for cut, v in enumerate(sent)]))
 
     done = []
     for c in range(CHUNKS):

time: 57.7 us -> 58.4 us (1.012)
  Pallas kernels: 14.2 us -> 15.9 us
  waiting for transfers between devices: 2.64 us -> 1.29 us
    pallas_call x14, Pallas kernels: 14.2 us -> 15.9 us  [call(): pl.pallas_call(kernel, out_shape=[jax.ShapeDtypeStruct(shape, F32) for sh...]
    ppermute x4, waiting for transfers between devices: 2.64 us -> 1.29 us  [swap(): return lax.ppermute(value, 'cols', pairs)]
  transfers between devices with their start and end apart: 4 -> 4, of which waited for: 2 -> 1; matrix products, arithmetic and copies ran while one was open for 0% -> 0% of each run, Pallas kernels for 18% -> 20%
where the time goes in v11:
time: 58.4 us; the launch traced here: 58.1 us
  blocking collectives  34.2 us (59%)
  Pallas kernels  15.9 us (27%)
  starting transfers between devices  6.04 us (10%)
  waiting for transfers between devices  1.29 us (2%)
  between operations  0.73 us (1%)
    all_to_all x2, blocking collectives, exchange(): lax.all_to_all(tiles, 'cols', split_axis=0, concat_axis=0, tiled=True, ax...  34.2 us
    pallas_call x14, Pallas kernels, call(): pl.pallas_call(kernel, out_shape=[jax.ShapeDtypeStruct(shape, F32) for sh...  15.9 us
    ppermute x4, starting transfers between devices, swap(): return lax.ppermute(value, 'cols', pairs)  6.04 us
    ppermute x4, waiting for transfers between devices, swap(): return lax.ppermute(value, 'cols', pairs)  1.29 us
  transfers between devices with their start and end apart: 4, of which 1 were waited for; matrix products, arithmetic and copies ran while one was open for 0% of the time, Pallas kernels for 20%

profile of v11, /device:TPU:0, one launch (start us, length us, event | category | flops | bytes accessed | tf_op | source)
XLA Modules:
  0.0 58.1 jit_solution(16361275767648855033)
XLA Ops:
  0.6 1.5 %pack.1 = f32[16,13,8,128]{3,2,1,0:T(8,128)S(1)} custom-call(f32[128,512]{1,0:T(8,128)} %suction.1, f32[128,512]{1,0:T(8,128)} %warmth.1, s32[128,512]{1,0:T(8,128)} %classes.1, f32[1,512]{1,0:T(1,128)} %bitcast.1), custom_call_target="tpu_custom_call" | custom-call | flops 2000000 | bytes 2000000 | tf_op jit(solution)/shard_map/pack/pallas_call | solution.py:555
  2.1 0.0 copy-start
  2.1 0.0 copy-start.1
  2.2 20.1 %all_to_all.10.got = f32[16,13,8,128]{3,2,1,0:T(8,128)S(1)} all-to-all(f32[16,13,8,128]{3,2,1,0:T(8,128)S(1)} %pack.1), channel_id=1, replica_groups={{0,1,2,3,4,5,6,7,8,9,10,11,12,13,14,15},{16,17,18,19,20,21,22,23,24,25,..., dimensions={0} | all-to-all | bytes 1703936 | tf_op jit(solution)/shard_map/all_to_all | solution.py:569
  22.3 0.0 copy-done
  22.3 0.0 copy-done.1
  22.3 0.9 %edges.1 = (f32[3,8,8,128]{3,2,1,0:T(8,128)S(1)}, f32[3,8,8,128]{3,2,1,0:T(8,128)S(1)}, f32[3,7,8,128]{3,2,1,0:T(8,128)S(1)}, f32[3,7,8,128]{3,2,1,0:T(8,128)S(1)}) custom-call(f32[16,13,8,128]{3,2,1,0:T(8,128)S(1)} %all_to_all.10.got, s32[2,128]{1,0:T(2,128)S(1)} %copy-done, f32[8]{0:T(128)S(1)} %copy-done.1), custom_call_target="tpu_custom_call" | custom-call | flops 2000000 | bytes 2000000 | tf_op jit(solution)/shard_map/edges/pallas_call | solution.py:555
  23.2 2.7 %collective-permute-start.2 = (f32[3,7,8,128]{3,2,1,0:T(8,128)S(1)}, f32[3,7,8,128]{3,2,1,0:T(8,128)S(1)}, u32[]{:S(2)}, u32[]{:S(2)}) collective-permute-start(f32[3,7,8,128]{3,2,1,0:T(8,128)S(1)} %get-tuple-element.80), channel_id=1, source_target_pairs={{0,16},{16,0},{1,17},{17,1},{2,18},{18,2},{3,19},{19,3},{4,20},{20... | collective-permute-start | bytes 258056 | tf_op jit(solution)/shard_map/ppermute | solution.py:579
  25.9 0.0 copy-start.2
  25.9 0.3 collective-permute-start
  26.2 0.3 masks.1.refs_0_
  26.5 0.1 copy-done.2
  26.6 0.9 %first.3 = (f32[8,8,512]{2,1,0:T(8,128)S(1)}, f32[8,8,512]{2,1,0:T(8,128)S(1)}, f32[8,8,512]{2,1,0:T(8,128)S(1)}, f32[8,8,512]{2,1,0:T(8,128)S(1)}, f32[8,8,512]...) custom-call(f32[16,13,8,128]{3,2,1,0:T(8,128)S(1)} %all_to_all.10.go, ...), custom_call_target="tpu_custom_call" | custom-call | flops 2000000 | bytes 2000000 | tf_op jit(solution)/shard_map/first/pallas_call | solution.py:555
  27.5 1.4 %team.6 = (f32[8,8,512]{2,1,0:T(8,128)S(1)}, f32[8,8,512]{2,1,0:T(8,128)S(1)}) custom-call(f32[21,8,128]{2,1,0:T(8,128)S(1)} %masks.1.refs_0_, f32[8,8,512]{2,1,0:T(8,128)S(1)} %get-tuple-element.68.head.refs_1_, f32[8,8,512]{2,1,0:T(8,128)S(1)} %get-tuple-element.69.warm.refs_2_, f32[8,8,512]{2,1,0:T(8,128)S(1)} %get-tuple-element.74.cond.refs_7_), custom_call_target="tpu_custom_call" | custom-call | flops 2000000 | bytes 2000000 | tf_op jit(solution)/shard_map/team/pallas_call | solution.py:555
  28.9 0.9 %first.2 = (f32[8,8,512]{2,1,0:T(8,128)S(1)}, f32[8,8,512]{2,1,0:T(8,128)S(1)}, f32[8,8,512]{2,1,0:T(8,128)S(1)}, f32[8,8,512]{2,1,0:T(8,128)S(1)}, f32[8,8,512]...) custom-call(f32[16,13,8,128]{3,2,1,0:T(8,128)S(1)} %all_to_all.10.go, ...), custom_call_target="tpu_custom_call" | custom-call | flops 2000000 | bytes 2000000 | tf_op jit(solution)/shard_map/first/pallas_call | solution.py:555
  29.8 1.4 %team.4 = (f32[8,8,512]{2,1,0:T(8,128)S(1)}, f32[8,8,512]{2,1,0:T(8,128)S(1)}) custom-call(f32[21,8,128]{2,1,0:T(8,128)S(1)} %masks.1.refs_0_, f32[8,8,512]{2,1,0:T(8,128)S(1)} %get-tuple-element.46.head.refs_1_, f32[8,8,512]{2,1,0:T(8,128)S(1)} %get-tuple-element.47.warm.refs_2_, f32[8,8,512]{2,1,0:T(8,128)S(1)} %get-tuple-element.52.cond.refs_7_), custom_call_target="tpu_custom_call" | custom-call | flops 2000000 | bytes 2000000 | tf_op jit(solution)/shard_map/team/pallas_call | solution.py:555
  31.2 1.3 %collective-permute-done.2.refs_14_.refs_15_ = f32[3,7,8,128]{3,2,1,0:T(8,128)S(1)} collective-permute-done((f32[3,7,8,128]{3,2,1,0:T(8,128)S(1)}, f32[3,7,8,128]{3,2,1,0:T(8,128)S(1)}, u32[]{:S(2)}, u32[]{:S(2)}) %collective-permute-start.2) | collective-permute-done | bytes 86048 | tf_op jit(solution)/shard_map/ppermute | solution.py:579
  32.4 1.5 %middle.3 = (f32[8,8,512]{2,1,0:T(8,128)S(1)}, f32[8,8,512]{2,1,0:T(8,128)S(1)}, f32[8,8,512]{2,1,0:T(8,128)S(1)}, f32[8,8,512]{2,1,0:T(8,128)S(1)}, f32[8,8,512...) custom-call(f32[21,8,128]{2,1,0:T(8,128)S(1)} %masks.1.refs_0_, ...), custom_call_target="tpu_custom_call" | custom-call | flops 2000000 | bytes 2000000 | tf_op jit(solution)/shard_map/middle/pallas_call | solution.py:555
  34.0 1.3 %collective-permute-start.3 = (f32[2,7,8,128]{3,2,1,0:T(8,128)S(1)}, f32[2,7,8,128]{3,2,1,0:T(8,128)S(1)}, u32[]{:S(2)}, u32[]{:S(2)}) collective-permute-start(f32[2,7,8,128]{3,2,1,0:T(8,128)S(1)} %get-tuple-element.89), channel_id=1, source_target_pairs={{0,16},{16,0},{1,17},{17,1},{2,18},{18,2},{3,19},{19,3},{4,20},{20... | collective-permute-start | bytes 172040 | tf_op jit(solution)/shard_map/ppermute | solution.py:579
  35.3 0.0 collective-permute-done.refs_14_.refs_15_
  35.3 1.5 %middle.2 = (f32[8,8,512]{2,1,0:T(8,128)S(1)}, f32[8,8,512]{2,1,0:T(8,128)S(1)}, f32[8,8,512]{2,1,0:T(8,128)S(1)}, f32[8,8,512]{2,1,0:T(8,128)S(1)}, f32[8,8,512...) custom-call(f32[21,8,128]{2,1,0:T(8,128)S(1)} %masks.1.refs_0_, ...), custom_call_target="tpu_custom_call" | custom-call | flops 2000000 | bytes 2000000 | tf_op jit(solution)/shard_map/middle/pallas_call | solution.py:555
  36.8 1.7 %collective-permute-start.1 = (f32[2,7,8,128]{3,2,1,0:T(8,128)S(1)}, f32[2,7,8,128]{3,2,1,0:T(8,128)S(1)}, u32[]{:S(2)}, u32[]{:S(2)}) collective-permute-start(f32[2,7,8,128]{3,2,1,0:T(8,128)S(1)} %get-tuple-element.67), channel_id=1, source_target_pairs={{0,16},{16,0},{1,17},{17,1},{2,18},{18,2},{3,19},{19,3},{4,20},{20... | collective-permute-start | bytes 172040 | tf_op jit(solution)/shard_map/ppermute | solution.py:579
  38.5 1.4 %team.7 = (f32[8,8,512]{2,1,0:T(8,128)S(1)}, f32[8,8,512]{2,1,0:T(8,128)S(1)}) custom-call(f32[21,8,128]{2,1,0:T(8,128)S(1)} %masks.1.refs_0_, f32[8,8,512]{2,1,0:T(8,128)S(1)} %get-tuple-element.81.head.refs_1_, f32[8,8,512]{2,1,0:T(8,128)S(1)} %get-tuple-element.82.warm.refs_2_, f32[8,8,512]{2,1,0:T(8,128)S(1)} %get-tuple-element.85.cond.refs_7_), custom_call_target="tpu_custom_call" | custom-call | flops 2000000 | bytes 2000000 | tf_op jit(solution)/shard_map/team/pallas_call | solution.py:555
  39.9 1.4 %team.5 = (f32[8,8,512]{2,1,0:T(8,128)S(1)}, f32[8,8,512]{2,1,0:T(8,128)S(1)}) custom-call(f32[21,8,128]{2,1,0:T(8,128)S(1)} %masks.1.refs_0_, f32[8,8,512]{2,1,0:T(8,128)S(1)} %get-tuple-element.59.head.refs_1_, f32[8,8,512]{2,1,0:T(8,128)S(1)} %get-tuple-element.60.warm.refs_2_, f32[8,8,512]{2,1,0:T(8,128)S(1)} %get-tuple-element.63.cond.refs_7_), custom_call_target="tpu_custom_call" | custom-call | flops 2000000 | bytes 2000000 | tf_op jit(solution)/shard_map/team/pallas_call | solution.py:555
  41.3 0.0 collective-permute-done.3.refs_13_
  41.3 0.9 %last.2.refs_16_ = f32[16,4,8,128]{3,2,1,0:T(8,128)S(1)} custom-call(f32[21,8,128]{2,1,0:T(8,128)S(1)} %masks.1.refs_0_, f32[8,8,512]{2,1,0:T(8,128)S(1)} %get-tuple-element.81.head.refs_1_, f32[8,8,512]{2,1,0:T(8,128)S(1)} %get-tuple-element.82.warm.refs_2_, f32[8,8,512]{2,1,0:T(8,128)S(1)} %get-tuple-element.71.refs_4_.refs_3_, ...), custom_call_target="tpu_custom_call" | custom-call | flops 2000000 | bytes 2000000 | tf_op jit(solution)/shard_map/last/pallas_call | solution.py:555
  42.2 0.0 collective-permute-done.1.refs_13_
  42.2 1.0 %last.3 = f32[16,8,8,128]{3,2,1,0:T(8,128)S(1)} custom-call(f32[21,8,128]{2,1,0:T(8,128)S(1)} %masks.1.refs_0_, f32[8,8,512]{2,1,0:T(8,128)S(1)} %get-tuple-element.59.head.refs_1_, f32[8,8,512]{2,1,0:T(8,128)S(1)} %get-tuple-element.60.warm.refs_2_, f32[8,8,512]{2,1,0:T(8,128)S(1)} %get-tuple-element.49.refs_4_.refs_3_, ...), custom_call_target="tpu_custom_call" | custom-call | flops 2000000 | bytes 2000000 | tf_op jit(solution)/shard_map/last/pallas_call | solution.py:555
  43.2 14.0 %all_to_all.11.got = f32[16,8,8,128]{3,2,1,0:T(8,128)S(1)} all-to-all(f32[16,8,8,128]{3,2,1,0:T(8,128)S(1)} %last.3), channel_id=1, replica_groups={{0,1,2,3,4,5,6,7,8,9,10,11,12,13,14,15},{16,17,18,19,20,21,22,23,24,25,..., dimensions={0} | all-to-all | bytes 1048576 | tf_op jit(solution)/shard_map/all_to_all | solution.py:569
  57.2 0.9 %unpack.1 = (f32[128,512]{1,0:T(8,128)}, f32[128,512]{1,0:T(8,128)}) custom-call(f32[16,8,8,128]{3,2,1,0:T(8,128)S(1)} %all_to_all.11.got), custom_call_target="tpu_custom_call" | custom-call | flops 2000000 | bytes 2000000 | tf_op jit(solution)/shard_map/unpack/pallas_call | solution.py:555
Async XLA Ops:
  2.1 20.2 %copy-start = (s32[2,128]{1,0:T(2,128)S(1)}, s32[2,128]{1,0:T(2,128)}, u32[]{:S(2)}) copy-start(s32[2,128]{1,0:T(2,128)} %refs_12_.3) | copy-start | bytes 3076
  2.1 20.2 %copy-start.1 = (f32[8]{0:T(128)S(1)}, f32[8]{0:T(128)}, u32[]{:S(2)}) copy-start(f32[8]{0:T(128)} %k_sat.5) | copy-start | bytes 100
  23.2 9.2 %collective-permute-start.2 = (f32[3,7,8,128]{3,2,1,0:T(8,128)S(1)}, f32[3,7,8,128]{3,2,1,0:T(8,128)S(1)}, u32[]{:S(2)}, u32[]{:S(2)}) collective-permute-start(f32[3,7,8,128]{3,2,1,0:T(8,128)S(1)} %get-tuple-element.80), channel_id=1, source_target_pairs={{0,16},{16,0},{1,17},{17,1},{2,18},{18,2},{3,19},{19,3},{4,20},{20... | collective-permute-start | bytes 258056 | tf_op jit(solution)/shard_map/ppermute | solution.py:579
  25.9 0.7 %copy-start.2 = (f32[8]{0:T(128)S(1)}, f32[8]{0:T(128)}, u32[]{:S(2)}) copy-start(f32[8]{0:T(128)} %heat_cond.3) | copy-start | bytes 100
  25.9 9.4 %collective-permute-start = (f32[3,7,8,128]{3,2,1,0:T(8,128)S(1)}, f32[3,7,8,128]{3,2,1,0:T(8,128)S(1)}, u32[]{:S(2)}, u32[]{:S(2)}) collective-permute-start(f32[3,7,8,128]{3,2,1,0:T(8,128)S(1)} %get-tuple-element.58), channel_id=1, source_target_pairs={{0,16},{16,0},{1,17},{17,1},{2,18},{18,2},{3,19},{19,3},{4,20},{20... | collective-permute-start | bytes 258056 | tf_op jit(solution)/shard_map/ppermute | solution.py:579
  34.0 7.3 %collective-permute-start.3 = (f32[2,7,8,128]{3,2,1,0:T(8,128)S(1)}, f32[2,7,8,128]{3,2,1,0:T(8,128)S(1)}, u32[]{:S(2)}, u32[]{:S(2)}) collective-permute-start(f32[2,7,8,128]{3,2,1,0:T(8,128)S(1)} %get-tuple-element.89), channel_id=1, source_target_pairs={{0,16},{16,0},{1,17},{17,1},{2,18},{18,2},{3,19},{19,3},{4,20},{20... | collective-permute-start | bytes 172040 | tf_op jit(solution)/shard_map/ppermute | solution.py:579
  36.8 5.4 %collective-permute-start.1 = (f32[2,7,8,128]{3,2,1,0:T(8,128)S(1)}, f32[2,7,8,128]{3,2,1,0:T(8,128)S(1)}, u32[]{:S(2)}, u32[]{:S(2)}) collective-permute-start(f32[2,7,8,128]{3,2,1,0:T(8,128)S(1)} %get-tuple-element.67), channel_id=1, source_target_pairs={{0,16},{16,0},{1,17},{17,1},{2,18},{18,2},{3,19},{19,3},{4,20},{20... | collective-permute-start | bytes 172040 | tf_op jit(solution)/shard_map/ppermute | solution.py:579

commit v12 on v11

--- a/solution.py
+++ b/solution.py
@@ -41,8 +41,7 @@
 
 
 def reciprocal(x):
-    r = pl.reciprocal(x, approx=True)
-    return r * (2.0 - x * r)
+    return pltpu.reciprocal(x, approx=True)
 
 
 def sigmoid(x):
@@ -117,11 +116,11 @@
 
 
 def mask_rows(cuts):
-    return 3 * PAIR_DEV + cuts * (2 * PAIR_DEV + 1)
+    return 3 * PAIR_DEV + cuts * (2 * PAIR_DEV + 2)
 
 
 def cut_row(cut):
-    return 3 * PAIR_DEV + cut * (2 * PAIR_DEV + 1)
+    return 3 * PAIR_DEV + cut * (2 * PAIR_DEV + 2)
 
 
 def mask_kernel(n, couplings, out):
@@ -167,6 +166,8 @@
             put(row + PAIR_DEV + s - 1, jnp.where(jnp.abs(theirs - block.astype(F32)) < 0.5, 1.0, 0.0))
         outward = jnp.where(above, LANES - 1 - lane_1, lane_1)
         put(row + 2 * PAIR_DEV, jnp.where(outward < EDGE, 1.0, 0.0))
+        single = jnp.logical_and(edge_1 == far_edge(above), block == 0)
+        put(row + 2 * PAIR_DEV + 1, jnp.where(single, mine, 0.0))
 
 
 def pack_kernel(suction, warmth, classes, surface, out, room, class_room, top, in_sems):
@@ -233,12 +234,10 @@
     return lax.rem(lax.broadcasted_iota(jnp.int32, (SUB, LANES), 1) // OWN, 2 * PAIR_DEV)
 
 
-def squeeze(cut, block, values):
+def squeeze(cut, other, values):
     above = place(cut)[1]
-    part = halo_parts()
-    single = jnp.where(block == 1, far_edge(above), -1)
-    values = [jnp.where(part == single, pltpu.roll(v, LANES - EDGE, axis=1), v) for v in values]
-    spare = part == PAIR_DEV + far_edge(above)
+    values = [jnp.where(other, pltpu.roll(v, LANES - EDGE, axis=1), v) for v in values]
+    spare = halo_parts() == PAIR_DEV + far_edge(above)
     return [
         jnp.where(spare, pltpu.roll(values[-1], shift, axis=1), v)
         for v, (_, shift) in zip(values[:-1], pieces(above))
@@ -287,7 +286,8 @@
                         v = k
                     halos[chunk * cuts + cut][f, j] = v
                     values.append(v)
-                for j, v in enumerate(squeeze(cut, needed_block(cut, couplings), values)):
+                single = jnp.where(needed_block(cut, couplings) == 1, far_edge(place(cut)[1]), -1)
+                for j, v in enumerate(squeeze(cut, halo_parts() == single, values)):
                     sent[chunk * cuts + cut][f, j] = v
 
 
@@ -481,11 +481,11 @@
 
 
 def middle_kernel(cuts, *refs):
-    masks, head, warm, perm, conduct, wet, melt, cond, energy, top, water, heat, couplings = refs[:13]
-    own, far = refs[13 : 13 + cuts], refs[13 + cuts : 13 + 2 * cuts]
-    new_head, new_warm, new_wet, new_melt, new_cond = refs[13 + 2 * cuts : 18 + 2 * cuts]
-    halos, sent = refs[18 + 2 * cuts : 18 + 3 * cuts], refs[18 + 3 * cuts : 18 + 4 * cuts]
-    inflow, warm_inflow, ratio, lead, value = refs[18 + 4 * cuts :]
+    masks, head, warm, perm, conduct, wet, melt, cond, energy, top, water, heat = refs[:12]
+    own, far = refs[12 : 12 + cuts], refs[12 + cuts : 12 + 2 * cuts]
+    new_head, new_warm, new_wet, new_melt, new_cond = refs[12 + 2 * cuts : 17 + 2 * cuts]
+    halos, sent = refs[17 + 2 * cuts : 17 + 3 * cuts], refs[17 + 3 * cuts : 17 + 4 * cuts]
+    inflow, warm_inflow, ratio, lead, value = refs[17 + 4 * cuts :]
     steps = head.shape[0]
     packed = {}
 
@@ -507,7 +507,8 @@
     )
     for cut in range(cuts):
         for i in range(2):
-            values = squeeze(cut, needed_block(cut, couplings), [packed[cut, i, j] for j in range(steps)])
+            other = masks[cut_row(cut) + 2 * PAIR_DEV + 1] > 0.5
+            values = squeeze(cut, other, [packed[cut, i, j] for j in range(steps)])
             for j, v in enumerate(values):
                 sent[cut][i, j] = v
 
@@ -644,10 +645,9 @@
         values = call(
             functools.partial(middle_kernel, cuts),
             "middle",
-            (masks, head, warm, perm, conduct, wet, melt, cond, energy, surface, water, heat, couplings, *mine, *theirs),
+            (masks, head, warm, perm, conduct, wet, melt, cond, energy, surface, water, heat, *mine, *theirs),
             [column] * 5 + [(2,) + halo] * cuts + [(2,) + squeezed] * cuts,
             scratch=[room] * 5,
-            specs=[whole()] * 12 + [smem] + [whole()] * (2 * cuts),
         )
         second.append(values[:5])
         mine, sent = values[5 : 5 + cuts], values[5 + cuts :]

time: 58.4 us -> 57.2 us (0.979)
  Pallas kernels: 15.9 us -> 14.7 us
    pallas_call x14, Pallas kernels: 15.9 us -> 14.7 us  [call(): pl.pallas_call(kernel, out_shape=[jax.ShapeDtypeStruct(shape, F32) for sh...]
  transfers between devices with their start and end apart: 4 -> 4, of which waited for: 1 -> 2; matrix products, arithmetic and copies ran while one was open for 0% -> 0% of each run, Pallas kernels for 20% -> 18%
where the time goes in v12:
time: 57.2 us; the launch traced here: 57 us
  blocking collectives  34.1 us (60%)
  Pallas kernels  14.7 us (26%)
  starting transfers between devices  6.02 us (11%)
  waiting for transfers between devices  1.37 us (2%)
  between operations  0.73 us (1%)
    all_to_all x2, blocking collectives, exchange(): lax.all_to_all(tiles, 'cols', split_axis=0, concat_axis=0, tiled=True, ax...  34.1 us
    pallas_call x14, Pallas kernels, call(): pl.pallas_call(kernel, out_shape=[jax.ShapeDtypeStruct(shape, F32) for sh...  14.7 us
    ppermute x4, starting transfers between devices, swap(): return lax.ppermute(value, 'cols', pairs)  6.02 us
    ppermute x4, waiting for transfers between devices, swap(): return lax.ppermute(value, 'cols', pairs)  1.37 us
  transfers between devices with their start and end apart: 4, of which 2 were waited for; matrix products, arithmetic and copies ran while one was open for 0% of the time, Pallas kernels for 18%

profile of v12, /device:TPU:0, one launch (start us, length us, event | category | flops | bytes accessed | tf_op | source)
XLA Modules:
  0.0 57.0 jit_solution(11704784814203233313)
XLA Ops:
  0.6 1.5 %pack.1 = f32[16,13,8,128]{3,2,1,0:T(8,128)S(1)} custom-call(f32[128,512]{1,0:T(8,128)} %suction.1, f32[128,512]{1,0:T(8,128)} %warmth.1, s32[128,512]{1,0:T(8,128)} %classes.1, f32[1,512]{1,0:T(1,128)} %bitcast.1), custom_call_target="tpu_custom_call" | custom-call | flops 2000000 | bytes 2000000 | tf_op jit(solution)/shard_map/pack/pallas_call | solution.py:556
  2.1 0.0 copy-start
  2.1 0.0 copy-start.1
  2.2 20.1 %all_to_all.10.got = f32[16,13,8,128]{3,2,1,0:T(8,128)S(1)} all-to-all(f32[16,13,8,128]{3,2,1,0:T(8,128)S(1)} %pack.1), channel_id=1, replica_groups={{0,1,2,3,4,5,6,7,8,9,10,11,12,13,14,15},{16,17,18,19,20,21,22,23,24,25,..., dimensions={0} | all-to-all | bytes 1703936 | tf_op jit(solution)/shard_map/all_to_all | solution.py:570
  22.3 0.0 copy-done
  22.3 0.0 copy-done.1
  22.3 0.9 %edges.1 = (f32[3,8,8,128]{3,2,1,0:T(8,128)S(1)}, f32[3,8,8,128]{3,2,1,0:T(8,128)S(1)}, f32[3,7,8,128]{3,2,1,0:T(8,128)S(1)}, f32[3,7,8,128]{3,2,1,0:T(8,128)S(1)}) custom-call(f32[16,13,8,128]{3,2,1,0:T(8,128)S(1)} %all_to_all.10.got, s32[2,128]{1,0:T(2,128)S(1)} %copy-done.1, f32[8]{0:T(128)S(1)} %copy-done), custom_call_target="tpu_custom_call" | custom-call | flops 2000000 | bytes 2000000 | tf_op jit(solution)/shard_map/edges/pallas_call | solution.py:556
  23.2 2.7 %collective-permute-start.2 = (f32[3,7,8,128]{3,2,1,0:T(8,128)S(1)}, f32[3,7,8,128]{3,2,1,0:T(8,128)S(1)}, u32[]{:S(2)}, u32[]{:S(2)}) collective-permute-start(f32[3,7,8,128]{3,2,1,0:T(8,128)S(1)} %get-tuple-element.80), channel_id=1, source_target_pairs={{0,16},{16,0},{1,17},{17,1},{2,18},{18,2},{3,19},{19,3},{4,20},{20... | collective-permute-start | bytes 258056 | tf_op jit(solution)/shard_map/ppermute | solution.py:580
  25.9 0.0 copy-start.2
  25.9 0.3 collective-permute-start
  26.2 0.3 masks.1.refs_0_
  26.5 0.1 copy-done.2
  26.6 0.9 %first.3 = (f32[8,8,512]{2,1,0:T(8,128)S(1)}, f32[8,8,512]{2,1,0:T(8,128)S(1)}, f32[8,8,512]{2,1,0:T(8,128)S(1)}, f32[8,8,512]{2,1,0:T(8,128)S(1)}, f32[8,8,512]...) custom-call(f32[16,13,8,128]{3,2,1,0:T(8,128)S(1)} %all_to_all.10.go, ...), custom_call_target="tpu_custom_call" | custom-call | flops 2000000 | bytes 2000000 | tf_op jit(solution)/shard_map/first/pallas_call | solution.py:556
  27.5 1.4 %team.6 = (f32[8,8,512]{2,1,0:T(8,128)S(1)}, f32[8,8,512]{2,1,0:T(8,128)S(1)}) custom-call(f32[22,8,128]{2,1,0:T(8,128)S(1)} %masks.1.refs_0_, f32[8,8,512]{2,1,0:T(8,128)S(1)} %get-tuple-element.68.head.refs_1_, f32[8,8,512]{2,1,0:T(8,128)S(1)} %get-tuple-element.69.warm.refs_2_, f32[8,8,512]{2,1,0:T(8,128)S(1)} %get-tuple-element.74.cond.refs_7_), custom_call_target="tpu_custom_call" | custom-call | flops 2000000 | bytes 2000000 | tf_op jit(solution)/shard_map/team/pallas_call | solution.py:556
  28.9 0.9 %first.2 = (f32[8,8,512]{2,1,0:T(8,128)S(1)}, f32[8,8,512]{2,1,0:T(8,128)S(1)}, f32[8,8,512]{2,1,0:T(8,128)S(1)}, f32[8,8,512]{2,1,0:T(8,128)S(1)}, f32[8,8,512]...) custom-call(f32[16,13,8,128]{3,2,1,0:T(8,128)S(1)} %all_to_all.10.go, ...), custom_call_target="tpu_custom_call" | custom-call | flops 2000000 | bytes 2000000 | tf_op jit(solution)/shard_map/first/pallas_call | solution.py:556
  29.8 1.4 %team.4 = (f32[8,8,512]{2,1,0:T(8,128)S(1)}, f32[8,8,512]{2,1,0:T(8,128)S(1)}) custom-call(f32[22,8,128]{2,1,0:T(8,128)S(1)} %masks.1.refs_0_, f32[8,8,512]{2,1,0:T(8,128)S(1)} %get-tuple-element.46.head.refs_1_, f32[8,8,512]{2,1,0:T(8,128)S(1)} %get-tuple-element.47.warm.refs_2_, f32[8,8,512]{2,1,0:T(8,128)S(1)} %get-tuple-element.52.cond.refs_7_), custom_call_target="tpu_custom_call" | custom-call | flops 2000000 | bytes 2000000 | tf_op jit(solution)/shard_map/team/pallas_call | solution.py:556
  31.2 1.3 %collective-permute-done.2.refs_13_.refs_15_ = f32[3,7,8,128]{3,2,1,0:T(8,128)S(1)} collective-permute-done((f32[3,7,8,128]{3,2,1,0:T(8,128)S(1)}, f32[3,7,8,128]{3,2,1,0:T(8,128)S(1)}, u32[]{:S(2)}, u32[]{:S(2)}) %collective-permute-start.2) | collective-permute-done | bytes 86048 | tf_op jit(solution)/shard_map/ppermute | solution.py:580
  32.4 1.0 %middle.3 = (f32[8,8,512]{2,1,0:T(8,128)S(1)}, f32[8,8,512]{2,1,0:T(8,128)S(1)}, f32[8,8,512]{2,1,0:T(8,128)S(1)}, f32[8,8,512]{2,1,0:T(8,128)S(1)}, f32[8,8,512...) custom-call(f32[22,8,128]{2,1,0:T(8,128)S(1)} %masks.1.refs_0_, ...), custom_call_target="tpu_custom_call" | custom-call | flops 2000000 | bytes 2000000 | tf_op jit(solution)/shard_map/middle/pallas_call | solution.py:556
  33.4 1.3 %collective-permute-start.3 = (f32[2,7,8,128]{3,2,1,0:T(8,128)S(1)}, f32[2,7,8,128]{3,2,1,0:T(8,128)S(1)}, u32[]{:S(2)}, u32[]{:S(2)}) collective-permute-start(f32[2,7,8,128]{3,2,1,0:T(8,128)S(1)} %get-tuple-element.89), channel_id=1, source_target_pairs={{0,16},{16,0},{1,17},{17,1},{2,18},{18,2},{3,19},{19,3},{4,20},{20... | collective-permute-start | bytes 172040 | tf_op jit(solution)/shard_map/ppermute | solution.py:580
  34.8 0.0 collective-permute-done.refs_13_.refs_15_
  34.8 1.0 %middle.2 = (f32[8,8,512]{2,1,0:T(8,128)S(1)}, f32[8,8,512]{2,1,0:T(8,128)S(1)}, f32[8,8,512]{2,1,0:T(8,128)S(1)}, f32[8,8,512]{2,1,0:T(8,128)S(1)}, f32[8,8,512...) custom-call(f32[22,8,128]{2,1,0:T(8,128)S(1)} %masks.1.refs_0_, ...), custom_call_target="tpu_custom_call" | custom-call | flops 2000000 | bytes 2000000 | tf_op jit(solution)/shard_map/middle/pallas_call | solution.py:556
  35.7 1.7 %collective-permute-start.1 = (f32[2,7,8,128]{3,2,1,0:T(8,128)S(1)}, f32[2,7,8,128]{3,2,1,0:T(8,128)S(1)}, u32[]{:S(2)}, u32[]{:S(2)}) collective-permute-start(f32[2,7,8,128]{3,2,1,0:T(8,128)S(1)} %get-tuple-element.67), channel_id=1, source_target_pairs={{0,16},{16,0},{1,17},{17,1},{2,18},{18,2},{3,19},{19,3},{4,20},{20... | collective-permute-start | bytes 172040 | tf_op jit(solution)/shard_map/ppermute | solution.py:580
  37.4 1.4 %team.7 = (f32[8,8,512]{2,1,0:T(8,128)S(1)}, f32[8,8,512]{2,1,0:T(8,128)S(1)}) custom-call(f32[22,8,128]{2,1,0:T(8,128)S(1)} %masks.1.refs_0_, f32[8,8,512]{2,1,0:T(8,128)S(1)} %get-tuple-element.81.head.refs_1_, f32[8,8,512]{2,1,0:T(8,128)S(1)} %get-tuple-element.82.warm.refs_2_, f32[8,8,512]{2,1,0:T(8,128)S(1)} %get-tuple-element.85.cond.refs_7_), custom_call_target="tpu_custom_call" | custom-call | flops 2000000 | bytes 2000000 | tf_op jit(solution)/shard_map/team/pallas_call | solution.py:556
  38.8 1.4 %team.5 = (f32[8,8,512]{2,1,0:T(8,128)S(1)}, f32[8,8,512]{2,1,0:T(8,128)S(1)}) custom-call(f32[22,8,128]{2,1,0:T(8,128)S(1)} %masks.1.refs_0_, f32[8,8,512]{2,1,0:T(8,128)S(1)} %get-tuple-element.59.head.refs_1_, f32[8,8,512]{2,1,0:T(8,128)S(1)} %get-tuple-element.60.warm.refs_2_, f32[8,8,512]{2,1,0:T(8,128)S(1)} %get-tuple-element.63.cond.refs_7_), custom_call_target="tpu_custom_call" | custom-call | flops 2000000 | bytes 2000000 | tf_op jit(solution)/shard_map/team/pallas_call | solution.py:556
  40.2 0.1 collective-permute-done.3.refs_13_
  40.2 0.9 %last.2.refs_16_ = f32[16,4,8,128]{3,2,1,0:T(8,128)S(1)} custom-call(f32[22,8,128]{2,1,0:T(8,128)S(1)} %masks.1.refs_0_, f32[8,8,512]{2,1,0:T(8,128)S(1)} %get-tuple-element.81.head.refs_1_, f32[8,8,512]{2,1,0:T(8,128)S(1)} %get-tuple-element.82.warm.refs_2_, f32[8,8,512]{2,1,0:T(8,128)S(1)} %get-tuple-element.71.refs_4_.refs_3_, ...), custom_call_target="tpu_custom_call" | custom-call | flops 2000000 | bytes 2000000 | tf_op jit(solution)/shard_map/last/pallas_call | solution.py:556
  41.2 0.0 collective-permute-done.1.refs_13_
  41.2 0.9 %last.3 = f32[16,8,8,128]{3,2,1,0:T(8,128)S(1)} custom-call(f32[22,8,128]{2,1,0:T(8,128)S(1)} %masks.1.refs_0_, f32[8,8,512]{2,1,0:T(8,128)S(1)} %get-tuple-element.59.head.refs_1_, f32[8,8,512]{2,1,0:T(8,128)S(1)} %get-tuple-element.60.warm.refs_2_, f32[8,8,512]{2,1,0:T(8,128)S(1)} %get-tuple-element.49.refs_4_.refs_3_, ...), custom_call_target="tpu_custom_call" | custom-call | flops 2000000 | bytes 2000000 | tf_op jit(solution)/shard_map/last/pallas_call | solution.py:556
  42.1 14.0 %all_to_all.11.got = f32[16,8,8,128]{3,2,1,0:T(8,128)S(1)} all-to-all(f32[16,8,8,128]{3,2,1,0:T(8,128)S(1)} %last.3), channel_id=1, replica_groups={{0,1,2,3,4,5,6,7,8,9,10,11,12,13,14,15},{16,17,18,19,20,21,22,23,24,25,..., dimensions={0} | all-to-all | bytes 1048576 | tf_op jit(solution)/shard_map/all_to_all | solution.py:570
  56.1 0.9 %unpack.1 = (f32[128,512]{1,0:T(8,128)}, f32[128,512]{1,0:T(8,128)}) custom-call(f32[16,8,8,128]{3,2,1,0:T(8,128)S(1)} %all_to_all.11.got), custom_call_target="tpu_custom_call" | custom-call | flops 2000000 | bytes 2000000 | tf_op jit(solution)/shard_map/unpack/pallas_call | solution.py:556
Async XLA Ops:
  2.1 20.2 %copy-start = (f32[8]{0:T(128)S(1)}, f32[8]{0:T(128)}, u32[]{:S(2)}) copy-start(f32[8]{0:T(128)} %k_sat.5) | copy-start | bytes 100
  2.1 20.2 %copy-start.1 = (s32[2,128]{1,0:T(2,128)S(1)}, s32[2,128]{1,0:T(2,128)}, u32[]{:S(2)}) copy-start(s32[2,128]{1,0:T(2,128)} %couplings.3) | copy-start | bytes 3076
  23.2 9.2 %collective-permute-start.2 = (f32[3,7,8,128]{3,2,1,0:T(8,128)S(1)}, f32[3,7,8,128]{3,2,1,0:T(8,128)S(1)}, u32[]{:S(2)}, u32[]{:S(2)}) collective-permute-start(f32[3,7,8,128]{3,2,1,0:T(8,128)S(1)} %get-tuple-element.80), channel_id=1, source_target_pairs={{0,16},{16,0},{1,17},{17,1},{2,18},{18,2},{3,19},{19,3},{4,20},{20... | collective-permute-start | bytes 258056 | tf_op jit(solution)/shard_map/ppermute | solution.py:580
  25.9 0.7 %copy-start.2 = (f32[8]{0:T(128)S(1)}, f32[8]{0:T(128)}, u32[]{:S(2)}) copy-start(f32[8]{0:T(128)} %heat_cond.3) | copy-start | bytes 100
  25.9 8.9 %collective-permute-start = (f32[3,7,8,128]{3,2,1,0:T(8,128)S(1)}, f32[3,7,8,128]{3,2,1,0:T(8,128)S(1)}, u32[]{:S(2)}, u32[]{:S(2)}) collective-permute-start(f32[3,7,8,128]{3,2,1,0:T(8,128)S(1)} %get-tuple-element.58), channel_id=1, source_target_pairs={{0,16},{16,0},{1,17},{17,1},{2,18},{18,2},{3,19},{19,3},{4,20},{20... | collective-permute-start | bytes 258056 | tf_op jit(solution)/shard_map/ppermute | solution.py:580
  33.4 6.8 %collective-permute-start.3 = (f32[2,7,8,128]{3,2,1,0:T(8,128)S(1)}, f32[2,7,8,128]{3,2,1,0:T(8,128)S(1)}, u32[]{:S(2)}, u32[]{:S(2)}) collective-permute-start(f32[2,7,8,128]{3,2,1,0:T(8,128)S(1)} %get-tuple-element.89), channel_id=1, source_target_pairs={{0,16},{16,0},{1,17},{17,1},{2,18},{18,2},{3,19},{19,3},{4,20},{20... | collective-permute-start | bytes 172040 | tf_op jit(solution)/shard_map/ppermute | solution.py:580
  35.7 5.4 %collective-permute-start.1 = (f32[2,7,8,128]{3,2,1,0:T(8,128)S(1)}, f32[2,7,8,128]{3,2,1,0:T(8,128)S(1)}, u32[]{:S(2)}, u32[]{:S(2)}) collective-permute-start(f32[2,7,8,128]{3,2,1,0:T(8,128)S(1)} %get-tuple-element.67), channel_id=1, source_target_pairs={{0,16},{16,0},{1,17},{17,1},{2,18},{18,2},{3,19},{19,3},{4,20},{20... | collective-permute-start | bytes 172040 | tf_op jit(solution)/shard_map/ppermute | solution.py:580

commit v13 on v12

--- a/solution.py
+++ b/solution.py
@@ -170,13 +170,32 @@
         put(row + 2 * PAIR_DEV + 1, jnp.where(single, mine, 0.0))
 
 
-def pack_kernel(suction, warmth, classes, surface, out, room, class_room, top, in_sems):
+def halo_parts():
+    return lax.rem(lax.broadcasted_iota(jnp.int32, (SUB, LANES), 1) // OWN, 2 * PAIR_DEV)
+
+
+def other_block(cut, couplings):
+    team, above = place(cut)
+    pair = (team * TEAM + jnp.where(above, TEAM - PAIR_DEV, -1)) * PAIR_DEV + PAIR_DEV - 1
+    row = jnp.where(above, 0, 1)
+    table = couplings[...].astype(F32)
+    wanted = jnp.logical_and(
+        lax.broadcasted_iota(jnp.int32, table.shape, 0) == row, lax.broadcasted_iota(jnp.int32, table.shape, 1) == pair
+    )
+    block = jnp.sum(jnp.sum(jnp.where(wanted, table, 0.0), axis=1, keepdims=True), axis=0, keepdims=True)
+    single = jnp.where(halo_parts() == far_edge(above), 1.0, 0.0)
+    return single * jnp.broadcast_to(block, (SUB, LANES))
+
+
+def pack_kernel(
+    cuts, suction, warmth, classes, surface, couplings, k_sat, out, consts, room, class_room, top, pairs, table, in_sems
+):
     cells = out.shape[-1]
     quarters = 2 * CHUNKS
     into = []
-    for f, field in enumerate((suction, warmth, classes, surface)):
-        target = (room.at[0], room.at[1], class_room, top)[f]
-        into.append(pltpu.make_async_copy(field, target, in_sems.at[f]))
+    rooms = (room.at[0], room.at[1], class_room, top, pairs, table)
+    for f, field in enumerate((suction, warmth, classes, surface, couplings, k_sat)):
+        into.append(pltpu.make_async_copy(field, rooms[f], in_sems.at[f]))
         into[-1].start()
 
     def put(slot, value):
@@ -187,7 +206,12 @@
         for q in range(quarters):
             lanes = slice(q * LANES, (q + 1) * LANES)
             put(f * quarters + q, class_room[:, lanes].astype(F32) if f == 2 else room[f, :, lanes])
-    into[3].wait()
+    for copy in into[3:]:
+        copy.wait()
+    for c in range(k_sat.shape[1]):
+        consts[c] = jnp.broadcast_to(table[0:1, c : c + 1], (SUB, LANES))
+    for cut in range(cuts):
+        consts[k_sat.shape[1] + cut] = other_block(cut, pairs)
     rows = [top[0:1, q * LANES : (q + 1) * LANES] for q in range(quarters)]
     put(3 * quarters, jnp.concatenate(rows + [jnp.zeros((cells - quarters, LANES), F32)], axis=0))
 
@@ -218,20 +242,10 @@
     return packed
 
 
-def needed_block(cut, couplings):
-    team, above = place(cut)
-    pair = (team * TEAM + jnp.where(above, TEAM - PAIR_DEV, -1)) * PAIR_DEV + PAIR_DEV - 1
-    return couplings[jnp.where(above, 0, 1), jnp.maximum(pair, 0)]
-
-
 def pieces(above):
     spare = PAIR_DEV + far_edge(above)
     parts = [j if j < PAIR_DEV else j + jnp.where(above, 1, 0) for j in range(2 * PAIR_DEV - 1)]
     return [(part, lax.rem((spare - part) * OWN + LANES, LANES)) for part in parts]
-
-
-def halo_parts():
-    return lax.rem(lax.broadcasted_iota(jnp.int32, (SUB, LANES), 1) // OWN, 2 * PAIR_DEV)
 
 
 def squeeze(cut, other, values):
@@ -252,43 +266,40 @@
     return list(values) + [last]
 
 
-def edge_kernel(cuts, got, couplings, k_sat, *refs):
-    halos, sent, load = refs[: CHUNKS * cuts], refs[CHUNKS * cuts : -1], refs[-1]
+def edge_kernel(chunk, cuts, got, consts, *refs):
+    halos, sent, load = refs[:cuts], refs[cuts:-1], refs[-1]
     cells = got.shape[-1]
     steps = halos[0].shape[1]
     stride = steps * GROUPS
     second = lax.broadcasted_iota(jnp.int32, (SUB, LANES), 1) >= 2 * EDGE
-    for chunk in range(CHUNKS):
-        for cut in range(cuts):
-            start = jnp.where(place(cut)[1], TEAM - PAIR_DEV, 0)
-            for f in range(3):
-                rows = [
-                    got[pl.ds(start, PAIR_DEV), (f * 2 + b) * CHUNKS + chunk].reshape(EDGE, cells)
-                    for b in range(2)
-                ]
-                slot = (chunk * cuts + cut) * 3 + f
-                load[slot] = jnp.concatenate(rows * GROUPS, axis=0).T
-    for chunk in range(CHUNKS):
-        for cut in range(cuts):
-            for f in range(3):
-                slot = (chunk * cuts + cut) * 3 + f
-                values = []
-                for j in range(steps):
-                    v = jnp.where(
-                        second,
-                        load[slot, pl.ds(steps + j, SUB, stride=stride), :],
-                        load[slot, pl.ds(j, SUB, stride=stride), :],
-                    )
-                    if f == 2:
-                        k = jnp.full_like(v, k_sat[0])
-                        for c in range(1, k_sat.shape[0]):
-                            k = jnp.where(v >= c, k_sat[c], k)
-                        v = k
-                    halos[chunk * cuts + cut][f, j] = v
-                    values.append(v)
-                single = jnp.where(needed_block(cut, couplings) == 1, far_edge(place(cut)[1]), -1)
-                for j, v in enumerate(squeeze(cut, halo_parts() == single, values)):
-                    sent[chunk * cuts + cut][f, j] = v
+    for cut in range(cuts):
+        start = jnp.where(place(cut)[1], TEAM - PAIR_DEV, 0)
+        for f in range(3):
+            rows = [
+                got[pl.ds(start, PAIR_DEV), (f * 2 + b) * CHUNKS + chunk].reshape(EDGE, cells) for b in range(2)
+            ]
+            load[cut * 3 + f] = jnp.concatenate(rows * GROUPS, axis=0).T
+    classes = consts.shape[0] - cuts
+    table = [consts[c] for c in range(classes)]
+    for cut in range(cuts):
+        other = consts[classes + cut] > 0.5
+        for f in range(3):
+            values = []
+            for j in range(steps):
+                v = jnp.where(
+                    second,
+                    load[cut * 3 + f, pl.ds(steps + j, SUB, stride=stride), :],
+                    load[cut * 3 + f, pl.ds(j, SUB, stride=stride), :],
+                )
+                if f == 2:
+                    k = table[0]
+                    for c in range(1, len(table)):
+                        k = jnp.where(v >= c, table[c], k)
+                    v = k
+                halos[cut][f, j] = v
+                values.append(v)
+            for j, v in enumerate(squeeze(cut, other, values)):
+                sent[cut][f, j] = v
 
 
 def first_kernel(
@@ -596,29 +607,34 @@
     masks = call(
         functools.partial(mask_kernel, n), "masks", (couplings,), [(mask_rows(cuts), SUB, LANES)]
     )[0]
-    packed = call(
-        pack_kernel,
+    arguments = (suction, warmth, classes, top.reshape(1, width), couplings, k_sat.reshape(1, -1))
+    packed, consts = call(
+        functools.partial(pack_kernel, cuts),
         "pack",
-        [pltpu.with_memory_space_constraint(v, pltpu.HBM) for v in (suction, warmth, classes, top.reshape(1, width))],
-        [(TEAM, 3 * quarters + 1, OWN, cells)],
+        [pltpu.with_memory_space_constraint(v, pltpu.HBM) for v in arguments],
+        [(TEAM, 3 * quarters + 1, OWN, cells), (k_sat.shape[0] + cuts, SUB, LANES)],
         scratch=[
             pltpu.VMEM((2, cells, width), F32),
             pltpu.VMEM((cells, width), classes.dtype),
             pltpu.VMEM((1, width), F32),
-            pltpu.SemaphoreType.DMA((4,)),
+            pltpu.VMEM(couplings.shape, couplings.dtype),
+            pltpu.VMEM((1, k_sat.shape[0]), F32),
+            pltpu.SemaphoreType.DMA((6,)),
         ],
-        specs=[hbm] * 4,
-    )[0]
+        specs=[hbm] * 6,
+    )
     got = exchange(packed, n)
 
-    edges = call(
-        functools.partial(edge_kernel, cuts),
-        "edges",
-        (got, couplings, k_sat),
-        [(3,) + halo] * (CHUNKS * cuts) + [(3,) + squeezed] * (CHUNKS * cuts),
-        scratch=[pltpu.VMEM((3 * CHUNKS * cuts, cells, LANES), F32)],
-        specs=[whole(), smem, smem],
-    )
+    edges = [
+        call(
+            functools.partial(edge_kernel, c, cuts),
+            "edges",
+            (got, consts),
+            [(3,) + halo] * cuts + [(3,) + squeezed] * cuts,
+            scratch=[pltpu.VMEM((3 * cuts, cells, LANES), F32)],
+        )
+        for c in range(CHUNKS)
+    ]
     first = [
         call(
             functools.partial(first_kernel, c),
@@ -632,8 +648,7 @@
     ]
     flows, sides = [], []
     for c in range(CHUNKS):
-        mine = edges[c * cuts : (c + 1) * cuts]
-        sent = edges[(CHUNKS + c) * cuts : (CHUNKS + c + 1) * cuts]
+        mine, sent = edges[c][:cuts], edges[c][cuts:]
         sides.append((mine, [swap(cut, n, v) for cut, v in enumerate(sent)]))
         flows.append(tuple(call(team_kernel, "team", (masks, first[c][0], first[c][1], first[c][6]), [column] * 2)))
 

time: 57.2 us -> 56.7 us (level)
    pallas_call x14 -> x15, Pallas kernels: 14.7 us -> 14.5 us  [call(): pl.pallas_call(kernel, out_shape=[jax.ShapeDtypeStruct(shape, F32) for sh...]
  transfers between devices with their start and end apart: 4 -> 4, of which waited for: 2 -> 2; matrix products, arithmetic and copies ran while one was open for 0% -> 0% of each run, Pallas kernels for 18% -> 19%
where the time goes in v13:
time: 56.7 us; the launch traced here: 56.4 us
  blocking collectives  34 us (60%)
  Pallas kernels  14.5 us (26%)
  starting transfers between devices  6.08 us (11%)
  waiting for transfers between devices  0.85 us (1%)
  between operations  0.73 us (1%)
    all_to_all x2, blocking collectives, exchange(): lax.all_to_all(tiles, 'cols', split_axis=0, concat_axis=0, tiled=True, ax...  34 us
    pallas_call x15, Pallas kernels, call(): pl.pallas_call(kernel, out_shape=[jax.ShapeDtypeStruct(shape, F32) for sh...  14.5 us
    ppermute x4, starting transfers between devices, swap(): return lax.ppermute(value, 'cols', pairs)  6.08 us
  transfers between devices with their start and end apart: 4, of which 2 were waited for; matrix products, arithmetic and copies ran while one was open for 0% of the time, Pallas kernels for 19%

profile of v13, /device:TPU:0, one launch (start us, length us, event | category | flops | bytes accessed | tf_op | source)
XLA Modules:
  0.0 56.4 jit_solution(11567459498689377917)
XLA Ops:
  0.6 1.6 %pack.1 = (f32[16,13,8,128]{3,2,1,0:T(8,128)S(1)}, f32[9,8,128]{2,1,0:T(8,128)S(1)}) custom-call(f32[128,512]{1,0:T(8,128)} %suction.1, f32[128,512]{1,0:T(8,128)} %warmth.1, s32[128,512]{1,0:T(8,128)} %classes.1, f32[1,512]{1,0:T(1,128)} %bitcast.3, s32[2,128]{1,0:T(2,128)} %couplings.3, f32[1,8]{1,0:T(1,128)} %bitcast.2), custom_call_target="tpu_custom_call" | custom-call | flops 2000000 | bytes 2000000 | tf_op jit(solution)/shard_map/pack/pallas_call | solution.py:567
  2.2 20.1 %all_to_all.10.got = f32[16,13,8,128]{3,2,1,0:T(8,128)S(1)} all-to-all(f32[16,13,8,128]{3,2,1,0:T(8,128)S(1)} %get-tuple-element.48), channel_id=1, replica_groups={{0,1,2,3,4,5,6,7,8,9,10,11,12,13,14,15},{16,17,18,19,20,21,22,23,24,25,..., dimensions={0} | all-to-all | bytes 1703936 | tf_op jit(solution)/shard_map/all_to_all | solution.py:581
  22.3 0.3 edges.3
  22.7 2.6 %collective-permute-start.2 = (f32[3,7,8,128]{3,2,1,0:T(8,128)S(1)}, f32[3,7,8,128]{3,2,1,0:T(8,128)S(1)}, u32[]{:S(2)}, u32[]{:S(2)}) collective-permute-start(f32[3,7,8,128]{3,2,1,0:T(8,128)S(1)} %get-tuple-element.84), channel_id=1, source_target_pairs={{0,16},{16,0},{1,17},{17,1},{2,18},{18,2},{3,19},{19,3},{4,20},{20... | collective-permute-start | bytes 258056 | tf_op jit(solution)/shard_map/ppermute | solution.py:591
  25.3 0.3 edges.2
  25.6 0.0 copy-start.1
  25.6 0.0 copy-start
  25.6 0.0 copy-start.2
  25.6 0.4 collective-permute-start
  26.0 0.3 copy-done.1
  26.3 0.3 masks.1.refs_0_
  26.6 0.0 copy-done
  26.6 0.0 copy-done.2
  26.6 0.9 %first.3 = (f32[8,8,512]{2,1,0:T(8,128)S(1)}, f32[8,8,512]{2,1,0:T(8,128)S(1)}, f32[8,8,512]{2,1,0:T(8,128)S(1)}, f32[8,8,512]{2,1,0:T(8,128)S(1)}, f32[8,8,512]...) custom-call(f32[16,13,8,128]{3,2,1,0:T(8,128)S(1)} %all_to_all.10.go, ...), custom_call_target="tpu_custom_call" | custom-call | flops 2000000 | bytes 2000000 | tf_op jit(solution)/shard_map/first/pallas_call | solution.py:567
  27.5 1.4 %team.6 = (f32[8,8,512]{2,1,0:T(8,128)S(1)}, f32[8,8,512]{2,1,0:T(8,128)S(1)}) custom-call(f32[22,8,128]{2,1,0:T(8,128)S(1)} %masks.1.refs_0_, f32[8,8,512]{2,1,0:T(8,128)S(1)} %get-tuple-element.72.head.refs_1_, f32[8,8,512]{2,1,0:T(8,128)S(1)} %get-tuple-element.73.warm.refs_2_, f32[8,8,512]{2,1,0:T(8,128)S(1)} %get-tuple-element.78.cond.refs_7_), custom_call_target="tpu_custom_call" | custom-call | flops 2000000 | bytes 2000000 | tf_op jit(solution)/shard_map/team/pallas_call | solution.py:567
  28.9 0.9 %first.2 = (f32[8,8,512]{2,1,0:T(8,128)S(1)}, f32[8,8,512]{2,1,0:T(8,128)S(1)}, f32[8,8,512]{2,1,0:T(8,128)S(1)}, f32[8,8,512]{2,1,0:T(8,128)S(1)}, f32[8,8,512]...) custom-call(f32[16,13,8,128]{3,2,1,0:T(8,128)S(1)} %all_to_all.10.go, ...), custom_call_target="tpu_custom_call" | custom-call | flops 2000000 | bytes 2000000 | tf_op jit(solution)/shard_map/first/pallas_call | solution.py:567
  29.8 1.4 %team.4 = (f32[8,8,512]{2,1,0:T(8,128)S(1)}, f32[8,8,512]{2,1,0:T(8,128)S(1)}) custom-call(f32[22,8,128]{2,1,0:T(8,128)S(1)} %masks.1.refs_0_, f32[8,8,512]{2,1,0:T(8,128)S(1)} %get-tuple-element.49.head.refs_1_, f32[8,8,512]{2,1,0:T(8,128)S(1)} %get-tuple-element.50.warm.refs_2_, f32[8,8,512]{2,1,0:T(8,128)S(1)} %get-tuple-element.55.cond.refs_7_), custom_call_target="tpu_custom_call" | custom-call | flops 2000000 | bytes 2000000 | tf_op jit(solution)/shard_map/team/pallas_call | solution.py:567
  31.2 0.7 %collective-permute-done.2.refs_13_.refs_15_ = f32[3,7,8,128]{3,2,1,0:T(8,128)S(1)} collective-permute-done((f32[3,7,8,128]{3,2,1,0:T(8,128)S(1)}, f32[3,7,8,128]{3,2,1,0:T(8,128)S(1)}, u32[]{:S(2)}, u32[]{:S(2)}) %collective-permute-start.2) | collective-permute-done | bytes 86048 | tf_op jit(solution)/shard_map/ppermute | solution.py:591
  31.8 1.0 %middle.3 = (f32[8,8,512]{2,1,0:T(8,128)S(1)}, f32[8,8,512]{2,1,0:T(8,128)S(1)}, f32[8,8,512]{2,1,0:T(8,128)S(1)}, f32[8,8,512]{2,1,0:T(8,128)S(1)}, f32[8,8,512...) custom-call(f32[22,8,128]{2,1,0:T(8,128)S(1)} %masks.1.refs_0_, ...), custom_call_target="tpu_custom_call" | custom-call | flops 2000000 | bytes 2000000 | tf_op jit(solution)/shard_map/middle/pallas_call | solution.py:567
  32.8 1.7 %collective-permute-start.3 = (f32[2,7,8,128]{3,2,1,0:T(8,128)S(1)}, f32[2,7,8,128]{3,2,1,0:T(8,128)S(1)}, u32[]{:S(2)}, u32[]{:S(2)}) collective-permute-start(f32[2,7,8,128]{3,2,1,0:T(8,128)S(1)} %get-tuple-element.93), channel_id=1, source_target_pairs={{0,16},{16,0},{1,17},{17,1},{2,18},{18,2},{3,19},{19,3},{4,20},{20... | collective-permute-start | bytes 172040 | tf_op jit(solution)/shard_map/ppermute | solution.py:591
  34.6 0.0 collective-permute-done.refs_13_.refs_15_
  34.6 1.0 %middle.2 = (f32[8,8,512]{2,1,0:T(8,128)S(1)}, f32[8,8,512]{2,1,0:T(8,128)S(1)}, f32[8,8,512]{2,1,0:T(8,128)S(1)}, f32[8,8,512]{2,1,0:T(8,128)S(1)}, f32[8,8,512...) custom-call(f32[22,8,128]{2,1,0:T(8,128)S(1)} %masks.1.refs_0_, ...), custom_call_target="tpu_custom_call" | custom-call | flops 2000000 | bytes 2000000 | tf_op jit(solution)/shard_map/middle/pallas_call | solution.py:567
  35.6 1.3 %collective-permute-start.1 = (f32[2,7,8,128]{3,2,1,0:T(8,128)S(1)}, f32[2,7,8,128]{3,2,1,0:T(8,128)S(1)}, u32[]{:S(2)}, u32[]{:S(2)}) collective-permute-start(f32[2,7,8,128]{3,2,1,0:T(8,128)S(1)} %get-tuple-element.71), channel_id=1, source_target_pairs={{0,16},{16,0},{1,17},{17,1},{2,18},{18,2},{3,19},{19,3},{4,20},{20... | collective-permute-start | bytes 172040 | tf_op jit(solution)/shard_map/ppermute | solution.py:591
  36.8 1.4 %team.7 = (f32[8,8,512]{2,1,0:T(8,128)S(1)}, f32[8,8,512]{2,1,0:T(8,128)S(1)}) custom-call(f32[22,8,128]{2,1,0:T(8,128)S(1)} %masks.1.refs_0_, f32[8,8,512]{2,1,0:T(8,128)S(1)} %get-tuple-element.85.head.refs_1_, f32[8,8,512]{2,1,0:T(8,128)S(1)} %get-tuple-element.86.warm.refs_2_, f32[8,8,512]{2,1,0:T(8,128)S(1)} %get-tuple-element.89.cond.refs_7_), custom_call_target="tpu_custom_call" | custom-call | flops 2000000 | bytes 2000000 | tf_op jit(solution)/shard_map/team/pallas_call | solution.py:567
  38.2 1.4 %team.5 = (f32[8,8,512]{2,1,0:T(8,128)S(1)}, f32[8,8,512]{2,1,0:T(8,128)S(1)}) custom-call(f32[22,8,128]{2,1,0:T(8,128)S(1)} %masks.1.refs_0_, f32[8,8,512]{2,1,0:T(8,128)S(1)} %get-tuple-element.63.head.refs_1_, f32[8,8,512]{2,1,0:T(8,128)S(1)} %get-tuple-element.64.warm.refs_2_, f32[8,8,512]{2,1,0:T(8,128)S(1)} %get-tuple-element.67.cond.refs_7_), custom_call_target="tpu_custom_call" | custom-call | flops 2000000 | bytes 2000000 | tf_op jit(solution)/shard_map/team/pallas_call | solution.py:567
  39.6 0.1 collective-permute-done.3.refs_13_
  39.7 0.9 %last.2.refs_16_ = f32[16,4,8,128]{3,2,1,0:T(8,128)S(1)} custom-call(f32[22,8,128]{2,1,0:T(8,128)S(1)} %masks.1.refs_0_, f32[8,8,512]{2,1,0:T(8,128)S(1)} %get-tuple-element.85.head.refs_1_, f32[8,8,512]{2,1,0:T(8,128)S(1)} %get-tuple-element.86.warm.refs_2_, f32[8,8,512]{2,1,0:T(8,128)S(1)} %get-tuple-element.75.refs_4_.refs_3_, ...), custom_call_target="tpu_custom_call" | custom-call | flops 2000000 | bytes 2000000 | tf_op jit(solution)/shard_map/last/pallas_call | solution.py:567
  40.6 0.0 collective-permute-done.1.refs_13_
  40.7 0.9 %last.3 = f32[16,8,8,128]{3,2,1,0:T(8,128)S(1)} custom-call(f32[22,8,128]{2,1,0:T(8,128)S(1)} %masks.1.refs_0_, f32[8,8,512]{2,1,0:T(8,128)S(1)} %get-tuple-element.63.head.refs_1_, f32[8,8,512]{2,1,0:T(8,128)S(1)} %get-tuple-element.64.warm.refs_2_, f32[8,8,512]{2,1,0:T(8,128)S(1)} %get-tuple-element.52.refs_4_.refs_3_, ...), custom_call_target="tpu_custom_call" | custom-call | flops 2000000 | bytes 2000000 | tf_op jit(solution)/shard_map/last/pallas_call | solution.py:567
  41.6 13.9 %all_to_all.11.got = f32[16,8,8,128]{3,2,1,0:T(8,128)S(1)} all-to-all(f32[16,8,8,128]{3,2,1,0:T(8,128)S(1)} %last.3), channel_id=1, replica_groups={{0,1,2,3,4,5,6,7,8,9,10,11,12,13,14,15},{16,17,18,19,20,21,22,23,24,25,..., dimensions={0} | all-to-all | bytes 1048576 | tf_op jit(solution)/shard_map/all_to_all | solution.py:581
  55.5 0.9 %unpack.1 = (f32[128,512]{1,0:T(8,128)}, f32[128,512]{1,0:T(8,128)}) custom-call(f32[16,8,8,128]{3,2,1,0:T(8,128)S(1)} %all_to_all.11.got), custom_call_target="tpu_custom_call" | custom-call | flops 2000000 | bytes 2000000 | tf_op jit(solution)/shard_map/unpack/pallas_call | solution.py:567
Async XLA Ops:
  22.7 9.2 %collective-permute-start.2 = (f32[3,7,8,128]{3,2,1,0:T(8,128)S(1)}, f32[3,7,8,128]{3,2,1,0:T(8,128)S(1)}, u32[]{:S(2)}, u32[]{:S(2)}) collective-permute-start(f32[3,7,8,128]{3,2,1,0:T(8,128)S(1)} %get-tuple-element.84), channel_id=1, source_target_pairs={{0,16},{16,0},{1,17},{17,1},{2,18},{18,2},{3,19},{19,3},{4,20},{20... | collective-permute-start | bytes 258056 | tf_op jit(solution)/shard_map/ppermute | solution.py:591
  25.6 0.7 %copy-start.1 = (s32[2,128]{1,0:T(2,128)S(1)}, s32[2,128]{1,0:T(2,128)}, u32[]{:S(2)}) copy-start(s32[2,128]{1,0:T(2,128)} %couplings.3) | copy-start | bytes 3076
  25.6 0.9 %copy-start = (f32[8]{0:T(128)S(1)}, f32[8]{0:T(128)}, u32[]{:S(2)}) copy-start(f32[8]{0:T(128)} %k_sat.3) | copy-start | bytes 100
  25.6 0.9 %copy-start.2 = (f32[8]{0:T(128)S(1)}, f32[8]{0:T(128)}, u32[]{:S(2)}) copy-start(f32[8]{0:T(128)} %heat_cond.3) | copy-start | bytes 100
  25.6 8.9 %collective-permute-start = (f32[3,7,8,128]{3,2,1,0:T(8,128)S(1)}, f32[3,7,8,128]{3,2,1,0:T(8,128)S(1)}, u32[]{:S(2)}, u32[]{:S(2)}) collective-permute-start(f32[3,7,8,128]{3,2,1,0:T(8,128)S(1)} %get-tuple-element.62), channel_id=1, source_target_pairs={{0,16},{16,0},{1,17},{17,1},{2,18},{18,2},{3,19},{19,3},{4,20},{20... | collective-permute-start | bytes 258056 | tf_op jit(solution)/shard_map/ppermute | solution.py:591
  32.8 6.9 %collective-permute-start.3 = (f32[2,7,8,128]{3,2,1,0:T(8,128)S(1)}, f32[2,7,8,128]{3,2,1,0:T(8,128)S(1)}, u32[]{:S(2)}, u32[]{:S(2)}) collective-permute-start(f32[2,7,8,128]{3,2,1,0:T(8,128)S(1)} %get-tuple-element.93), channel_id=1, source_target_pairs={{0,16},{16,0},{1,17},{17,1},{2,18},{18,2},{3,19},{19,3},{4,20},{20... | collective-permute-start | bytes 172040 | tf_op jit(solution)/shard_map/ppermute | solution.py:591
  35.6 5.1 %collective-permute-start.1 = (f32[2,7,8,128]{3,2,1,0:T(8,128)S(1)}, f32[2,7,8,128]{3,2,1,0:T(8,128)S(1)}, u32[]{:S(2)}, u32[]{:S(2)}) collective-permute-start(f32[2,7,8,128]{3,2,1,0:T(8,128)S(1)} %get-tuple-element.71), channel_id=1, source_target_pairs={{0,16},{16,0},{1,17},{17,1},{2,18},{18,2},{3,19},{19,3},{4,20},{20... | collective-permute-start | bytes 172040 | tf_op jit(solution)/shard_map/ppermute | solution.py:591

commit v14 on v13

--- a/solution.py
+++ b/solution.py
@@ -124,7 +124,7 @@
 
 
 def mask_kernel(n, couplings, out):
-    pair_rows = couplings[...].astype(F32)
+    pair_rows = couplings[...]
     pairs = couplings.shape[1]
     pair_id = lax.broadcasted_iota(jnp.int32, (pairs, LANES), 0)
     lane = lax.broadcasted_iota(jnp.int32, (pairs, LANES), 1)
@@ -188,13 +188,14 @@
 
 
 def pack_kernel(
-    cuts, suction, warmth, classes, surface, couplings, k_sat, out, consts, room, class_room, top, pairs, table, in_sems
+    cuts, suction, warmth, classes, surface, couplings, k_sat, heat_cond, out, consts, pair_rows,
+    room, class_room, top, pairs, k_table, heat_table, in_sems,
 ):
     cells = out.shape[-1]
     quarters = 2 * CHUNKS
     into = []
-    rooms = (room.at[0], room.at[1], class_room, top, pairs, table)
-    for f, field in enumerate((suction, warmth, classes, surface, couplings, k_sat)):
+    rooms = (room.at[0], room.at[1], class_room, top, pairs, k_table, heat_table)
+    for f, field in enumerate((suction, warmth, classes, surface, couplings, k_sat, heat_cond)):
         into.append(pltpu.make_async_copy(field, rooms[f], in_sems.at[f]))
         into[-1].start()
 
@@ -208,10 +209,13 @@
             put(f * quarters + q, class_room[:, lanes].astype(F32) if f == 2 else room[f, :, lanes])
     for copy in into[3:]:
         copy.wait()
-    for c in range(k_sat.shape[1]):
-        consts[c] = jnp.broadcast_to(table[0:1, c : c + 1], (SUB, LANES))
+    kinds = k_sat.shape[1]
+    for c in range(kinds):
+        consts[c] = jnp.broadcast_to(k_table[0:1, c : c + 1], (SUB, LANES))
+        consts[kinds + c] = jnp.broadcast_to(heat_table[0:1, c : c + 1], (SUB, LANES))
     for cut in range(cuts):
-        consts[k_sat.shape[1] + cut] = other_block(cut, pairs)
+        consts[2 * kinds + cut] = other_block(cut, pairs)
+    pair_rows[...] = pairs[...].astype(F32)
     rows = [top[0:1, q * LANES : (q + 1) * LANES] for q in range(quarters)]
     put(3 * quarters, jnp.concatenate(rows + [jnp.zeros((cells - quarters, LANES), F32)], axis=0))
 
@@ -279,10 +283,10 @@
                 got[pl.ds(start, PAIR_DEV), (f * 2 + b) * CHUNKS + chunk].reshape(EDGE, cells) for b in range(2)
             ]
             load[cut * 3 + f] = jnp.concatenate(rows * GROUPS, axis=0).T
-    classes = consts.shape[0] - cuts
-    table = [consts[c] for c in range(classes)]
+    kinds = (consts.shape[0] - cuts) // 2
+    table = [consts[c] for c in range(kinds)]
     for cut in range(cuts):
-        other = consts[classes + cut] > 0.5
+        other = consts[2 * kinds + cut] > 0.5
         for f in range(3):
             values = []
             for j in range(steps):
@@ -303,7 +307,7 @@
 
 
 def first_kernel(
-    chunk, got, k_sat, heat_cond, head, warm, perm, conduct, wet, melt, cond, energy, top, load
+    chunk, kinds, got, consts, head, warm, perm, conduct, wet, melt, cond, energy, top, load
 ):
     cells = got.shape[-1]
     steps = head.shape[0]
@@ -324,14 +328,21 @@
         ]
         return jnp.concatenate(parts, axis=1)
 
+    def pick(v):
+        parts = []
+        for m in range(2 * GROUPS):
+            part = v[:, m * LANES : (m + 1) * LANES]
+            k, lam = consts[0], consts[kinds]
+            for c in range(1, kinds):
+                here = part >= c
+                k = jnp.where(here, consts[c], k)
+                lam = jnp.where(here, consts[kinds + c], lam)
+            parts.append((k, lam))
+        return [jnp.concatenate(side, axis=1) for side in zip(*parts)]
+
     for j in range(steps):
         h, t, v = [fetch(field, j) for field in range(3)]
-        k = jnp.full_like(v, k_sat[0])
-        lam = jnp.full_like(v, heat_cond[0])
-        for c in range(1, k_sat.shape[0]):
-            here = v >= c
-            k = jnp.where(here, k_sat[c], k)
-            lam = jnp.where(here, heat_cond[c], lam)
+        k, lam = pick(v)
         s, f = sigmoid(h), sigmoid(2.0 * t)
         m = 0.05 + 0.4 * s
         head[j], warm[j], perm[j], conduct[j] = h, t, k, lam
@@ -601,28 +612,29 @@
     halo = (steps, SUB, LANES)
     squeezed = (steps - 1, SUB, LANES)
     room = pltpu.VMEM(column, F32)
-    smem = whole(pltpu.SMEM)
     hbm = whole(pltpu.HBM)
 
-    masks = call(
-        functools.partial(mask_kernel, n), "masks", (couplings,), [(mask_rows(cuts), SUB, LANES)]
-    )[0]
-    arguments = (suction, warmth, classes, top.reshape(1, width), couplings, k_sat.reshape(1, -1))
-    packed, consts = call(
+    arguments = (suction, warmth, classes, top.reshape(1, width), couplings, k_sat.reshape(1, -1), heat_cond.reshape(1, -1))
+    kinds = k_sat.shape[0]
+    packed, consts, pair_rows = call(
         functools.partial(pack_kernel, cuts),
         "pack",
         [pltpu.with_memory_space_constraint(v, pltpu.HBM) for v in arguments],
-        [(TEAM, 3 * quarters + 1, OWN, cells), (k_sat.shape[0] + cuts, SUB, LANES)],
+        [(TEAM, 3 * quarters + 1, OWN, cells), (2 * kinds + cuts, SUB, LANES), couplings.shape],
         scratch=[
             pltpu.VMEM((2, cells, width), F32),
             pltpu.VMEM((cells, width), classes.dtype),
             pltpu.VMEM((1, width), F32),
             pltpu.VMEM(couplings.shape, couplings.dtype),
-            pltpu.VMEM((1, k_sat.shape[0]), F32),
-            pltpu.SemaphoreType.DMA((6,)),
+            pltpu.VMEM((1, kinds), F32),
+            pltpu.VMEM((1, kinds), F32),
+            pltpu.SemaphoreType.DMA((7,)),
         ],
-        specs=[hbm] * 6,
+        specs=[hbm] * 7,
     )
+    masks = call(
+        functools.partial(mask_kernel, n), "masks", (pair_rows,), [(mask_rows(cuts), SUB, LANES)]
+    )[0]
     got = exchange(packed, n)
 
     edges = [
@@ -637,12 +649,11 @@
     ]
     first = [
         call(
-            functools.partial(first_kernel, c),
+            functools.partial(first_kernel, c, kinds),
             "first",
-            (got, k_sat, heat_cond),
+            (got, consts),
             [column] * 8 + [(1, ALL)],
             scratch=[pltpu.VMEM((6, cells, LANES), F32)],
-            specs=[whole(), smem, smem],
         )
         for c in range(CHUNKS)
     ]

time: 56.7 us -> 56.6 us (level)
  waiting for transfers between devices: 0.85 us -> 2.07 us
  Pallas kernels: 14.5 us -> 13.4 us
    ppermute x4, waiting for transfers between devices: 0.85 us -> 2.07 us  [swap(): return lax.ppermute(value, 'cols', pairs)]
    pallas_call x15, Pallas kernels: 14.5 us -> 13.4 us  [call(): pl.pallas_call(kernel, out_shape=[jax.ShapeDtypeStruct(shape, F32) for sh...]
  transfers between devices with their start and end apart: 4 -> 4, of which waited for: 2 -> 1; matrix products, arithmetic and copies ran while one was open for 0% -> 0% of each run, Pallas kernels for 19% -> 17%
where the time goes in v14:
time: 56.6 us; the launch traced here: 56.4 us
  blocking collectives  34.2 us (60%)
  Pallas kernels  13.4 us (24%)
  starting transfers between devices  6.07 us (11%)
  waiting for transfers between devices  2.07 us (4%)
  between operations  0.72 us (1%)
    all_to_all x2, blocking collectives, exchange(): lax.all_to_all(tiles, 'cols', split_axis=0, concat_axis=0, tiled=True, ax...  34.2 us
    pallas_call x15, Pallas kernels, call(): pl.pallas_call(kernel, out_shape=[jax.ShapeDtypeStruct(shape, F32) for sh...  13.4 us
    ppermute x4, starting transfers between devices, swap(): return lax.ppermute(value, 'cols', pairs)  6.07 us
    ppermute x4, waiting for transfers between devices, swap(): return lax.ppermute(value, 'cols', pairs)  2.07 us
  transfers between devices with their start and end apart: 4, of which 1 were waited for; matrix products, arithmetic and copies ran while one was open for 0% of the time, Pallas kernels for 17%

profile of v14, /device:TPU:0, one launch (start us, length us, event | category | flops | bytes accessed | tf_op | source)
XLA Modules:
  0.0 56.4 jit_solution(17859157543542697080)
XLA Ops:
  0.6 1.6 %pack.1 = (f32[16,13,8,128]{3,2,1,0:T(8,128)S(1)}, f32[17,8,128]{2,1,0:T(8,128)S(1)}, f32[2,128]{1,0:T(2,128)S(1)}) custom-call(f32[128,512]{1,0:T(8,128)} %suction.1, f32[128,512]{1,0:T(8,128)} %warmth.1, s32[128,512]{1,0:T(8,128)} %classes.1, f32[1,512]{1,0:T(1,128)} %bitcast.3, s32[2,128]{1,0:T(2,128)} %couplings.1, f32[1,8]{1,0:T(1,128)} %bitcast.4, ...), custom_call_target="tpu_custom_call" | custom-call | flops 2000000 | bytes 2000000 | tf_op jit(solution)/shard_map/pack/pallas_call | solution.py:578
  2.2 20.1 %all_to_all.10.got = f32[16,13,8,128]{3,2,1,0:T(8,128)S(1)} all-to-all(f32[16,13,8,128]{3,2,1,0:T(8,128)S(1)} %get-tuple-element.50), channel_id=1, replica_groups={{0,1,2,3,4,5,6,7,8,9,10,11,12,13,14,15},{16,17,18,19,20,21,22,23,24,25,..., dimensions={0} | all-to-all | bytes 1703936 | tf_op jit(solution)/shard_map/all_to_all | solution.py:592
  22.4 0.3 edges.3
  22.7 2.6 %collective-permute-start.2 = (f32[3,7,8,128]{3,2,1,0:T(8,128)S(1)}, f32[3,7,8,128]{3,2,1,0:T(8,128)S(1)}, u32[]{:S(2)}, u32[]{:S(2)}) collective-permute-start(f32[3,7,8,128]{3,2,1,0:T(8,128)S(1)} %get-tuple-element.86), channel_id=1, source_target_pairs={{0,16},{16,0},{1,17},{17,1},{2,18},{18,2},{3,19},{19,3},{4,20},{20... | collective-permute-start | bytes 258056 | tf_op jit(solution)/shard_map/ppermute | solution.py:602
  25.3 0.3 edges.2
  25.6 0.4 collective-permute-start
  26.0 0.3 masks.1.refs_0_
  26.3 0.4 first.3
  26.7 1.4 %team.6 = (f32[8,8,512]{2,1,0:T(8,128)S(1)}, f32[8,8,512]{2,1,0:T(8,128)S(1)}) custom-call(f32[22,8,128]{2,1,0:T(8,128)S(1)} %masks.1.refs_0_, f32[8,8,512]{2,1,0:T(8,128)S(1)} %get-tuple-element.74.head.refs_1_, f32[8,8,512]{2,1,0:T(8,128)S(1)} %get-tuple-element.75.warm.refs_2_, f32[8,8,512]{2,1,0:T(8,128)S(1)} %get-tuple-element.80.cond.refs_7_), custom_call_target="tpu_custom_call" | custom-call | flops 2000000 | bytes 2000000 | tf_op jit(solution)/shard_map/team/pallas_call | solution.py:578
  28.0 0.4 first.2
  28.4 1.4 %team.4 = (f32[8,8,512]{2,1,0:T(8,128)S(1)}, f32[8,8,512]{2,1,0:T(8,128)S(1)}) custom-call(f32[22,8,128]{2,1,0:T(8,128)S(1)} %masks.1.refs_0_, f32[8,8,512]{2,1,0:T(8,128)S(1)} %get-tuple-element.52.head.refs_1_, f32[8,8,512]{2,1,0:T(8,128)S(1)} %get-tuple-element.53.warm.refs_2_, f32[8,8,512]{2,1,0:T(8,128)S(1)} %get-tuple-element.58.cond.refs_7_), custom_call_target="tpu_custom_call" | custom-call | flops 2000000 | bytes 2000000 | tf_op jit(solution)/shard_map/team/pallas_call | solution.py:578
  29.8 2.1 %collective-permute-done.2.refs_13_.refs_15_ = f32[3,7,8,128]{3,2,1,0:T(8,128)S(1)} collective-permute-done((f32[3,7,8,128]{3,2,1,0:T(8,128)S(1)}, f32[3,7,8,128]{3,2,1,0:T(8,128)S(1)}, u32[]{:S(2)}, u32[]{:S(2)}) %collective-permute-start.2) | collective-permute-done | bytes 86048 | tf_op jit(solution)/shard_map/ppermute | solution.py:602
  31.9 1.0 %middle.3 = (f32[8,8,512]{2,1,0:T(8,128)S(1)}, f32[8,8,512]{2,1,0:T(8,128)S(1)}, f32[8,8,512]{2,1,0:T(8,128)S(1)}, f32[8,8,512]{2,1,0:T(8,128)S(1)}, f32[8,8,512...) custom-call(f32[22,8,128]{2,1,0:T(8,128)S(1)} %masks.1.refs_0_, ...), custom_call_target="tpu_custom_call" | custom-call | flops 2000000 | bytes 2000000 | tf_op jit(solution)/shard_map/middle/pallas_call | solution.py:578
  32.8 0.6 %collective-permute-start.3 = (f32[2,7,8,128]{3,2,1,0:T(8,128)S(1)}, f32[2,7,8,128]{3,2,1,0:T(8,128)S(1)}, u32[]{:S(2)}, u32[]{:S(2)}) collective-permute-start(f32[2,7,8,128]{3,2,1,0:T(8,128)S(1)} %get-tuple-element.95), channel_id=1, source_target_pairs={{0,16},{16,0},{1,17},{17,1},{2,18},{18,2},{3,19},{19,3},{4,20},{20... | collective-permute-start | bytes 172040 | tf_op jit(solution)/shard_map/ppermute | solution.py:602
  33.4 0.0 collective-permute-done.refs_13_.refs_15_
  33.4 1.0 %middle.2 = (f32[8,8,512]{2,1,0:T(8,128)S(1)}, f32[8,8,512]{2,1,0:T(8,128)S(1)}, f32[8,8,512]{2,1,0:T(8,128)S(1)}, f32[8,8,512]{2,1,0:T(8,128)S(1)}, f32[8,8,512...) custom-call(f32[22,8,128]{2,1,0:T(8,128)S(1)} %masks.1.refs_0_, ...), custom_call_target="tpu_custom_call" | custom-call | flops 2000000 | bytes 2000000 | tf_op jit(solution)/shard_map/middle/pallas_call | solution.py:578
  34.4 2.4 %collective-permute-start.1 = (f32[2,7,8,128]{3,2,1,0:T(8,128)S(1)}, f32[2,7,8,128]{3,2,1,0:T(8,128)S(1)}, u32[]{:S(2)}, u32[]{:S(2)}) collective-permute-start(f32[2,7,8,128]{3,2,1,0:T(8,128)S(1)} %get-tuple-element.73), channel_id=1, source_target_pairs={{0,16},{16,0},{1,17},{17,1},{2,18},{18,2},{3,19},{19,3},{4,20},{20... | collective-permute-start | bytes 172040 | tf_op jit(solution)/shard_map/ppermute | solution.py:602
  36.8 1.4 %team.7 = (f32[8,8,512]{2,1,0:T(8,128)S(1)}, f32[8,8,512]{2,1,0:T(8,128)S(1)}) custom-call(f32[22,8,128]{2,1,0:T(8,128)S(1)} %masks.1.refs_0_, f32[8,8,512]{2,1,0:T(8,128)S(1)} %get-tuple-element.87.head.refs_1_, f32[8,8,512]{2,1,0:T(8,128)S(1)} %get-tuple-element.88.warm.refs_2_, f32[8,8,512]{2,1,0:T(8,128)S(1)} %get-tuple-element.91.cond.refs_7_), custom_call_target="tpu_custom_call" | custom-call | flops 2000000 | bytes 2000000 | tf_op jit(solution)/shard_map/team/pallas_call | solution.py:578
  38.2 1.4 %team.5 = (f32[8,8,512]{2,1,0:T(8,128)S(1)}, f32[8,8,512]{2,1,0:T(8,128)S(1)}) custom-call(f32[22,8,128]{2,1,0:T(8,128)S(1)} %masks.1.refs_0_, f32[8,8,512]{2,1,0:T(8,128)S(1)} %get-tuple-element.65.head.refs_1_, f32[8,8,512]{2,1,0:T(8,128)S(1)} %get-tuple-element.66.warm.refs_2_, f32[8,8,512]{2,1,0:T(8,128)S(1)} %get-tuple-element.69.cond.refs_7_), custom_call_target="tpu_custom_call" | custom-call | flops 2000000 | bytes 2000000 | tf_op jit(solution)/shard_map/team/pallas_call | solution.py:578
  39.6 0.0 collective-permute-done.3.refs_13_
  39.6 0.9 %last.2.refs_16_ = f32[16,4,8,128]{3,2,1,0:T(8,128)S(1)} custom-call(f32[22,8,128]{2,1,0:T(8,128)S(1)} %masks.1.refs_0_, f32[8,8,512]{2,1,0:T(8,128)S(1)} %get-tuple-element.87.head.refs_1_, f32[8,8,512]{2,1,0:T(8,128)S(1)} %get-tuple-element.88.warm.refs_2_, f32[8,8,512]{2,1,0:T(8,128)S(1)} %get-tuple-element.77.refs_4_.refs_3_, ...), custom_call_target="tpu_custom_call" | custom-call | flops 2000000 | bytes 2000000 | tf_op jit(solution)/shard_map/last/pallas_call | solution.py:578
  40.5 0.0 collective-permute-done.1.refs_13_
  40.5 0.9 %last.3 = f32[16,8,8,128]{3,2,1,0:T(8,128)S(1)} custom-call(f32[22,8,128]{2,1,0:T(8,128)S(1)} %masks.1.refs_0_, f32[8,8,512]{2,1,0:T(8,128)S(1)} %get-tuple-element.65.head.refs_1_, f32[8,8,512]{2,1,0:T(8,128)S(1)} %get-tuple-element.66.warm.refs_2_, f32[8,8,512]{2,1,0:T(8,128)S(1)} %get-tuple-element.55.refs_4_.refs_3_, ...), custom_call_target="tpu_custom_call" | custom-call | flops 2000000 | bytes 2000000 | tf_op jit(solution)/shard_map/last/pallas_call | solution.py:578
  41.4 14.0 %all_to_all.11.got = f32[16,8,8,128]{3,2,1,0:T(8,128)S(1)} all-to-all(f32[16,8,8,128]{3,2,1,0:T(8,128)S(1)} %last.3), channel_id=1, replica_groups={{0,1,2,3,4,5,6,7,8,9,10,11,12,13,14,15},{16,17,18,19,20,21,22,23,24,25,..., dimensions={0} | all-to-all | bytes 1048576 | tf_op jit(solution)/shard_map/all_to_all | solution.py:592
  55.5 0.9 %unpack.1 = (f32[128,512]{1,0:T(8,128)}, f32[128,512]{1,0:T(8,128)}) custom-call(f32[16,8,8,128]{3,2,1,0:T(8,128)S(1)} %all_to_all.11.got), custom_call_target="tpu_custom_call" | custom-call | flops 2000000 | bytes 2000000 | tf_op jit(solution)/shard_map/unpack/pallas_call | solution.py:578
Async XLA Ops:
  22.7 9.2 %collective-permute-start.2 = (f32[3,7,8,128]{3,2,1,0:T(8,128)S(1)}, f32[3,7,8,128]{3,2,1,0:T(8,128)S(1)}, u32[]{:S(2)}, u32[]{:S(2)}) collective-permute-start(f32[3,7,8,128]{3,2,1,0:T(8,128)S(1)} %get-tuple-element.86), channel_id=1, source_target_pairs={{0,16},{16,0},{1,17},{17,1},{2,18},{18,2},{3,19},{19,3},{4,20},{20... | collective-permute-start | bytes 258056 | tf_op jit(solution)/shard_map/ppermute | solution.py:602
  25.6 7.8 %collective-permute-start = (f32[3,7,8,128]{3,2,1,0:T(8,128)S(1)}, f32[3,7,8,128]{3,2,1,0:T(8,128)S(1)}, u32[]{:S(2)}, u32[]{:S(2)}) collective-permute-start(f32[3,7,8,128]{3,2,1,0:T(8,128)S(1)} %get-tuple-element.64), channel_id=1, source_target_pairs={{0,16},{16,0},{1,17},{17,1},{2,18},{18,2},{3,19},{19,3},{4,20},{20... | collective-permute-start | bytes 258056 | tf_op jit(solution)/shard_map/ppermute | solution.py:602
  32.8 6.7 %collective-permute-start.3 = (f32[2,7,8,128]{3,2,1,0:T(8,128)S(1)}, f32[2,7,8,128]{3,2,1,0:T(8,128)S(1)}, u32[]{:S(2)}, u32[]{:S(2)}) collective-permute-start(f32[2,7,8,128]{3,2,1,0:T(8,128)S(1)} %get-tuple-element.95), channel_id=1, source_target_pairs={{0,16},{16,0},{1,17},{17,1},{2,18},{18,2},{3,19},{19,3},{4,20},{20... | collective-permute-start | bytes 172040 | tf_op jit(solution)/shard_map/ppermute | solution.py:602
  34.4 6.1 %collective-permute-start.1 = (f32[2,7,8,128]{3,2,1,0:T(8,128)S(1)}, f32[2,7,8,128]{3,2,1,0:T(8,128)S(1)}, u32[]{:S(2)}, u32[]{:S(2)}) collective-permute-start(f32[2,7,8,128]{3,2,1,0:T(8,128)S(1)} %get-tuple-element.73), channel_id=1, source_target_pairs={{0,16},{16,0},{1,17},{17,1},{2,18},{18,2},{3,19},{19,3},{4,20},{20... | collective-permute-start | bytes 172040 | tf_op jit(solution)/shard_map/ppermute | solution.py:602

commit v15 on v14

--- a/solution.py
+++ b/solution.py
@@ -12,6 +12,7 @@
 LANES = 128
 CHUNKS = SPAN // LANES
 TEAM = 16
+ORDER = (0, 14, 2, 12, 4, 10, 6, 8, 1, 15, 3, 13, 5, 11, 7, 9)
 OWN = LANES // TEAM
 SUB = 8
 GROUPS = 2
@@ -21,6 +22,16 @@
 VMEM_LIMIT = 32 * 1024 * 1024
 DISTANCES = range(1, PAIR_DEV + 1)
 F32 = jnp.float32
+
+
+def tiles_of(chunks, slot):
+    return jnp.concatenate([chunks[ORDER.index(m), slot] for m in range(TEAM)], axis=0)
+
+
+def put_tiles(chunks, slot, rows):
+    tiles = rows.reshape(TEAM, OWN, rows.shape[1])
+    for place_in_order, m in enumerate(ORDER):
+        chunks[place_in_order, slot] = tiles[m]
 
 
 def cut_count(n):
@@ -200,7 +211,7 @@
         into[-1].start()
 
     def put(slot, value):
-        out[:, slot] = value.T.reshape(TEAM, OWN, cells)
+        put_tiles(out, slot, value.T)
 
     for f in range(3):
         into[f].wait()
@@ -226,7 +237,7 @@
     sent = []
     for f, out in enumerate((suction, warmth)):
         for q in range(quarters):
-            room[f, :, q * LANES : (q + 1) * LANES] = got[:, f * quarters + q].reshape(LANES, cells).T
+            room[f, :, q * LANES : (q + 1) * LANES] = tiles_of(got, f * quarters + q).T
         sent.append(pltpu.make_async_copy(room.at[f], out, sems.at[f]))
         sent[-1].start()
     for copy in sent:
@@ -277,11 +288,14 @@
     stride = steps * GROUPS
     second = lax.broadcasted_iota(jnp.int32, (SUB, LANES), 1) >= 2 * EDGE
     for cut in range(cuts):
-        start = jnp.where(place(cut)[1], TEAM - PAIR_DEV, 0)
+        above = place(cut)[1]
         for f in range(3):
-            rows = [
-                got[pl.ds(start, PAIR_DEV), (f * 2 + b) * CHUNKS + chunk].reshape(EDGE, cells) for b in range(2)
-            ]
+            rows = []
+            for b in range(2):
+                slot = (f * 2 + b) * CHUNKS + chunk
+                for m in range(PAIR_DEV):
+                    high, low = ORDER.index(TEAM - PAIR_DEV + m), ORDER.index(m)
+                    rows.append(jnp.where(above, got[high, slot], got[low, slot]))
             load[cut * 3 + f] = jnp.concatenate(rows * GROUPS, axis=0).T
     kinds = (consts.shape[0] - cuts) // 2
     table = [consts[c] for c in range(kinds)]
@@ -315,8 +329,8 @@
 
     for field in range(3):
         for b in range(2):
-            load[field * 2 + b] = got[:, (field * 2 + b) * CHUNKS + chunk].reshape(LANES, cells).T
-    surface = got[:, 6 * CHUNKS].reshape(LANES, cells).T[0:SUB]
+            load[field * 2 + b] = tiles_of(got, (field * 2 + b) * CHUNKS + chunk).T
+    surface = tiles_of(got, 6 * CHUNKS).T[0:SUB]
     rows = [surface[b * CHUNKS + chunk : b * CHUNKS + chunk + 1] for b in range(2)]
     top[...] = jnp.concatenate(rows * GROUPS, axis=1)
 
@@ -561,13 +575,10 @@
             for j in range(steps):
                 for g in range(GROUPS):
                     load[slot, pl.ds(g * steps + j, SUB, stride=stride), :] = field[j, :, lanes_of(g, b)]
-            turned = load[slot].T.reshape(TEAM, OWN, cells)
+            put_tiles(out, slot * CHUNKS + chunk if final else slot, load[slot].T)
             if final:
-                out[:, slot * CHUNKS + chunk] = turned
                 for c, other in enumerate(others):
                     out[:, slot * CHUNKS + c] = other[:, slot]
-            else:
-                out[:, slot] = turned
 
 
 def whole(memory=pltpu.VMEM):
@@ -588,7 +599,7 @@
 
 
 def exchange(tiles, n):
-    teams = [list(range(start, start + TEAM)) for start in range(0, n, TEAM)]
+    teams = [[start + m for m in ORDER] for start in range(0, n, TEAM)]
     return lax.all_to_all(
         tiles, "cols", split_axis=0, concat_axis=0, tiled=True, axis_index_groups=teams
     )

time: 56.6 us -> 56.7 us (level)
  blocking collectives: 34.2 us -> 34.9 us
  waiting for transfers between devices: 2.07 us -> 1.39 us
    all_to_all x2, blocking collectives: 34.2 us -> 34.9 us  [exchange(): lax.all_to_all(tiles, 'cols', split_axis=0, concat_axis=0, tiled=True, ax...]
    ppermute x4, waiting for transfers between devices: 2.07 us -> 1.39 us  [swap(): return lax.ppermute(value, 'cols', pairs)]
where the time goes in v15:
time: 56.7 us; the launch traced here: 56.5 us
  blocking collectives  34.9 us (62%)
  Pallas kernels  13.4 us (24%)
  starting transfers between devices  6.07 us (11%)
  waiting for transfers between devices  1.39 us (2%)
  between operations  0.72 us (1%)
    all_to_all x2, blocking collectives, exchange(): lax.all_to_all(tiles, 'cols', split_axis=0, concat_axis=0, tiled=True, ax...  34.9 us
    pallas_call x15, Pallas kernels, call(): pl.pallas_call(kernel, out_shape=[jax.ShapeDtypeStruct(shape, F32) for sh...  13.4 us
    ppermute x4, starting transfers between devices, swap(): return lax.ppermute(value, 'cols', pairs)  6.07 us
    ppermute x4, waiting for transfers between devices, swap(): return lax.ppermute(value, 'cols', pairs)  1.39 us
  transfers between devices with their start and end apart: 4, of which 1 were waited for; matrix products, arithmetic and copies ran while one was open for 0% of the time, Pallas kernels for 17%

profile of v15, /device:TPU:0, one launch (start us, length us, event | category | flops | bytes accessed | tf_op | source)
XLA Modules:
  0.0 56.5 jit_solution(13311144075008184454)
XLA Ops:
  0.6 1.6 %pack.1 = (f32[16,13,8,128]{3,2,1,0:T(8,128)S(1)}, f32[17,8,128]{2,1,0:T(8,128)S(1)}, f32[2,128]{1,0:T(2,128)S(1)}) custom-call(f32[128,512]{1,0:T(8,128)} %suction.1, f32[128,512]{1,0:T(8,128)} %warmth.1, s32[128,512]{1,0:T(8,128)} %classes.1, f32[1,512]{1,0:T(1,128)} %bitcast.3, s32[2,128]{1,0:T(2,128)} %couplings.1, f32[1,8]{1,0:T(1,128)} %bitcast.4, ...), custom_call_target="tpu_custom_call" | custom-call | flops 2000000 | bytes 2000000 | tf_op jit(solution)/shard_map/pack/pallas_call | solution.py:589
  2.2 20.1 %all_to_all.10.got = f32[16,13,8,128]{3,2,1,0:T(8,128)S(1)} all-to-all(f32[16,13,8,128]{3,2,1,0:T(8,128)S(1)} %get-tuple-element.50), channel_id=1, replica_groups={{0,14,2,12,4,10,6,8,1,15,3,13,5,11,7,9},{16,30,18,28,20,26,22,24,17,31,..., dimensions={0} | all-to-all | bytes 1703936 | tf_op jit(solution)/shard_map/all_to_all | solution.py:603
  22.4 0.3 edges.3
  22.7 2.6 %collective-permute-start.2 = (f32[3,7,8,128]{3,2,1,0:T(8,128)S(1)}, f32[3,7,8,128]{3,2,1,0:T(8,128)S(1)}, u32[]{:S(2)}, u32[]{:S(2)}) collective-permute-start(f32[3,7,8,128]{3,2,1,0:T(8,128)S(1)} %get-tuple-element.86), channel_id=1, source_target_pairs={{0,16},{16,0},{1,17},{17,1},{2,18},{18,2},{3,19},{19,3},{4,20},{20... | collective-permute-start | bytes 258056 | tf_op jit(solution)/shard_map/ppermute | solution.py:613
  25.3 0.3 edges.2
  25.7 0.4 collective-permute-start
  26.0 0.3 masks.1.refs_0_
  26.3 0.4 first.3
  26.7 1.4 %team.6 = (f32[8,8,512]{2,1,0:T(8,128)S(1)}, f32[8,8,512]{2,1,0:T(8,128)S(1)}) custom-call(f32[22,8,128]{2,1,0:T(8,128)S(1)} %masks.1.refs_0_, f32[8,8,512]{2,1,0:T(8,128)S(1)} %get-tuple-element.74.head.refs_1_, f32[8,8,512]{2,1,0:T(8,128)S(1)} %get-tuple-element.75.warm.refs_2_, f32[8,8,512]{2,1,0:T(8,128)S(1)} %get-tuple-element.80.cond.refs_7_), custom_call_target="tpu_custom_call" | custom-call | flops 2000000 | bytes 2000000 | tf_op jit(solution)/shard_map/team/pallas_call | solution.py:589
  28.1 0.4 first.2
  28.5 1.4 %team.4 = (f32[8,8,512]{2,1,0:T(8,128)S(1)}, f32[8,8,512]{2,1,0:T(8,128)S(1)}) custom-call(f32[22,8,128]{2,1,0:T(8,128)S(1)} %masks.1.refs_0_, f32[8,8,512]{2,1,0:T(8,128)S(1)} %get-tuple-element.52.head.refs_1_, f32[8,8,512]{2,1,0:T(8,128)S(1)} %get-tuple-element.53.warm.refs_2_, f32[8,8,512]{2,1,0:T(8,128)S(1)} %get-tuple-element.58.cond.refs_7_), custom_call_target="tpu_custom_call" | custom-call | flops 2000000 | bytes 2000000 | tf_op jit(solution)/shard_map/team/pallas_call | solution.py:589
  29.8 1.4 %collective-permute-done.2.refs_13_.refs_15_ = f32[3,7,8,128]{3,2,1,0:T(8,128)S(1)} collective-permute-done((f32[3,7,8,128]{3,2,1,0:T(8,128)S(1)}, f32[3,7,8,128]{3,2,1,0:T(8,128)S(1)}, u32[]{:S(2)}, u32[]{:S(2)}) %collective-permute-start.2) | collective-permute-done | bytes 86048 | tf_op jit(solution)/shard_map/ppermute | solution.py:613
  31.2 1.0 %middle.3 = (f32[8,8,512]{2,1,0:T(8,128)S(1)}, f32[8,8,512]{2,1,0:T(8,128)S(1)}, f32[8,8,512]{2,1,0:T(8,128)S(1)}, f32[8,8,512]{2,1,0:T(8,128)S(1)}, f32[8,8,512...) custom-call(f32[22,8,128]{2,1,0:T(8,128)S(1)} %masks.1.refs_0_, ...), custom_call_target="tpu_custom_call" | custom-call | flops 2000000 | bytes 2000000 | tf_op jit(solution)/shard_map/middle/pallas_call | solution.py:589
  32.2 1.3 %collective-permute-start.3 = (f32[2,7,8,128]{3,2,1,0:T(8,128)S(1)}, f32[2,7,8,128]{3,2,1,0:T(8,128)S(1)}, u32[]{:S(2)}, u32[]{:S(2)}) collective-permute-start(f32[2,7,8,128]{3,2,1,0:T(8,128)S(1)} %get-tuple-element.95), channel_id=1, source_target_pairs={{0,16},{16,0},{1,17},{17,1},{2,18},{18,2},{3,19},{19,3},{4,20},{20... | collective-permute-start | bytes 172040 | tf_op jit(solution)/shard_map/ppermute | solution.py:613
  33.4 0.0 collective-permute-done.refs_13_.refs_15_
  33.5 1.0 %middle.2 = (f32[8,8,512]{2,1,0:T(8,128)S(1)}, f32[8,8,512]{2,1,0:T(8,128)S(1)}, f32[8,8,512]{2,1,0:T(8,128)S(1)}, f32[8,8,512]{2,1,0:T(8,128)S(1)}, f32[8,8,512...) custom-call(f32[22,8,128]{2,1,0:T(8,128)S(1)} %masks.1.refs_0_, ...), custom_call_target="tpu_custom_call" | custom-call | flops 2000000 | bytes 2000000 | tf_op jit(solution)/shard_map/middle/pallas_call | solution.py:589
  34.4 1.8 %collective-permute-start.1 = (f32[2,7,8,128]{3,2,1,0:T(8,128)S(1)}, f32[2,7,8,128]{3,2,1,0:T(8,128)S(1)}, u32[]{:S(2)}, u32[]{:S(2)}) collective-permute-start(f32[2,7,8,128]{3,2,1,0:T(8,128)S(1)} %get-tuple-element.73), channel_id=1, source_target_pairs={{0,16},{16,0},{1,17},{17,1},{2,18},{18,2},{3,19},{19,3},{4,20},{20... | collective-permute-start | bytes 172040 | tf_op jit(solution)/shard_map/ppermute | solution.py:613
  36.2 1.4 %team.7 = (f32[8,8,512]{2,1,0:T(8,128)S(1)}, f32[8,8,512]{2,1,0:T(8,128)S(1)}) custom-call(f32[22,8,128]{2,1,0:T(8,128)S(1)} %masks.1.refs_0_, f32[8,8,512]{2,1,0:T(8,128)S(1)} %get-tuple-element.87.head.refs_1_, f32[8,8,512]{2,1,0:T(8,128)S(1)} %get-tuple-element.88.warm.refs_2_, f32[8,8,512]{2,1,0:T(8,128)S(1)} %get-tuple-element.91.cond.refs_7_), custom_call_target="tpu_custom_call" | custom-call | flops 2000000 | bytes 2000000 | tf_op jit(solution)/shard_map/team/pallas_call | solution.py:589
  37.5 1.4 %team.5 = (f32[8,8,512]{2,1,0:T(8,128)S(1)}, f32[8,8,512]{2,1,0:T(8,128)S(1)}) custom-call(f32[22,8,128]{2,1,0:T(8,128)S(1)} %masks.1.refs_0_, f32[8,8,512]{2,1,0:T(8,128)S(1)} %get-tuple-element.65.head.refs_1_, f32[8,8,512]{2,1,0:T(8,128)S(1)} %get-tuple-element.66.warm.refs_2_, f32[8,8,512]{2,1,0:T(8,128)S(1)} %get-tuple-element.69.cond.refs_7_), custom_call_target="tpu_custom_call" | custom-call | flops 2000000 | bytes 2000000 | tf_op jit(solution)/shard_map/team/pallas_call | solution.py:589
  38.9 0.0 collective-permute-done.3.refs_13_
  38.9 0.9 %last.2.refs_16_ = f32[16,4,8,128]{3,2,1,0:T(8,128)S(1)} custom-call(f32[22,8,128]{2,1,0:T(8,128)S(1)} %masks.1.refs_0_, f32[8,8,512]{2,1,0:T(8,128)S(1)} %get-tuple-element.87.head.refs_1_, f32[8,8,512]{2,1,0:T(8,128)S(1)} %get-tuple-element.88.warm.refs_2_, f32[8,8,512]{2,1,0:T(8,128)S(1)} %get-tuple-element.77.refs_4_.refs_3_, ...), custom_call_target="tpu_custom_call" | custom-call | flops 2000000 | bytes 2000000 | tf_op jit(solution)/shard_map/last/pallas_call | solution.py:589
  39.8 0.0 collective-permute-done.1.refs_13_
  39.8 0.9 %last.3 = f32[16,8,8,128]{3,2,1,0:T(8,128)S(1)} custom-call(f32[22,8,128]{2,1,0:T(8,128)S(1)} %masks.1.refs_0_, f32[8,8,512]{2,1,0:T(8,128)S(1)} %get-tuple-element.65.head.refs_1_, f32[8,8,512]{2,1,0:T(8,128)S(1)} %get-tuple-element.66.warm.refs_2_, f32[8,8,512]{2,1,0:T(8,128)S(1)} %get-tuple-element.55.refs_4_.refs_3_, ...), custom_call_target="tpu_custom_call" | custom-call | flops 2000000 | bytes 2000000 | tf_op jit(solution)/shard_map/last/pallas_call | solution.py:589
  40.8 14.8 %all_to_all.11.got = f32[16,8,8,128]{3,2,1,0:T(8,128)S(1)} all-to-all(f32[16,8,8,128]{3,2,1,0:T(8,128)S(1)} %last.3), channel_id=1, replica_groups={{0,14,2,12,4,10,6,8,1,15,3,13,5,11,7,9},{16,30,18,28,20,26,22,24,17,31,..., dimensions={0} | all-to-all | bytes 1048576 | tf_op jit(solution)/shard_map/all_to_all | solution.py:603
  55.5 0.9 %unpack.1 = (f32[128,512]{1,0:T(8,128)}, f32[128,512]{1,0:T(8,128)}) custom-call(f32[16,8,8,128]{3,2,1,0:T(8,128)S(1)} %all_to_all.11.got), custom_call_target="tpu_custom_call" | custom-call | flops 2000000 | bytes 2000000 | tf_op jit(solution)/shard_map/unpack/pallas_call | solution.py:589
Async XLA Ops:
  22.7 8.5 %collective-permute-start.2 = (f32[3,7,8,128]{3,2,1,0:T(8,128)S(1)}, f32[3,7,8,128]{3,2,1,0:T(8,128)S(1)}, u32[]{:S(2)}, u32[]{:S(2)}) collective-permute-start(f32[3,7,8,128]{3,2,1,0:T(8,128)S(1)} %get-tuple-element.86), channel_id=1, source_target_pairs={{0,16},{16,0},{1,17},{17,1},{2,18},{18,2},{3,19},{19,3},{4,20},{20... | collective-permute-start | bytes 258056 | tf_op jit(solution)/shard_map/ppermute | solution.py:613
  25.7 7.8 %collective-permute-start = (f32[3,7,8,128]{3,2,1,0:T(8,128)S(1)}, f32[3,7,8,128]{3,2,1,0:T(8,128)S(1)}, u32[]{:S(2)}, u32[]{:S(2)}) collective-permute-start(f32[3,7,8,128]{3,2,1,0:T(8,128)S(1)} %get-tuple-element.64), channel_id=1, source_target_pairs={{0,16},{16,0},{1,17},{17,1},{2,18},{18,2},{3,19},{19,3},{4,20},{20... | collective-permute-start | bytes 258056 | tf_op jit(solution)/shard_map/ppermute | solution.py:613
  32.2 6.7 %collective-permute-start.3 = (f32[2,7,8,128]{3,2,1,0:T(8,128)S(1)}, f32[2,7,8,128]{3,2,1,0:T(8,128)S(1)}, u32[]{:S(2)}, u32[]{:S(2)}) collective-permute-start(f32[2,7,8,128]{3,2,1,0:T(8,128)S(1)} %get-tuple-element.95), channel_id=1, source_target_pairs={{0,16},{16,0},{1,17},{17,1},{2,18},{18,2},{3,19},{19,3},{4,20},{20... | collective-permute-start | bytes 172040 | tf_op jit(solution)/shard_map/ppermute | solution.py:613
  34.4 5.4 %collective-permute-start.1 = (f32[2,7,8,128]{3,2,1,0:T(8,128)S(1)}, f32[2,7,8,128]{3,2,1,0:T(8,128)S(1)}, u32[]{:S(2)}, u32[]{:S(2)}) collective-permute-start(f32[2,7,8,128]{3,2,1,0:T(8,128)S(1)} %get-tuple-element.73), channel_id=1, source_target_pairs={{0,16},{16,0},{1,17},{17,1},{2,18},{18,2},{3,19},{19,3},{4,20},{20... | collective-permute-start | bytes 172040 | tf_op jit(solution)/shard_map/ppermute | solution.py:613

commit v16 on v14

--- a/solution.py
+++ b/solution.py
@@ -20,6 +20,7 @@
 EDGE = PAIR_DEV * OWN
 VMEM_LIMIT = 32 * 1024 * 1024
 DISTANCES = range(1, PAIR_DEV + 1)
+COPIES = 4
 F32 = jnp.float32
 
 
@@ -193,21 +194,28 @@
 ):
     cells = out.shape[-1]
     quarters = 2 * CHUNKS
+    block = cells // COPIES
     into = []
-    rooms = (room.at[0], room.at[1], class_room, top, pairs, k_table, heat_table)
-    for f, field in enumerate((suction, warmth, classes, surface, couplings, k_sat, heat_cond)):
-        into.append(pltpu.make_async_copy(field, rooms[f], in_sems.at[f]))
+    for f, field in enumerate((suction, warmth, classes)):
+        target = (room.at[0], room.at[1], class_room)[f]
+        for i in range(COPIES):
+            here = pl.ds(i * block, block)
+            into.append(pltpu.make_async_copy(field.at[here], target.at[here], in_sems.at[f, i]))
+            into[-1].start()
+    for f, (field, target) in enumerate(((surface, top), (couplings, pairs), (k_sat, k_table), (heat_cond, heat_table))):
+        into.append(pltpu.make_async_copy(field, target, in_sems.at[3, f]))
         into[-1].start()
 
     def put(slot, value):
         out[:, slot] = value.T.reshape(TEAM, OWN, cells)
 
     for f in range(3):
-        into[f].wait()
+        for copy in into[f * COPIES : (f + 1) * COPIES]:
+            copy.wait()
         for q in range(quarters):
             lanes = slice(q * LANES, (q + 1) * LANES)
             put(f * quarters + q, class_room[:, lanes].astype(F32) if f == 2 else room[f, :, lanes])
-    for copy in into[3:]:
+    for copy in into[3 * COPIES :]:
         copy.wait()
     kinds = k_sat.shape[1]
     for c in range(kinds):
@@ -227,8 +235,11 @@
     for f, out in enumerate((suction, warmth)):
         for q in range(quarters):
             room[f, :, q * LANES : (q + 1) * LANES] = got[:, f * quarters + q].reshape(LANES, cells).T
-        sent.append(pltpu.make_async_copy(room.at[f], out, sems.at[f]))
-        sent[-1].start()
+        block = out.shape[0] // COPIES
+        for i in range(COPIES):
+            here = pl.ds(i * block, block)
+            sent.append(pltpu.make_async_copy(room.at[f, here], out.at[here], sems.at[f, i]))
+            sent[-1].start()
     for copy in sent:
         copy.wait()
 
@@ -390,7 +401,7 @@
             heat[j, :, l0] = 2.0 * (total[2] - total[3])
             heat[j, :, l1] = 2.0 * total[3]
 
-    lax.fori_loop(0, steps, step, None)
+    lax.fori_loop(0, steps, step, None, unroll=2)
 
 
 def cross_flows(cut, masks, mine, theirs):
@@ -628,7 +639,7 @@
             pltpu.VMEM(couplings.shape, couplings.dtype),
             pltpu.VMEM((1, kinds), F32),
             pltpu.VMEM((1, kinds), F32),
-            pltpu.SemaphoreType.DMA((7,)),
+            pltpu.SemaphoreType.DMA((4, COPIES)),
         ],
         specs=[hbm] * 7,
     )
@@ -706,7 +717,7 @@
             [(cells, width)] * 2,
             scratch=[
                 pltpu.VMEM((2, cells, width), F32),
-                pltpu.SemaphoreType.DMA((2,)),
+                pltpu.SemaphoreType.DMA((2, COPIES)),
             ],
             out_specs=[hbm, hbm],
         )

time: 56.6 us -> 56.8 us (level)
  Pallas kernels: 13.4 us -> 11.3 us
  waiting for transfers between devices: 2.07 us -> 3.67 us
  blocking collectives: 34.2 us -> 34.8 us
    pallas_call x15, Pallas kernels: 13.4 us -> 11.3 us  [call(): pl.pallas_call(kernel, out_shape=[jax.ShapeDtypeStruct(shape, F32) for sh...]
    ppermute x4, waiting for transfers between devices: 2.07 us -> 3.67 us  [swap(): return lax.ppermute(value, 'cols', pairs)]
    all_to_all x2, blocking collectives: 34.2 us -> 34.8 us  [exchange(): lax.all_to_all(tiles, 'cols', split_axis=0, concat_axis=0, tiled=True, ax...]
  transfers between devices with their start and end apart: 4 -> 4, of which waited for: 1 -> 3; matrix products, arithmetic and copies ran while one was open for 0% -> 0% of each run, Pallas kernels for 17% -> 13%
where the time goes in v16:
time: 56.8 us; the launch traced here: 56.5 us
  blocking collectives  34.8 us (61%)
  Pallas kernels  11.3 us (20%)
  starting transfers between devices  6.02 us (11%)
  waiting for transfers between devices  3.67 us (6%)
  between operations  0.71 us (1%)
    all_to_all x2, blocking collectives, exchange(): lax.all_to_all(tiles, 'cols', split_axis=0, concat_axis=0, tiled=True, ax...  34.8 us
    pallas_call x15, Pallas kernels, call(): pl.pallas_call(kernel, out_shape=[jax.ShapeDtypeStruct(shape, F32) for sh...  11.3 us
    ppermute x4, starting transfers between devices, swap(): return lax.ppermute(value, 'cols', pairs)  6.02 us
    ppermute x4, waiting for transfers between devices, swap(): return lax.ppermute(value, 'cols', pairs)  3.67 us
  transfers between devices with their start and end apart: 4, of which 3 were waited for; matrix products, arithmetic and copies ran while one was open for 0% of the time, Pallas kernels for 13%

profile of v16, /device:TPU:0, one launch (start us, length us, event | category | flops | bytes accessed | tf_op | source)
XLA Modules:
  0.0 56.5 jit_solution(5468754672045922951)
XLA Ops:
  0.6 1.6 %pack.1 = (f32[16,13,8,128]{3,2,1,0:T(8,128)S(1)}, f32[17,8,128]{2,1,0:T(8,128)S(1)}, f32[2,128]{1,0:T(2,128)S(1)}) custom-call(f32[128,512]{1,0:T(8,128)} %suction.1, f32[128,512]{1,0:T(8,128)} %warmth.1, s32[128,512]{1,0:T(8,128)} %classes.1, f32[1,512]{1,0:T(1,128)} %bitcast.3, s32[2,128]{1,0:T(2,128)} %couplings.1, f32[1,8]{1,0:T(1,128)} %bitcast.4, ...), custom_call_target="tpu_custom_call" | custom-call | flops 2000000 | bytes 2000000 | tf_op jit(solution)/shard_map/pack/pallas_call | solution.py:589
  2.3 20.1 %all_to_all.10.got = f32[16,13,8,128]{3,2,1,0:T(8,128)S(1)} all-to-all(f32[16,13,8,128]{3,2,1,0:T(8,128)S(1)} %get-tuple-element.50), channel_id=1, replica_groups={{0,1,2,3,4,5,6,7,8,9,10,11,12,13,14,15},{16,17,18,19,20,21,22,23,24,25,..., dimensions={0} | all-to-all | bytes 1703936 | tf_op jit(solution)/shard_map/all_to_all | solution.py:603
  22.4 0.3 edges.3
  22.8 2.6 %collective-permute-start.2 = (f32[3,7,8,128]{3,2,1,0:T(8,128)S(1)}, f32[3,7,8,128]{3,2,1,0:T(8,128)S(1)}, u32[]{:S(2)}, u32[]{:S(2)}) collective-permute-start(f32[3,7,8,128]{3,2,1,0:T(8,128)S(1)} %get-tuple-element.86), channel_id=1, source_target_pairs={{0,16},{16,0},{1,17},{17,1},{2,18},{18,2},{3,19},{19,3},{4,20},{20... | collective-permute-start | bytes 258056 | tf_op jit(solution)/shard_map/ppermute | solution.py:613
  25.4 0.3 edges.2
  25.7 0.4 collective-permute-start
  26.1 0.3 masks.1.refs_0_
  26.4 0.4 first.3
  26.8 0.8 %team.6 = (f32[8,8,512]{2,1,0:T(8,128)S(1)}, f32[8,8,512]{2,1,0:T(8,128)S(1)}) custom-call(f32[22,8,128]{2,1,0:T(8,128)S(1)} %masks.1.refs_0_, f32[8,8,512]{2,1,0:T(8,128)S(1)} %get-tuple-element.74.head.refs_1_, f32[8,8,512]{2,1,0:T(8,128)S(1)} %get-tuple-element.75.warm.refs_2_, f32[8,8,512]{2,1,0:T(8,128)S(1)} %get-tuple-element.80.cond.refs_7_), custom_call_target="tpu_custom_call" | custom-call | flops 2000000 | bytes 2000000 | tf_op jit(solution)/shard_map/team/pallas_call | solution.py:589
  27.6 0.4 first.2
  28.0 0.8 %team.4 = (f32[8,8,512]{2,1,0:T(8,128)S(1)}, f32[8,8,512]{2,1,0:T(8,128)S(1)}) custom-call(f32[22,8,128]{2,1,0:T(8,128)S(1)} %masks.1.refs_0_, f32[8,8,512]{2,1,0:T(8,128)S(1)} %get-tuple-element.52.head.refs_1_, f32[8,8,512]{2,1,0:T(8,128)S(1)} %get-tuple-element.53.warm.refs_2_, f32[8,8,512]{2,1,0:T(8,128)S(1)} %get-tuple-element.58.cond.refs_7_), custom_call_target="tpu_custom_call" | custom-call | flops 2000000 | bytes 2000000 | tf_op jit(solution)/shard_map/team/pallas_call | solution.py:589
  28.8 3.1 %collective-permute-done.2.refs_13_.refs_15_ = f32[3,7,8,128]{3,2,1,0:T(8,128)S(1)} collective-permute-done((f32[3,7,8,128]{3,2,1,0:T(8,128)S(1)}, f32[3,7,8,128]{3,2,1,0:T(8,128)S(1)}, u32[]{:S(2)}, u32[]{:S(2)}) %collective-permute-start.2) | collective-permute-done | bytes 86048 | tf_op jit(solution)/shard_map/ppermute | solution.py:613
  31.9 1.0 %middle.3 = (f32[8,8,512]{2,1,0:T(8,128)S(1)}, f32[8,8,512]{2,1,0:T(8,128)S(1)}, f32[8,8,512]{2,1,0:T(8,128)S(1)}, f32[8,8,512]{2,1,0:T(8,128)S(1)}, f32[8,8,512...) custom-call(f32[22,8,128]{2,1,0:T(8,128)S(1)} %masks.1.refs_0_, ...), custom_call_target="tpu_custom_call" | custom-call | flops 2000000 | bytes 2000000 | tf_op jit(solution)/shard_map/middle/pallas_call | solution.py:589
  32.9 0.1 collective-permute-start.3
  33.0 0.0 collective-permute-done.refs_13_.refs_15_
  33.0 1.0 %middle.2 = (f32[8,8,512]{2,1,0:T(8,128)S(1)}, f32[8,8,512]{2,1,0:T(8,128)S(1)}, f32[8,8,512]{2,1,0:T(8,128)S(1)}, f32[8,8,512]{2,1,0:T(8,128)S(1)}, f32[8,8,512...) custom-call(f32[22,8,128]{2,1,0:T(8,128)S(1)} %masks.1.refs_0_, ...), custom_call_target="tpu_custom_call" | custom-call | flops 2000000 | bytes 2000000 | tf_op jit(solution)/shard_map/middle/pallas_call | solution.py:589
  34.0 2.9 %collective-permute-start.1 = (f32[2,7,8,128]{3,2,1,0:T(8,128)S(1)}, f32[2,7,8,128]{3,2,1,0:T(8,128)S(1)}, u32[]{:S(2)}, u32[]{:S(2)}) collective-permute-start(f32[2,7,8,128]{3,2,1,0:T(8,128)S(1)} %get-tuple-element.73), channel_id=1, source_target_pairs={{0,16},{16,0},{1,17},{17,1},{2,18},{18,2},{3,19},{19,3},{4,20},{20... | collective-permute-start | bytes 172040 | tf_op jit(solution)/shard_map/ppermute | solution.py:613
  36.9 0.8 %team.7 = (f32[8,8,512]{2,1,0:T(8,128)S(1)}, f32[8,8,512]{2,1,0:T(8,128)S(1)}) custom-call(f32[22,8,128]{2,1,0:T(8,128)S(1)} %masks.1.refs_0_, f32[8,8,512]{2,1,0:T(8,128)S(1)} %get-tuple-element.87.head.refs_1_, f32[8,8,512]{2,1,0:T(8,128)S(1)} %get-tuple-element.88.warm.refs_2_, f32[8,8,512]{2,1,0:T(8,128)S(1)} %get-tuple-element.91.cond.refs_7_), custom_call_target="tpu_custom_call" | custom-call | flops 2000000 | bytes 2000000 | tf_op jit(solution)/shard_map/team/pallas_call | solution.py:589
  37.7 0.8 %team.5 = (f32[8,8,512]{2,1,0:T(8,128)S(1)}, f32[8,8,512]{2,1,0:T(8,128)S(1)}) custom-call(f32[22,8,128]{2,1,0:T(8,128)S(1)} %masks.1.refs_0_, f32[8,8,512]{2,1,0:T(8,128)S(1)} %get-tuple-element.65.head.refs_1_, f32[8,8,512]{2,1,0:T(8,128)S(1)} %get-tuple-element.66.warm.refs_2_, f32[8,8,512]{2,1,0:T(8,128)S(1)} %get-tuple-element.69.cond.refs_7_), custom_call_target="tpu_custom_call" | custom-call | flops 2000000 | bytes 2000000 | tf_op jit(solution)/shard_map/team/pallas_call | solution.py:589
  38.6 0.2 collective-permute-done.3.refs_13_
  38.7 0.9 %last.2.refs_16_ = f32[16,4,8,128]{3,2,1,0:T(8,128)S(1)} custom-call(f32[22,8,128]{2,1,0:T(8,128)S(1)} %masks.1.refs_0_, f32[8,8,512]{2,1,0:T(8,128)S(1)} %get-tuple-element.87.head.refs_1_, f32[8,8,512]{2,1,0:T(8,128)S(1)} %get-tuple-element.88.warm.refs_2_, f32[8,8,512]{2,1,0:T(8,128)S(1)} %get-tuple-element.77.refs_4_.refs_3_, ...), custom_call_target="tpu_custom_call" | custom-call | flops 2000000 | bytes 2000000 | tf_op jit(solution)/shard_map/last/pallas_call | solution.py:589
  39.7 0.3 collective-permute-done.1.refs_13_
  40.0 0.9 %last.3 = f32[16,8,8,128]{3,2,1,0:T(8,128)S(1)} custom-call(f32[22,8,128]{2,1,0:T(8,128)S(1)} %masks.1.refs_0_, f32[8,8,512]{2,1,0:T(8,128)S(1)} %get-tuple-element.65.head.refs_1_, f32[8,8,512]{2,1,0:T(8,128)S(1)} %get-tuple-element.66.warm.refs_2_, f32[8,8,512]{2,1,0:T(8,128)S(1)} %get-tuple-element.55.refs_4_.refs_3_, ...), custom_call_target="tpu_custom_call" | custom-call | flops 2000000 | bytes 2000000 | tf_op jit(solution)/shard_map/last/pallas_call | solution.py:589
  40.9 14.7 %all_to_all.11.got = f32[16,8,8,128]{3,2,1,0:T(8,128)S(1)} all-to-all(f32[16,8,8,128]{3,2,1,0:T(8,128)S(1)} %last.3), channel_id=1, replica_groups={{0,1,2,3,4,5,6,7,8,9,10,11,12,13,14,15},{16,17,18,19,20,21,22,23,24,25,..., dimensions={0} | all-to-all | bytes 1048576 | tf_op jit(solution)/shard_map/all_to_all | solution.py:603
  55.6 1.0 %unpack.1 = (f32[128,512]{1,0:T(8,128)}, f32[128,512]{1,0:T(8,128)}) custom-call(f32[16,8,8,128]{3,2,1,0:T(8,128)S(1)} %all_to_all.11.got), custom_call_target="tpu_custom_call" | custom-call | flops 2000000 | bytes 2000000 | tf_op jit(solution)/shard_map/unpack/pallas_call | solution.py:589
Async XLA Ops:
  22.8 9.2 %collective-permute-start.2 = (f32[3,7,8,128]{3,2,1,0:T(8,128)S(1)}, f32[3,7,8,128]{3,2,1,0:T(8,128)S(1)}, u32[]{:S(2)}, u32[]{:S(2)}) collective-permute-start(f32[3,7,8,128]{3,2,1,0:T(8,128)S(1)} %get-tuple-element.86), channel_id=1, source_target_pairs={{0,16},{16,0},{1,17},{17,1},{2,18},{18,2},{3,19},{19,3},{4,20},{20... | collective-permute-start | bytes 258056 | tf_op jit(solution)/shard_map/ppermute | solution.py:613
  25.7 7.3 %collective-permute-start = (f32[3,7,8,128]{3,2,1,0:T(8,128)S(1)}, f32[3,7,8,128]{3,2,1,0:T(8,128)S(1)}, u32[]{:S(2)}, u32[]{:S(2)}) collective-permute-start(f32[3,7,8,128]{3,2,1,0:T(8,128)S(1)} %get-tuple-element.64), channel_id=1, source_target_pairs={{0,16},{16,0},{1,17},{17,1},{2,18},{18,2},{3,19},{19,3},{4,20},{20... | collective-permute-start | bytes 258056 | tf_op jit(solution)/shard_map/ppermute | solution.py:613
  32.9 5.8 %collective-permute-start.3 = (f32[2,7,8,128]{3,2,1,0:T(8,128)S(1)}, f32[2,7,8,128]{3,2,1,0:T(8,128)S(1)}, u32[]{:S(2)}, u32[]{:S(2)}) collective-permute-start(f32[2,7,8,128]{3,2,1,0:T(8,128)S(1)} %get-tuple-element.95), channel_id=1, source_target_pairs={{0,16},{16,0},{1,17},{17,1},{2,18},{18,2},{3,19},{19,3},{4,20},{20... | collective-permute-start | bytes 172040 | tf_op jit(solution)/shard_map/ppermute | solution.py:613
  34.0 6.0 %collective-permute-start.1 = (f32[2,7,8,128]{3,2,1,0:T(8,128)S(1)}, f32[2,7,8,128]{3,2,1,0:T(8,128)S(1)}, u32[]{:S(2)}, u32[]{:S(2)}) collective-permute-start(f32[2,7,8,128]{3,2,1,0:T(8,128)S(1)} %get-tuple-element.73), channel_id=1, source_target_pairs={{0,16},{16,0},{1,17},{17,1},{2,18},{18,2},{3,19},{19,3},{4,20},{20... | collective-permute-start | bytes 172040 | tf_op jit(solution)/shard_map/ppermute | solution.py:613

commit v17 on v14

--- a/solution.py
+++ b/solution.py
@@ -390,7 +390,7 @@
             heat[j, :, l0] = 2.0 * (total[2] - total[3])
             heat[j, :, l1] = 2.0 * total[3]
 
-    lax.fori_loop(0, steps, step, None)
+    lax.fori_loop(0, steps, step, None, unroll=2)
 
 
 def cross_flows(cut, masks, mine, theirs):
@@ -676,8 +676,9 @@
             scratch=[room] * 5,
         )
         second.append(values[:5])
-        mine, sent = values[5 : 5 + cuts], values[5 + cuts :]
-        later.append((mine, [swap(cut, n, v) for cut, v in enumerate(sent)]))
+        later.append((values[5 : 5 + cuts], values[5 + cuts :]))
+    leaving = lax.optimization_barrier([sent for _, sent in later])
+    later = [(mine, [swap(cut, n, v) for cut, v in enumerate(sent)]) for (mine, _), sent in zip(later, leaving)]
 
     done = []
     for c in range(CHUNKS):

time: 56.6 us -> 56.8 us (level)
  waiting for transfers between devices: 2.07 us -> 5.21 us
  Pallas kernels: 13.4 us -> 11.2 us
  blocking collectives: 34.2 us -> 33.5 us
    ppermute x4, waiting for transfers between devices: 2.07 us -> 5.21 us  [swap(): return lax.ppermute(value, 'cols', pairs)]
    pallas_call x15, Pallas kernels: 13.4 us -> 11.2 us  [call(): pl.pallas_call(kernel, out_shape=[jax.ShapeDtypeStruct(shape, F32) for sh...]
    all_to_all x2, blocking collectives: 34.2 us -> 33.5 us  [exchange(): lax.all_to_all(tiles, 'cols', split_axis=0, concat_axis=0, tiled=True, ax...]
  transfers between devices with their start and end apart: 4 -> 4, of which waited for: 1 -> 3; matrix products, arithmetic and copies ran while one was open for 0% -> 0% of each run, Pallas kernels for 17% -> 11%
where the time goes in v17:
time: 56.8 us; the launch traced here: 56.6 us
  blocking collectives  33.5 us (59%)
  Pallas kernels  11.2 us (20%)
  starting transfers between devices  6 us (11%)
  waiting for transfers between devices  5.21 us (9%)
  between operations  0.72 us (1%)
    all_to_all x2, blocking collectives, exchange(): lax.all_to_all(tiles, 'cols', split_axis=0, concat_axis=0, tiled=True, ax...  33.5 us
    pallas_call x15, Pallas kernels, call(): pl.pallas_call(kernel, out_shape=[jax.ShapeDtypeStruct(shape, F32) for sh...  11.2 us
    ppermute x4, starting transfers between devices, swap(): return lax.ppermute(value, 'cols', pairs)  6 us
    ppermute x4, waiting for transfers between devices, swap(): return lax.ppermute(value, 'cols', pairs)  5.21 us
  transfers between devices with their start and end apart: 4, of which 3 were waited for; matrix products, arithmetic and copies ran while one was open for 0% of the time, Pallas kernels for 11%

profile of v17, /device:TPU:0, one launch (start us, length us, event | category | flops | bytes accessed | tf_op | source)
XLA Modules:
  0.0 56.6 jit_solution(12734793969560642845)
XLA Ops:
  0.6 1.6 %pack.1 = (f32[16,13,8,128]{3,2,1,0:T(8,128)S(1)}, f32[17,8,128]{2,1,0:T(8,128)S(1)}, f32[2,128]{1,0:T(2,128)S(1)}) custom-call(f32[128,512]{1,0:T(8,128)} %suction.1, f32[128,512]{1,0:T(8,128)} %warmth.1, s32[128,512]{1,0:T(8,128)} %classes.1, f32[1,512]{1,0:T(1,128)} %bitcast.3, s32[2,128]{1,0:T(2,128)} %couplings.1, f32[1,8]{1,0:T(1,128)} %bitcast.4, ...), custom_call_target="tpu_custom_call" | custom-call | flops 2000000 | bytes 2000000 | tf_op jit(solution)/shard_map/pack/pallas_call | solution.py:578
  2.2 20.1 %all_to_all.10.got = f32[16,13,8,128]{3,2,1,0:T(8,128)S(1)} all-to-all(f32[16,13,8,128]{3,2,1,0:T(8,128)S(1)} %get-tuple-element.52), channel_id=1, replica_groups={{0,1,2,3,4,5,6,7,8,9,10,11,12,13,14,15},{16,17,18,19,20,21,22,23,24,25,..., dimensions={0} | all-to-all | bytes 1703936 | tf_op jit(solution)/shard_map/all_to_all | solution.py:592
  22.4 0.3 edges.2
  22.7 2.6 %collective-permute-start = (f32[3,7,8,128]{3,2,1,0:T(8,128)S(1)}, f32[3,7,8,128]{3,2,1,0:T(8,128)S(1)}, u32[]{:S(2)}, u32[]{:S(2)}) collective-permute-start(f32[3,7,8,128]{3,2,1,0:T(8,128)S(1)} %get-tuple-element.66), channel_id=1, source_target_pairs={{0,16},{16,0},{1,17},{17,1},{2,18},{18,2},{3,19},{19,3},{4,20},{20... | collective-permute-start | bytes 258056 | tf_op jit(solution)/shard_map/ppermute | solution.py:602
  25.3 0.3 edges.3
  25.6 0.4 collective-permute-start.1
  26.0 0.3 masks.1.refs_0_
  26.3 0.4 first.2
  26.7 0.8 %team.4 = (f32[8,8,512]{2,1,0:T(8,128)S(1)}, f32[8,8,512]{2,1,0:T(8,128)S(1)}) custom-call(f32[22,8,128]{2,1,0:T(8,128)S(1)} %masks.1.refs_0_, f32[8,8,512]{2,1,0:T(8,128)S(1)} %get-tuple-element.54.head.refs_1_, f32[8,8,512]{2,1,0:T(8,128)S(1)} %get-tuple-element.55.warm.refs_2_, f32[8,8,512]{2,1,0:T(8,128)S(1)} %get-tuple-element.60.cond.refs_7_), custom_call_target="tpu_custom_call" | custom-call | flops 2000000 | bytes 2000000 | tf_op jit(solution)/shard_map/team/pallas_call | solution.py:578
  27.5 0.4 first.3
  27.9 0.8 %team.6 = (f32[8,8,512]{2,1,0:T(8,128)S(1)}, f32[8,8,512]{2,1,0:T(8,128)S(1)}) custom-call(f32[22,8,128]{2,1,0:T(8,128)S(1)} %masks.1.refs_0_, f32[8,8,512]{2,1,0:T(8,128)S(1)} %get-tuple-element.75.head.refs_1_, f32[8,8,512]{2,1,0:T(8,128)S(1)} %get-tuple-element.76.warm.refs_2_, f32[8,8,512]{2,1,0:T(8,128)S(1)} %get-tuple-element.81.cond.refs_7_), custom_call_target="tpu_custom_call" | custom-call | flops 2000000 | bytes 2000000 | tf_op jit(solution)/shard_map/team/pallas_call | solution.py:578
  28.7 3.1 %collective-permute-done.refs_13_.refs_15_ = f32[3,7,8,128]{3,2,1,0:T(8,128)S(1)} collective-permute-done((f32[3,7,8,128]{3,2,1,0:T(8,128)S(1)}, f32[3,7,8,128]{3,2,1,0:T(8,128)S(1)}, u32[]{:S(2)}, u32[]{:S(2)}) %collective-permute-start) | collective-permute-done | bytes 86048 | tf_op jit(solution)/shard_map/ppermute | solution.py:602
  31.9 1.0 %middle.2 = (f32[8,8,512]{2,1,0:T(8,128)S(1)}, f32[8,8,512]{2,1,0:T(8,128)S(1)}, f32[8,8,512]{2,1,0:T(8,128)S(1)}, f32[8,8,512]{2,1,0:T(8,128)S(1)}, f32[8,8,512...) custom-call(f32[22,8,128]{2,1,0:T(8,128)S(1)} %masks.1.refs_0_, ...), custom_call_target="tpu_custom_call" | custom-call | flops 2000000 | bytes 2000000 | tf_op jit(solution)/shard_map/middle/pallas_call | solution.py:578
  32.8 0.1 collective-permute-done.1.refs_13_.refs_15_
  32.9 1.0 %middle.3 = (f32[8,8,512]{2,1,0:T(8,128)S(1)}, f32[8,8,512]{2,1,0:T(8,128)S(1)}, f32[8,8,512]{2,1,0:T(8,128)S(1)}, f32[8,8,512]{2,1,0:T(8,128)S(1)}, f32[8,8,512...) custom-call(f32[22,8,128]{2,1,0:T(8,128)S(1)} %masks.1.refs_0_, ...), custom_call_target="tpu_custom_call" | custom-call | flops 2000000 | bytes 2000000 | tf_op jit(solution)/shard_map/middle/pallas_call | solution.py:578
  33.9 0.1 collective-permute-start.3
  34.0 2.9 %collective-permute-start.2 = (f32[2,7,8,128]{3,2,1,0:T(8,128)S(1)}, f32[2,7,8,128]{3,2,1,0:T(8,128)S(1)}, u32[]{:S(2)}, u32[]{:S(2)}) collective-permute-start(f32[2,7,8,128]{3,2,1,0:T(8,128)S(1)} %get-tuple-element.90), channel_id=1, source_target_pairs={{0,16},{16,0},{1,17},{17,1},{2,18},{18,2},{3,19},{19,3},{4,20},{20... | collective-permute-start | bytes 172040 | tf_op jit(solution)/shard_map/ppermute | solution.py:602
  36.9 0.8 %team.5 = (f32[8,8,512]{2,1,0:T(8,128)S(1)}, f32[8,8,512]{2,1,0:T(8,128)S(1)}) custom-call(f32[22,8,128]{2,1,0:T(8,128)S(1)} %masks.1.refs_0_, f32[8,8,512]{2,1,0:T(8,128)S(1)} %get-tuple-element.67.head.refs_1_, f32[8,8,512]{2,1,0:T(8,128)S(1)} %get-tuple-element.68.warm.refs_2_, f32[8,8,512]{2,1,0:T(8,128)S(1)} %get-tuple-element.71.cond.refs_7_), custom_call_target="tpu_custom_call" | custom-call | flops 2000000 | bytes 2000000 | tf_op jit(solution)/shard_map/team/pallas_call | solution.py:578
  37.7 0.8 %team.7 = (f32[8,8,512]{2,1,0:T(8,128)S(1)}, f32[8,8,512]{2,1,0:T(8,128)S(1)}) custom-call(f32[22,8,128]{2,1,0:T(8,128)S(1)} %masks.1.refs_0_, f32[8,8,512]{2,1,0:T(8,128)S(1)} %get-tuple-element.91.head.refs_1_, f32[8,8,512]{2,1,0:T(8,128)S(1)} %get-tuple-element.92.warm.refs_2_, f32[8,8,512]{2,1,0:T(8,128)S(1)} %get-tuple-element.95.cond.refs_7_), custom_call_target="tpu_custom_call" | custom-call | flops 2000000 | bytes 2000000 | tf_op jit(solution)/shard_map/team/pallas_call | solution.py:578
  38.5 2.0 %collective-permute-done.3.refs_13_ = f32[2,7,8,128]{3,2,1,0:T(8,128)S(1)} collective-permute-done((f32[2,7,8,128]{3,2,1,0:T(8,128)S(1)}, f32[2,7,8,128]{3,2,1,0:T(8,128)S(1)}, u32[]{:S(2)}, u32[]{:S(2)}) %collective-permute-start.3) | collective-permute-done | bytes 57376 | tf_op jit(solution)/shard_map/ppermute | solution.py:602
  40.5 0.9 %last.2.refs_16_ = f32[16,4,8,128]{3,2,1,0:T(8,128)S(1)} custom-call(f32[22,8,128]{2,1,0:T(8,128)S(1)} %masks.1.refs_0_, f32[8,8,512]{2,1,0:T(8,128)S(1)} %get-tuple-element.91.head.refs_1_, f32[8,8,512]{2,1,0:T(8,128)S(1)} %get-tuple-element.92.warm.refs_2_, f32[8,8,512]{2,1,0:T(8,128)S(1)} %get-tuple-element.78.refs_4_.refs_3_, ...), custom_call_target="tpu_custom_call" | custom-call | flops 2000000 | bytes 2000000 | tf_op jit(solution)/shard_map/last/pallas_call | solution.py:578
  41.4 0.0 collective-permute-done.2.refs_13_
  41.4 0.9 %last.3 = f32[16,8,8,128]{3,2,1,0:T(8,128)S(1)} custom-call(f32[22,8,128]{2,1,0:T(8,128)S(1)} %masks.1.refs_0_, f32[8,8,512]{2,1,0:T(8,128)S(1)} %get-tuple-element.67.head.refs_1_, f32[8,8,512]{2,1,0:T(8,128)S(1)} %get-tuple-element.68.warm.refs_2_, f32[8,8,512]{2,1,0:T(8,128)S(1)} %get-tuple-element.57.refs_4_.refs_3_, ...), custom_call_target="tpu_custom_call" | custom-call | flops 2000000 | bytes 2000000 | tf_op jit(solution)/shard_map/last/pallas_call | solution.py:578
  42.3 13.3 %all_to_all.11.got = f32[16,8,8,128]{3,2,1,0:T(8,128)S(1)} all-to-all(f32[16,8,8,128]{3,2,1,0:T(8,128)S(1)} %last.3), channel_id=1, replica_groups={{0,1,2,3,4,5,6,7,8,9,10,11,12,13,14,15},{16,17,18,19,20,21,22,23,24,25,..., dimensions={0} | all-to-all | bytes 1048576 | tf_op jit(solution)/shard_map/all_to_all | solution.py:592
  55.7 0.9 %unpack.1 = (f32[128,512]{1,0:T(8,128)}, f32[128,512]{1,0:T(8,128)}) custom-call(f32[16,8,8,128]{3,2,1,0:T(8,128)S(1)} %all_to_all.11.got), custom_call_target="tpu_custom_call" | custom-call | flops 2000000 | bytes 2000000 | tf_op jit(solution)/shard_map/unpack/pallas_call | solution.py:578
Async XLA Ops:
  22.7 9.2 %collective-permute-start = (f32[3,7,8,128]{3,2,1,0:T(8,128)S(1)}, f32[3,7,8,128]{3,2,1,0:T(8,128)S(1)}, u32[]{:S(2)}, u32[]{:S(2)}) collective-permute-start(f32[3,7,8,128]{3,2,1,0:T(8,128)S(1)} %get-tuple-element.66), channel_id=1, source_target_pairs={{0,16},{16,0},{1,17},{17,1},{2,18},{18,2},{3,19},{19,3},{4,20},{20... | collective-permute-start | bytes 258056 | tf_op jit(solution)/shard_map/ppermute | solution.py:602
  25.6 7.3 %collective-permute-start.1 = (f32[3,7,8,128]{3,2,1,0:T(8,128)S(1)}, f32[3,7,8,128]{3,2,1,0:T(8,128)S(1)}, u32[]{:S(2)}, u32[]{:S(2)}) collective-permute-start(f32[3,7,8,128]{3,2,1,0:T(8,128)S(1)} %get-tuple-element.87), channel_id=1, source_target_pairs={{0,16},{16,0},{1,17},{17,1},{2,18},{18,2},{3,19},{19,3},{4,20},{20... | collective-permute-start | bytes 258056 | tf_op jit(solution)/shard_map/ppermute | solution.py:602
  33.9 6.6 %collective-permute-start.3 = (f32[2,7,8,128]{3,2,1,0:T(8,128)S(1)}, f32[2,7,8,128]{3,2,1,0:T(8,128)S(1)}, u32[]{:S(2)}, u32[]{:S(2)}) collective-permute-start(f32[2,7,8,128]{3,2,1,0:T(8,128)S(1)} %get-tuple-element.99), channel_id=1, source_target_pairs={{0,16},{16,0},{1,17},{17,1},{2,18},{18,2},{3,19},{19,3},{4,20},{20... | collective-permute-start | bytes 172040 | tf_op jit(solution)/shard_map/ppermute | solution.py:602
  34.0 7.4 %collective-permute-start.2 = (f32[2,7,8,128]{3,2,1,0:T(8,128)S(1)}, f32[2,7,8,128]{3,2,1,0:T(8,128)S(1)}, u32[]{:S(2)}, u32[]{:S(2)}) collective-permute-start(f32[2,7,8,128]{3,2,1,0:T(8,128)S(1)} %get-tuple-element.90), channel_id=1, source_target_pairs={{0,16},{16,0},{1,17},{17,1},{2,18},{18,2},{3,19},{19,3},{4,20},{20... | collective-permute-start | bytes 172040 | tf_op jit(solution)/shard_map/ppermute | solution.py:602

commit v18 on v14

--- a/solution.py
+++ b/solution.py
@@ -307,7 +307,7 @@
 
 
 def first_kernel(
-    chunk, kinds, got, consts, head, warm, perm, conduct, wet, melt, cond, energy, top, load
+    chunk, kinds, got, consts, head, warm, perm, conduct, wet, energy, top, load
 ):
     cells = got.shape[-1]
     steps = head.shape[0]
@@ -347,12 +347,10 @@
         m = 0.05 + 0.4 * s
         head[j], warm[j], perm[j], conduct[j] = h, t, k, lam
         wet[j] = s
-        melt[j] = f
-        cond[j] = k * (f * s * s + 0.02)
         energy[j] = (1.0 + 2.0 * m) * t + 2.0 * m * f
 
 
-def team_kernel(masks, head, warm, cond, water, heat):
+def team_kernel(masks, head, warm, perm, wet, melt, cond, water, heat):
     steps = head.shape[0]
     upper = [masks[s - 1] > 0.5 for s in DISTANCES]
     lower = [masks[PAIR_DEV + s - 1] > 0.5 for s in DISTANCES]
@@ -362,7 +360,13 @@
             l0, l1 = lanes_of(g, 0), lanes_of(g, 1)
             h0, h1 = head[j, :, l0], head[j, :, l1]
             t0, t1 = warm[j, :, l0], warm[j, :, l1]
-            c0, c1 = cond[j, :, l0], cond[j, :, l1]
+            conductivity = []
+            for t, lanes in ((t0, l0), (t1, l1)):
+                s, f = wet[j, :, lanes], sigmoid(2.0 * t)
+                melt[j, :, lanes] = f
+                conductivity.append(perm[j, :, lanes] * (f * s * s + 0.02))
+                cond[j, :, lanes] = conductivity[-1]
+            c0, c1 = conductivity
             total = None
             for s in DISTANCES:
                 up, low = upper[s - 1], lower[s - 1]
@@ -390,7 +394,7 @@
             heat[j, :, l0] = 2.0 * (total[2] - total[3])
             heat[j, :, l1] = 2.0 * total[3]
 
-    lax.fori_loop(0, steps, step, None)
+    lax.fori_loop(0, steps, step, None, unroll=2)
 
 
 def cross_flows(cut, masks, mine, theirs):
@@ -503,18 +507,15 @@
 
 
 def middle_kernel(cuts, *refs):
-    masks, head, warm, perm, conduct, wet, melt, cond, energy, top, water, heat = refs[:12]
-    own, far = refs[12 : 12 + cuts], refs[12 + cuts : 12 + 2 * cuts]
-    new_head, new_warm, new_wet, new_melt, new_cond = refs[12 + 2 * cuts : 17 + 2 * cuts]
-    halos, sent = refs[17 + 2 * cuts : 17 + 3 * cuts], refs[17 + 3 * cuts : 17 + 4 * cuts]
-    inflow, warm_inflow, ratio, lead, value = refs[17 + 4 * cuts :]
+    masks, head, warm, conduct, wet, melt, cond, energy, top, water, heat = refs[:11]
+    own, far = refs[11 : 11 + cuts], refs[11 + cuts : 11 + 2 * cuts]
+    new_head, new_warm, new_wet = refs[11 + 2 * cuts : 14 + 2 * cuts]
+    halos, sent = refs[14 + 2 * cuts : 14 + 3 * cuts], refs[14 + 3 * cuts : 14 + 4 * cuts]
+    inflow, warm_inflow, ratio, lead, value = refs[14 + 4 * cuts :]
     steps = head.shape[0]
     packed = {}
 
     def finish(j, t):
-        s, f = new_wet[j], sigmoid(2.0 * t)
-        new_melt[j] = f
-        new_cond[j] = perm[j] * (f * s * s + 0.02)
         for cut in range(cuts):
             for i, v in enumerate((new_head[j], t)):
                 packed[cut, i, j] = halo_of(cut, v)
@@ -652,7 +653,7 @@
             functools.partial(first_kernel, c, kinds),
             "first",
             (got, consts),
-            [column] * 8 + [(1, ALL)],
+            [column] * 6 + [(1, ALL)],
             scratch=[pltpu.VMEM((6, cells, LANES), F32)],
         )
         for c in range(CHUNKS)
@@ -661,29 +662,30 @@
     for c in range(CHUNKS):
         mine, sent = edges[c][:cuts], edges[c][cuts:]
         sides.append((mine, [swap(cut, n, v) for cut, v in enumerate(sent)]))
-        flows.append(tuple(call(team_kernel, "team", (masks, first[c][0], first[c][1], first[c][6]), [column] * 2)))
+        head, warm, perm, conduct, wet, energy, surface = first[c]
+        flows.append(call(team_kernel, "team", (masks, head, warm, perm, wet), [column] * 4))
 
     second, later = [], []
     for c in range(CHUNKS):
-        head, warm, perm, conduct, wet, melt, cond, energy, surface = first[c]
-        water, heat = flows[c]
+        head, warm, perm, conduct, wet, energy, surface = first[c]
+        melt, cond, water, heat = flows[c]
         mine, theirs = sides[c]
         values = call(
             functools.partial(middle_kernel, cuts),
             "middle",
-            (masks, head, warm, perm, conduct, wet, melt, cond, energy, surface, water, heat, *mine, *theirs),
-            [column] * 5 + [(2,) + halo] * cuts + [(2,) + squeezed] * cuts,
+            (masks, head, warm, conduct, wet, melt, cond, energy, surface, water, heat, *mine, *theirs),
+            [column] * 3 + [(2,) + halo] * cuts + [(2,) + squeezed] * cuts,
             scratch=[room] * 5,
         )
-        second.append(values[:5])
-        mine, sent = values[5 : 5 + cuts], values[5 + cuts :]
+        second.append(values[:3])
+        mine, sent = values[3 : 3 + cuts], values[3 + cuts :]
         later.append((mine, [swap(cut, n, v) for cut, v in enumerate(sent)]))
 
     done = []
     for c in range(CHUNKS):
-        conduct, stored, energy, surface = first[c][3], first[c][4], first[c][7], first[c][8]
-        head, warm, wet, melt, cond = second[c]
-        water, heat = call(team_kernel, "team", (masks, head, warm, cond), [column] * 2)
+        _, _, perm, conduct, stored, energy, surface = first[c]
+        head, warm, wet = second[c]
+        melt, cond, water, heat = call(team_kernel, "team", (masks, head, warm, perm, wet), [column] * 4)
         mine, theirs = later[c]
         mine_k, theirs_k = sides[c]
         final = c == CHUNKS - 1

time: 56.6 us -> 56.6 us (level)
  Pallas kernels: 13.4 us -> 11.4 us
  waiting for transfers between devices: 2.07 us -> 3.51 us
  blocking collectives: 34.2 us -> 34.8 us
    pallas_call x15, Pallas kernels: 13.4 us -> 11.4 us  [call(): pl.pallas_call(kernel, out_shape=[jax.ShapeDtypeStruct(shape, F32) for sh...]
    ppermute x4, waiting for transfers between devices: 2.07 us -> 3.51 us  [swap(): return lax.ppermute(value, 'cols', pairs)]
    all_to_all x2, blocking collectives: 34.2 us -> 34.8 us  [exchange(): lax.all_to_all(tiles, 'cols', split_axis=0, concat_axis=0, tiled=True, ax...]
  transfers between devices with their start and end apart: 4 -> 4, of which waited for: 1 -> 3; matrix products, arithmetic and copies ran while one was open for 0% -> 0% of each run, Pallas kernels for 17% -> 14%
where the time goes in v18:
time: 56.6 us; the launch traced here: 56.4 us
  blocking collectives  34.8 us (61%)
  Pallas kernels  11.4 us (20%)
  starting transfers between devices  6.01 us (11%)
  waiting for transfers between devices  3.51 us (6%)
  between operations  0.71 us (1%)
    all_to_all x2, blocking collectives, exchange(): lax.all_to_all(tiles, 'cols', split_axis=0, concat_axis=0, tiled=True, ax...  34.8 us
    pallas_call x15, Pallas kernels, call(): pl.pallas_call(kernel, out_shape=[jax.ShapeDtypeStruct(shape, F32) for sh...  11.4 us
    ppermute x4, starting transfers between devices, swap(): return lax.ppermute(value, 'cols', pairs)  6.01 us
    ppermute x4, waiting for transfers between devices, swap(): return lax.ppermute(value, 'cols', pairs)  3.51 us
  transfers between devices with their start and end apart: 4, of which 3 were waited for; matrix products, arithmetic and copies ran while one was open for 0% of the time, Pallas kernels for 14%

profile of v18, /device:TPU:0, one launch (start us, length us, event | category | flops | bytes accessed | tf_op | source)
XLA Modules:
  0.0 56.4 jit_solution(16874904289536663368)
XLA Ops:
  0.6 1.6 %pack.1 = (f32[16,13,8,128]{3,2,1,0:T(8,128)S(1)}, f32[17,8,128]{2,1,0:T(8,128)S(1)}, f32[2,128]{1,0:T(2,128)S(1)}) custom-call(f32[128,512]{1,0:T(8,128)} %suction.1, f32[128,512]{1,0:T(8,128)} %warmth.1, s32[128,512]{1,0:T(8,128)} %classes.1, f32[1,512]{1,0:T(1,128)} %bitcast.3, s32[2,128]{1,0:T(2,128)} %couplings.1, f32[1,8]{1,0:T(1,128)} %bitcast.4, ...), custom_call_target="tpu_custom_call" | custom-call | flops 2000000 | bytes 2000000 | tf_op jit(solution)/shard_map/pack/pallas_call | solution.py:579
  2.2 20.1 %all_to_all.10.got = f32[16,13,8,128]{3,2,1,0:T(8,128)S(1)} all-to-all(f32[16,13,8,128]{3,2,1,0:T(8,128)S(1)} %get-tuple-element.50), channel_id=1, replica_groups={{0,1,2,3,4,5,6,7,8,9,10,11,12,13,14,15},{16,17,18,19,20,21,22,23,24,25,..., dimensions={0} | all-to-all | bytes 1703936 | tf_op jit(solution)/shard_map/all_to_all | solution.py:593
  22.4 0.3 edges.3
  22.7 2.6 %collective-permute-start.2 = (f32[3,7,8,128]{3,2,1,0:T(8,128)S(1)}, f32[3,7,8,128]{3,2,1,0:T(8,128)S(1)}, u32[]{:S(2)}, u32[]{:S(2)}) collective-permute-start(f32[3,7,8,128]{3,2,1,0:T(8,128)S(1)} %get-tuple-element.86), channel_id=1, source_target_pairs={{0,16},{16,0},{1,17},{17,1},{2,18},{18,2},{3,19},{19,3},{4,20},{20... | collective-permute-start | bytes 258056 | tf_op jit(solution)/shard_map/ppermute | solution.py:603
  25.3 0.3 edges.2
  25.6 0.4 collective-permute-start
  26.0 0.3 masks.1.refs_0_
  26.3 0.4 first.3
  26.7 0.9 %team.6 = (f32[8,8,512]{2,1,0:T(8,128)S(1)}, f32[8,8,512]{2,1,0:T(8,128)S(1)}, f32[8,8,512]{2,1,0:T(8,128)S(1)}, f32[8,8,512]{2,1,0:T(8,128)S(1)}) custom-call(f32[22,8,128]{2,1,0:T(8,128)S(1)} %masks.1.refs_0_, f32[8,8,512]{2,1,0:T(8,128)S(1)} %get-tuple-element.74.head.refs_1_, f32[8,8,512]{2,1,0:T(8,128)S(1)} %get-tuple-element.75.warm.refs_2_, ...), custom_call_target="tpu_custom_call" | custom-call | flops 2000000 | bytes 2000000 | tf_op jit(solution)/shard_map/team/pallas_call | solution.py:579
  27.5 0.4 first.2
  27.9 0.9 %team.4 = (f32[8,8,512]{2,1,0:T(8,128)S(1)}, f32[8,8,512]{2,1,0:T(8,128)S(1)}, f32[8,8,512]{2,1,0:T(8,128)S(1)}, f32[8,8,512]{2,1,0:T(8,128)S(1)}) custom-call(f32[22,8,128]{2,1,0:T(8,128)S(1)} %masks.1.refs_0_, f32[8,8,512]{2,1,0:T(8,128)S(1)} %get-tuple-element.52.head.refs_1_, f32[8,8,512]{2,1,0:T(8,128)S(1)} %get-tuple-element.53.warm.refs_2_, ...), custom_call_target="tpu_custom_call" | custom-call | flops 2000000 | bytes 2000000 | tf_op jit(solution)/shard_map/team/pallas_call | solution.py:579
  28.8 3.1 %collective-permute-done.2.refs_12_.refs_15_ = f32[3,7,8,128]{3,2,1,0:T(8,128)S(1)} collective-permute-done((f32[3,7,8,128]{3,2,1,0:T(8,128)S(1)}, f32[3,7,8,128]{3,2,1,0:T(8,128)S(1)}, u32[]{:S(2)}, u32[]{:S(2)}) %collective-permute-start.2) | collective-permute-done | bytes 86048 | tf_op jit(solution)/shard_map/ppermute | solution.py:603
  31.9 1.0 %middle.3 = (f32[8,8,512]{2,1,0:T(8,128)S(1)}, f32[8,8,512]{2,1,0:T(8,128)S(1)}, f32[8,8,512]{2,1,0:T(8,128)S(1)}, f32[2,8,8,128]{3,2,1,0:T(8,128)S(1)}, f32[2,7,8,128]{3,2,1,0:T(8,128)S(1)}) custom-call(f32[22,8,128]{2,1,0:T(8,128)S(1)} %masks.1.refs_0_, f32[8,8,512]{2,1,0:T(8,128)S(1)} %get-tuple-element.74.head.refs_1_, ...), custom_call_target="tpu_custom_call" | custom-call | flops 2000000 | bytes 2000000 | tf_op jit(solution)/shard_map/middle/pallas_call | solution.py:579
  32.8 0.1 collective-permute-start.3
  32.9 0.0 collective-permute-done.refs_12_.refs_15_
  32.9 1.0 %middle.2 = (f32[8,8,512]{2,1,0:T(8,128)S(1)}, f32[8,8,512]{2,1,0:T(8,128)S(1)}, f32[8,8,512]{2,1,0:T(8,128)S(1)}, f32[2,8,8,128]{3,2,1,0:T(8,128)S(1)}, f32[2,7,8,128]{3,2,1,0:T(8,128)S(1)}) custom-call(f32[22,8,128]{2,1,0:T(8,128)S(1)} %masks.1.refs_0_, f32[8,8,512]{2,1,0:T(8,128)S(1)} %get-tuple-element.52.head.refs_1_, ...), custom_call_target="tpu_custom_call" | custom-call | flops 2000000 | bytes 2000000 | tf_op jit(solution)/shard_map/middle/pallas_call | solution.py:579
  33.9 2.9 %collective-permute-start.1 = (f32[2,7,8,128]{3,2,1,0:T(8,128)S(1)}, f32[2,7,8,128]{3,2,1,0:T(8,128)S(1)}, u32[]{:S(2)}, u32[]{:S(2)}) collective-permute-start(f32[2,7,8,128]{3,2,1,0:T(8,128)S(1)} %get-tuple-element.73), channel_id=1, source_target_pairs={{0,16},{16,0},{1,17},{17,1},{2,18},{18,2},{3,19},{19,3},{4,20},{20... | collective-permute-start | bytes 172040 | tf_op jit(solution)/shard_map/ppermute | solution.py:603
  36.8 0.8 %team.7 = (f32[8,8,512]{2,1,0:T(8,128)S(1)}, f32[8,8,512]{2,1,0:T(8,128)S(1)}, f32[8,8,512]{2,1,0:T(8,128)S(1)}, f32[8,8,512]{2,1,0:T(8,128)S(1)}) custom-call(f32[22,8,128]{2,1,0:T(8,128)S(1)} %masks.1.refs_0_, f32[8,8,512]{2,1,0:T(8,128)S(1)} %get-tuple-element.87.head.refs_1_, f32[8,8,512]{2,1,0:T(8,128)S(1)} %get-tuple-element.88.warm.refs_2_, ...), custom_call_target="tpu_custom_call" | custom-call | flops 2000000 | bytes 2000000 | tf_op jit(solution)/shard_map/team/pallas_call | solution.py:579
  37.7 0.9 %team.5 = (f32[8,8,512]{2,1,0:T(8,128)S(1)}, f32[8,8,512]{2,1,0:T(8,128)S(1)}, f32[8,8,512]{2,1,0:T(8,128)S(1)}, f32[8,8,512]{2,1,0:T(8,128)S(1)}) custom-call(f32[22,8,128]{2,1,0:T(8,128)S(1)} %masks.1.refs_0_, f32[8,8,512]{2,1,0:T(8,128)S(1)} %get-tuple-element.65.head.refs_1_, f32[8,8,512]{2,1,0:T(8,128)S(1)} %get-tuple-element.66.warm.refs_2_, ...), custom_call_target="tpu_custom_call" | custom-call | flops 2000000 | bytes 2000000 | tf_op jit(solution)/shard_map/team/pallas_call | solution.py:579
  38.6 0.1 collective-permute-done.3.refs_13_
  38.7 0.9 %last.2.refs_16_ = f32[16,4,8,128]{3,2,1,0:T(8,128)S(1)} custom-call(f32[22,8,128]{2,1,0:T(8,128)S(1)} %masks.1.refs_0_, f32[8,8,512]{2,1,0:T(8,128)S(1)} %get-tuple-element.87.head.refs_1_, f32[8,8,512]{2,1,0:T(8,128)S(1)} %get-tuple-element.88.warm.refs_2_, f32[8,8,512]{2,1,0:T(8,128)S(1)} %get-tuple-element.76.refs_3_, ...), custom_call_target="tpu_custom_call" | custom-call | flops 2000000 | bytes 2000000 | tf_op jit(solution)/shard_map/last/pallas_call | solution.py:579
  39.6 0.3 collective-permute-done.1.refs_13_
  39.9 0.9 %last.3 = f32[16,8,8,128]{3,2,1,0:T(8,128)S(1)} custom-call(f32[22,8,128]{2,1,0:T(8,128)S(1)} %masks.1.refs_0_, f32[8,8,512]{2,1,0:T(8,128)S(1)} %get-tuple-element.65.head.refs_1_, f32[8,8,512]{2,1,0:T(8,128)S(1)} %get-tuple-element.66.warm.refs_2_, f32[8,8,512]{2,1,0:T(8,128)S(1)} %get-tuple-element.54.refs_3_, ...), custom_call_target="tpu_custom_call" | custom-call | flops 2000000 | bytes 2000000 | tf_op jit(solution)/shard_map/last/pallas_call | solution.py:579
  40.8 14.7 %all_to_all.11.got = f32[16,8,8,128]{3,2,1,0:T(8,128)S(1)} all-to-all(f32[16,8,8,128]{3,2,1,0:T(8,128)S(1)} %last.3), channel_id=1, replica_groups={{0,1,2,3,4,5,6,7,8,9,10,11,12,13,14,15},{16,17,18,19,20,21,22,23,24,25,..., dimensions={0} | all-to-all | bytes 1048576 | tf_op jit(solution)/shard_map/all_to_all | solution.py:593
  55.5 0.9 %unpack.1 = (f32[128,512]{1,0:T(8,128)}, f32[128,512]{1,0:T(8,128)}) custom-call(f32[16,8,8,128]{3,2,1,0:T(8,128)S(1)} %all_to_all.11.got), custom_call_target="tpu_custom_call" | custom-call | flops 2000000 | bytes 2000000 | tf_op jit(solution)/shard_map/unpack/pallas_call | solution.py:579
Async XLA Ops:
  22.7 9.2 %collective-permute-start.2 = (f32[3,7,8,128]{3,2,1,0:T(8,128)S(1)}, f32[3,7,8,128]{3,2,1,0:T(8,128)S(1)}, u32[]{:S(2)}, u32[]{:S(2)}) collective-permute-start(f32[3,7,8,128]{3,2,1,0:T(8,128)S(1)} %get-tuple-element.86), channel_id=1, source_target_pairs={{0,16},{16,0},{1,17},{17,1},{2,18},{18,2},{3,19},{19,3},{4,20},{20... | collective-permute-start | bytes 258056 | tf_op jit(solution)/shard_map/ppermute | solution.py:603
  25.6 7.3 %collective-permute-start = (f32[3,7,8,128]{3,2,1,0:T(8,128)S(1)}, f32[3,7,8,128]{3,2,1,0:T(8,128)S(1)}, u32[]{:S(2)}, u32[]{:S(2)}) collective-permute-start(f32[3,7,8,128]{3,2,1,0:T(8,128)S(1)} %get-tuple-element.64), channel_id=1, source_target_pairs={{0,16},{16,0},{1,17},{17,1},{2,18},{18,2},{3,19},{19,3},{4,20},{20... | collective-permute-start | bytes 258056 | tf_op jit(solution)/shard_map/ppermute | solution.py:603
  32.8 5.8 %collective-permute-start.3 = (f32[2,7,8,128]{3,2,1,0:T(8,128)S(1)}, f32[2,7,8,128]{3,2,1,0:T(8,128)S(1)}, u32[]{:S(2)}, u32[]{:S(2)}) collective-permute-start(f32[2,7,8,128]{3,2,1,0:T(8,128)S(1)} %get-tuple-element.95), channel_id=1, source_target_pairs={{0,16},{16,0},{1,17},{17,1},{2,18},{18,2},{3,19},{19,3},{4,20},{20... | collective-permute-start | bytes 172040 | tf_op jit(solution)/shard_map/ppermute | solution.py:603
  33.9 6.0 %collective-permute-start.1 = (f32[2,7,8,128]{3,2,1,0:T(8,128)S(1)}, f32[2,7,8,128]{3,2,1,0:T(8,128)S(1)}, u32[]{:S(2)}, u32[]{:S(2)}) collective-permute-start(f32[2,7,8,128]{3,2,1,0:T(8,128)S(1)} %get-tuple-element.73), channel_id=1, source_target_pairs={{0,16},{16,0},{1,17},{17,1},{2,18},{18,2},{3,19},{19,3},{4,20},{20... | collective-permute-start | bytes 172040 | tf_op jit(solution)/shard_map/ppermute | solution.py:603

commit v19 on v13

--- a/solution.py
+++ b/solution.py
@@ -409,7 +409,103 @@
     return water, heat
 
 
-def advance(steps, cuts, masks, head, warm, conduct, stored, energy, wet, melt, cond, water, heat, top,
+def ends():
+    part = lax.broadcasted_iota(jnp.int32, (SUB, ALL), 0)
+    group = lax.broadcasted_iota(jnp.int32, (SUB, ALL), 1) // WIDTH
+    return (
+        jnp.logical_and(part == 0, group == 0),
+        jnp.logical_and(part == SUB - 1, group == GROUPS - 1),
+    )
+
+
+def faces(steps, last_part, fields, potential):
+    face_of, rise_of = [], []
+    for j in range(steps):
+        if j + 1 < steps:
+            c_next, v_next = fields[j + 1], potential[j + 1]
+            face = 0.5 * (fields[j] + c_next)
+        else:
+            c_next, v_next = following(fields[0]), following(potential[0])
+            face = jnp.where(last_part, 0.0, 0.5 * (fields[j] + c_next))
+        face_of.append(face)
+        rise_of.append(v_next - potential[j])
+    return face_of, rise_of
+
+
+def levels():
+    found = [(following, preceding)]
+    step = 1
+    while step < SUB:
+        found.append(
+            (functools.partial(pltpu.roll, shift=SUB - step, axis=0), functools.partial(pltpu.roll, shift=step, axis=0))
+        )
+        step *= 2
+    return found
+
+
+def factor_kernel(cond, wet, stored, head, water, base, inverse, over, ratio, lead, reduced):
+    steps = head.shape[0]
+    first_part, last_part = ends()
+    k_face, rise = faces(steps, last_part, [cond[j] for j in range(steps)], head)
+    k_top = jnp.where(first_part, 0.0, preceding(k_face[-1]))
+    q_face = [k * (1.0 - d) for k, d in zip(k_face, rise)]
+    q_top = jnp.where(first_part, 0.0, preceding(q_face[-1]))
+    c_all, a_all = [], []
+    for j in range(steps):
+        above = k_top if j == 0 else k_face[j - 1]
+        into = q_top if j == 0 else q_face[j - 1]
+        s = wet[j]
+        base[j] = water[j] + into - q_face[j] - 0.8 * (s - stored[j])
+        main = 0.8 * s * (1.0 - s) + 0.02 + above + k_face[j]
+        r = reciprocal(main - above * c_all[-1]) if j else reciprocal(main)
+        o = above * r
+        inverse[j] = r
+        over[j] = o
+        c_all.append(k_face[j] * r)
+        a_all.append(a_all[-1] * o if j else o)
+        ratio[j] = c_all[-1]
+        lead[j] = a_all[-1]
+    p_first, a_first = c_all[-2], a_all[-2]
+    for j in range(steps - 3, -1, -1):
+        p_first = c_all[j] * p_first
+        a_first = a_all[j] + c_all[j] * a_first
+    last_c, last_a = c_all[-1], a_all[-1]
+    g = reciprocal(1.0 - last_c * following(a_first))
+    reduced[0] = g
+    reduced[1] = last_c * g
+    up = last_c * following(p_first) * g
+    down = last_a * g
+    for i, (after, before) in enumerate(levels()):
+        g = reciprocal(1.0 - up * after(down) - down * before(up))
+        reduced[3 * i + 2] = g
+        reduced[3 * i + 3] = up * g
+        reduced[3 * i + 4] = down * g
+        up = up * after(up) * g
+        down = down * before(down) * g
+
+
+def apply_factors(steps, factors, source, value, update):
+    inverse, over, ratio, lead, reduced = factors
+    d = source(0) * inverse[0]
+    value[0] = d
+    for j in range(1, steps):
+        d = source(j) * inverse[j] + d * over[j]
+        value[j] = d
+    d_first = value[steps - 2]
+    for j in range(steps - 3, -1, -1):
+        d_first = value[j] + ratio[j] * d_first
+    own = d * reduced[0] + reduced[1] * following(d_first)
+    for i, (after, before) in enumerate(levels()):
+        own = own * reduced[3 * i + 2] + reduced[3 * i + 3] * after(own) + reduced[3 * i + 4] * before(own)
+    above = preceding(own)
+    x = own
+    update(steps - 1, x)
+    for j in range(steps - 2, -1, -1):
+        x = ratio[j] * x + (lead[j] * above + value[j])
+        update(j, x)
+
+
+def advance(steps, cuts, masks, head, warm, conduct, energy, melt, factors, water, heat, top,
             mine, theirs, new_head, new_warm, new_wet, inflow, warm_inflow, ratio, lead, value, finish):
     for j in range(steps):
         w_parts = [water[j, :, m * LANES : (m + 1) * LANES] for m in range(2 * GROUPS)]
@@ -425,46 +521,17 @@
             inflow[j, :, m * LANES : (m + 1) * LANES] = w_parts[m]
             warm_inflow[j, :, m * LANES : (m + 1) * LANES] = q_parts[m]
 
-    part = lax.broadcasted_iota(jnp.int32, (SUB, ALL), 0)
-    group = lax.broadcasted_iota(jnp.int32, (SUB, ALL), 1) // WIDTH
-    first_part = jnp.logical_and(part == 0, group == 0)
-    last_part = jnp.logical_and(part == SUB - 1, group == GROUPS - 1)
-
-    def faces(fields, potential):
-        face_of, rise_of = [], []
-        for j in range(steps):
-            if j + 1 < steps:
-                c_next, v_next = fields[j + 1], potential[j + 1]
-                face = 0.5 * (fields[j] + c_next)
-            else:
-                c_next, v_next = following(fields[0]), following(potential[0])
-                face = jnp.where(last_part, 0.0, 0.5 * (fields[j] + c_next))
-            face_of.append(face)
-            rise_of.append(v_next - potential[j])
-        return face_of, rise_of
-
-    k_face, rise = faces([cond[j] for j in range(steps)], head)
-    k_top = jnp.where(first_part, 0.0, preceding(k_face[-1]))
-    q_face = [k * (1.0 - d) for k, d in zip(k_face, rise)]
-    q_top = jnp.where(first_part, 0.0, preceding(q_face[-1]))
-
-    def water_matrix(j):
-        above = k_top if j == 0 else k_face[j - 1]
-        into = q_top if j == 0 else q_face[j - 1]
-        s = wet[j]
-        main = 0.8 * s * (1.0 - s) + 0.02 + above + k_face[j]
-        source = inflow[j] + into - q_face[j] - 0.8 * (s - stored[j])
-        return above, main, k_face[j], source
+    first_part, last_part = ends()
 
     def water_done(j, x):
         h = head[j] + x
         new_head[j] = h
         new_wet[j] = sigmoid(h)
 
-    solve(steps, water_matrix, ratio, lead, value, water_done)
+    apply_factors(steps, factors, lambda j: inflow[j], value, water_done)
 
     l_cell = [conduct[j] * (1.5 - 0.5 * melt[j]) for j in range(steps)]
-    l_face, rise = faces(l_cell, warm)
+    l_face, rise = faces(steps, last_part, l_cell, warm)
     l_top = jnp.where(first_part, 0.0, preceding(l_face[-1]))
     g_face = [l * d for l, d in zip(l_face, rise)]
     g_top = jnp.where(first_part, 0.0, preceding(g_face[-1]))
@@ -492,7 +559,8 @@
 
 
 def middle_kernel(cuts, *refs):
-    masks, head, warm, perm, conduct, wet, melt, cond, energy, top, water, heat = refs[:12]
+    masks, head, warm, perm, conduct, melt, energy, top, heat, water = refs[:10]
+    factors, refs = refs[10:15], refs[3:]
     own, far = refs[12 : 12 + cuts], refs[12 + cuts : 12 + 2 * cuts]
     new_head, new_warm, new_wet, new_melt, new_cond = refs[12 + 2 * cuts : 17 + 2 * cuts]
     halos, sent = refs[17 + 2 * cuts : 17 + 3 * cuts], refs[17 + 3 * cuts : 17 + 4 * cuts]
@@ -511,7 +579,7 @@
 
     theirs = [[unsqueeze(cut, [far[cut][i, j] for j in range(steps - 1)]) for i in range(3)] for cut in range(cuts)]
     advance(
-        steps, cuts, masks, head, warm, conduct, wet, energy, wet, melt, cond, water, heat, top,
+        steps, cuts, masks, head, warm, conduct, energy, melt, factors, water, heat, top,
         lambda cut, j: [own[cut][i, j] for i in range(3)],
         lambda cut, j: [theirs[cut][i][j] for i in range(3)],
         new_head, new_warm, new_wet, inflow, warm_inflow, ratio, lead, value, finish,
@@ -525,7 +593,8 @@
 
 
 def last_kernel(chunk, cuts, *refs):
-    masks, head, warm, conduct, stored, wet, melt, cond, energy, top, water, heat = refs[:12]
+    masks, head, warm, conduct, melt, energy, top, heat, water = refs[:9]
+    factors, refs = refs[9:14], refs[2:]
     own, far = refs[12 : 12 + cuts], refs[12 + cuts : 12 + 2 * cuts]
     own_k, far_k = refs[12 + 2 * cuts : 12 + 3 * cuts], refs[12 + 3 * cuts : 12 + 4 * cuts]
     others = refs[12 + 4 * cuts : -10]
@@ -538,7 +607,7 @@
         for cut in range(cuts)
     ]
     advance(
-        steps, cuts, masks, head, warm, conduct, stored, energy, wet, melt, cond, water, heat, top,
+        steps, cuts, masks, head, warm, conduct, energy, melt, factors, water, heat, top,
         lambda cut, j: [own[cut][0, j], own[cut][1, j], own_k[cut][2, j]],
         lambda cut, j: [theirs[cut][i][j] for i in range(3)],
         new_head, new_warm, new_wet, inflow, warm_inflow, ratio, lead, value, lambda j, t: None,
@@ -646,21 +715,25 @@
         )
         for c in range(CHUNKS)
     ]
+    def prepare(cond, wet, stored, head, warm):
+        water, heat = call(team_kernel, "team", (masks, head, warm, cond), [column] * 2)
+        reduced = (2 + 3 * len(levels()), SUB, ALL)
+        return (heat, *call(factor_kernel, "factor", (cond, wet, stored, head, water), [column] * 5 + [reduced]))
+
     flows, sides = [], []
     for c in range(CHUNKS):
         mine, sent = edges[c][:cuts], edges[c][cuts:]
         sides.append((mine, [swap(cut, n, v) for cut, v in enumerate(sent)]))
-        flows.append(tuple(call(team_kernel, "team", (masks, first[c][0], first[c][1], first[c][6]), [column] * 2)))
+        flows.append(prepare(first[c][6], first[c][4], first[c][4], first[c][0], first[c][1]))
 
     second, later = [], []
     for c in range(CHUNKS):
         head, warm, perm, conduct, wet, melt, cond, energy, surface = first[c]
-        water, heat = flows[c]
         mine, theirs = sides[c]
         values = call(
             functools.partial(middle_kernel, cuts),
             "middle",
-            (masks, head, warm, perm, conduct, wet, melt, cond, energy, surface, water, heat, *mine, *theirs),
+            (masks, head, warm, perm, conduct, melt, energy, surface, *flows[c], *mine, *theirs),
             [column] * 5 + [(2,) + halo] * cuts + [(2,) + squeezed] * cuts,
             scratch=[room] * 5,
         )
@@ -672,7 +745,7 @@
     for c in range(CHUNKS):
         conduct, stored, energy, surface = first[c][3], first[c][4], first[c][7], first[c][8]
         head, warm, wet, melt, cond = second[c]
-        water, heat = call(team_kernel, "team", (masks, head, warm, cond), [column] * 2)
+        flow = prepare(cond, wet, stored, head, warm)
         mine, theirs = later[c]
         mine_k, theirs_k = sides[c]
         final = c == CHUNKS - 1
@@ -680,7 +753,7 @@
             functools.partial(last_kernel, c, cuts),
             "last",
             (
-                masks, head, warm, conduct, stored, wet, melt, cond, energy, surface, water, heat,
+                masks, head, warm, conduct, melt, energy, surface, *flow,
                 *mine, *theirs, *mine_k, *theirs_k, *(done if final else ()),
             ),
             [(TEAM, 2 * quarters if final else 4, OWN, cells)],

time: 56.7 us -> 56.4 us (level)
    pallas_call x15 -> x19, Pallas kernels: 14.5 us -> 14.9 us  [call(): pl.pallas_call(kernel, out_shape=[jax.ShapeDtypeStruct(shape, F32) for sh...]
  transfers between devices with their start and end apart: 4 -> 4, of which waited for: 2 -> 2; matrix products, arithmetic and copies ran while one was open for 0% -> 0% of each run, Pallas kernels for 19% -> 20%
where the time goes in v19:
time: 56.4 us; the launch traced here: 56.2 us
  blocking collectives  33.6 us (60%)
  Pallas kernels  14.9 us (26%)
  starting transfers between devices  6.1 us (11%)
  between operations  0.74 us (1%)
    all_to_all x2, blocking collectives, exchange(): lax.all_to_all(tiles, 'cols', split_axis=0, concat_axis=0, tiled=True, ax...  33.6 us
    pallas_call x19, Pallas kernels, call(): pl.pallas_call(kernel, out_shape=[jax.ShapeDtypeStruct(shape, F32) for sh...  14.9 us
    ppermute x4, starting transfers between devices, swap(): return lax.ppermute(value, 'cols', pairs)  6.1 us
  transfers between devices with their start and end apart: 4, of which 2 were waited for; matrix products, arithmetic and copies ran while one was open for 0% of the time, Pallas kernels for 20%

profile of v19, /device:TPU:0, one launch (start us, length us, event | category | flops | bytes accessed | tf_op | source)
XLA Modules:
  0.0 56.2 jit_solution(17418477448890845665)
XLA Ops:
  0.6 1.6 %pack.1 = (f32[16,13,8,128]{3,2,1,0:T(8,128)S(1)}, f32[9,8,128]{2,1,0:T(8,128)S(1)}) custom-call(f32[128,512]{1,0:T(8,128)} %suction.1, f32[128,512]{1,0:T(8,128)} %warmth.1, s32[128,512]{1,0:T(8,128)} %classes.1, f32[1,512]{1,0:T(1,128)} %bitcast.3, s32[2,128]{1,0:T(2,128)} %couplings.3, f32[1,8]{1,0:T(1,128)} %bitcast.2), custom_call_target="tpu_custom_call" | custom-call | flops 2000000 | bytes 2000000 | tf_op jit(solution)/shard_map/pack/pallas_call | solution.py:636
  2.2 20.1 %all_to_all.10.got = f32[16,13,8,128]{3,2,1,0:T(8,128)S(1)} all-to-all(f32[16,13,8,128]{3,2,1,0:T(8,128)S(1)} %get-tuple-element.72), channel_id=1, replica_groups={{0,1,2,3,4,5,6,7,8,9,10,11,12,13,14,15},{16,17,18,19,20,21,22,23,24,25,..., dimensions={0} | all-to-all | bytes 1703936 | tf_op jit(solution)/shard_map/all_to_all | solution.py:650
  22.3 0.3 edges.3
  22.7 2.6 %collective-permute-start.2 = (f32[3,7,8,128]{3,2,1,0:T(8,128)S(1)}, f32[3,7,8,128]{3,2,1,0:T(8,128)S(1)}, u32[]{:S(2)}, u32[]{:S(2)}) collective-permute-start(f32[3,7,8,128]{3,2,1,0:T(8,128)S(1)} %get-tuple-element.126), channel_id=1, source_target_pairs={{0,16},{16,0},{1,17},{17,1},{2,18},{18,2},{3,19},{19,3},{4,20},{20... | collective-permute-start | bytes 258056 | tf_op jit(solution)/shard_map/ppermute | solution.py:660
  25.3 0.3 edges.2
  25.6 0.0 copy-start
  25.6 0.0 copy-start.2
  25.6 0.4 collective-permute-start
  26.0 0.3 copy-done.1
  26.3 0.3 masks.1.refs_0_
  26.6 0.9 %first.3 = (f32[8,8,512]{2,1,0:T(8,128)S(1)}, f32[8,8,512]{2,1,0:T(8,128)S(1)}, f32[8,8,512]{2,1,0:T(8,128)S(1)}, f32[8,8,512]{2,1,0:T(8,128)S(1)}, f32[8,8,512]...) custom-call(f32[16,13,8,128]{3,2,1,0:T(8,128)S(1)} %all_to_all.10.go, ...), custom_call_target="tpu_custom_call" | custom-call | flops 2000000 | bytes 2000000 | tf_op jit(solution)/shard_map/first/pallas_call | solution.py:636
  27.5 1.4 %team.6 = (f32[8,8,512]{2,1,0:T(8,128)S(1)}, f32[8,8,512]{2,1,0:T(8,128)S(1)}) custom-call(f32[22,8,128]{2,1,0:T(8,128)S(1)} %masks.1.refs_0_, f32[8,8,512]{2,1,0:T(8,128)S(1)} %get-tuple-element.108.head.refs_1_, f32[8,8,512]{2,1,0:T(8,128)S(1)} %get-tuple-element.109.warm.refs_2_, f32[8,8,512]{2,1,0:T(8,128)S(1)} %get-tuple-element.115.cond), custom_call_target="tpu_custom_call" | custom-call | flops 2000000 | bytes 2000000 | tf_op jit(solution)/shard_map/team/pallas_call | solution.py:636
  28.9 0.2 factor.6
  29.1 0.9 %first.2 = (f32[8,8,512]{2,1,0:T(8,128)S(1)}, f32[8,8,512]{2,1,0:T(8,128)S(1)}, f32[8,8,512]{2,1,0:T(8,128)S(1)}, f32[8,8,512]{2,1,0:T(8,128)S(1)}, f32[8,8,512]...) custom-call(f32[16,13,8,128]{3,2,1,0:T(8,128)S(1)} %all_to_all.10.go, ...), custom_call_target="tpu_custom_call" | custom-call | flops 2000000 | bytes 2000000 | tf_op jit(solution)/shard_map/first/pallas_call | solution.py:636
  30.0 1.4 %team.4 = (f32[8,8,512]{2,1,0:T(8,128)S(1)}, f32[8,8,512]{2,1,0:T(8,128)S(1)}) custom-call(f32[22,8,128]{2,1,0:T(8,128)S(1)} %masks.1.refs_0_, f32[8,8,512]{2,1,0:T(8,128)S(1)} %get-tuple-element.73.head.refs_1_, f32[8,8,512]{2,1,0:T(8,128)S(1)} %get-tuple-element.74.warm.refs_2_, f32[8,8,512]{2,1,0:T(8,128)S(1)} %get-tuple-element.80.cond), custom_call_target="tpu_custom_call" | custom-call | flops 2000000 | bytes 2000000 | tf_op jit(solution)/shard_map/team/pallas_call | solution.py:636
  31.4 0.2 factor.4
  31.6 0.3 collective-permute-done.2.refs_16_.refs_17_
  31.8 0.9 %middle.3 = (f32[8,8,512]{2,1,0:T(8,128)S(1)}, f32[8,8,512]{2,1,0:T(8,128)S(1)}, f32[8,8,512]{2,1,0:T(8,128)S(1)}, f32[8,8,512]{2,1,0:T(8,128)S(1)}, f32[8,8,512...) custom-call(f32[22,8,128]{2,1,0:T(8,128)S(1)} %masks.1.refs_0_, ...), custom_call_target="tpu_custom_call" | custom-call | flops 2000000 | bytes 2000000 | tf_op jit(solution)/shard_map/middle/pallas_call | solution.py:636
  32.7 2.1 %collective-permute-start.3 = (f32[2,7,8,128]{3,2,1,0:T(8,128)S(1)}, f32[2,7,8,128]{3,2,1,0:T(8,128)S(1)}, u32[]{:S(2)}, u32[]{:S(2)}) collective-permute-start(f32[2,7,8,128]{3,2,1,0:T(8,128)S(1)} %get-tuple-element.141), channel_id=1, source_target_pairs={{0,16},{16,0},{1,17},{17,1},{2,18},{18,2},{3,19},{19,3},{4,20},{20... | collective-permute-start | bytes 172040 | tf_op jit(solution)/shard_map/ppermute | solution.py:660
  34.9 0.0 collective-permute-done.refs_16_.refs_17_
  34.9 0.9 %middle.2 = (f32[8,8,512]{2,1,0:T(8,128)S(1)}, f32[8,8,512]{2,1,0:T(8,128)S(1)}, f32[8,8,512]{2,1,0:T(8,128)S(1)}, f32[8,8,512]{2,1,0:T(8,128)S(1)}, f32[8,8,512...) custom-call(f32[22,8,128]{2,1,0:T(8,128)S(1)} %masks.1.refs_0_, ...), custom_call_target="tpu_custom_call" | custom-call | flops 2000000 | bytes 2000000 | tf_op jit(solution)/shard_map/middle/pallas_call | solution.py:636
  35.8 0.9 %collective-permute-start.1 = (f32[2,7,8,128]{3,2,1,0:T(8,128)S(1)}, f32[2,7,8,128]{3,2,1,0:T(8,128)S(1)}, u32[]{:S(2)}, u32[]{:S(2)}) collective-permute-start(f32[2,7,8,128]{3,2,1,0:T(8,128)S(1)} %get-tuple-element.107), channel_id=1, source_target_pairs={{0,16},{16,0},{1,17},{17,1},{2,18},{18,2},{3,19},{19,3},{4,20},{20... | collective-permute-start | bytes 172040 | tf_op jit(solution)/shard_map/ppermute | solution.py:660
  36.7 1.4 %team.7 = (f32[8,8,512]{2,1,0:T(8,128)S(1)}, f32[8,8,512]{2,1,0:T(8,128)S(1)}) custom-call(f32[22,8,128]{2,1,0:T(8,128)S(1)} %masks.1.refs_0_, f32[8,8,512]{2,1,0:T(8,128)S(1)} %get-tuple-element.127.head.refs_1_, f32[8,8,512]{2,1,0:T(8,128)S(1)} %get-tuple-element.128.warm.refs_2_, f32[8,8,512]{2,1,0:T(8,128)S(1)} %get-tuple-element.130.cond), custom_call_target="tpu_custom_call" | custom-call | flops 2000000 | bytes 2000000 | tf_op jit(solution)/shard_map/team/pallas_call | solution.py:636
  38.1 0.2 factor.7
  38.3 1.4 %team.5 = (f32[8,8,512]{2,1,0:T(8,128)S(1)}, f32[8,8,512]{2,1,0:T(8,128)S(1)}) custom-call(f32[22,8,128]{2,1,0:T(8,128)S(1)} %masks.1.refs_0_, f32[8,8,512]{2,1,0:T(8,128)S(1)} %get-tuple-element.93.head.refs_1_, f32[8,8,512]{2,1,0:T(8,128)S(1)} %get-tuple-element.94.warm.refs_2_, f32[8,8,512]{2,1,0:T(8,128)S(1)} %get-tuple-element.96.cond), custom_call_target="tpu_custom_call" | custom-call | flops 2000000 | bytes 2000000 | tf_op jit(solution)/shard_map/team/pallas_call | solution.py:636
  39.6 0.2 factor.5
  39.8 0.0 collective-permute-done.3.refs_15_
  39.8 0.9 %last.2.refs_18_ = f32[16,4,8,128]{3,2,1,0:T(8,128)S(1)} custom-call(f32[22,8,128]{2,1,0:T(8,128)S(1)} %masks.1.refs_0_, f32[8,8,512]{2,1,0:T(8,128)S(1)} %get-tuple-element.127.head.refs_1_, f32[8,8,512]{2,1,0:T(8,128)S(1)} %get-tuple-element.128.warm.refs_2_, f32[8,8,512]{2,1,0:T(8,128)S(1)} %get-tuple-element.111.refs_4_.refs_3_, ...), custom_call_target="tpu_custom_call" | custom-call | flops 2000000 | bytes 2000000 | tf_op jit(solution)/shard_map/last/pallas_call | solution.py:636
  40.7 0.3 collective-permute-done.1.refs_15_
  40.9 0.9 %last.3 = f32[16,8,8,128]{3,2,1,0:T(8,128)S(1)} custom-call(f32[22,8,128]{2,1,0:T(8,128)S(1)} %masks.1.refs_0_, f32[8,8,512]{2,1,0:T(8,128)S(1)} %get-tuple-element.93.head.refs_1_, f32[8,8,512]{2,1,0:T(8,128)S(1)} %get-tuple-element.94.warm.refs_2_, f32[8,8,512]{2,1,0:T(8,128)S(1)} %get-tuple-element.76.refs_4_.refs_3_, ...), custom_call_target="tpu_custom_call" | custom-call | flops 2000000 | bytes 2000000 | tf_op jit(solution)/shard_map/last/pallas_call | solution.py:636
  41.8 13.5 %all_to_all.11.got = f32[16,8,8,128]{3,2,1,0:T(8,128)S(1)} all-to-all(f32[16,8,8,128]{3,2,1,0:T(8,128)S(1)} %last.3), channel_id=1, replica_groups={{0,1,2,3,4,5,6,7,8,9,10,11,12,13,14,15},{16,17,18,19,20,21,22,23,24,25,..., dimensions={0} | all-to-all | bytes 1048576 | tf_op jit(solution)/shard_map/all_to_all | solution.py:650
  55.3 0.9 %unpack.1 = (f32[128,512]{1,0:T(8,128)}, f32[128,512]{1,0:T(8,128)}) custom-call(f32[16,8,8,128]{3,2,1,0:T(8,128)S(1)} %all_to_all.11.got), custom_call_target="tpu_custom_call" | custom-call | flops 2000000 | bytes 2000000 | tf_op jit(solution)/shard_map/unpack/pallas_call | solution.py:636
  (3 shorter events, 0.0 us)
Async XLA Ops:
  22.7 9.2 %collective-permute-start.2 = (f32[3,7,8,128]{3,2,1,0:T(8,128)S(1)}, f32[3,7,8,128]{3,2,1,0:T(8,128)S(1)}, u32[]{:S(2)}, u32[]{:S(2)}) collective-permute-start(f32[3,7,8,128]{3,2,1,0:T(8,128)S(1)} %get-tuple-element.126), channel_id=1, source_target_pairs={{0,16},{16,0},{1,17},{17,1},{2,18},{18,2},{3,19},{19,3},{4,20},{20... | collective-permute-start | bytes 258056 | tf_op jit(solution)/shard_map/ppermute | solution.py:660
  25.6 0.7 %copy-start.1 = (s32[2,128]{1,0:T(2,128)S(1)}, s32[2,128]{1,0:T(2,128)}, u32[]{:S(2)}) copy-start(s32[2,128]{1,0:T(2,128)} %couplings.3) | copy-start | bytes 3076
  25.6 0.9 %copy-start = (f32[8]{0:T(128)S(1)}, f32[8]{0:T(128)}, u32[]{:S(2)}) copy-start(f32[8]{0:T(128)} %k_sat.3) | copy-start | bytes 100
  25.6 0.9 %copy-start.2 = (f32[8]{0:T(128)S(1)}, f32[8]{0:T(128)}, u32[]{:S(2)}) copy-start(f32[8]{0:T(128)} %heat_cond.3) | copy-start | bytes 100
  25.6 9.2 %collective-permute-start = (f32[3,7,8,128]{3,2,1,0:T(8,128)S(1)}, f32[3,7,8,128]{3,2,1,0:T(8,128)S(1)}, u32[]{:S(2)}, u32[]{:S(2)}) collective-permute-start(f32[3,7,8,128]{3,2,1,0:T(8,128)S(1)} %get-tuple-element.92), channel_id=1, source_target_pairs={{0,16},{16,0},{1,17},{17,1},{2,18},{18,2},{3,19},{19,3},{4,20},{20... | collective-permute-start | bytes 258056 | tf_op jit(solution)/shard_map/ppermute | solution.py:660
  32.7 7.1 %collective-permute-start.3 = (f32[2,7,8,128]{3,2,1,0:T(8,128)S(1)}, f32[2,7,8,128]{3,2,1,0:T(8,128)S(1)}, u32[]{:S(2)}, u32[]{:S(2)}) collective-permute-start(f32[2,7,8,128]{3,2,1,0:T(8,128)S(1)} %get-tuple-element.141), channel_id=1, source_target_pairs={{0,16},{16,0},{1,17},{17,1},{2,18},{18,2},{3,19},{19,3},{4,20},{20... | collective-permute-start | bytes 172040 | tf_op jit(solution)/shard_map/ppermute | solution.py:660
  35.8 5.1 %collective-permute-start.1 = (f32[2,7,8,128]{3,2,1,0:T(8,128)S(1)}, f32[2,7,8,128]{3,2,1,0:T(8,128)S(1)}, u32[]{:S(2)}, u32[]{:S(2)}) collective-permute-start(f32[2,7,8,128]{3,2,1,0:T(8,128)S(1)} %get-tuple-element.107), channel_id=1, source_target_pairs={{0,16},{16,0},{1,17},{17,1},{2,18},{18,2},{3,19},{19,3},{4,20},{20... | collective-permute-start | bytes 172040 | tf_op jit(solution)/shard_map/ppermute | solution.py:660

commit v20 on v19

--- a/solution.py
+++ b/solution.py
@@ -124,7 +124,7 @@
 
 
 def mask_kernel(n, couplings, out):
-    pair_rows = couplings[...].astype(F32)
+    pair_rows = couplings[...]
     pairs = couplings.shape[1]
     pair_id = lax.broadcasted_iota(jnp.int32, (pairs, LANES), 0)
     lane = lax.broadcasted_iota(jnp.int32, (pairs, LANES), 1)
@@ -188,13 +188,14 @@
 
 
 def pack_kernel(
-    cuts, suction, warmth, classes, surface, couplings, k_sat, out, consts, room, class_room, top, pairs, table, in_sems
+    cuts, suction, warmth, classes, surface, couplings, k_sat, heat_cond, out, consts, pair_rows,
+    room, class_room, top, pairs, k_table, heat_table, in_sems,
 ):
     cells = out.shape[-1]
     quarters = 2 * CHUNKS
     into = []
-    rooms = (room.at[0], room.at[1], class_room, top, pairs, table)
-    for f, field in enumerate((suction, warmth, classes, surface, couplings, k_sat)):
+    rooms = (room.at[0], room.at[1], class_room, top, pairs, k_table, heat_table)
+    for f, field in enumerate((suction, warmth, classes, surface, couplings, k_sat, heat_cond)):
         into.append(pltpu.make_async_copy(field, rooms[f], in_sems.at[f]))
         into[-1].start()
 
@@ -208,10 +209,13 @@
             put(f * quarters + q, class_room[:, lanes].astype(F32) if f == 2 else room[f, :, lanes])
     for copy in into[3:]:
         copy.wait()
-    for c in range(k_sat.shape[1]):
-        consts[c] = jnp.broadcast_to(table[0:1, c : c + 1], (SUB, LANES))
+    kinds = k_sat.shape[1]
+    for c in range(kinds):
+        consts[c] = jnp.broadcast_to(k_table[0:1, c : c + 1], (SUB, LANES))
+        consts[kinds + c] = jnp.broadcast_to(heat_table[0:1, c : c + 1], (SUB, LANES))
     for cut in range(cuts):
-        consts[k_sat.shape[1] + cut] = other_block(cut, pairs)
+        consts[2 * kinds + cut] = other_block(cut, pairs)
+    pair_rows[...] = pairs[...].astype(F32)
     rows = [top[0:1, q * LANES : (q + 1) * LANES] for q in range(quarters)]
     put(3 * quarters, jnp.concatenate(rows + [jnp.zeros((cells - quarters, LANES), F32)], axis=0))
 
@@ -279,10 +283,10 @@
                 got[pl.ds(start, PAIR_DEV), (f * 2 + b) * CHUNKS + chunk].reshape(EDGE, cells) for b in range(2)
             ]
             load[cut * 3 + f] = jnp.concatenate(rows * GROUPS, axis=0).T
-    classes = consts.shape[0] - cuts
-    table = [consts[c] for c in range(classes)]
+    kinds = (consts.shape[0] - cuts) // 2
+    table = [consts[c] for c in range(kinds)]
     for cut in range(cuts):
-        other = consts[classes + cut] > 0.5
+        other = consts[2 * kinds + cut] > 0.5
         for f in range(3):
             values = []
             for j in range(steps):
@@ -303,7 +307,7 @@
 
 
 def first_kernel(
-    chunk, got, k_sat, heat_cond, head, warm, perm, conduct, wet, melt, cond, energy, top, load
+    chunk, kinds, got, consts, head, warm, perm, conduct, wet, melt, cond, energy, top, load
 ):
     cells = got.shape[-1]
     steps = head.shape[0]
@@ -324,14 +328,21 @@
         ]
         return jnp.concatenate(parts, axis=1)
 
+    def pick(v):
+        parts = []
+        for m in range(2 * GROUPS):
+            part = v[:, m * LANES : (m + 1) * LANES]
+            k, lam = consts[0], consts[kinds]
+            for c in range(1, kinds):
+                here = part >= c
+                k = jnp.where(here, consts[c], k)
+                lam = jnp.where(here, consts[kinds + c], lam)
+            parts.append((k, lam))
+        return [jnp.concatenate(side, axis=1) for side in zip(*parts)]
+
     for j in range(steps):
         h, t, v = [fetch(field, j) for field in range(3)]
-        k = jnp.full_like(v, k_sat[0])
-        lam = jnp.full_like(v, heat_cond[0])
-        for c in range(1, k_sat.shape[0]):
-            here = v >= c
-            k = jnp.where(here, k_sat[c], k)
-            lam = jnp.where(here, heat_cond[c], lam)
+        k, lam = pick(v)
         s, f = sigmoid(h), sigmoid(2.0 * t)
         m = 0.05 + 0.4 * s
         head[j], warm[j], perm[j], conduct[j] = h, t, k, lam
@@ -379,7 +390,7 @@
             heat[j, :, l0] = 2.0 * (total[2] - total[3])
             heat[j, :, l1] = 2.0 * total[3]
 
-    lax.fori_loop(0, steps, step, None)
+    lax.fori_loop(0, steps, step, None, unroll=2)
 
 
 def cross_flows(cut, masks, mine, theirs):
@@ -670,28 +681,29 @@
     halo = (steps, SUB, LANES)
     squeezed = (steps - 1, SUB, LANES)
     room = pltpu.VMEM(column, F32)
-    smem = whole(pltpu.SMEM)
     hbm = whole(pltpu.HBM)
 
-    masks = call(
-        functools.partial(mask_kernel, n), "masks", (couplings,), [(mask_rows(cuts), SUB, LANES)]
-    )[0]
-    arguments = (suction, warmth, classes, top.reshape(1, width), couplings, k_sat.reshape(1, -1))
-    packed, consts = call(
+    arguments = (suction, warmth, classes, top.reshape(1, width), couplings, k_sat.reshape(1, -1), heat_cond.reshape(1, -1))
+    kinds = k_sat.shape[0]
+    packed, consts, pair_rows = call(
         functools.partial(pack_kernel, cuts),
         "pack",
         [pltpu.with_memory_space_constraint(v, pltpu.HBM) for v in arguments],
-        [(TEAM, 3 * quarters + 1, OWN, cells), (k_sat.shape[0] + cuts, SUB, LANES)],
+        [(TEAM, 3 * quarters + 1, OWN, cells), (2 * kinds + cuts, SUB, LANES), couplings.shape],
         scratch=[
             pltpu.VMEM((2, cells, width), F32),
             pltpu.VMEM((cells, width), classes.dtype),
             pltpu.VMEM((1, width), F32),
             pltpu.VMEM(couplings.shape, couplings.dtype),
-            pltpu.VMEM((1, k_sat.shape[0]), F32),
-            pltpu.SemaphoreType.DMA((6,)),
+            pltpu.VMEM((1, kinds), F32),
+            pltpu.VMEM((1, kinds), F32),
+            pltpu.SemaphoreType.DMA((7,)),
         ],
-        specs=[hbm] * 6,
+        specs=[hbm] * 7,
     )
+    masks = call(
+        functools.partial(mask_kernel, n), "masks", (pair_rows,), [(mask_rows(cuts), SUB, LANES)]
+    )[0]
     got = exchange(packed, n)
 
     edges = [
@@ -706,12 +718,11 @@
     ]
     first = [
         call(
-            functools.partial(first_kernel, c),
+            functools.partial(first_kernel, c, kinds),
             "first",
-            (got, k_sat, heat_cond),
+            (got, consts),
             [column] * 8 + [(1, ALL)],
             scratch=[pltpu.VMEM((6, cells, LANES), F32)],
-            specs=[whole(), smem, smem],
         )
         for c in range(CHUNKS)
     ]

time: 56.4 us -> 56.5 us (level)
  Pallas kernels: 14.9 us -> 11.7 us
  waiting for transfers between devices: 0.56 us -> 3.11 us
  blocking collectives: 33.6 us -> 34.8 us
    pallas_call x19, Pallas kernels: 14.9 us -> 11.7 us  [call(): pl.pallas_call(kernel, out_shape=[jax.ShapeDtypeStruct(shape, F32) for sh...]
    ppermute x4, waiting for transfers between devices: 0.56 us -> 3.11 us  [swap(): return lax.ppermute(value, 'cols', pairs)]
    all_to_all x2, blocking collectives: 33.6 us -> 34.8 us  [exchange(): lax.all_to_all(tiles, 'cols', split_axis=0, concat_axis=0, tiled=True, ax...]
  transfers between devices with their start and end apart: 4 -> 4, of which waited for: 2 -> 3; matrix products, arithmetic and copies ran while one was open for 0% -> 0% of each run, Pallas kernels for 20% -> 14%
where the time goes in v20:
time: 56.5 us; the launch traced here: 56.2 us
  blocking collectives  34.8 us (62%)
  Pallas kernels  11.7 us (21%)
  starting transfers between devices  5.97 us (11%)
  waiting for transfers between devices  3.11 us (6%)
  between operations  0.72 us (1%)
    all_to_all x2, blocking collectives, exchange(): lax.all_to_all(tiles, 'cols', split_axis=0, concat_axis=0, tiled=True, ax...  34.8 us
    pallas_call x19, Pallas kernels, call(): pl.pallas_call(kernel, out_shape=[jax.ShapeDtypeStruct(shape, F32) for sh...  11.7 us
    ppermute x4, starting transfers between devices, swap(): return lax.ppermute(value, 'cols', pairs)  5.97 us
    ppermute x4, waiting for transfers between devices, swap(): return lax.ppermute(value, 'cols', pairs)  3.11 us
  transfers between devices with their start and end apart: 4, of which 3 were waited for; matrix products, arithmetic and copies ran while one was open for 0% of the time, Pallas kernels for 14%

profile of v20, /device:TPU:0, one launch (start us, length us, event | category | flops | bytes accessed | tf_op | source)
XLA Modules:
  0.0 56.2 jit_solution(7434713796240052348)
XLA Ops:
  0.6 1.6 %pack.1 = (f32[16,13,8,128]{3,2,1,0:T(8,128)S(1)}, f32[17,8,128]{2,1,0:T(8,128)S(1)}, f32[2,128]{1,0:T(2,128)S(1)}) custom-call(f32[128,512]{1,0:T(8,128)} %suction.1, f32[128,512]{1,0:T(8,128)} %warmth.1, s32[128,512]{1,0:T(8,128)} %classes.1, f32[1,512]{1,0:T(1,128)} %bitcast.3, s32[2,128]{1,0:T(2,128)} %couplings.1, f32[1,8]{1,0:T(1,128)} %bitcast.4, ...), custom_call_target="tpu_custom_call" | custom-call | flops 2000000 | bytes 2000000 | tf_op jit(solution)/shard_map/pack/pallas_call | solution.py:647
  2.2 20.1 %all_to_all.10.got = f32[16,13,8,128]{3,2,1,0:T(8,128)S(1)} all-to-all(f32[16,13,8,128]{3,2,1,0:T(8,128)S(1)} %get-tuple-element.74), channel_id=1, replica_groups={{0,1,2,3,4,5,6,7,8,9,10,11,12,13,14,15},{16,17,18,19,20,21,22,23,24,25,..., dimensions={0} | all-to-all | bytes 1703936 | tf_op jit(solution)/shard_map/all_to_all | solution.py:661
  22.4 0.3 edges.3
  22.7 2.6 %collective-permute-start.2 = (f32[3,7,8,128]{3,2,1,0:T(8,128)S(1)}, f32[3,7,8,128]{3,2,1,0:T(8,128)S(1)}, u32[]{:S(2)}, u32[]{:S(2)}) collective-permute-start(f32[3,7,8,128]{3,2,1,0:T(8,128)S(1)} %get-tuple-element.128), channel_id=1, source_target_pairs={{0,16},{16,0},{1,17},{17,1},{2,18},{18,2},{3,19},{19,3},{4,20},{20... | collective-permute-start | bytes 258056 | tf_op jit(solution)/shard_map/ppermute | solution.py:671
  25.3 0.3 edges.2
  25.6 0.4 collective-permute-start
  26.0 0.3 masks.1.refs_0_
  26.3 0.4 first.3
  26.7 0.8 %team.6 = (f32[8,8,512]{2,1,0:T(8,128)S(1)}, f32[8,8,512]{2,1,0:T(8,128)S(1)}) custom-call(f32[22,8,128]{2,1,0:T(8,128)S(1)} %masks.1.refs_0_, f32[8,8,512]{2,1,0:T(8,128)S(1)} %get-tuple-element.110.head.refs_1_, f32[8,8,512]{2,1,0:T(8,128)S(1)} %get-tuple-element.111.warm.refs_2_, f32[8,8,512]{2,1,0:T(8,128)S(1)} %get-tuple-element.117.cond), custom_call_target="tpu_custom_call" | custom-call | flops 2000000 | bytes 2000000 | tf_op jit(solution)/shard_map/team/pallas_call | solution.py:647
  27.5 0.2 factor.6
  27.7 0.4 first.2
  28.1 0.8 %team.4 = (f32[8,8,512]{2,1,0:T(8,128)S(1)}, f32[8,8,512]{2,1,0:T(8,128)S(1)}) custom-call(f32[22,8,128]{2,1,0:T(8,128)S(1)} %masks.1.refs_0_, f32[8,8,512]{2,1,0:T(8,128)S(1)} %get-tuple-element.76.head.refs_1_, f32[8,8,512]{2,1,0:T(8,128)S(1)} %get-tuple-element.77.warm.refs_2_, f32[8,8,512]{2,1,0:T(8,128)S(1)} %get-tuple-element.83.cond), custom_call_target="tpu_custom_call" | custom-call | flops 2000000 | bytes 2000000 | tf_op jit(solution)/shard_map/team/pallas_call | solution.py:647
  28.9 0.2 factor.4
  29.1 2.8 %collective-permute-done.2.refs_16_.refs_17_ = f32[3,7,8,128]{3,2,1,0:T(8,128)S(1)} collective-permute-done((f32[3,7,8,128]{3,2,1,0:T(8,128)S(1)}, f32[3,7,8,128]{3,2,1,0:T(8,128)S(1)}, u32[]{:S(2)}, u32[]{:S(2)}) %collective-permute-start.2) | collective-permute-done | bytes 86048 | tf_op jit(solution)/shard_map/ppermute | solution.py:671
  31.9 0.9 %middle.3 = (f32[8,8,512]{2,1,0:T(8,128)S(1)}, f32[8,8,512]{2,1,0:T(8,128)S(1)}, f32[8,8,512]{2,1,0:T(8,128)S(1)}, f32[8,8,512]{2,1,0:T(8,128)S(1)}, f32[8,8,512...) custom-call(f32[22,8,128]{2,1,0:T(8,128)S(1)} %masks.1.refs_0_, ...), custom_call_target="tpu_custom_call" | custom-call | flops 2000000 | bytes 2000000 | tf_op jit(solution)/shard_map/middle/pallas_call | solution.py:647
  32.8 0.1 collective-permute-start.3
  32.8 0.1 collective-permute-done.refs_16_.refs_17_
  32.9 0.9 %middle.2 = (f32[8,8,512]{2,1,0:T(8,128)S(1)}, f32[8,8,512]{2,1,0:T(8,128)S(1)}, f32[8,8,512]{2,1,0:T(8,128)S(1)}, f32[8,8,512]{2,1,0:T(8,128)S(1)}, f32[8,8,512...) custom-call(f32[22,8,128]{2,1,0:T(8,128)S(1)} %masks.1.refs_0_, ...), custom_call_target="tpu_custom_call" | custom-call | flops 2000000 | bytes 2000000 | tf_op jit(solution)/shard_map/middle/pallas_call | solution.py:647
  33.9 2.9 %collective-permute-start.1 = (f32[2,7,8,128]{3,2,1,0:T(8,128)S(1)}, f32[2,7,8,128]{3,2,1,0:T(8,128)S(1)}, u32[]{:S(2)}, u32[]{:S(2)}) collective-permute-start(f32[2,7,8,128]{3,2,1,0:T(8,128)S(1)} %get-tuple-element.109), channel_id=1, source_target_pairs={{0,16},{16,0},{1,17},{17,1},{2,18},{18,2},{3,19},{19,3},{4,20},{20... | collective-permute-start | bytes 172040 | tf_op jit(solution)/shard_map/ppermute | solution.py:671
  36.7 0.8 %team.7 = (f32[8,8,512]{2,1,0:T(8,128)S(1)}, f32[8,8,512]{2,1,0:T(8,128)S(1)}) custom-call(f32[22,8,128]{2,1,0:T(8,128)S(1)} %masks.1.refs_0_, f32[8,8,512]{2,1,0:T(8,128)S(1)} %get-tuple-element.129.head.refs_1_, f32[8,8,512]{2,1,0:T(8,128)S(1)} %get-tuple-element.130.warm.refs_2_, f32[8,8,512]{2,1,0:T(8,128)S(1)} %get-tuple-element.132.cond), custom_call_target="tpu_custom_call" | custom-call | flops 2000000 | bytes 2000000 | tf_op jit(solution)/shard_map/team/pallas_call | solution.py:647
  37.5 0.2 factor.7
  37.7 0.8 %team.5 = (f32[8,8,512]{2,1,0:T(8,128)S(1)}, f32[8,8,512]{2,1,0:T(8,128)S(1)}) custom-call(f32[22,8,128]{2,1,0:T(8,128)S(1)} %masks.1.refs_0_, f32[8,8,512]{2,1,0:T(8,128)S(1)} %get-tuple-element.95.head.refs_1_, f32[8,8,512]{2,1,0:T(8,128)S(1)} %get-tuple-element.96.warm.refs_2_, f32[8,8,512]{2,1,0:T(8,128)S(1)} %get-tuple-element.98.cond), custom_call_target="tpu_custom_call" | custom-call | flops 2000000 | bytes 2000000 | tf_op jit(solution)/shard_map/team/pallas_call | solution.py:647
  38.5 0.2 factor.5
  38.7 0.0 collective-permute-done.3.refs_15_
  38.7 0.9 %last.2.refs_18_ = f32[16,4,8,128]{3,2,1,0:T(8,128)S(1)} custom-call(f32[22,8,128]{2,1,0:T(8,128)S(1)} %masks.1.refs_0_, f32[8,8,512]{2,1,0:T(8,128)S(1)} %get-tuple-element.129.head.refs_1_, f32[8,8,512]{2,1,0:T(8,128)S(1)} %get-tuple-element.130.warm.refs_2_, f32[8,8,512]{2,1,0:T(8,128)S(1)} %get-tuple-element.113.refs_4_.refs_3_, ...), custom_call_target="tpu_custom_call" | custom-call | flops 2000000 | bytes 2000000 | tf_op jit(solution)/shard_map/last/pallas_call | solution.py:647
  39.6 0.2 collective-permute-done.1.refs_15_
  39.8 0.9 %last.3 = f32[16,8,8,128]{3,2,1,0:T(8,128)S(1)} custom-call(f32[22,8,128]{2,1,0:T(8,128)S(1)} %masks.1.refs_0_, f32[8,8,512]{2,1,0:T(8,128)S(1)} %get-tuple-element.95.head.refs_1_, f32[8,8,512]{2,1,0:T(8,128)S(1)} %get-tuple-element.96.warm.refs_2_, f32[8,8,512]{2,1,0:T(8,128)S(1)} %get-tuple-element.79.refs_4_.refs_3_, ...), custom_call_target="tpu_custom_call" | custom-call | flops 2000000 | bytes 2000000 | tf_op jit(solution)/shard_map/last/pallas_call | solution.py:647
  40.7 14.6 %all_to_all.11.got = f32[16,8,8,128]{3,2,1,0:T(8,128)S(1)} all-to-all(f32[16,8,8,128]{3,2,1,0:T(8,128)S(1)} %last.3), channel_id=1, replica_groups={{0,1,2,3,4,5,6,7,8,9,10,11,12,13,14,15},{16,17,18,19,20,21,22,23,24,25,..., dimensions={0} | all-to-all | bytes 1048576 | tf_op jit(solution)/shard_map/all_to_all | solution.py:661
  55.3 0.9 %unpack.1 = (f32[128,512]{1,0:T(8,128)}, f32[128,512]{1,0:T(8,128)}) custom-call(f32[16,8,8,128]{3,2,1,0:T(8,128)S(1)} %all_to_all.11.got), custom_call_target="tpu_custom_call" | custom-call | flops 2000000 | bytes 2000000 | tf_op jit(solution)/shard_map/unpack/pallas_call | solution.py:647
Async XLA Ops:
  22.7 9.2 %collective-permute-start.2 = (f32[3,7,8,128]{3,2,1,0:T(8,128)S(1)}, f32[3,7,8,128]{3,2,1,0:T(8,128)S(1)}, u32[]{:S(2)}, u32[]{:S(2)}) collective-permute-start(f32[3,7,8,128]{3,2,1,0:T(8,128)S(1)} %get-tuple-element.128), channel_id=1, source_target_pairs={{0,16},{16,0},{1,17},{17,1},{2,18},{18,2},{3,19},{19,3},{4,20},{20... | collective-permute-start | bytes 258056 | tf_op jit(solution)/shard_map/ppermute | solution.py:671
  25.6 7.3 %collective-permute-start = (f32[3,7,8,128]{3,2,1,0:T(8,128)S(1)}, f32[3,7,8,128]{3,2,1,0:T(8,128)S(1)}, u32[]{:S(2)}, u32[]{:S(2)}) collective-permute-start(f32[3,7,8,128]{3,2,1,0:T(8,128)S(1)} %get-tuple-element.94), channel_id=1, source_target_pairs={{0,16},{16,0},{1,17},{17,1},{2,18},{18,2},{3,19},{19,3},{4,20},{20... | collective-permute-start | bytes 258056 | tf_op jit(solution)/shard_map/ppermute | solution.py:671
  32.8 6.0 %collective-permute-start.3 = (f32[2,7,8,128]{3,2,1,0:T(8,128)S(1)}, f32[2,7,8,128]{3,2,1,0:T(8,128)S(1)}, u32[]{:S(2)}, u32[]{:S(2)}) collective-permute-start(f32[2,7,8,128]{3,2,1,0:T(8,128)S(1)} %get-tuple-element.143), channel_id=1, source_target_pairs={{0,16},{16,0},{1,17},{17,1},{2,18},{18,2},{3,19},{19,3},{4,20},{20... | collective-permute-start | bytes 172040 | tf_op jit(solution)/shard_map/ppermute | solution.py:671
  33.9 6.0 %collective-permute-start.1 = (f32[2,7,8,128]{3,2,1,0:T(8,128)S(1)}, f32[2,7,8,128]{3,2,1,0:T(8,128)S(1)}, u32[]{:S(2)}, u32[]{:S(2)}) collective-permute-start(f32[2,7,8,128]{3,2,1,0:T(8,128)S(1)} %get-tuple-element.109), channel_id=1, source_target_pairs={{0,16},{16,0},{1,17},{17,1},{2,18},{18,2},{3,19},{19,3},{4,20},{20... | collective-permute-start | bytes 172040 | tf_op jit(solution)/shard_map/ppermute | solution.py:671
